TPU v7x, 32 devices: a whole 2x2x4 slice. The times are simulated.
32 devices in a mesh: ha: 2 (over x), wa: 4 (over y, core), ba: 4 (over z).
Axes of the slice: x: 2, y: 2, z: 4, core: 2. Of those that a mesh axis runs over, the one named last changes fastest.
Arguments:
- images: bfloat16 [128, 8, 8, 512], P(('ha', 'wa', 'ba')), may hold values from -6 to 6
- valid_masks: int32 [128, 8, 8], P(('ha', 'wa', 'ba')), may hold values from 0 to 1, as said below
- cotangent: bfloat16 [128, 8, 8, 512], P(('ha', 'wa', 'ba')), may hold values from -6 to 6
- conv_weights: float32 [2, 9, 512, 512], P(None, None, ('ha', 'wa'), 'ba'), may hold values from -0.09375 to 0.09375
- conv_first: float32 [2, 9, 512, 512], P(None, None, ('ha', 'wa'), 'ba'), as said below
- conv_second: float32 [2, 9, 512, 512], P(None, None, ('ha', 'wa'), 'ba'), as said below
- norm_params: float32 [4, 512], replicated, may hold values from 0.3 to 1.3
- norm_first: float32 [4, 512], replicated, may hold values from -117.66257 to 117.66257
- norm_second: float32 [4, 512], replicated, may hold values from 819.2 to 3276.8
Outputs:
- block_output: bfloat16 [128, 8, 8, 512], P(('ha', 'wa', 'ba'))
- input_grad: bfloat16 [128, 8, 8, 512], P(('ha', 'wa', 'ba'))
- new_weights: float32 [2, 9, 512, 512], P(None, None, ('ha', 'wa'), 'ba')
- weight_copies: bfloat16 [2, 9, 512, 512], P(None, None, ('ha', 'wa'), 'ba')
- conv_first_new: float32 [2, 9, 512, 512], P(None, None, ('ha', 'wa'), 'ba')
- conv_second_new: float32 [2, 9, 512, 512], P(None, None, ('ha', 'wa'), 'ba')
- new_norm_params: float32 [4, 512], replicated
- norm_first_new: float32 [4, 512], replicated
- norm_second_new: float32 [4, 512], replicated
- trust_norms: float32 [2, 6], replicated
Inputs may be any that keep to these rules, and one draw needn't show every extreme that they name: `valid_masks`: each image's valid pixels form a top-left rectangle of 1 to 8 rows and 1 to 8 columns; image 0 is whole. `conv_first`: of both signs, of the size of the kernels' gradients. `conv_second`: Positive, of the size of the squared kernels' gradients.
All inputs are finite; a program needn't handle non-finite values.
Results may differ from a plain program's by a relative error of at most 0.0039.
The roundings to bfloat16 on the way count: a program that leaves them out, or rounds other values in their place, can miss the bound.
Values may be sent and summed in bfloat16 or wider, within the bound.
No kernel may reach another device: no remote copies, remote signals or barrier semaphores. Data moves between devices by JAX's collectives and lax.ppermute only.
A program may use at most 128 MiB of HBM per device.

v0:
```python
import jax
import jax.numpy as jnp
from jax import lax
from jax.sharding import PartitionSpec as P

STEP = 3


learning_rate = 0.5
weight_decay = 0.01
beta_moment = 0.5


def gelu_slope(value, upstream):
    return jax.vjp(jax.nn.gelu, value)[1](upstream)[0]


def make_taps(feature, mirror):
    map_rows = feature.shape[1]
    breadth = feature.shape[2]
    padded = jnp.pad(feature, ((0, 0), (1, 1), (1, 1), (0, 0)))
    pieces = []
    for position in range(9):
        down_step = position // 3
        side_step = position % 3
        if mirror:
            down_step = 2 - down_step
            side_step = 2 - side_step
        pieces.append(
            padded[:, down_step : down_step + map_rows, side_step : side_step + breadth, :]
        )
    stacked = jnp.stack(pieces, axis=3)
    return stacked.reshape(-1, 9, feature.shape[3])


def norm_forward(conv_out, valid_mask, gain_row, shift_row):
    valid_count, valid_total = lax.psum(
        (jnp.sum(valid_mask), jnp.sum(valid_mask * conv_out, axis=0)), ("ha", "wa", "ba")
    )
    mean_value = valid_total / valid_count
    centered = conv_out - mean_value
    spread = lax.psum(jnp.sum(valid_mask * centered * centered, axis=0), ("ha", "wa", "ba"))
    variance = spread / valid_count
    inv_std = lax.rsqrt(variance + 1e-05)
    normed = centered * inv_std
    return (valid_mask * (gain_row * normed + shift_row), normed, inv_std, valid_count)


def norm_backward(upstream, valid_mask, normed, inv_std, valid_count, gain_row):
    masked = valid_mask * upstream
    shift_grad, gain_grad = lax.psum(
        (jnp.sum(masked, axis=0), jnp.sum(masked * normed, axis=0)), ("ha", "wa", "ba")
    )
    conv_grad = (
        inv_std
        * valid_mask
        * gain_row
        * (upstream - (shift_grad + normed * gain_grad) / valid_count)
    )
    return (conv_grad, gain_grad, shift_grad)


def lamb_direction(gradient, first_moment, second_moment, param_value, decay_rate):
    new_first = beta_moment * first_moment + (1.0 - beta_moment) * gradient
    new_second = beta_moment * second_moment + (1.0 - beta_moment) * gradient * gradient
    bias_first = 1.0 - beta_moment**STEP
    bias_second = 1.0 - beta_moment**STEP
    direction = (
        new_first / bias_first / (jnp.sqrt(new_second / bias_second) + 1e-06)
        + decay_rate * param_value
    )
    return (new_first, new_second, direction)


def shards(
    images,
    valid_masks,
    cotangent,
    conv_weights,
    conv_first,
    conv_second,
    norm_params,
    norm_first,
    norm_second,
):
    count_images, map_rows, breadth, channels = images.shape
    pixels = count_images * map_rows * breadth
    valid_mask = valid_masks.reshape(pixels, 1).astype(jnp.float32)
    low_weights = conv_weights.astype(jnp.bfloat16)
    kernels = lax.all_gather(
        lax.all_gather(low_weights, "ba", axis=3, tiled=True), ("ha", "wa"), axis=2, tiled=True
    )
    taps_input = make_taps(images, False)
    first_out = jnp.einsum(
        "pki,kio->po", taps_input, kernels[0], preferred_element_type=jnp.float32
    )
    first_act, first_normed, first_inv, valid_count = norm_forward(
        first_out, valid_mask, norm_params[0], norm_params[1]
    )
    hidden_low = (
        jax.nn.gelu(first_act)
        .astype(jnp.bfloat16)
        .reshape(count_images, map_rows, breadth, channels)
    )
    taps_hidden = make_taps(hidden_low, False)
    second_out = jnp.einsum(
        "pki,kio->po", taps_hidden, kernels[1], preferred_element_type=jnp.float32
    )
    second_act, second_normed, second_inv, unused_count = norm_forward(
        second_out, valid_mask, norm_params[2], norm_params[3]
    )
    summed = second_act + images.reshape(pixels, channels).astype(jnp.float32)
    block_output = jax.nn.gelu(summed).astype(jnp.bfloat16).reshape(images.shape)
    upstream = gelu_slope(summed, cotangent.reshape(pixels, channels).astype(jnp.float32))
    second_grad, gain_two, shift_two = norm_backward(
        upstream, valid_mask, second_normed, second_inv, valid_count, norm_params[2]
    )
    second_low = second_grad.astype(jnp.bfloat16)
    weight_two = jnp.einsum(
        "pki,po->kio", taps_hidden, second_low, preferred_element_type=jnp.float32
    )
    back_kernels = lax.all_gather(
        lax.all_gather(low_weights, "ba", axis=3, tiled=True), ("ha", "wa"), axis=2, tiled=True
    )
    second_taps = make_taps(second_low.reshape(count_images, map_rows, breadth, channels), True)
    hidden_grad = jnp.einsum(
        "pko,kio->pi", second_taps, back_kernels[1], preferred_element_type=jnp.float32
    )
    first_up = gelu_slope(first_act, hidden_grad)
    first_grad, gain_one, shift_one = norm_backward(
        first_up, valid_mask, first_normed, first_inv, valid_count, norm_params[0]
    )
    first_low = first_grad.astype(jnp.bfloat16)
    weight_one = jnp.einsum(
        "pki,po->kio", taps_input, first_low, preferred_element_type=jnp.float32
    )
    first_taps = make_taps(first_low.reshape(count_images, map_rows, breadth, channels), True)
    input_full = (
        jnp.einsum("pko,kio->pi", first_taps, back_kernels[0], preferred_element_type=jnp.float32)
        + upstream
    )
    input_grad = input_full.astype(jnp.bfloat16).reshape(images.shape)
    full_grads = jnp.stack([weight_one, weight_two])
    partial_value = lax.psum_scatter(full_grads, "ba", scatter_dimension=3, tiled=True)
    grad_shard = lax.psum_scatter(partial_value, ("ha", "wa"), scatter_dimension=2, tiled=True)
    new_first, new_second, direction = lamb_direction(
        grad_shard, conv_first, conv_second, conv_weights, weight_decay
    )
    weight_sq, direction_sq = lax.psum(
        (
            jnp.sum(conv_weights * conv_weights, axis=(1, 2, 3)),
            jnp.sum(direction * direction, axis=(1, 2, 3)),
        ),
        ("ha", "wa", "ba"),
    )
    weight_norm = jnp.sqrt(weight_sq)
    direction_norm = jnp.sqrt(direction_sq)
    new_weights = (
        conv_weights
        - learning_rate * (weight_norm / (direction_norm + 1e-06))[:, None, None, None] * direction
    )
    param_grad = jnp.stack([gain_one, shift_one, gain_two, shift_two])
    param_first, param_second, param_direction = lamb_direction(
        param_grad, norm_first, norm_second, norm_params, 0.0
    )
    param_norm = jnp.sqrt(jnp.sum(norm_params * norm_params, axis=1))
    param_dir_norm = jnp.sqrt(jnp.sum(param_direction * param_direction, axis=1))
    new_params = (
        norm_params
        - learning_rate * (param_norm / (param_dir_norm + 1e-06))[:, None] * param_direction
    )
    trust_norms = jnp.stack(
        [
            jnp.concatenate([weight_norm, param_norm]),
            jnp.concatenate([direction_norm, param_dir_norm]),
        ]
    )
    return (
        block_output,
        input_grad,
        new_weights,
        new_weights.astype(jnp.bfloat16),
        new_first,
        new_second,
        new_params,
        param_first,
        param_second,
        trust_norms,
    )


def solution(mesh):
    placed = (
        P(("ha", "wa", "ba"), None, None, None),
        P(("ha", "wa", "ba"), None, None),
        P(("ha", "wa", "ba"), None, None, None),
        P(None, None, ("ha", "wa"), "ba"),
        P(None, None, ("ha", "wa"), "ba"),
        P(None, None, ("ha", "wa"), "ba"),
        P(),
        P(),
        P(),
    )
    return jax.shard_map(
        shards,
        mesh=mesh,
        in_specs=placed,
        out_specs=(
            P(("ha", "wa", "ba"), None, None, None),
            P(("ha", "wa", "ba"), None, None, None),
            P(None, None, ("ha", "wa"), "ba"),
            P(None, None, ("ha", "wa"), "ba"),
            P(None, None, ("ha", "wa"), "ba"),
            P(None, None, ("ha", "wa"), "ba"),
            P(),
            P(),
            P(),
            P(),
        ),
        check_vma=False,
    )
```

profile of v0, /device:TPU:0, one launch (start us, length us, event | category | flops | bytes accessed | tf_op | source)
XLA Modules:
  0.0 810.2 jit_solution(374338124485680552)
XLA Ops:
  7.2 0.0 copy-start.9
  7.2 0.0 copy-start.2
  7.2 0.0 all-gather.3.cloned.1.call-start
  7.2 1.9 convert_element_type.52
  9.1 0.0 all-gather.3.cloned.1.call-update
  9.1 0.0 all-gather.5.cloned.1.call-start
  9.2 35.5 %all-gather.3.cloned.1.call-done = bf16[2,9,64,512]{3,2,1,0:T(8,128)(2,1)} async-done(((bf16[2,9,64,128]{3,2,1,0:T(8,128)(2,1)}), bf16[2,9,64,512]{3,2,1,0:T(8,128)(2,1)}) %all-gather.3.cloned.1.call-update) | async-done | bytes 1179664 | tf_op jit(solution)/shard_map/all_gather | solution.py:91
  44.7 0.0 all-gather.5.cloned.1.call-update
  44.7 0.0 reduce-scatter.3.cloned.1.call-start
  44.7 0.0 copy-done.9
  44.8 0.1 convert_element_type.51
  44.9 0.6 convert_reduce_fusion
  45.5 0.0 copy-done.2
  45.5 0.2 pad_slice_fusion.24
  45.7 0.0 copy-start.8
  46.0 0.4 copy-done.8
  46.4 57.4 %all-gather.5.cloned.1.call-done = bf16[2,9,512,512]{3,2,1,0:T(8,128)(2,1)} async-done(((bf16[2,9,64,512]{3,2,1,0:T(8,128)(2,1)}), bf16[2,9,512,512]{3,2,1,0:T(8,128)(2,1)}) %all-gather.5.cloned.1.call-update) | async-done | bytes 9437200 | tf_op jit(solution)/shard_map/all_gather | solution.py:90
  103.8 3.7 multiply_reduce_fusion.5
  107.5 39.6 %all-reduce.7 = (f32[512]{0:T(512)S(1)}, f32[]{:T(128)}) all-reduce(f32[512]{0:T(512)S(1)} %get-tuple-element.77, f32[]{:T(128)} %convert_reduce_fusion), channel_id=1, replica_groups=mesh['ha'=2,'wa'=4,'ba'=4] {'ha','wa','ba'}, use_global_device_ids=true, to_apply=%region_1.2 | all-reduce | flops 513 | bytes 4104 | tf_op jit(solution)/shard_map/psum | solution.py:37
  147.1 0.6 broadcast_divide_fusion.1
  147.8 0.1 fusion.26
  147.9 41.2 %psum.82 = f32[512]{0:T(512)S(1)} all-reduce(f32[512]{0:T(512)S(1)} %fusion.26), channel_id=1, replica_groups=mesh['ha'=2,'wa'=4,'ba'=4] {'ha','wa','ba'}, use_global_device_ids=true, to_apply=%region_5.6 | all-reduce | flops 512 | bytes 4096 | tf_op jit(solution)/shard_map/psum | solution.py:42
  189.1 0.7 add_rsqrt_fusion.1
  189.8 0.3 multiply_convert_fusion.3
  190.1 0.2 pad_slice_fusion.16
  190.4 0.3 bitcast_dynamic-update-slice_fusion.2
  190.8 0.0 copy-start.1
  190.8 4.6 multiply_reduce_fusion.4
  195.4 39.1 %psum.83 = f32[512]{0:T(512)S(1)} all-reduce(f32[512]{0:T(512)S(1)} %get-tuple-element.79), channel_id=1, replica_groups=mesh['ha'=2,'wa'=4,'ba'=4] {'ha','wa','ba'}, use_global_device_ids=true, to_apply=%region_7.8 | all-reduce | flops 512 | bytes 4096 | tf_op jit(solution)/shard_map/psum | solution.py:37
  234.6 0.6 broadcast_divide_fusion
  235.2 0.1 fusion.27
  235.3 41.0 %psum.84 = f32[512]{0:T(512)S(1)} all-reduce(f32[512]{0:T(512)S(1)} %fusion.27), channel_id=1, replica_groups=mesh['ha'=2,'wa'=4,'ba'=4] {'ha','wa','ba'}, use_global_device_ids=true, to_apply=%region_9.10 | all-reduce | flops 512 | bytes 4096 | tf_op jit(solution)/shard_map/psum | solution.py:42
  276.4 0.7 add_rsqrt_fusion
  277.0 2.6 multiply_reduce_fusion.7
  279.6 39.1 %all-reduce.6 = (f32[512]{0:T(512)S(1)}, f32[512]{0:T(512)S(1)}) all-reduce(f32[512]{0:T(512)S(1)} %get-tuple-element.15, f32[512]{0:T(512)S(1)} %get-tuple-element.14), channel_id=1, replica_groups=mesh['ha'=2,'wa'=4,'ba'=4] {'ha','wa','ba'}, use_global_device_ids=true, to_apply=%region_13.14 | all-reduce | flops 1024 | bytes 8192 | tf_op jit(solution)/shard_map/psum | solution.py:51
  318.7 1.9 multiply_convert_fusion.1
  320.5 6.7 convolution_bitcast_fusion
  327.3 0.2 pad_slice_fusion.8
  327.8 4.9 multiply_reduce_fusion.6
  332.7 41.1 %all-reduce.5 = (f32[512]{0:T(512)S(1)}, f32[512]{0:T(512)S(1)}) all-reduce(f32[512]{0:T(512)S(1)} %get-tuple-element.13, f32[512]{0:T(512)S(1)} %get-tuple-element.12), channel_id=1, replica_groups=mesh['ha'=2,'wa'=4,'ba'=4] {'ha','wa','ba'}, use_global_device_ids=true, to_apply=%region_17.18 | all-reduce | flops 1024 | bytes 8192 | tf_op jit(solution)/shard_map/psum | solution.py:51
  373.8 1.9 multiply_convert_fusion
  375.7 1.4 convolution_bitcast_fusion.1
  377.1 11.2 %pad_maximum_fusion = f32[2,9,512,512]{3,2,1,0:T(8,128)} fusion(f32[1,9,512,512]{3,2,1,0:T(8,128)} %convolution_bitcast_fusion, f32[1,9,512,512]{3,2,1,0:T(8,128)S(1)} %convolution_bitcast_fusion.1), kind=kLoop, calls=%fused_computation | loop fusion | flops 4718592 | bytes 37748736 | tf_op jit(solution)/shard_map/stack | solution.py:143
  388.3 0.0 reduce-scatter.3.cloned.1.call-update
  388.3 0.0 reduce-scatter.5.cloned.1.call-start
  388.3 313.7 %reduce-scatter.3.cloned.1.call-done = f32[2,9,512,128]{3,2,1,0:T(8,128)} async-done(((f32[2,9,512,512]{3,2,1,0:T(8,128)}), f32[2,9,512,128]{3,2,1,0:T(8,128)}) %reduce-scatter.3.cloned.1.call-update) | async-done | bytes 4718608 | tf_op jit(solution)/shard_map/reduce_scatter | solution.py:144
  702.0 0.0 reduce-scatter.5.cloned.1.call-update
  702.0 0.2 pad_slice_fusion
  702.2 0.0 copy-start.10
  702.2 0.0 copy-start.11
  702.3 0.0 copy-start.5
  702.5 0.4 copy-done.10
  702.9 0.0 copy-done.11
  702.9 0.8 multiply_reduce_fusion.8
  703.7 0.7 multiply_subtract_fusion.1
  704.4 4.6 fusion.9
  709.0 51.7 %reduce-scatter.5.cloned.1.call-done = f32[2,9,64,128]{3,2,1,0:T(8,128)} async-done(((f32[2,9,512,128]{3,2,1,0:T(8,128)}), f32[2,9,64,128]{3,2,1,0:T(8,128)}) %reduce-scatter.5.cloned.1.call-update) | async-done | bytes 589840 | tf_op jit(solution)/shard_map/reduce_scatter | solution.py:145
  760.7 0.0 copy-done
  760.7 1.6 multiply_reduce_fusion.1
  762.4 39.3 %all-reduce.4 = (f32[2]{0:T(128)S(1)}, f32[2]{0:T(128)S(1)}) all-reduce(f32[2]{0:T(128)S(1)} %get-tuple-element.11, f32[2]{0:T(128)S(1)} %get-tuple-element.10), channel_id=1, replica_groups=mesh['ha'=2,'wa'=4,'ba'=4] {'ha','wa','ba'}, use_global_device_ids=true, to_apply=%region_23.24 | all-reduce | flops 4 | bytes 32 | tf_op jit(solution)/shard_map/psum | solution.py:149
  801.7 0.1 maximum_bitcast_fusion
  801.8 0.6 pad_maximum_fusion.2
  802.4 1.3 fusion.34
  803.6 0.0 copy-done.3
  (49 shorter events, 0.7 us)
Async XLA Ops:
  7.2 37.6 %copy-start.9 = (s32[4,8,8]{2,1,0:T(8,128)S(1)}, s32[4,8,8]{2,1,0:T(8,128)}, u32[]{:S(2)}) copy-start(s32[4,8,8]{2,1,0:T(8,128)} %param.10) | copy-start | bytes 3076
  7.2 38.3 %copy-start.2 = (bf16[4,8,8,512]{3,2,1,0:T(8,128)(2,1)S(1)}, bf16[4,8,8,512]{3,2,1,0:T(8,128)(2,1)}, u32[]{:S(2)}) copy-start(bf16[4,8,8,512]{3,2,1,0:T(8,128)(2,1)} %param.9) | copy-start | bytes 786436
  7.2 37.5 %all-gather.3.cloned.1.call-start = ((), (), s32[]{:S(2)}) async-start(), calls=%async_computation.2 | async-start | bytes 1474560 | tf_op jit(solution)/shard_map/all_gather | solution.py:91
  9.1 94.6 %all-gather.5.cloned.1.call-start = ((), (), s32[]{:S(2)}) async-start(), calls=%async_computation.3 | async-start | bytes 10616832 | tf_op jit(solution)/shard_map/all_gather | solution.py:90
  44.7 657.3 %reduce-scatter.3.cloned.1.call-start = ((), (), s32[]{:S(2)}) async-start(), calls=%async_computation.4 | async-start | bytes 23592960 | tf_op jit(solution)/shard_map/reduce_scatter | solution.py:144
  45.7 0.7 copy-start.8
  190.8 4.6 copy-start.1
  388.3 372.4 %reduce-scatter.5.cloned.1.call-start = ((), (), s32[]{:S(2)}) async-start(), calls=%async_computation.5 | async-start | bytes 5308416 | tf_op jit(solution)/shard_map/reduce_scatter | solution.py:145
  702.2 0.7 copy-start.10
  702.2 0.7 copy-start.11
  702.3 2.2 copy-start.5
  704.4 56.3 %copy-start = (f32[2,9,64,128]{3,2,1,0:T(8,128)S(1)}, f32[2,9,64,128]{3,2,1,0:T(8,128)}, u32[]{:S(2)}) copy-start(f32[2,9,64,128]{3,2,1,0:T(8,128)} %param.12) | copy-start | bytes 1769476
  704.4 56.3 %copy-start.6 = (f32[2,9,64,128]{3,2,1,0:T(8,128)S(1)}, f32[2,9,64,128]{3,2,1,0:T(8,128)}, u32[]{:S(2)}) copy-start(f32[2,9,64,128]{3,2,1,0:T(8,128)} %param.13) | copy-start | bytes 1769476
  704.4 56.3 %copy-start.7 = (f32[2,9,64,128]{3,2,1,0:T(8,128)S(1)}, f32[2,9,64,128]{3,2,1,0:T(8,128)}, u32[]{:S(2)}) copy-start(f32[2,9,64,128]{3,2,1,0:T(8,128)} %param.14) | copy-start | bytes 1769476
  762.4 41.3 %copy-start.3 = (f32[2,9,64,128]{3,2,1,0:T(8,128)}, f32[2,9,64,128]{3,2,1,0:T(8,128)S(1)}, u32[]{:S(2)}) copy-start(f32[2,9,64,128]{3,2,1,0:T(8,128)S(1)} %get-tuple-element.30) | copy-start | bytes 1769476
  762.4 41.3 %copy-start.4 = (f32[2,9,64,128]{3,2,1,0:T(8,128)}, f32[2,9,64,128]{3,2,1,0:T(8,128)S(1)}, u32[]{:S(2)}) copy-start(f32[2,9,64,128]{3,2,1,0:T(8,128)S(1)} %get-tuple-element.31) | copy-start | bytes 1769476
Sparse Core Ops, SparseCore 0:
  10.2 34.4 all-gather.2
  46.6 57.1 all-gather.4
  388.4 313.5 reduce-scatter.2
  705.7 54.9 reduce-scatter.4
where the time goes:
time: 812 us; the launch traced here: 810 us
  waiting for transfers between devices  458 us (56%)
  blocking collectives  280 us (34%)
  other arithmetic  28.4 us (3%)
  matrix products  26 us (3%)
  between operations  14.3 us (2%)
    reduce_scatter x1, waiting for transfers between devices, shards(): lax.psum_scatter(full_grads, 'ba', scatter_dimension=3, tiled=True)  314 us
    psum x2, blocking collectives, norm_forward(): lax.psum(jnp.sum(valid_mask * centered * centered, axis=0), ('ha', 'wa',...  82.2 us
    psum x2, blocking collectives, norm_backward(): lax.psum((jnp.sum(masked, axis=0), jnp.sum(masked * normed, axis=0)), ('h...  80.2 us
    psum x2, blocking collectives, norm_forward(): lax.psum((jnp.sum(valid_mask), jnp.sum(valid_mask * conv_out, axis=0)), (...  78.7 us
    all_gather x1, waiting for transfers between devices, shards(): lax.all_gather(lax.all_gather(low_weights, 'ba', axis=3, tiled=True), ('h...  57.4 us
    reduce_scatter x1, waiting for transfers between devices, shards(): lax.psum_scatter(partial_value, ('ha', 'wa'), scatter_dimension=2, tiled=...  51.7 us
    psum x1, blocking collectives, shards(): lax.psum((jnp.sum(conv_weights * conv_weights, axis=(1, 2, 3)), jnp.sum(d...  39.3 us
    all_gather x1, waiting for transfers between devices, shards(): lax.all_gather(low_weights, 'ba', axis=3, tiled=True)  35.5 us
  transfers between devices with their start and end apart: 4, of which 4 were waited for; matrix products, arithmetic and copies ran while one was open for 1% of the time, Pallas kernels for 0%

commit v1 on v0

v1 whole, which is shorter than its diff:
```python
import functools

import jax
import jax.numpy as jnp
from jax import lax
from jax.experimental import pallas as pl
from jax.experimental.pallas import tpu as pltpu
from jax.sharding import Mesh
from jax.sharding import PartitionSpec as P

STEP = 3
RATE = 0.5
DECAY = 0.01
BETA = 0.5
BIAS = 1.0 - BETA**STEP
EPS = 1e-05
TINY = 1e-06
ROOT = 0.7978845608028654
CUBE = 0.044715
LANES = 128
VMEM_BYTES = 56 * 1024 * 1024
F32 = jnp.float32
BF16 = jnp.bfloat16


def gelu(v):
    return 0.5 * v * (1.0 + jnp.tanh(ROOT * (v + CUBE * (v * v * v))))


def gelu_both(v):
    t = jnp.tanh(ROOT * (v + CUBE * (v * v * v)))
    value = 0.5 * v * (1.0 + t)
    slope = 0.5 * (1.0 + t) + 0.5 * v * (1.0 - t * t) * (ROOT * (1.0 + (3.0 * CUBE) * (v * v)))
    return value, slope


class Sizes:
    def __init__(self, mesh, images, weights):
        self.Z = mesh.shape["ba"]
        self.R = mesh.shape["ha"] * mesh.shape["wa"]
        self.Q = self.Z
        self.S = self.R // self.Q
        n, self.H, self.W, self.C = images
        self.n_own = n // (self.R * self.Z)
        self.own = self.n_own * self.H * self.W
        self.n_group = self.n_own * self.Q
        self.G = self.own * self.Q
        self.L = self.C // self.Q
        self.LP = max(self.L, LANES)
        self.IB = self.C // self.R
        self.K = weights[1]


def call(body, out_shape, args, scratch=(), flops=0, nbytes=0):
    smem = [a.dtype == jnp.int32 and a.ndim == 1 for a in args]
    return pl.pallas_call(
        body,
        out_shape=out_shape,
        in_specs=[
            pl.BlockSpec(memory_space=pltpu.SMEM if m else pltpu.VMEM) for m in smem
        ],
        out_specs=jax.tree.map(lambda _: pl.BlockSpec(memory_space=pltpu.VMEM), out_shape),
        scratch_shapes=list(scratch),
        compiler_params=pltpu.CompilerParams(vmem_limit_bytes=VMEM_BYTES),
        cost_estimate=pl.CostEstimate(flops=flops, bytes_accessed=nbytes, transcendentals=0),
    )(*args)


def shape(dims, dtype=F32):
    return jax.ShapeDtypeStruct(tuple(dims), dtype)


def image_mask(z, hw):
    dims = (z.H, z.W, z.L)
    rows = lax.broadcasted_iota(jnp.int32, dims, 0).astype(F32)
    cols = lax.broadcasted_iota(jnp.int32, dims, 1).astype(F32)
    tall = hw[0:1, : z.L].reshape(1, 1, z.L)
    wide = hw[1:2, : z.L].reshape(1, 1, z.L)
    return jnp.where((rows < tall) & (cols < wide), 1.0, 0.0).reshape(z.H * z.W, z.L)


def shifted_sum(z, taps, sign):
    dims = (z.n_own, z.H, z.W, z.L)
    cols = lax.broadcasted_iota(jnp.int32, dims, 2)
    total = None
    for c in range(3):
        column = None
        for r in range(3):
            part = taps(3 * r + c).reshape(dims)
            move = (r - 1) * sign
            if move == 1:
                part = jnp.concatenate([part[:, 1:], jnp.zeros_like(part[:, :1])], axis=1)
            elif move == -1:
                part = jnp.concatenate([jnp.zeros_like(part[:, :1]), part[:, :-1]], axis=1)
            column = part if column is None else column + part
        move = (c - 1) * sign
        if move:
            flat = column.reshape(z.n_own * z.H, z.W, z.L)
            flat = pltpu.roll(flat, (-move) % z.W, 1)
            column = flat.reshape(dims)
            edge = z.W - 1 if move == 1 else 0
            column = jnp.where(cols == edge, 0.0, column)
        total = column if total is None else total + column
    return total.reshape(z.own, z.L)


def moved_taps(z, feature):
    dims = (z.n_own, z.H, z.W, z.L)
    cols = lax.broadcasted_iota(jnp.int32, dims, 2)
    out = [None] * 9
    for c in range(3):
        move = c - 1
        column = feature.reshape(dims)
        if move:
            flat = feature.reshape(z.n_own * z.H, z.W, z.L)
            column = pltpu.roll(flat, (-move) % z.W, 1).reshape(dims)
            edge = z.W - 1 if move == 1 else 0
            column = jnp.where(cols == edge, 0.0, column)
        for r in range(3):
            if r == 2:
                part = jnp.concatenate([column[:, 1:], jnp.zeros_like(column[:, :1])], axis=1)
            elif r == 0:
                part = jnp.concatenate([jnp.zeros_like(column[:, :1]), column[:, :-1]], axis=1)
            else:
                part = column
            out[3 * r + c] = part.reshape(z.own, z.L)
    return out


def spread(ref, rows):
    used = rows[0].shape[1]
    if len(rows) < 8:
        rows = rows + [jnp.zeros((8 - len(rows), used), F32)]
    stat = jnp.concatenate(rows, axis=0)
    if used < LANES:
        stat = jnp.concatenate([stat, jnp.zeros((8, LANES - used), F32)], axis=1)
    for k in range(ref.shape[0]):
        ref[k] = stat


def local_stats(z, z_ref, hw_ref, stats_ref):
    px = z.H * z.W

    def first(n, carry):
        count, total = carry
        mask = image_mask(z, hw_ref[n])
        block = z_ref[pl.ds(pl.multiple_of(n * px, px), px), :]
        return count + jnp.sum(mask, 0, keepdims=True), total + jnp.sum(mask * block, 0, keepdims=True)

    zero = jnp.zeros((1, z.L), F32)
    count, total = lax.fori_loop(0, z.n_group, first, (zero, zero), unroll=4)
    mean = total / count

    def second(n, spread_sum):
        mask = image_mask(z, hw_ref[n])
        centered = z_ref[pl.ds(pl.multiple_of(n * px, px), px), :] - mean
        return spread_sum + jnp.sum(mask * centered * centered, 0, keepdims=True)

    squares = lax.fori_loop(0, z.n_group, second, zero, unroll=4)
    spread(stats_ref, [count, mean, squares])


def conv_into(z, x_of, row_of, wcat, y_ref, z_ref, sign=1):
    for m in range(z.Q):
        y_ref[...] = x_of(m)
        z_ref[pl.ds(row_of(m), z.own), :] = shifted_sum(
            z, lambda k: y_ref[:, k * z.LP : k * z.LP + z.L], sign
        )


def fill_kernels(z, at, own, others, wcat):
    for t, blocks in enumerate([own] + others):
        s = at[1] ^ t
        for m, block in enumerate(blocks):
            row = pl.multiple_of((at[2] ^ m) * z.L + s * z.IB, z.IB)
            for k in range(z.K):
                wcat[pl.ds(row, z.IB), k * z.LP : k * z.LP + z.L] = block[k]


def first_conv(z, *refs):
    at = refs[0]
    xs, refs = refs[1 : 1 + z.Q], refs[1 + z.Q :]
    blocks = [refs[t * z.Z : (t + 1) * z.Z] for t in range(z.S)]
    z_ref, slice_ref, hw_ref, stats_ref, wcat, y_ref = refs[z.S * z.Z :]
    fill_kernels(z, at, blocks[0], list(blocks[1:]), wcat)
    for m in range(z.Q):
        j = at[0] ^ m
        for n in range(z.n_own):
            two = xs[m][z.own + 2 * n : z.own + 2 * n + 2, :LANES].astype(F32)
            hw_ref[j * z.n_own + n] = jnp.concatenate([two, jnp.zeros((6, LANES), F32)], axis=0)
        for slot in range(z.Q):

            @pl.when(at[0] == slot)
            def _(m=m, j=j, slot=slot):
                slice_ref[pl.ds(pl.multiple_of(j * z.own, z.own), z.own), :] = xs[m][
                    : z.own, slot * z.L : (slot + 1) * z.L
                ]

    conv_into(
        z,
        lambda m: jnp.dot(xs[m][: z.own, :], wcat[...], preferred_element_type=F32),
        lambda m: pl.multiple_of((at[0] ^ m) * z.own, z.own),
        wcat,
        y_ref,
        z_ref,
    )
    local_stats(z, z_ref, hw_ref, stats_ref)


def second_conv(z, *refs):
    at = refs[0]
    hs, refs = refs[1 : 1 + z.Q], refs[1 + z.Q :]
    blocks = [refs[t * z.Z : (t + 1) * z.Z] for t in range(z.S)]
    hw_ref, z_ref, stats_ref, wcat, h_ref, y_ref = refs[z.S * z.Z :]
    fill_kernels(z, at, blocks[0], list(blocks[1:]), wcat)
    for m in range(z.Q):
        h_ref[at[0] ^ m] = hs[m][...]

    def product(j):
        rows = slice(j * z.own, (j + 1) * z.own)
        if z.L % LANES == 0:
            whole = jnp.concatenate([h_ref[i, rows, :] for i in range(z.Q)], axis=1)
            return jnp.dot(whole, wcat[...], preferred_element_type=F32)
        return sum(
            jnp.dot(h_ref[i, rows, :], wcat[i * z.L : (i + 1) * z.L, :], preferred_element_type=F32)
            for i in range(z.Q)
        )

    conv_into(z, product, lambda j: j * z.own, wcat, y_ref, z_ref)
    local_stats(z, z_ref, hw_ref, stats_ref)


def merged(z, all_ref):
    counts = [all_ref[k, 0:1, : z.L] for k in range(z.S * z.Z)]
    means = [all_ref[k, 1:2, : z.L] for k in range(z.S * z.Z)]
    count = sum(counts)
    mean = sum(c * m for c, m in zip(counts, means)) / count
    squares = sum(
        all_ref[k, 2:3, : z.L] + counts[k] * (means[k] - mean) * (means[k] - mean)
        for k in range(z.S * z.Z)
    )
    return mean, lax.rsqrt(squares / count + EPS), count


def keep(ref, rows):
    used = rows[0].shape[1]
    ref[...] = jnp.concatenate(rows + [jnp.zeros((8 - len(rows), used), F32)], axis=0)


def over_images(z, step, init=0, unroll=2):
    px = z.H * z.W

    def one(n, carry):
        return step(n, pl.ds(pl.multiple_of(n * px, px), px), carry)

    return lax.fori_loop(0, z.n_group, one, init, unroll=unroll)


def hidden(z, z_ref, all_ref, hw_ref, par_ref, h_ref, sum_ref):
    mean, inv, count = merged(z, all_ref)
    keep(sum_ref, [mean, inv, count])
    gain, shift = par_ref[0:1, :], par_ref[1:2, :]

    def step(n, rows, carry):
        mask = image_mask(z, hw_ref[n])
        act = mask * (gain * ((z_ref[rows, :] - mean) * inv) + shift)
        h_ref[rows, :] = gelu(act).astype(BF16)
        return carry

    over_images(z, step)


def middle(z, at, z_ref, all_ref, hw_ref, par_ref, x_ref, *refs):
    cots, refs = refs[: z.Q], refs[z.Q :]
    outs, refs = refs[: z.Q], refs[z.Q :]
    d_ref, sum_ref, stats_ref = refs
    mean, inv, count = merged(z, all_ref)
    keep(sum_ref, [mean, inv, count])
    gain, shift = par_ref[2:3, :], par_ref[3:4, :]
    px = z.H * z.W
    carry = (jnp.zeros((1, z.L), F32), jnp.zeros((1, z.L), F32))
    for m in range(z.Q):
        j = at[0] ^ m

        def step(n, carry, m=m, j=j):
            near = pl.ds(pl.multiple_of(n * px, px), px)
            far = pl.ds(pl.multiple_of(j * z.own + n * px, px), px)
            mask = image_mask(z, hw_ref[j * z.n_own + n])
            normed = (z_ref[far, :] - mean) * inv
            summed = mask * (gain * normed + shift) + x_ref[far, :].astype(F32)
            value, slope = gelu_both(summed)
            outs[m][near, :] = value.astype(BF16)
            d = cots[m][near, :].astype(F32) * slope
            d_ref[far, :] = d
            masked = mask * d
            return (
                carry[0] + jnp.sum(masked, 0, keepdims=True),
                carry[1] + jnp.sum(masked * normed, 0, keepdims=True),
            )

        carry = lax.fori_loop(0, z.n_own, step, carry, unroll=2)
    spread(stats_ref, list(carry))


def norm_grad(z, row, z_ref, up_ref, sum_ref, all_ref, hw_ref, par_ref, out_ref, par_grad_ref):
    mean, inv, count = sum_ref[0:1, :], sum_ref[1:2, :], sum_ref[2:3, :]
    shift_grad = sum(all_ref[k, 0:1, : z.L] for k in range(z.S * z.Z))
    gain_grad = sum(all_ref[k, 1:2, : z.L] for k in range(z.S * z.Z))
    keep(par_grad_ref, [gain_grad, shift_grad])
    gain = par_ref[row : row + 1, :]

    def step(n, rows, carry):
        mask = image_mask(z, hw_ref[n])
        normed = (z_ref[rows, :] - mean) * inv
        grad = inv * mask * gain * (up_ref[rows, :] - (shift_grad + normed * gain_grad) / count)
        out_ref[rows, :] = grad.astype(BF16)
        return carry

    over_images(z, step)


def back_product(z, conv, at, dzs, w_ref, wcat, dz_ref):
    OB = z.C // z.Z
    for s in range(z.S):
        for b in range(z.Z):
            for k in range(z.K):
                block = w_ref[s * z.Z + b, conv, k]
                if z.L % LANES == 0:
                    wcat[0, k * z.LP + s * z.IB : k * z.LP + (s + 1) * z.IB, b * OB : (b + 1) * OB] = block
                else:
                    wcat[b, k * z.LP + s * z.IB : k * z.LP + (s + 1) * z.IB, :] = block
    for m in range(z.Q):
        dz_ref[at[0] ^ m] = dzs[m][...]
    contract = (((1,), (1,)), ((), ()))

    def product(j):
        rows = slice(j * z.own, (j + 1) * z.own)
        if z.L % LANES == 0:
            whole = jnp.concatenate([dz_ref[i, rows, :] for i in range(z.Q)], axis=1)
            return lax.dot_general(whole, wcat[0], contract, preferred_element_type=F32)
        return sum(
            lax.dot_general(dz_ref[i, rows, :], wcat[i], contract, preferred_element_type=F32)
            for i in range(z.Q)
        )

    return product


def back_scratch(z):
    if z.L % LANES == 0:
        wide = pltpu.VMEM((1, z.K * z.LP, z.C), BF16)
    else:
        wide = pltpu.VMEM((z.Z, z.K * z.LP, z.C // z.Z), BF16)
    return [wide, pltpu.VMEM((z.Q, z.G, z.L), BF16), pltpu.VMEM((z.own, z.K * z.LP), F32)]


def hidden_grad(z, *refs):
    at = refs[0]
    dzs, refs = refs[1 : 1 + z.Q], refs[1 + z.Q :]
    w_ref, z_ref, sum_ref, hw_ref, par_ref, da_ref, stats_ref, wcat, dz_ref, y_ref = refs
    product = back_product(z, 1, at, dzs, w_ref, wcat, dz_ref)
    conv_into(z, product, lambda j: j * z.own, wcat, y_ref, da_ref, -1)
    mean, inv = sum_ref[0:1, :], sum_ref[1:2, :]
    gain, shift = par_ref[0:1, :], par_ref[1:2, :]

    def step(n, rows, carry):
        mask = image_mask(z, hw_ref[n])
        normed = (z_ref[rows, :] - mean) * inv
        da = da_ref[rows, :] * gelu_both(mask * (gain * normed + shift))[1]
        da_ref[rows, :] = da
        masked = mask * da
        return (
            carry[0] + jnp.sum(masked, 0, keepdims=True),
            carry[1] + jnp.sum(masked * normed, 0, keepdims=True),
        )

    zero = jnp.zeros((1, z.L), F32)
    spread(stats_ref, list(over_images(z, step, (zero, zero))))


def input_grad(z, *refs):
    at = refs[0]
    dzs, refs = refs[1 : 1 + z.Q], refs[1 + z.Q :]
    w_ref, d_ref = refs[:2]
    outs, refs = refs[2 : 2 + z.Q], refs[2 + z.Q :]
    wcat, dz_ref, y_ref, dx_ref = refs
    product = back_product(z, 0, at, dzs, w_ref, wcat, dz_ref)
    conv_into(z, product, lambda j: j * z.own, wcat, y_ref, dx_ref, -1)
    for m in range(z.Q):
        rows = pl.ds(pl.multiple_of((at[0] ^ m) * z.own, z.own), z.own)
        outs[m][...] = (dx_ref[rows, :] + d_ref[rows, :]).astype(BF16)


def kernel_grad(z, *refs):
    at = refs[0]
    f_ref, refs = refs[1], refs[2:]
    dzs, refs = refs[: z.Q], refs[z.Q :]
    mine_ref, theirs_ref, moved_ref, full_ref = refs
    for j in range(z.Q):
        rows = slice(j * z.own, (j + 1) * z.own)
        for k, part in enumerate(moved_taps(z, f_ref[rows, :].astype(F32))):
            moved_ref[rows, k * z.LP : k * z.LP + z.L] = part.astype(BF16)
    contract = (((0,), (0,)), ((), ()))
    if z.L % LANES == 0:
        whole = jnp.concatenate([dz[...] for dz in dzs], axis=1)
        full_ref[...] = lax.dot_general(moved_ref[...], whole, contract, preferred_element_type=F32)
    else:
        for m in range(z.Q):
            full_ref[:, m * z.LP : m * z.LP + z.L] = lax.dot_general(
                moved_ref[...], dzs[m][...], contract, preferred_element_type=F32
            )
    for m in range(z.Q):
        to = at[2] ^ at[0] ^ m
        for t in range(z.S):
            s = at[1] ^ t
            for k in range(z.K):
                part = full_ref[
                    pl.ds(pl.multiple_of(k * z.LP + s * z.IB, z.IB), z.IB), m * z.LP : m * z.LP + z.L
                ]
                if t == 0:
                    mine_ref[to, k] = part
                else:
                    theirs_ref[t - 1, to, k] = part


def add_sharers(z, *refs):
    mine_ref, refs = refs[0], refs[1:]
    others, outs = refs[: z.S - 1], refs[z.S - 1 :]
    for m in range(z.Z):
        total = mine_ref[m]
        for other in others:
            total = total + other[m]
        outs[m][...] = total.astype(outs[m].dtype)


def direction_of(grad, first, second, param, decay):
    new_first = BETA * first + (1.0 - BETA) * grad
    new_second = BETA * second + (1.0 - BETA) * grad * grad
    move = new_first / BIAS / (jnp.sqrt(new_second / BIAS) + TINY) + decay * param
    return new_first, new_second, move


def moments(z, *refs):
    parts = [refs[j * z.Z : (j + 1) * z.Z] for j in range(2)]
    refs = refs[2 * z.Z :]
    w_ref, first_ref, second_ref, g1_ref, g2_ref, nf_ref, ns_ref, u_ref, stats_ref = refs
    rows = []
    weight_rows = []
    for j in range(2):
        total_u = jnp.zeros((1, z.L), F32)
        total_w = jnp.zeros((1, z.L), F32)
        for k in range(z.K):
            grad = sum(part[k].astype(F32) for part in parts[j])
            w = w_ref[j, k]
            nf, ns, u = direction_of(grad, first_ref[j, k], second_ref[j, k], w, DECAY)
            nf_ref[j, k] = nf
            ns_ref[j, k] = ns
            u_ref[j, k] = u
            total_u = total_u + jnp.sum(u * u, 0, keepdims=True)
            total_w = total_w + jnp.sum(w * w, 0, keepdims=True)
        rows.append(total_u)
        weight_rows.append(total_w)
    spread(
        stats_ref,
        rows + weight_rows + [g1_ref[0:1, :], g1_ref[1:2, :], g2_ref[0:1, :], g2_ref[1:2, :]],
    )


def finish(z, all_ref, w_ref, u_ref, np_ref, nf_ref, ns_ref, *outs):
    nw_ref, copy_ref, nnp_ref, nnf_ref, nns_ref, trust_ref = outs
    total = all_ref[0]
    for k in range(1, z.R * z.Z):
        total = total + all_ref[k]
    tops, bottoms = [], []
    for j in range(2):
        un = jnp.sqrt(jnp.sum(total[j : j + 1, : z.L], axis=1, keepdims=True))
        wn = jnp.sqrt(jnp.sum(total[2 + j : 3 + j, : z.L], axis=1, keepdims=True))
        tops.append(wn)
        bottoms.append(un)
        scale = RATE * (wn / (un + TINY))
        for k in range(z.K):
            new = w_ref[j, k] - scale * u_ref[j, k]
            nw_ref[j, k] = new
            copy_ref[j, k] = new.astype(BF16)
    for j in range(z.Q):
        nnp_ref[:, j * z.L : (j + 1) * z.L] = all_ref[j * z.Z, 4:8, : z.L]
    param = np_ref[...]
    nf, ns, move = direction_of(nnp_ref[...], nf_ref[...], ns_ref[...], param, 0.0)
    nnf_ref[...] = nf
    nns_ref[...] = ns
    pn = jnp.sqrt(jnp.sum(param * param, axis=1, keepdims=True))
    qn = jnp.sqrt(jnp.sum(move * move, axis=1, keepdims=True))
    nnp_ref[...] = param - RATE * (pn / (qn + TINY)) * move
    for r in range(4):
        tops.append(pn[r : r + 1])
        bottoms.append(qn[r : r + 1])
    at_row = lax.broadcasted_iota(jnp.int32, (2, 6), 0)
    at_col = lax.broadcasted_iota(jnp.int32, (2, 6), 1)
    trust = jnp.zeros((2, 6), F32)
    for c in range(6):
        trust = jnp.where(at_col == c, jnp.where(at_row == 0, tops[c], bottoms[c]), trust)
    trust_ref[...] = trust


def prepare(z, x_ref, valid_ref, cot_ref, at, ext_ref, *cots):
    ext_ref[: z.own, :] = x_ref[...]
    rows = []
    for n in range(z.n_own):
        valid = valid_ref[n].astype(F32)
        tall = jnp.sum(valid[:, 0:1], axis=0, keepdims=True)
        wide = jnp.sum(valid[0:1, :], axis=1, keepdims=True)
        rows += [tall, wide]
    rows = [jnp.broadcast_to(r, (1, z.C)) for r in rows]
    fill = ext_ref.shape[0] - z.own - len(rows)
    ext_ref[z.own :, :] = jnp.concatenate(rows + [jnp.zeros((fill, z.C), F32)], axis=0).astype(BF16)
    for m in range(z.Q):
        for slot in range(z.Q):

            @pl.when((at[0] ^ m) == slot)
            def _(m=m, slot=slot):
                cots[m][...] = cot_ref[:, slot * z.L : (slot + 1) * z.L]


def assemble(z, at, *refs):
    parts, out_ref, hold = refs[: z.Q], refs[z.Q], refs[z.Q + 1]
    for m in range(z.Q):
        hold[at[0] ^ m] = parts[m][...]
    for j in range(z.Q):
        out_ref[:, j * z.L : (j + 1) * z.L] = hold[j]


def shards(z, images, masks, cotangent, weights, first, second, params, p_first, p_second):
    q, s, b = lax.axis_index("q"), lax.axis_index("s"), lax.axis_index("z")
    at = jnp.stack([q, s, b]).astype(jnp.int32)
    everyone = ("q", "s", "z")

    def place(a, c, e):
        return (a * z.S + c) * z.Z + e

    def over_q(v, m):
        return lax.ppermute(v, "q", [(i, i ^ m) for i in range(z.Q)]) if m else v

    def over_z(v, m):
        return lax.ppermute(v, "z", [(i, i ^ m) for i in range(z.Z)]) if m else v

    def over_s(v, m):
        return lax.ppermute(v, "s", [(i, i ^ m) for i in range(z.S)]) if m else v

    def gather_q(v):
        return [over_q(v, m) for m in range(z.Q)]

    def sharers(v):
        return lax.all_to_all(v, ("s", "z"), 0, 0)

    def fetch(w):
        own = []
        for m in range(z.Z):
            pairs = [
                (place(a, c, e), place(e, c, a ^ m))
                for a in range(z.Q)
                for c in range(z.S)
                for e in range(z.Z)
            ]
            own.append(lax.ppermute(w, everyone, pairs))
        return own

    def share(own):
        return [[over_s(v, t) for v in own] for t in range(1, z.S)]

    rows = z.own
    GL = (z.G, z.L)
    conv_flops = 2 * z.G * z.C * z.K * z.L
    many = z.S * z.Z
    low = [weights[j].astype(BF16) for j in range(2)]
    extra = 16 * ((2 * z.n_own + 15) // 16)
    prepared = call(
        functools.partial(prepare, z),
        [shape((rows + extra, z.C), BF16)] + [shape((rows, z.L), BF16)] * z.Q,
        (images.reshape(rows, z.C), masks, cotangent.reshape(rows, z.C), at),
    )
    x_ext, cots = prepared[0], prepared[1:]
    own_one = fetch(low[0])
    xs = gather_q(x_ext)
    others_one = share(own_one)
    slice_params = lax.dynamic_slice(params, (0, q * z.L), (4, z.L))

    conv_scratch = [pltpu.VMEM((z.C, z.K * z.LP), BF16)]
    y_scratch = [pltpu.VMEM((rows, z.K * z.LP), F32)]
    z1, x_slice, hw, stats = call(
        functools.partial(first_conv, z),
        [shape(GL), shape(GL, BF16), shape((z.n_group, 8, LANES)), shape((many, 8, LANES))],
        (at, *xs, *own_one, *[v for o in others_one for v in o]),
        conv_scratch + y_scratch,
        flops=conv_flops,
    )
    own_two = fetch(low[1])
    others_two = share(own_two)
    cots = [over_q(cots[m], m) for m in range(z.Q)]
    h1, sum_one = call(
        functools.partial(hidden, z),
        [shape(GL, BF16), shape((8, z.L))],
        (z1, sharers(stats), hw, slice_params),
        flops=z.G * z.L * 20,
    )
    hs = gather_q(h1)
    z2, stats = call(
        functools.partial(second_conv, z),
        [shape(GL), shape((many, 8, LANES))],
        (at, *hs, *own_two, *[v for o in others_two for v in o], hw),
        conv_scratch + [pltpu.VMEM((z.Q, z.G, z.L), BF16)] + y_scratch,
        flops=conv_flops,
    )
    back = lax.all_gather(jnp.stack(low), ("s", "z"))
    mid = call(
        functools.partial(middle, z),
        [shape((rows, z.L), BF16)] * z.Q + [shape(GL), shape((8, z.L)), shape((many, 8, LANES))],
        (at, z2, sharers(stats), hw, slice_params, x_slice, *cots),
        flops=z.G * z.L * 40,
    )
    outs, (d, sum_two, stats) = mid[: z.Q], mid[z.Q :]
    dz2, grad_two = call(
        functools.partial(norm_grad, z, 2),
        [shape(GL, BF16), shape((8, z.L))],
        (z2, d, sum_two, sharers(stats), hw, slice_params),
        flops=z.G * z.L * 10,
    )
    dz2s = gather_q(dz2)
    da1, stats = call(
        functools.partial(hidden_grad, z),
        [shape(GL), shape((many, 8, LANES))],
        (at, *dz2s, back, z1, sum_one, hw, slice_params),
        back_scratch(z),
        flops=conv_flops,
    )
    grad_scratch = [pltpu.VMEM((z.G, z.K * z.LP), BF16), pltpu.VMEM((z.K * z.LP, z.Q * z.LP), F32)]
    piece = (z.K, z.IB, z.L)

    def reduce_kernels(feature, dzs):
        mine, theirs = call(
            functools.partial(kernel_grad, z),
            [shape((z.Z, *piece)), shape((z.S - 1, z.Z, *piece))],
            (at, feature, *dzs),
            grad_scratch,
            flops=conv_flops,
        )
        received = [over_s(theirs[t - 1], t) for t in range(1, z.S)]
        parts = call(
            functools.partial(add_sharers, z),
            [shape(piece)] + [shape(piece, BF16)] * (z.Z - 1),
            (mine, *received),
        )
        return [over_z(parts[m], m) for m in range(z.Z)]

    parts_two = reduce_kernels(h1, dz2s)
    dz1, grad_one = call(
        functools.partial(norm_grad, z, 0),
        [shape(GL, BF16), shape((8, z.L))],
        (z1, da1, sum_one, sharers(stats), hw, slice_params),
        flops=z.G * z.L * 10,
    )
    dz1s = gather_q(dz1)
    parts_one = reduce_kernels(x_slice, dz1s)
    dxs = call(
        functools.partial(input_grad, z),
        [shape((rows, z.L), BF16)] * z.Q,
        (at, *dz1s, back, d),
        back_scratch(z) + [pltpu.VMEM(GL, F32)],
        flops=conv_flops,
    )

    def give_back(parts):
        parts = [over_q(parts[m], m) for m in range(z.Q)]
        return call(
            functools.partial(assemble, z),
            shape((rows, z.C), BF16),
            (at, *parts),
            [pltpu.VMEM((z.Q, rows, z.L), BF16)],
        ).reshape(images.shape)

    block_output = give_back(outs)
    dx = give_back(dxs)
    new_first, new_second, move, stats = call(
        functools.partial(moments, z),
        [shape(weights.shape)] * 3 + [shape((z.R * z.Z, 8, LANES))],
        (*parts_one, *parts_two, weights, first, second, grad_one, grad_two),
    )
    stats = lax.all_to_all(stats, ("s", "q", "z"), 0, 0)
    new_weights, copies, new_params, new_p_first, new_p_second, trust = call(
        functools.partial(finish, z),
        [shape(weights.shape), shape(weights.shape, BF16)] + [shape(params.shape)] * 3 + [shape((2, 6))],
        (stats, weights, move, params, p_first, p_second),
    )
    return (
        block_output,
        dx,
        new_weights,
        copies,
        new_first,
        new_second,
        new_params,
        new_p_first,
        new_p_second,
        trust,
    )


def solution(mesh):
    def whole(images, masks, cotangent, weights, first, second, params, p_first, p_second):
        z = Sizes(mesh, images.shape, weights.shape)
        inner = Mesh(mesh.devices.reshape(z.Q, z.S, z.Z), ("q", "s", "z"))
        pixels = P(("q", "s", "z"), None, None, None)
        kernels = P(None, None, ("q", "s"), "z")
        return jax.shard_map(
            functools.partial(shards, z),
            mesh=inner,
            in_specs=(pixels, P(("q", "s", "z"), None, None), pixels, kernels, kernels, kernels, P(), P(), P()),
            out_specs=(pixels, pixels, kernels, kernels, kernels, kernels, P(), P(), P(), P()),
            check_vma=False,
        )(images, masks, cotangent, weights, first, second, params, p_first, p_second)

    return whole
```

time: 812 us -> 258 us (0.32)
  waiting for transfers between devices: 458 us -> 57.3 us
  blocking collectives: 280 us -> 19.4 us
  starting transfers between devices: 0.16 us -> 98.9 us
  Pallas kernels: 0 us -> 53.7 us
  other arithmetic: 28.4 us -> 1.35 us
  matrix products: 26 us -> 0 us
  local copies, waits for them, and re-layouts: 2.59 us -> 11.3 us
    reduce_scatter x2 -> x0, waiting for transfers between devices: 365 us -> none  [the longest x1 314 us: shards(): lax.psum_scatter(full_grads, 'ba', scatter_dimension=3, tiled=True)]
    psum x7 -> x0, blocking collectives: 280 us -> none  [the longest x2 82.2 us: norm_forward(): lax.psum(jnp.sum(valid_mask * centered * centered, axis=0), ('ha', 'wa',...]
    all_gather x2 -> x1, waiting for transfers between devices: 92.8 us -> 0.01 us  [shards(): back = lax.all_gather(jnp.stack(low), ('s', 'z'))]
    ppermute x0 -> x45, starting transfers between devices: none -> 86.6 us  [the longest x21 44.3 us: over_q(): return lax.ppermute(v, 'q', [(i, i ^ m) for i in range(z.Q)]) if m else v]
    pallas_call x0 -> x17, Pallas kernels: none -> 53.7 us  [call(): pl.pallas_call(body, out_shape=out_shape, in_specs=[pl.BlockSpec(memory_s...]
    ppermute x0 -> x45, waiting for transfers between devices: none -> 47.2 us  [the longest x21 31.3 us: over_q(): return lax.ppermute(v, 'q', [(i, i ^ m) for i in range(z.Q)]) if m else v]
    dot_general x6 -> x0, matrix products: 26 us -> none  [the longest x1 6.73 us: shards(): jnp.einsum('pki,po->kio', taps_hidden, second_low, preferred_element_type...]
    all_to_all x0 -> x2, blocking collectives: none -> 19.4 us  [sharers(): return lax.all_to_all(v, ('s', 'z'), 0, 0)]
  transfers between devices with their start and end apart: 4 -> 49, of which waited for: 4 -> 17; matrix products, arithmetic and copies ran while one was open for 1% -> 1% of each run, Pallas kernels for 0% -> 16%
where the time goes in v1:
time: 258 us; the launch traced here: 257 us
  starting transfers between devices  98.9 us (38%)
  waiting for transfers between devices  57.3 us (22%)
  Pallas kernels  53.7 us (21%)
  blocking collectives  19.4 us (8%)
  between operations  14.5 us (6%)
  local copies, waits for them, and re-layouts  11.3 us (4%)
    pallas_call x17, Pallas kernels, call(): pl.pallas_call(body, out_shape=out_shape, in_specs=[pl.BlockSpec(memory_s...  53.7 us
    ppermute x21, starting transfers between devices, over_q(): return lax.ppermute(v, 'q', [(i, i ^ m) for i in range(z.Q)]) if m else v  44.3 us
    ppermute x8, starting transfers between devices, fetch(): own.append(lax.ppermute(w, everyone, pairs))  31.4 us
    ppermute x21, waiting for transfers between devices, over_q(): return lax.ppermute(v, 'q', [(i, i ^ m) for i in range(z.Q)]) if m else v  31.3 us
    all_to_all x2, blocking collectives, sharers(): return lax.all_to_all(v, ('s', 'z'), 0, 0)  19.4 us
    ppermute x6, waiting for transfers between devices, over_z(): return lax.ppermute(v, 'z', [(i, i ^ m) for i in range(z.Z)]) if m else v  15 us
    all_to_all x2, waiting for transfers between devices, sharers(): return lax.all_to_all(v, ('s', 'z'), 0, 0)  10 us
    unnamed x108, local copies, waits for them, and re-layouts  8.89 us
  transfers between devices with their start and end apart: 49, of which 17 were waited for; matrix products, arithmetic and copies ran while one was open for 1% of the time, Pallas kernels for 16%

profile of v1, /device:TPU:0, one launch (start us, length us, event | category | flops | bytes accessed | tf_op | source)
XLA Modules:
  0.0 256.5 jit_solution(4298644515436668473)
XLA Ops:
  7.2 1.1 fusion
  9.8 5.7 %collective-permute-start.4 = (bf16[9,64,128]{2,1,0:T(8,128)(2,1)S(1)}, bf16[9,64,128]{2,1,0:T(8,128)(2,1)S(1)}, u32[]{:S(2)}, u32[]{:S(2)}) collective-permute-start(bf16[9,64,128]{2,1,0:T(8,128)(2,1)S(1)} %bitcast.17), channel_id=1, source_target_pairs={{0,1},{1,9},{2,17},{3,25},{4,5},{5,13},{6,21},{7,29},{8,0},{9,8},{... | collective-permute-start | bytes 442376 | tf_op jit(solution)/shard_map/ppermute | solution.py:564
  15.5 3.5 %collective-permute-start.5 = (bf16[9,64,128]{2,1,0:T(8,128)(2,1)S(1)}, bf16[9,64,128]{2,1,0:T(8,128)(2,1)S(1)}, u32[]{:S(2)}, u32[]{:S(2)}) collective-permute-start(bf16[9,64,128]{2,1,0:T(8,128)(2,1)S(1)} %bitcast.18), channel_id=1, source_target_pairs={{0,2},{1,10},{2,18},{3,26},{4,6},{5,14},{6,22},{7,30},{8,3},{9,11}... | collective-permute-start | bytes 442376 | tf_op jit(solution)/shard_map/ppermute | solution.py:564
  19.0 1.9 collective-permute-start.6
  21.5 2.0 shard_map.168
  23.5 1.5 collective-permute-start
  25.1 7.8 %collective-permute-start.1 = (bf16[272,512]{1,0:T(8,128)(2,1)}, bf16[272,512]{1,0:T(8,128)(2,1)S(1)}, u32[]{:S(2)}, u32[]{:S(2)}) collective-permute-start(bf16[272,512]{1,0:T(8,128)(2,1)} %get-tuple-element.62.refs_1_), channel_id=1, source_target_pairs={{0,16},{8,24},{16,0},{24,8},{1,17},{9,25},{17,1},{25,9},{2,18},{10... | collective-permute-start | bytes 835592 | tf_op jit(solution)/shard_map/ppermute | solution.py:541
  33.6 4.1 %collective-permute-start.15 = (bf16[9,64,128]{2,1,0:T(8,128)(2,1)S(1)}, bf16[9,64,128]{2,1,0:T(8,128)(2,1)S(1)}, u32[]{:S(2)}, u32[]{:S(2)}) collective-permute-start(bf16[9,64,128]{2,1,0:T(8,128)(2,1)S(1)} %bitcast.13), channel_id=1, source_target_pairs={{0,1},{1,9},{2,17},{3,25},{4,5},{5,13},{6,21},{7,29},{8,0},{9,8},{... | collective-permute-start | bytes 442376 | tf_op jit(solution)/shard_map/ppermute | solution.py:564
  37.6 11.2 %collective-permute-start.2 = (bf16[272,512]{1,0:T(8,128)(2,1)}, bf16[272,512]{1,0:T(8,128)(2,1)S(1)}, u32[]{:S(2)}, u32[]{:S(2)}) collective-permute-start(bf16[272,512]{1,0:T(8,128)(2,1)} %get-tuple-element.62.refs_1_), channel_id=1, source_target_pairs={{0,24},{8,16},{16,8},{24,0},{1,25},{9,17},{17,9},{25,1},{2,26},{10... | collective-permute-start | bytes 835592 | tf_op jit(solution)/shard_map/ppermute | solution.py:541
  49.9 4.1 %collective-permute-done.2.refs_4_ = bf16[272,512]{1,0:T(8,128)(2,1)S(1)} collective-permute-done((bf16[272,512]{1,0:T(8,128)(2,1)}, bf16[272,512]{1,0:T(8,128)(2,1)S(1)}, u32[]{:S(2)}, u32[]{:S(2)}) %collective-permute-start.2) | collective-permute-done | bytes 278560 | tf_op jit(solution)/shard_map/ppermute | solution.py:541
  54.0 14.9 %collective-permute-start.16 = (bf16[9,64,128]{2,1,0:T(8,128)(2,1)S(1)}, bf16[9,64,128]{2,1,0:T(8,128)(2,1)S(1)}, u32[]{:S(2)}, u32[]{:S(2)}) collective-permute-start(bf16[9,64,128]{2,1,0:T(8,128)(2,1)S(1)} %bitcast.14), channel_id=1, source_target_pairs={{0,2},{1,10},{2,18},{3,26},{4,6},{5,14},{6,22},{7,30},{8,3},{9,11}... | collective-permute-start | bytes 442376 | tf_op jit(solution)/shard_map/ppermute | solution.py:564
  70.3 4.6 %shard_map.169 = (f32[1024,128]{1,0:T(8,128)}, bf16[1024,128]{1,0:T(8,128)(2,1)}, f32[16,8,128]{2,1,0:T(8,128)}, f32[8,8,128]{2,1,0:T(8,128)}) custom-call(s32[3]{0:T(128)} %pad_add_fusion.at.refs_0_, bf16[272,512]{1,0:T(8,128)(2,1)} %get-tuple-element.62.refs_1_, bf16[272,512]{1,0:T(8,128)(2,1)} %copy-done.20, bf16[272,512]{1,0:T(8,128)(2,1)} %copy-done.21, ...), custom_call_target="tpu_custom_call" | custom-call | flops 1207959552 | tf_op jit(solution)/shard_map/pallas_call | solution.py:56
  75.0 3.3 %all-to-all-start = ((f32[8,8,128]{2,1,0:T(8,128)}), f32[8,8,128]{2,1,0:T(8,128)S(1)}, u32[]{:S(2)}, u32[]{:S(2)}) async-start(f32[8,8,128]{2,1,0:T(8,128)} %get-tuple-element.64), calls=%async_computation | async-start | bytes 65536 | tf_op jit(solution)/shard_map/all_to_all | solution.py:553
  78.3 1.3 constant_dynamic-slice_fusion.par_ref.refs_9_
  79.6 4.4 %all-to-all-done.all_ref = f32[8,8,128]{2,1,0:T(8,128)S(1)} async-done(((f32[8,8,128]{2,1,0:T(8,128)}), f32[8,8,128]{2,1,0:T(8,128)S(1)}, u32[]{:S(2)}, u32[]{:S(2)}) %all-to-all-start) | async-done | bytes 32800 | tf_op jit(solution)/shard_map/all_to_all | solution.py:553
  84.6 2.2 shard_map.170
  86.8 1.5 collective-permute-start.11
  88.3 2.0 collective-permute-start.12
  91.7 1.5 collective-permute-start.22
  93.2 2.0 collective-permute-start.23
  95.2 1.5 collective-permute-done.11.refs_2_
  96.7 2.9 %collective-permute-start.24 = (bf16[256,128]{1,0:T(8,128)(2,1)S(1)}, bf16[256,128]{1,0:T(8,128)(2,1)S(1)}, u32[]{:S(2)}, u32[]{:S(2)}) collective-permute-start(bf16[256,128]{1,0:T(8,128)(2,1)S(1)} %copy-done.51), channel_id=1, source_target_pairs={{0,24},{8,16},{16,8},{24,0},{1,25},{9,17},{17,9},{25,1},{2,26},{10... | collective-permute-start | bytes 196616 | tf_op jit(solution)/shard_map/ppermute | solution.py:541
  99.6 3.8 %collective-permute-done.13.refs_4_ = bf16[1024,128]{1,0:T(8,128)(2,1)S(1)} collective-permute-done((bf16[1024,128]{1,0:T(8,128)(2,1)}, bf16[1024,128]{1,0:T(8,128)(2,1)S(1)}, u32[]{:S(2)}, u32[]{:S(2)}) %collective-permute-start.13) | collective-permute-done | bytes 262176 | tf_op jit(solution)/shard_map/ppermute | solution.py:541
  104.1 4.4 %shard_map.171 = (f32[1024,128]{1,0:T(8,128)}, f32[8,8,128]{2,1,0:T(8,128)}) custom-call(s32[3]{0:T(128)} %pad_add_fusion.at.refs_0_, bf16[1024,128]{1,0:T(8,128)(2,1)} %get-tuple-element.66.refs_1_, bf16[1024,128]{1,0:T(8,128)(2,1)} %copy-done.26, bf16[1024,128]{1,0:T(8,128)(2,1)} %copy-done.27, bf16[1024,128]{1,0:T(8,128)(2,1)} %copy-done.29, ...), custom_call_target="tpu_custom_call" | custom-call | flops 1207959552 | tf_op jit(solution)/shard_map/pallas_call | solution.py:56
  108.5 3.3 %all-to-all-start.1 = ((f32[8,8,128]{2,1,0:T(8,128)}), f32[8,8,128]{2,1,0:T(8,128)S(1)}, u32[]{:S(2)}, u32[]{:S(2)}) async-start(f32[8,8,128]{2,1,0:T(8,128)} %get-tuple-element.68), calls=%async_computation.1 | async-start | bytes 65536 | tf_op jit(solution)/shard_map/all_to_all | solution.py:553
  111.9 5.6 %all-to-all-done.1.all_ref = f32[8,8,128]{2,1,0:T(8,128)S(1)} async-done(((f32[8,8,128]{2,1,0:T(8,128)}), f32[8,8,128]{2,1,0:T(8,128)S(1)}, u32[]{:S(2)}, u32[]{:S(2)}) %all-to-all-start.1) | async-done | bytes 32800 | tf_op jit(solution)/shard_map/all_to_all | solution.py:553
  118.2 2.8 %shard_map.172 = (bf16[256,128]{1,0:T(8,128)(2,1)}, bf16[256,128]{1,0:T(8,128)(2,1)}, bf16[256,128]{1,0:T(8,128)(2,1)}, bf16[256,128]{1,0:T(8,128)(2,1)}, f32[10...) custom-call(s32[3]{0:T(128)} %pad_add_fusion.at.refs_0_, f32[1024,128]{1,0:T(8,128)} %get-tuple-element.67.z_ref, ...), custom_call_target="tpu_custom_call" | custom-call | flops 5242880 | tf_op jit(solution)/shard_map/pallas_call | solution.py:56
  121.0 9.7 %all_to_all.25.all_ref = f32[8,8,128]{2,1,0:T(8,128)} all-to-all(f32[8,8,128]{2,1,0:T(8,128)} %get-tuple-element.80), channel_id=1, replica_groups=mesh['ha'=2,'wa'=4,'ba'=4] {'wa':(2)2,'ba'}, dimensions={0} | all-to-all | bytes 65536 | tf_op jit(solution)/shard_map/all_to_all | solution.py:553
  130.7 2.2 shard_map.174
  132.9 1.4 collective-permute-start.28
  134.3 2.0 collective-permute-start.29
  136.4 5.0 %collective-permute-done.28.refs_2_.refs_3_ = bf16[1024,128]{1,0:T(8,128)(2,1)S(1)} collective-permute-done((bf16[1024,128]{1,0:T(8,128)(2,1)}, bf16[1024,128]{1,0:T(8,128)(2,1)S(1)}, u32[]{:S(2)}, u32[]{:S(2)}) %collective-permute-start.28) | collective-permute-done | bytes 262176 | tf_op jit(solution)/shard_map/ppermute | solution.py:541
  141.4 2.3 collective-permute-done.29.refs_3_.refs_4_
  143.7 4.5 %collective-permute-done.30.refs_4_.refs_5_ = bf16[1024,128]{1,0:T(8,128)(2,1)S(1)} collective-permute-done((bf16[1024,128]{1,0:T(8,128)(2,1)}, bf16[1024,128]{1,0:T(8,128)(2,1)S(1)}, u32[]{:S(2)}, u32[]{:S(2)}) %collective-permute-start.30) | collective-permute-done | bytes 262176 | tf_op jit(solution)/shard_map/ppermute | solution.py:541
  148.9 5.3 %shard_map.175 = (f32[1024,128]{1,0:T(8,128)}, f32[8,8,128]{2,1,0:T(8,128)}) custom-call(s32[3]{0:T(128)} %pad_add_fusion.at.refs_0_, bf16[1024,128]{1,0:T(8,128)(2,1)} %get-tuple-element.81.refs_1_.refs_2_, bf16[1024,128]{1,0:T(8,128)(2,1)} %copy-done.28, bf16[1024,128]{1,0:T(8,128)(2,1)} %copy-done.30, bf16[1024,128]{1,0:T(8,128)(2,1)} %copy-done.31, ...), custom_call_target="tpu_custom_call" | custom-call | flops 1207959552 | tf_op jit(solution)/shard_map/pallas_call | solution.py:56
  154.3 9.7 %all_to_all.26.all_ref = f32[8,8,128]{2,1,0:T(8,128)} all-to-all(f32[8,8,128]{2,1,0:T(8,128)} %get-tuple-element.84), channel_id=1, replica_groups=mesh['ha'=2,'wa'=4,'ba'=4] {'wa':(2)2,'ba'}, dimensions={0} | all-to-all | bytes 65536 | tf_op jit(solution)/shard_map/all_to_all | solution.py:553
  164.0 2.2 shard_map.176
  166.2 1.7 collective-permute-start.31
  167.9 1.7 collective-permute-start.32
  169.7 4.5 %shard_map.181 = (f32[4,9,64,128]{3,2,1,0:T(8,128)}, f32[1,4,9,64,128]{4,3,2,1,0:T(8,128)}) custom-call(s32[3]{0:T(128)} %pad_add_fusion.at.refs_0_, bf16[1024,128]{1,0:T(8,128)(2,1)} %get-tuple-element.66.refs_1_, bf16[1024,128]{1,0:T(8,128)(2,1)} %get-tuple-element.81.refs_1_.refs_2_, bf16[1024,128]{1,0:T(8,128)(2,1)} %copy-done.28, ...), custom_call_target="tpu_custom_call" | custom-call | flops 1207959552 | tf_op jit(solution)/shard_map/pallas_call | solution.py:56
  174.7 2.6 %collective-permute-done.32.refs_3_.refs_4_ = bf16[1024,128]{1,0:T(8,128)(2,1)S(1)} collective-permute-done((bf16[1024,128]{1,0:T(8,128)(2,1)}, bf16[1024,128]{1,0:T(8,128)(2,1)S(1)}, u32[]{:S(2)}, u32[]{:S(2)}) %collective-permute-start.32) | collective-permute-done | bytes 262176 | tf_op jit(solution)/shard_map/ppermute | solution.py:541
  177.3 4.2 %collective-permute-done.33.refs_4_.refs_5_ = bf16[1024,128]{1,0:T(8,128)(2,1)S(1)} collective-permute-done((bf16[1024,128]{1,0:T(8,128)(2,1)}, bf16[1024,128]{1,0:T(8,128)(2,1)S(1)}, u32[]{:S(2)}, u32[]{:S(2)}) %collective-permute-start.33) | collective-permute-done | bytes 262176 | tf_op jit(solution)/shard_map/ppermute | solution.py:541
  182.2 4.4 %shard_map.179 = (f32[4,9,64,128]{3,2,1,0:T(8,128)}, f32[1,4,9,64,128]{4,3,2,1,0:T(8,128)}) custom-call(s32[3]{0:T(128)} %pad_add_fusion.at.refs_0_, bf16[1024,128]{1,0:T(8,128)(2,1)} %get-tuple-element.69.x_ref.refs_1_, bf16[1024,128]{1,0:T(8,128)(2,1)} %get-tuple-element.85.refs_1_.refs_2_, bf16[1024,128]{1,0:T(8,128)(2,1)} %copy-done.23, ...), custom_call_target="tpu_custom_call" | custom-call | flops 1207959552 | tf_op jit(solution)/shard_map/pallas_call | solution.py:56
  186.6 1.1 copy-done.1
  187.7 2.5 shard_map.182
  191.2 3.4 %collective-permute-start.44 = (bf16[9,64,128]{2,1,0:T(8,128)(2,1)}, bf16[9,64,128]{2,1,0:T(8,128)(2,1)S(1)}, u32[]{:S(2)}, u32[]{:S(2)}) collective-permute-start(bf16[9,64,128]{2,1,0:T(8,128)(2,1)} %get-tuple-element.101), channel_id=1, source_target_pairs={{0,3},{1,2},{2,1},{3,0},{4,7},{5,6},{6,5},{7,4},{8,11},{9,10},{10,... | collective-permute-start | bytes 442376 | tf_op jit(solution)/shard_map/ppermute | solution.py:544
  194.6 1.0 copy-done
  195.6 2.5 shard_map.180
  198.1 1.0 collective-permute-start.39
  199.1 3.4 %collective-permute-start.40 = (bf16[9,64,128]{2,1,0:T(8,128)(2,1)}, bf16[9,64,128]{2,1,0:T(8,128)(2,1)S(1)}, u32[]{:S(2)}, u32[]{:S(2)}) collective-permute-start(bf16[9,64,128]{2,1,0:T(8,128)(2,1)} %get-tuple-element.95), channel_id=1, source_target_pairs={{0,3},{1,2},{2,1},{3,0},{4,7},{5,6},{6,5},{7,4},{8,11},{9,10},{10,... | collective-permute-start | bytes 442376 | tf_op jit(solution)/shard_map/ppermute | solution.py:544
  202.5 2.4 collective-permute-done.43.refs_6_
  204.9 2.4 collective-permute-done.38.refs_1_
  207.3 10.2 %collective-permute-done.39.refs_2_ = bf16[9,64,128]{2,1,0:T(8,128)(2,1)S(1)} collective-permute-done((bf16[9,64,128]{2,1,0:T(8,128)(2,1)}, bf16[9,64,128]{2,1,0:T(8,128)(2,1)S(1)}, u32[]{:S(2)}, u32[]{:S(2)}) %collective-permute-start.39) | collective-permute-done | bytes 147488 | tf_op jit(solution)/shard_map/ppermute | solution.py:544
  218.2 3.8 %shard_map.183 = (f32[2,9,64,128]{3,2,1,0:T(8,128)}, f32[2,9,64,128]{3,2,1,0:T(8,128)}, f32[2,9,64,128]{3,2,1,0:T(8,128)}, f32[32,8,128]{2,1,0:T(8,128)}) custom-call(f32[9,64,128]{2,1,0:T(8,128)} %get-tuple-element.92.refs_0_, bf16[9,64,128]{2,1,0:T(8,128)(2,1)} %copy-done.6, bf16[9,64,128]{2,1,0:T(8,128)(2,1)} %copy-done.7, bf16[9,64,128]{2,1,0:T(8,128)(2,1)} %copy-done.8, ...), custom_call_target="tpu_custom_call" | custom-call | tf_op jit(solution)/shard_map/pallas_call | solution.py:56
  222.0 5.6 %all-to-all-start.4 = ((f32[32,8,128]{2,1,0:T(8,128)}), f32[32,8,128]{2,1,0:T(8,128)S(1)}, u32[]{:S(2)}, u32[]{:S(2)}) async-start(f32[32,8,128]{2,1,0:T(8,128)} %get-tuple-element.104), calls=%async_computation.4 | async-start | bytes 262144 | tf_op jit(solution)/shard_map/all_to_all | solution.py:687
  227.6 1.8 collective-permute-start.25
  229.5 1.5 collective-permute-start.26
  231.2 4.5 %shard_map.177 = (bf16[256,128]{1,0:T(8,128)(2,1)}, bf16[256,128]{1,0:T(8,128)(2,1)}, bf16[256,128]{1,0:T(8,128)(2,1)}, bf16[256,128]{1,0:T(8,128)(2,1)}) custom-call(s32[3]{0:T(128)} %pad_add_fusion.at.refs_0_, bf16[1024,128]{1,0:T(8,128)(2,1)} %get-tuple-element.85.refs_1_.refs_2_, bf16[1024,128]{1,0:T(8,128)(2,1)} %copy-done.23, ...), custom_call_target="tpu_custom_call" | custom-call | flops 1207959552 | tf_op jit(solution)/shard_map/pallas_call | solution.py:56
  235.7 1.8 collective-permute-start.34
  237.4 1.5 collective-permute-start.35
  239.8 1.7 shard_map.173
  241.9 2.4 collective-permute-done.36.refs_3_
  244.9 1.7 shard_map.178
  247.3 2.4 shard_map.184
  (166 shorter events, 15.2 us)
Async XLA Ops:
  7.2 141.1 %all-gather.3.cloned.1.call-start = ((), (), s32[]{:S(2)}) async-start(), calls=%async_computation.5 | async-start | bytes 2654208 | tf_op jit(solution)/shard_map/all_gather | solution.py:613
  9.1 16.0 %collective-permute-start.3 = (bf16[9,64,128]{2,1,0:T(8,128)(2,1)S(1)}, bf16[9,64,128]{2,1,0:T(8,128)(2,1)S(1)}, u32[]{:S(2)}, u32[]{:S(2)}) collective-permute-start(bf16[9,64,128]{2,1,0:T(8,128)(2,1)S(1)} %bitcast.16), channel_id=1, source_target_pairs={{0,0},{1,8},{2,16},{3,24},{4,4},{5,12},{6,20},{7,28},{8,1},{9,9},{... | collective-permute-start | bytes 442376 | tf_op jit(solution)/shard_map/ppermute | solution.py:564
  9.8 23.1 %collective-permute-start.4 = (bf16[9,64,128]{2,1,0:T(8,128)(2,1)S(1)}, bf16[9,64,128]{2,1,0:T(8,128)(2,1)S(1)}, u32[]{:S(2)}, u32[]{:S(2)}) collective-permute-start(bf16[9,64,128]{2,1,0:T(8,128)(2,1)S(1)} %bitcast.17), channel_id=1, source_target_pairs={{0,1},{1,9},{2,17},{3,25},{4,5},{5,13},{6,21},{7,29},{8,0},{9,8},{... | collective-permute-start | bytes 442376 | tf_op jit(solution)/shard_map/ppermute | solution.py:564
  15.5 18.0 %collective-permute-start.5 = (bf16[9,64,128]{2,1,0:T(8,128)(2,1)S(1)}, bf16[9,64,128]{2,1,0:T(8,128)(2,1)S(1)}, u32[]{:S(2)}, u32[]{:S(2)}) collective-permute-start(bf16[9,64,128]{2,1,0:T(8,128)(2,1)S(1)} %bitcast.18), channel_id=1, source_target_pairs={{0,2},{1,10},{2,18},{3,26},{4,6},{5,14},{6,22},{7,30},{8,3},{9,11}... | collective-permute-start | bytes 442376 | tf_op jit(solution)/shard_map/ppermute | solution.py:564
  19.0 18.7 %collective-permute-start.6 = (bf16[9,64,128]{2,1,0:T(8,128)(2,1)S(1)}, bf16[9,64,128]{2,1,0:T(8,128)(2,1)S(1)}, u32[]{:S(2)}, u32[]{:S(2)}) collective-permute-start(bf16[9,64,128]{2,1,0:T(8,128)(2,1)S(1)} %bitcast.19), channel_id=1, source_target_pairs={{0,3},{1,11},{2,19},{3,27},{4,7},{5,15},{6,23},{7,31},{8,2},{9,10}... | collective-permute-start | bytes 442376 | tf_op jit(solution)/shard_map/ppermute | solution.py:564
  23.5 25.8 %collective-permute-start = (bf16[272,512]{1,0:T(8,128)(2,1)}, bf16[272,512]{1,0:T(8,128)(2,1)S(1)}, u32[]{:S(2)}, u32[]{:S(2)}) collective-permute-start(bf16[272,512]{1,0:T(8,128)(2,1)} %get-tuple-element.62.refs_1_), channel_id=1, source_target_pairs={{0,8},{8,0},{16,24},{24,16},{1,9},{9,1},{17,25},{25,17},{2,10},{10... | collective-permute-start | bytes 835592 | tf_op jit(solution)/shard_map/ppermute | solution.py:541
  25.1 44.4 %copy-start.34 = (bf16[9,64,128]{2,1,0:T(8,128)(2,1)}, bf16[9,64,128]{2,1,0:T(8,128)(2,1)S(1)}, u32[]{:S(2)}) copy-start(bf16[9,64,128]{2,1,0:T(8,128)(2,1)S(1)} %collective-permute-done.3.refs_5_) | copy-start | bytes 442372
  25.1 24.4 %collective-permute-start.1 = (bf16[272,512]{1,0:T(8,128)(2,1)}, bf16[272,512]{1,0:T(8,128)(2,1)S(1)}, u32[]{:S(2)}, u32[]{:S(2)}) collective-permute-start(bf16[272,512]{1,0:T(8,128)(2,1)} %get-tuple-element.62.refs_1_), channel_id=1, source_target_pairs={{0,16},{8,24},{16,0},{24,8},{1,17},{9,25},{17,1},{25,9},{2,18},{10... | collective-permute-start | bytes 835592 | tf_op jit(solution)/shard_map/ppermute | solution.py:541
  32.9 36.6 %copy-start.35 = (bf16[9,64,128]{2,1,0:T(8,128)(2,1)}, bf16[9,64,128]{2,1,0:T(8,128)(2,1)S(1)}, u32[]{:S(2)}) copy-start(bf16[9,64,128]{2,1,0:T(8,128)(2,1)S(1)} %collective-permute-done.4.refs_6_) | copy-start | bytes 442372
  32.9 16.0 %collective-permute-start.14 = (bf16[9,64,128]{2,1,0:T(8,128)(2,1)S(1)}, bf16[9,64,128]{2,1,0:T(8,128)(2,1)S(1)}, u32[]{:S(2)}, u32[]{:S(2)}) collective-permute-start(bf16[9,64,128]{2,1,0:T(8,128)(2,1)S(1)} %bitcast.12), channel_id=1, source_target_pairs={{0,0},{1,8},{2,16},{3,24},{4,4},{5,12},{6,20},{7,28},{8,1},{9,9},{... | collective-permute-start | bytes 442376 | tf_op jit(solution)/shard_map/ppermute | solution.py:564
  33.5 36.0 %copy-start.36 = (bf16[9,64,128]{2,1,0:T(8,128)(2,1)}, bf16[9,64,128]{2,1,0:T(8,128)(2,1)S(1)}, u32[]{:S(2)}) copy-start(bf16[9,64,128]{2,1,0:T(8,128)(2,1)S(1)} %collective-permute-done.5.refs_7_) | copy-start | bytes 442372
  33.6 15.3 %collective-permute-start.15 = (bf16[9,64,128]{2,1,0:T(8,128)(2,1)S(1)}, bf16[9,64,128]{2,1,0:T(8,128)(2,1)S(1)}, u32[]{:S(2)}, u32[]{:S(2)}) collective-permute-start(bf16[9,64,128]{2,1,0:T(8,128)(2,1)S(1)} %bitcast.13), channel_id=1, source_target_pairs={{0,1},{1,9},{2,17},{3,25},{4,5},{5,13},{6,21},{7,29},{8,0},{9,8},{... | collective-permute-start | bytes 442376 | tf_op jit(solution)/shard_map/ppermute | solution.py:564
  37.6 31.9 %copy-start.37 = (bf16[9,64,128]{2,1,0:T(8,128)(2,1)}, bf16[9,64,128]{2,1,0:T(8,128)(2,1)S(1)}, u32[]{:S(2)}) copy-start(bf16[9,64,128]{2,1,0:T(8,128)(2,1)S(1)} %collective-permute-done.6.refs_8_) | copy-start | bytes 442372
  37.6 16.3 %collective-permute-start.2 = (bf16[272,512]{1,0:T(8,128)(2,1)}, bf16[272,512]{1,0:T(8,128)(2,1)S(1)}, u32[]{:S(2)}, u32[]{:S(2)}) collective-permute-start(bf16[272,512]{1,0:T(8,128)(2,1)} %get-tuple-element.62.refs_1_), channel_id=1, source_target_pairs={{0,24},{8,16},{16,8},{24,0},{1,25},{9,17},{17,9},{25,1},{2,26},{10... | collective-permute-start | bytes 835592 | tf_op jit(solution)/shard_map/ppermute | solution.py:541
  48.8 54.5 %copy-start.32 = (bf16[9,64,128]{2,1,0:T(8,128)(2,1)}, bf16[9,64,128]{2,1,0:T(8,128)(2,1)S(1)}, u32[]{:S(2)}) copy-start(bf16[9,64,128]{2,1,0:T(8,128)(2,1)S(1)} %collective-permute-done.14.refs_5_) | copy-start | bytes 442372
  48.8 20.1 %collective-permute-start.7 = (bf16[9,64,128]{2,1,0:T(8,128)(2,1)S(1)}, bf16[9,64,128]{2,1,0:T(8,128)(2,1)S(1)}, u32[]{:S(2)}, u32[]{:S(2)}) collective-permute-start(bf16[9,64,128]{2,1,0:T(8,128)(2,1)S(1)} %collective-permute-done.3.refs_5_), channel_id=1, source_target_pairs={{0,4},{4,0},{1,5},{5,1},{2,6},{6,2},{3,7},{7,3},{8,12},{12,8},{9,1... | collective-permute-start | bytes 442376 | tf_op jit(solution)/shard_map/ppermute | solution.py:547
  48.8 54.5 %copy-start.33 = (bf16[9,64,128]{2,1,0:T(8,128)(2,1)}, bf16[9,64,128]{2,1,0:T(8,128)(2,1)S(1)}, u32[]{:S(2)}) copy-start(bf16[9,64,128]{2,1,0:T(8,128)(2,1)S(1)} %collective-permute-done.15.refs_6_) | copy-start | bytes 442372
  48.8 20.0 %collective-permute-start.8 = (bf16[9,64,128]{2,1,0:T(8,128)(2,1)S(1)}, bf16[9,64,128]{2,1,0:T(8,128)(2,1)S(1)}, u32[]{:S(2)}, u32[]{:S(2)}) collective-permute-start(bf16[9,64,128]{2,1,0:T(8,128)(2,1)S(1)} %collective-permute-done.4.refs_6_), channel_id=1, source_target_pairs={{0,4},{4,0},{1,5},{5,1},{2,6},{6,2},{3,7},{7,3},{8,12},{12,8},{9,1... | collective-permute-start | bytes 442376 | tf_op jit(solution)/shard_map/ppermute | solution.py:547
  49.3 20.2 %copy-start.20 = (bf16[272,512]{1,0:T(8,128)(2,1)}, bf16[272,512]{1,0:T(8,128)(2,1)S(1)}, u32[]{:S(2)}) copy-start(bf16[272,512]{1,0:T(8,128)(2,1)S(1)} %collective-permute-done.refs_2_) | copy-start | bytes 835588
  49.3 19.6 %collective-permute-start.9 = (bf16[9,64,128]{2,1,0:T(8,128)(2,1)S(1)}, bf16[9,64,128]{2,1,0:T(8,128)(2,1)S(1)}, u32[]{:S(2)}, u32[]{:S(2)}) collective-permute-start(bf16[9,64,128]{2,1,0:T(8,128)(2,1)S(1)} %collective-permute-done.5.refs_7_), channel_id=1, source_target_pairs={{0,4},{4,0},{1,5},{5,1},{2,6},{6,2},{3,7},{7,3},{8,12},{12,8},{9,1... | collective-permute-start | bytes 442376 | tf_op jit(solution)/shard_map/ppermute | solution.py:547
  49.4 20.1 %copy-start.21 = (bf16[272,512]{1,0:T(8,128)(2,1)}, bf16[272,512]{1,0:T(8,128)(2,1)S(1)}, u32[]{:S(2)}) copy-start(bf16[272,512]{1,0:T(8,128)(2,1)S(1)} %collective-permute-done.1.refs_3_) | copy-start | bytes 835588
  49.4 20.1 %collective-permute-start.10 = (bf16[9,64,128]{2,1,0:T(8,128)(2,1)S(1)}, bf16[9,64,128]{2,1,0:T(8,128)(2,1)S(1)}, u32[]{:S(2)}, u32[]{:S(2)}) collective-permute-start(bf16[9,64,128]{2,1,0:T(8,128)(2,1)S(1)} %collective-permute-done.6.refs_8_), channel_id=1, source_target_pairs={{0,4},{4,0},{1,5},{5,1},{2,6},{6,2},{3,7},{7,3},{8,12},{12,8},{9,1... | collective-permute-start | bytes 442376 | tf_op jit(solution)/shard_map/ppermute | solution.py:547
  49.9 41.8 %copy-start.53 = (bf16[256,128]{1,0:T(8,128)(2,1)S(1)}, bf16[256,128]{1,0:T(8,128)(2,1)}, u32[]{:S(2)}) copy-start(bf16[256,128]{1,0:T(8,128)(2,1)} %get-tuple-element.71) | copy-start | bytes 196612
  49.9 43.3 %copy-start.52 = (bf16[256,128]{1,0:T(8,128)(2,1)S(1)}, bf16[256,128]{1,0:T(8,128)(2,1)}, u32[]{:S(2)}) copy-start(bf16[256,128]{1,0:T(8,128)(2,1)} %get-tuple-element.72) | copy-start | bytes 196612
  49.9 46.8 %copy-start.51 = (bf16[256,128]{1,0:T(8,128)(2,1)S(1)}, bf16[256,128]{1,0:T(8,128)(2,1)}, u32[]{:S(2)}) copy-start(bf16[256,128]{1,0:T(8,128)(2,1)} %get-tuple-element.73) | copy-start | bytes 196612
  54.0 15.6 %copy-start.22 = (bf16[272,512]{1,0:T(8,128)(2,1)}, bf16[272,512]{1,0:T(8,128)(2,1)S(1)}, u32[]{:S(2)}) copy-start(bf16[272,512]{1,0:T(8,128)(2,1)S(1)} %collective-permute-done.2.refs_4_) | copy-start | bytes 835588
  54.0 34.3 %collective-permute-start.16 = (bf16[9,64,128]{2,1,0:T(8,128)(2,1)S(1)}, bf16[9,64,128]{2,1,0:T(8,128)(2,1)S(1)}, u32[]{:S(2)}, u32[]{:S(2)}) collective-permute-start(bf16[9,64,128]{2,1,0:T(8,128)(2,1)S(1)} %bitcast.14), channel_id=1, source_target_pairs={{0,2},{1,10},{2,18},{3,26},{4,6},{5,14},{6,22},{7,30},{8,3},{9,11}... | collective-permute-start | bytes 442376 | tf_op jit(solution)/shard_map/ppermute | solution.py:564
  68.9 21.3 %collective-permute-start.17 = (bf16[9,64,128]{2,1,0:T(8,128)(2,1)S(1)}, bf16[9,64,128]{2,1,0:T(8,128)(2,1)S(1)}, u32[]{:S(2)}, u32[]{:S(2)}) collective-permute-start(bf16[9,64,128]{2,1,0:T(8,128)(2,1)S(1)} %bitcast.15), channel_id=1, source_target_pairs={{0,3},{1,11},{2,19},{3,27},{4,7},{5,15},{6,23},{7,31},{8,2},{9,10}... | collective-permute-start | bytes 442376 | tf_op jit(solution)/shard_map/ppermute | solution.py:564
  68.9 21.4 %collective-permute-start.18 = (bf16[9,64,128]{2,1,0:T(8,128)(2,1)S(1)}, bf16[9,64,128]{2,1,0:T(8,128)(2,1)S(1)}, u32[]{:S(2)}, u32[]{:S(2)}) collective-permute-start(bf16[9,64,128]{2,1,0:T(8,128)(2,1)S(1)} %collective-permute-done.14.refs_5_), channel_id=1, source_target_pairs={{0,4},{4,0},{1,5},{5,1},{2,6},{6,2},{3,7},{7,3},{8,12},{12,8},{9,1... | collective-permute-start | bytes 442376 | tf_op jit(solution)/shard_map/ppermute | solution.py:547
  69.0 21.3 %collective-permute-start.19 = (bf16[9,64,128]{2,1,0:T(8,128)(2,1)S(1)}, bf16[9,64,128]{2,1,0:T(8,128)(2,1)S(1)}, u32[]{:S(2)}, u32[]{:S(2)}) collective-permute-start(bf16[9,64,128]{2,1,0:T(8,128)(2,1)S(1)} %collective-permute-done.15.refs_6_), channel_id=1, source_target_pairs={{0,4},{4,0},{1,5},{5,1},{2,6},{6,2},{3,7},{7,3},{8,12},{12,8},{9,1... | collective-permute-start | bytes 442376 | tf_op jit(solution)/shard_map/ppermute | solution.py:547
  75.0 9.0 %all-to-all-start = ((f32[8,8,128]{2,1,0:T(8,128)}), f32[8,8,128]{2,1,0:T(8,128)S(1)}, u32[]{:S(2)}, u32[]{:S(2)}) async-start(f32[8,8,128]{2,1,0:T(8,128)} %get-tuple-element.64), calls=%async_computation | async-start | bytes 65536 | tf_op jit(solution)/shard_map/all_to_all | solution.py:553
  86.8 9.9 %collective-permute-start.11 = (bf16[1024,128]{1,0:T(8,128)(2,1)}, bf16[1024,128]{1,0:T(8,128)(2,1)S(1)}, u32[]{:S(2)}, u32[]{:S(2)}) collective-permute-start(bf16[1024,128]{1,0:T(8,128)(2,1)} %get-tuple-element.66.refs_1_), channel_id=1, source_target_pairs={{0,8},{8,0},{16,24},{24,16},{1,9},{9,1},{17,25},{25,17},{2,10},{10... | collective-permute-start | bytes 786440 | tf_op jit(solution)/shard_map/ppermute | solution.py:541
  88.2 15.1 %copy-start.38 = (bf16[9,64,128]{2,1,0:T(8,128)(2,1)}, bf16[9,64,128]{2,1,0:T(8,128)(2,1)S(1)}, u32[]{:S(2)}) copy-start(bf16[9,64,128]{2,1,0:T(8,128)(2,1)S(1)} %collective-permute-done.16.refs_7_) | copy-start | bytes 442372
  88.3 11.3 %collective-permute-start.12 = (bf16[1024,128]{1,0:T(8,128)(2,1)}, bf16[1024,128]{1,0:T(8,128)(2,1)S(1)}, u32[]{:S(2)}, u32[]{:S(2)}) collective-permute-start(bf16[1024,128]{1,0:T(8,128)(2,1)} %get-tuple-element.66.refs_1_), channel_id=1, source_target_pairs={{0,16},{8,24},{16,0},{24,8},{1,17},{9,25},{17,1},{25,9},{2,18},{10... | collective-permute-start | bytes 786440 | tf_op jit(solution)/shard_map/ppermute | solution.py:541
  90.2 13.1 %copy-start.39 = (bf16[9,64,128]{2,1,0:T(8,128)(2,1)}, bf16[9,64,128]{2,1,0:T(8,128)(2,1)S(1)}, u32[]{:S(2)}) copy-start(bf16[9,64,128]{2,1,0:T(8,128)(2,1)S(1)} %collective-permute-done.17.refs_8_) | copy-start | bytes 442372
  90.2 13.1 %collective-permute-start.13 = (bf16[1024,128]{1,0:T(8,128)(2,1)}, bf16[1024,128]{1,0:T(8,128)(2,1)S(1)}, u32[]{:S(2)}, u32[]{:S(2)}) collective-permute-start(bf16[1024,128]{1,0:T(8,128)(2,1)} %get-tuple-element.66.refs_1_), channel_id=1, source_target_pairs={{0,24},{8,16},{16,8},{24,0},{1,25},{9,17},{17,9},{25,1},{2,26},{10... | collective-permute-start | bytes 786440 | tf_op jit(solution)/shard_map/ppermute | solution.py:541
  90.3 1.4 collective-permute-start.20
  90.3 2.8 %collective-permute-start.21 = (bf16[9,64,128]{2,1,0:T(8,128)(2,1)S(1)}, bf16[9,64,128]{2,1,0:T(8,128)(2,1)S(1)}, u32[]{:S(2)}, u32[]{:S(2)}) collective-permute-start(bf16[9,64,128]{2,1,0:T(8,128)(2,1)S(1)} %collective-permute-done.17.refs_8_), channel_id=1, source_target_pairs={{0,4},{4,0},{1,5},{5,1},{2,6},{6,2},{3,7},{7,3},{8,12},{12,8},{9,1... | collective-permute-start | bytes 442376 | tf_op jit(solution)/shard_map/ppermute | solution.py:547
  91.7 20.2 %collective-permute-start.22 = (bf16[256,128]{1,0:T(8,128)(2,1)S(1)}, bf16[256,128]{1,0:T(8,128)(2,1)S(1)}, u32[]{:S(2)}, u32[]{:S(2)}) collective-permute-start(bf16[256,128]{1,0:T(8,128)(2,1)S(1)} %copy-done.53), channel_id=1, source_target_pairs={{0,8},{8,0},{16,24},{24,16},{1,9},{9,1},{17,25},{25,17},{2,10},{10... | collective-permute-start | bytes 196616 | tf_op jit(solution)/shard_map/ppermute | solution.py:541
  93.2 18.7 %collective-permute-start.23 = (bf16[256,128]{1,0:T(8,128)(2,1)S(1)}, bf16[256,128]{1,0:T(8,128)(2,1)S(1)}, u32[]{:S(2)}, u32[]{:S(2)}) collective-permute-start(bf16[256,128]{1,0:T(8,128)(2,1)S(1)} %copy-done.52), channel_id=1, source_target_pairs={{0,16},{8,24},{16,0},{24,8},{1,17},{9,25},{17,1},{25,9},{2,18},{10... | collective-permute-start | bytes 196616 | tf_op jit(solution)/shard_map/ppermute | solution.py:541
  96.7 15.3 %collective-permute-start.24 = (bf16[256,128]{1,0:T(8,128)(2,1)S(1)}, bf16[256,128]{1,0:T(8,128)(2,1)S(1)}, u32[]{:S(2)}, u32[]{:S(2)}) collective-permute-start(bf16[256,128]{1,0:T(8,128)(2,1)S(1)} %copy-done.51), channel_id=1, source_target_pairs={{0,24},{8,16},{16,8},{24,0},{1,25},{9,17},{17,9},{25,1},{2,26},{10... | collective-permute-start | bytes 196616 | tf_op jit(solution)/shard_map/ppermute | solution.py:541
  108.5 9.0 %all-to-all-start.1 = ((f32[8,8,128]{2,1,0:T(8,128)}), f32[8,8,128]{2,1,0:T(8,128)S(1)}, u32[]{:S(2)}, u32[]{:S(2)}) async-start(f32[8,8,128]{2,1,0:T(8,128)} %get-tuple-element.68), calls=%async_computation.1 | async-start | bytes 65536 | tf_op jit(solution)/shard_map/all_to_all | solution.py:553
  132.9 8.5 %collective-permute-start.28 = (bf16[1024,128]{1,0:T(8,128)(2,1)}, bf16[1024,128]{1,0:T(8,128)(2,1)S(1)}, u32[]{:S(2)}, u32[]{:S(2)}) collective-permute-start(bf16[1024,128]{1,0:T(8,128)(2,1)} %get-tuple-element.81.refs_1_.refs_2_), channel_id=1, source_target_pairs={{0,8},{8,0},{16,24},{24,16},{1,9},{9,1},{17,25},{25,17},{2,10},{10... | collective-permute-start | bytes 786440 | tf_op jit(solution)/shard_map/ppermute | solution.py:541
  134.3 9.4 %collective-permute-start.29 = (bf16[1024,128]{1,0:T(8,128)(2,1)}, bf16[1024,128]{1,0:T(8,128)(2,1)S(1)}, u32[]{:S(2)}, u32[]{:S(2)}) collective-permute-start(bf16[1024,128]{1,0:T(8,128)(2,1)} %get-tuple-element.81.refs_1_.refs_2_), channel_id=1, source_target_pairs={{0,16},{8,24},{16,0},{24,8},{1,17},{9,25},{17,1},{25,9},{2,18},{10... | collective-permute-start | bytes 786440 | tf_op jit(solution)/shard_map/ppermute | solution.py:541
  136.3 11.9 %collective-permute-start.30 = (bf16[1024,128]{1,0:T(8,128)(2,1)}, bf16[1024,128]{1,0:T(8,128)(2,1)S(1)}, u32[]{:S(2)}, u32[]{:S(2)}) collective-permute-start(bf16[1024,128]{1,0:T(8,128)(2,1)} %get-tuple-element.81.refs_1_.refs_2_), channel_id=1, source_target_pairs={{0,24},{8,16},{16,8},{24,0},{1,25},{9,17},{17,9},{25,1},{2,26},{10... | collective-permute-start | bytes 786440 | tf_op jit(solution)/shard_map/ppermute | solution.py:541
  166.2 8.5 %collective-permute-start.31 = (bf16[1024,128]{1,0:T(8,128)(2,1)}, bf16[1024,128]{1,0:T(8,128)(2,1)S(1)}, u32[]{:S(2)}, u32[]{:S(2)}) collective-permute-start(bf16[1024,128]{1,0:T(8,128)(2,1)} %get-tuple-element.85.refs_1_.refs_2_), channel_id=1, source_target_pairs={{0,8},{8,0},{16,24},{24,16},{1,9},{9,1},{17,25},{25,17},{2,10},{10... | collective-permute-start | bytes 786440 | tf_op jit(solution)/shard_map/ppermute | solution.py:541
  167.9 9.4 %collective-permute-start.32 = (bf16[1024,128]{1,0:T(8,128)(2,1)}, bf16[1024,128]{1,0:T(8,128)(2,1)S(1)}, u32[]{:S(2)}, u32[]{:S(2)}) collective-permute-start(bf16[1024,128]{1,0:T(8,128)(2,1)} %get-tuple-element.85.refs_1_.refs_2_), channel_id=1, source_target_pairs={{0,16},{8,24},{16,0},{24,8},{1,17},{9,25},{17,1},{25,9},{2,18},{10... | collective-permute-start | bytes 786440 | tf_op jit(solution)/shard_map/ppermute | solution.py:541
  169.6 11.9 %collective-permute-start.33 = (bf16[1024,128]{1,0:T(8,128)(2,1)}, bf16[1024,128]{1,0:T(8,128)(2,1)S(1)}, u32[]{:S(2)}, u32[]{:S(2)}) collective-permute-start(bf16[1024,128]{1,0:T(8,128)(2,1)} %get-tuple-element.85.refs_1_.refs_2_), channel_id=1, source_target_pairs={{0,24},{8,16},{16,8},{24,0},{1,25},{9,17},{17,9},{25,1},{2,26},{10... | collective-permute-start | bytes 786440 | tf_op jit(solution)/shard_map/ppermute | solution.py:541
  174.1 12.4 %collective-permute-start.41 = (f32[4,9,64,128]{3,2,1,0:T(8,128)}, f32[4,9,64,128]{3,2,1,0:T(8,128)S(1)}, u32[]{:S(2)}, u32[]{:S(2)}) collective-permute-start(f32[4,9,64,128]{3,2,1,0:T(8,128)} %bitcast.27), channel_id=1, source_target_pairs={{0,4},{4,0},{1,5},{5,1},{2,6},{6,2},{3,7},{7,3},{8,12},{12,8},{9,1... | collective-permute-start | bytes 3538952 | tf_op jit(solution)/shard_map/ppermute | solution.py:547
  186.6 8.0 %collective-permute-start.37 = (f32[4,9,64,128]{3,2,1,0:T(8,128)}, f32[4,9,64,128]{3,2,1,0:T(8,128)S(1)}, u32[]{:S(2)}, u32[]{:S(2)}) collective-permute-start(f32[4,9,64,128]{3,2,1,0:T(8,128)} %bitcast.26), channel_id=1, source_target_pairs={{0,4},{4,0},{1,5},{5,1},{2,6},{6,2},{3,7},{7,3},{8,12},{12,8},{9,1... | collective-permute-start | bytes 3538952 | tf_op jit(solution)/shard_map/ppermute | solution.py:547
  190.2 8.9 %collective-permute-start.42 = (bf16[9,64,128]{2,1,0:T(8,128)(2,1)}, bf16[9,64,128]{2,1,0:T(8,128)(2,1)S(1)}, u32[]{:S(2)}, u32[]{:S(2)}) collective-permute-start(bf16[9,64,128]{2,1,0:T(8,128)(2,1)} %get-tuple-element.99), channel_id=1, source_target_pairs={{0,1},{1,0},{2,3},{3,2},{4,5},{5,4},{6,7},{7,6},{8,9},{9,8},{10,11... | collective-permute-start | bytes 442376 | tf_op jit(solution)/shard_map/ppermute | solution.py:544
  190.7 14.2 %collective-permute-start.43 = (bf16[9,64,128]{2,1,0:T(8,128)(2,1)}, bf16[9,64,128]{2,1,0:T(8,128)(2,1)S(1)}, u32[]{:S(2)}, u32[]{:S(2)}) collective-permute-start(bf16[9,64,128]{2,1,0:T(8,128)(2,1)} %get-tuple-element.100), channel_id=1, source_target_pairs={{0,2},{1,3},{2,0},{3,1},{4,6},{5,7},{6,4},{7,5},{8,10},{9,11},{10,... | collective-permute-start | bytes 442376 | tf_op jit(solution)/shard_map/ppermute | solution.py:544
  191.2 13.7 %collective-permute-start.44 = (bf16[9,64,128]{2,1,0:T(8,128)(2,1)}, bf16[9,64,128]{2,1,0:T(8,128)(2,1)S(1)}, u32[]{:S(2)}, u32[]{:S(2)}) collective-permute-start(bf16[9,64,128]{2,1,0:T(8,128)(2,1)} %get-tuple-element.101), channel_id=1, source_target_pairs={{0,3},{1,2},{2,1},{3,0},{4,7},{5,6},{6,5},{7,4},{8,11},{9,10},{10,... | collective-permute-start | bytes 442376 | tf_op jit(solution)/shard_map/ppermute | solution.py:544
  198.1 9.2 %collective-permute-start.38 = (bf16[9,64,128]{2,1,0:T(8,128)(2,1)}, bf16[9,64,128]{2,1,0:T(8,128)(2,1)S(1)}, u32[]{:S(2)}, u32[]{:S(2)}) collective-permute-start(bf16[9,64,128]{2,1,0:T(8,128)(2,1)} %get-tuple-element.93), channel_id=1, source_target_pairs={{0,1},{1,0},{2,3},{3,2},{4,5},{5,4},{6,7},{7,6},{8,9},{9,8},{10,11... | collective-permute-start | bytes 442376 | tf_op jit(solution)/shard_map/ppermute | solution.py:544
  198.1 19.4 %collective-permute-start.39 = (bf16[9,64,128]{2,1,0:T(8,128)(2,1)}, bf16[9,64,128]{2,1,0:T(8,128)(2,1)S(1)}, u32[]{:S(2)}, u32[]{:S(2)}) collective-permute-start(bf16[9,64,128]{2,1,0:T(8,128)(2,1)} %get-tuple-element.94), channel_id=1, source_target_pairs={{0,2},{1,3},{2,0},{3,1},{4,6},{5,7},{6,4},{7,5},{8,10},{9,11},{10,... | collective-permute-start | bytes 442376 | tf_op jit(solution)/shard_map/ppermute | solution.py:544
  199.1 18.4 %copy-start.3 = (bf16[9,64,128]{2,1,0:T(8,128)(2,1)}, bf16[9,64,128]{2,1,0:T(8,128)(2,1)S(1)}, u32[]{:S(2)}) copy-start(bf16[9,64,128]{2,1,0:T(8,128)(2,1)S(1)} %collective-permute-done.42.refs_5_) | copy-start | bytes 442372
  199.1 18.4 %collective-permute-start.40 = (bf16[9,64,128]{2,1,0:T(8,128)(2,1)}, bf16[9,64,128]{2,1,0:T(8,128)(2,1)S(1)}, u32[]{:S(2)}, u32[]{:S(2)}) collective-permute-start(bf16[9,64,128]{2,1,0:T(8,128)(2,1)} %get-tuple-element.95), channel_id=1, source_target_pairs={{0,3},{1,2},{2,1},{3,0},{4,7},{5,6},{6,5},{7,4},{8,11},{9,10},{10,... | collective-permute-start | bytes 442376 | tf_op jit(solution)/shard_map/ppermute | solution.py:544
  222.0 24.6 %all-to-all-start.4 = ((f32[32,8,128]{2,1,0:T(8,128)}), f32[32,8,128]{2,1,0:T(8,128)S(1)}, u32[]{:S(2)}, u32[]{:S(2)}) async-start(f32[32,8,128]{2,1,0:T(8,128)} %get-tuple-element.104), calls=%async_computation.4 | async-start | bytes 262144 | tf_op jit(solution)/shard_map/all_to_all | solution.py:687
  227.6 11.3 %collective-permute-start.25 = (bf16[256,128]{1,0:T(8,128)(2,1)S(1)}, bf16[256,128]{1,0:T(8,128)(2,1)S(1)}, u32[]{:S(2)}, u32[]{:S(2)}) collective-permute-start(bf16[256,128]{1,0:T(8,128)(2,1)S(1)} %copy-done.50), channel_id=1, source_target_pairs={{0,8},{8,0},{16,24},{24,16},{1,9},{9,1},{17,25},{25,17},{2,10},{10... | collective-permute-start | bytes 196616 | tf_op jit(solution)/shard_map/ppermute | solution.py:541
  229.5 9.7 %collective-permute-start.26 = (bf16[256,128]{1,0:T(8,128)(2,1)S(1)}, bf16[256,128]{1,0:T(8,128)(2,1)S(1)}, u32[]{:S(2)}, u32[]{:S(2)}) collective-permute-start(bf16[256,128]{1,0:T(8,128)(2,1)S(1)} %copy-done.49), channel_id=1, source_target_pairs={{0,16},{8,24},{16,0},{24,8},{1,17},{9,25},{17,1},{25,9},{2,18},{10... | collective-permute-start | bytes 196616 | tf_op jit(solution)/shard_map/ppermute | solution.py:541
  230.9 8.2 %collective-permute-start.27 = (bf16[256,128]{1,0:T(8,128)(2,1)S(1)}, bf16[256,128]{1,0:T(8,128)(2,1)S(1)}, u32[]{:S(2)}, u32[]{:S(2)}) collective-permute-start(bf16[256,128]{1,0:T(8,128)(2,1)S(1)} %copy-done.48), channel_id=1, source_target_pairs={{0,24},{8,16},{16,8},{24,0},{1,25},{9,17},{17,9},{25,1},{2,26},{10... | collective-permute-start | bytes 196616 | tf_op jit(solution)/shard_map/ppermute | solution.py:541
  235.7 5.9 %collective-permute-start.34 = (bf16[256,128]{1,0:T(8,128)(2,1)}, bf16[256,128]{1,0:T(8,128)(2,1)S(1)}, u32[]{:S(2)}, u32[]{:S(2)}) collective-permute-start(bf16[256,128]{1,0:T(8,128)(2,1)} %get-tuple-element.87), channel_id=1, source_target_pairs={{0,8},{8,0},{16,24},{24,16},{1,9},{9,1},{17,25},{25,17},{2,10},{10... | collective-permute-start | bytes 196616 | tf_op jit(solution)/shard_map/ppermute | solution.py:541
  237.4 4.5 %collective-permute-start.35 = (bf16[256,128]{1,0:T(8,128)(2,1)}, bf16[256,128]{1,0:T(8,128)(2,1)S(1)}, u32[]{:S(2)}, u32[]{:S(2)}) collective-permute-start(bf16[256,128]{1,0:T(8,128)(2,1)} %get-tuple-element.88), channel_id=1, source_target_pairs={{0,16},{8,24},{16,0},{24,8},{1,17},{9,25},{17,1},{25,9},{2,18},{10... | collective-permute-start | bytes 196616 | tf_op jit(solution)/shard_map/ppermute | solution.py:541
  238.9 5.4 %collective-permute-start.36 = (bf16[256,128]{1,0:T(8,128)(2,1)}, bf16[256,128]{1,0:T(8,128)(2,1)S(1)}, u32[]{:S(2)}, u32[]{:S(2)}) collective-permute-start(bf16[256,128]{1,0:T(8,128)(2,1)} %get-tuple-element.89), channel_id=1, source_target_pairs={{0,24},{8,16},{16,8},{24,0},{1,25},{9,17},{17,9},{25,1},{2,26},{10... | collective-permute-start | bytes 196616 | tf_op jit(solution)/shard_map/ppermute | solution.py:541
  (39 other events, 184.7 us)
Sparse Core Ops, SparseCore 0:
  10.2 49.9 all-gather.2

commit v2 on v1

v2 whole, which is shorter than its diff:
```python
import functools

import jax
import jax.numpy as jnp
from jax import lax
from jax.experimental import pallas as pl
from jax.experimental.pallas import tpu as pltpu
from jax.sharding import Mesh
from jax.sharding import PartitionSpec as P

STEP = 3
RATE = 0.5
DECAY = 0.01
BETA = 0.5
BIAS = 1.0 - BETA**STEP
EPS = 1e-05
TINY = 1e-06
ROOT = 0.7978845608028654
CUBE = 0.044715
LANES = 128
COST_GRAD = 3 * 10**9
F32 = jnp.float32
BF16 = jnp.bfloat16


def gelu(v):
    return 0.5 * v * (1.0 + jnp.tanh(ROOT * (v + CUBE * (v * v * v))))


def gelu_both(v):
    t = jnp.tanh(ROOT * (v + CUBE * (v * v * v)))
    value = 0.5 * v * (1.0 + t)
    slope = 0.5 * (1.0 + t) + 0.5 * v * (1.0 - t * t) * (ROOT * (1.0 + (3.0 * CUBE) * (v * v)))
    return value, slope


class Sizes:
    def __init__(self, mesh, images, weights):
        self.Z = mesh.shape["ba"]
        self.R = mesh.shape["ha"] * mesh.shape["wa"]
        self.Q = self.Z
        self.S = self.R // self.Q
        n, self.H, self.W, self.C = images
        self.n_own = n // (self.R * self.Z)
        self.own = self.n_own * self.H * self.W
        self.n_group = self.n_own * self.Q
        self.G = self.own * self.Q
        self.L = self.C // self.Q
        self.LP = max(self.L, LANES)
        self.IB = self.C // self.R
        self.K = weights[1]
        self.extra = 16 * ((2 * self.n_own + 15) // 16)
        self.sent = self.own + self.extra + self.own // self.Q


def call(body, out_shape, args, scratch=(), limit=8, far=(), after=(), cost=1, raw=()):
    smem = [a.dtype == jnp.int32 and a.ndim == 1 for a in args]
    away = [any(a is f for f in far) for a in args]
    args = [
        a if m else pltpu.with_memory_space_constraint(a, pltpu.HBM if w else pltpu.VMEM)
        for a, m, w in zip(args, smem, away)
    ]
    n = len(args)

    def run(*refs):
        body(*refs[:n], *refs[n + len(after) :])

    return pl.pallas_call(
        run,
        out_shape=out_shape,
        in_specs=[pl.BlockSpec(memory_space=pltpu.SMEM if m else pltpu.VMEM) for m in smem]
        + [pl.BlockSpec(memory_space=pl.ANY)] * len(after),
        out_specs=jax.tree.map(
            lambda o: pl.BlockSpec(memory_space=pltpu.HBM if any(o is r for r in raw) else pltpu.VMEM),
            out_shape,
        ),
        scratch_shapes=list(scratch),
        compiler_params=pltpu.CompilerParams(vmem_limit_bytes=limit * 1024 * 1024),
        cost_estimate=pl.CostEstimate(flops=cost, bytes_accessed=1, transcendentals=0),
    )(*args, *after)


together = lax.optimization_barrier


def near(dims, dtype=F32):
    return pltpu.VMEM(tuple(dims), dtype)


def away(dims, dtype=F32):
    return pltpu.HBM(tuple(dims), dtype)


def shape(dims, dtype=F32):
    return jax.ShapeDtypeStruct(tuple(dims), dtype)


def image_mask(z, hw):
    dims = (z.H, z.W, z.L)
    rows = lax.broadcasted_iota(jnp.int32, dims, 0).astype(F32)
    cols = lax.broadcasted_iota(jnp.int32, dims, 1).astype(F32)
    tall = hw[0:1, : z.L].reshape(1, 1, z.L)
    wide = hw[1:2, : z.L].reshape(1, 1, z.L)
    return jnp.where((rows < tall) & (cols < wide), 1.0, 0.0).reshape(z.H * z.W, z.L)


def shifted_sum(z, taps, sign):
    dims = (z.n_own, z.H, z.W, z.L)
    cols = lax.broadcasted_iota(jnp.int32, dims, 2)
    total = None
    for c in range(3):
        column = None
        for r in range(3):
            part = taps(3 * r + c).reshape(dims)
            move = (r - 1) * sign
            if move == 1:
                part = jnp.concatenate([part[:, 1:], jnp.zeros_like(part[:, :1])], axis=1)
            elif move == -1:
                part = jnp.concatenate([jnp.zeros_like(part[:, :1]), part[:, :-1]], axis=1)
            column = part if column is None else column + part
        move = (c - 1) * sign
        if move:
            flat = column.reshape(z.n_own * z.H, z.W, z.L)
            flat = pltpu.roll(flat, (-move) % z.W, 1)
            column = flat.reshape(dims)
            edge = z.W - 1 if move == 1 else 0
            column = jnp.where(cols == edge, 0.0, column)
        total = column if total is None else total + column
    return total.reshape(z.own, z.L)


def moved_taps(z, feature):
    dims = (z.n_own, z.H, z.W, z.L)
    cols = lax.broadcasted_iota(jnp.int32, dims, 2)
    out = [None] * 9
    for c in range(3):
        move = 1 - c
        column = feature.reshape(dims)
        if move:
            flat = feature.reshape(z.n_own * z.H, z.W, z.L)
            column = pltpu.roll(flat, (-move) % z.W, 1).reshape(dims)
            edge = z.W - 1 if move == 1 else 0
            column = jnp.where(cols == edge, 0.0, column)
        for r in range(3):
            if r == 0:
                part = jnp.concatenate([column[:, 1:], jnp.zeros_like(column[:, :1])], axis=1)
            elif r == 2:
                part = jnp.concatenate([jnp.zeros_like(column[:, :1]), column[:, :-1]], axis=1)
            else:
                part = column
            out[3 * r + c] = part.reshape(z.own, z.L)
    return out


def fill_moved(z, a_ref, b_ref, moved_ref):
    half = z.Q // 2
    for j in range(z.Q):
        ref, at_row = (a_ref, j) if j < half else (b_ref, j - half)
        block = ref[at_row * z.own : (at_row + 1) * z.own, :].astype(F32)
        for k, part in enumerate(moved_taps(z, block)):
            moved_ref[j * z.own : (j + 1) * z.own, k * z.LP : k * z.LP + z.L] = part.astype(BF16)


def spread(ref, rows):
    used = rows[0].shape[1]
    if len(rows) < 8:
        rows = rows + [jnp.zeros((8 - len(rows), used), F32)]
    stat = jnp.concatenate(rows, axis=0)
    if used < LANES:
        stat = jnp.concatenate([stat, jnp.zeros((8, LANES - used), F32)], axis=1)
    for k in range(ref.shape[0]):
        ref[k] = stat


def local_stats(z, z_ref, hw_ref, stats_ref):
    px = z.H * z.W

    def first(n, carry):
        count, total = carry
        mask = image_mask(z, hw_ref[n])
        block = z_ref[pl.ds(pl.multiple_of(n * px, px), px), :]
        return count + jnp.sum(mask, 0, keepdims=True), total + jnp.sum(mask * block, 0, keepdims=True)

    zero = jnp.zeros((1, z.L), F32)
    count, total = lax.fori_loop(0, z.n_group, first, (zero, zero), unroll=4)
    mean = total / count

    def second(n, spread_sum):
        mask = image_mask(z, hw_ref[n])
        centered = z_ref[pl.ds(pl.multiple_of(n * px, px), px), :] - mean
        return spread_sum + jnp.sum(mask * centered * centered, 0, keepdims=True)

    squares = lax.fori_loop(0, z.n_group, second, zero, unroll=4)
    spread(stats_ref, [count, mean, squares])


def conv_into(z, product, y_ref, z_ref, sign=1):
    for j in range(z.Q):
        y_ref[...] = product(j)
        z_ref[j * z.own : (j + 1) * z.own, :] = shifted_sum(
            z, lambda k: y_ref[:, k * z.LP : k * z.LP + z.L], sign
        )


def fill_kernels(z, at, blocks, wcat):
    for t, block in enumerate(blocks):
        s = at[1] ^ t
        for a in range(z.Z):
            row = pl.multiple_of(a * z.L + s * z.IB, z.IB)
            for k in range(z.K):
                wcat[pl.ds(row, z.IB), k * z.LP : k * z.LP + z.L] = block[a, k]


def first_conv(z, at, np_ref, x_ref, *refs):
    blocks, refs = refs[: z.S], refs[z.S :]
    z_ref, slice_ref, cot_ref, par_ref, hw_ref, stats_ref, far_w, far_x, wcat, y_ref, sem = refs
    start, high = z.own + z.extra, z.own // z.Q
    fill_kernels(z, at, blocks, wcat)
    copies = [
        pltpu.make_async_copy(wcat, far_w, sem.at[0]),
        pltpu.make_async_copy(x_ref.at[:, : z.own, :], far_x, sem.at[1]),
    ]
    for copy in copies:
        copy.start()
    for j in range(z.Q):
        for n in range(z.n_own):
            row = z.own + 2 * n
            two = x_ref[j, row : row + 2, :LANES].astype(F32)
            hw_ref[j * z.n_own + n] = jnp.concatenate([two, jnp.zeros((6, LANES), F32)], axis=0)
        for i in range(z.Q):
            row = j * z.own + i * high
            cot_ref[row : row + high, :] = x_ref[j, start:, i * z.L : (i + 1) * z.L]
    for slot in range(z.Q):

        @pl.when(at[0] == slot)
        def _(slot=slot):
            par_ref[...] = np_ref[:, slot * z.L : (slot + 1) * z.L]
            for j in range(z.Q):
                slice_ref[j * z.own : (j + 1) * z.own, :] = x_ref[
                    j, : z.own, slot * z.L : (slot + 1) * z.L
                ]

    def product(j):
        return jnp.dot(x_ref[j, : z.own, :], wcat[...], preferred_element_type=F32)

    conv_into(z, product, y_ref, z_ref)
    local_stats(z, z_ref, hw_ref, stats_ref)
    for copy in copies:
        copy.wait()


def gathered(z, at, parts, hold):
    half = z.G // 2
    for m in range(z.Q):
        hold[at[0] ^ m, :half] = parts[m][...]
        hold[at[0] ^ m, half:] = parts[z.Q + m][...]


def second_conv(z, at, *refs):
    hs, refs = refs[: 2 * z.Q], refs[2 * z.Q :]
    blocks, refs = refs[: z.S], refs[z.S :]
    hw_ref, z_ref, stats_ref, far_ref, refs = *refs[:4], refs[4:]
    outs, (wcat, y_ref, h_ref, sem) = refs[: z.Q], refs[z.Q :]
    for m in range(z.Q):
        outs[m][...] = blocks[0][at[0] ^ m]
    gathered(z, at, hs, h_ref)
    copy = pltpu.make_async_copy(h_ref, far_ref, sem)
    copy.start()
    fill_kernels(z, at, blocks, wcat)

    def product(j):
        rows = slice(j * z.own, (j + 1) * z.own)
        if z.L % LANES == 0:
            whole = jnp.concatenate([h_ref[i, rows, :] for i in range(z.Q)], axis=1)
            return jnp.dot(whole, wcat[...], preferred_element_type=F32)
        return sum(
            jnp.dot(h_ref[i, rows, :], wcat[i * z.L : (i + 1) * z.L, :], preferred_element_type=F32)
            for i in range(z.Q)
        )

    conv_into(z, product, y_ref, z_ref)
    local_stats(z, z_ref, hw_ref, stats_ref)
    copy.wait()


def merged(z, all_ref):
    counts = [all_ref[k, 0:1, : z.L] for k in range(z.S * z.Z)]
    means = [all_ref[k, 1:2, : z.L] for k in range(z.S * z.Z)]
    count = sum(counts)
    mean = sum(c * m for c, m in zip(counts, means)) / count
    squares = sum(
        all_ref[k, 2:3, : z.L] + counts[k] * (means[k] - mean) * (means[k] - mean)
        for k in range(z.S * z.Z)
    )
    return mean, lax.rsqrt(squares / count + EPS), count


def keep(ref, rows):
    used = rows[0].shape[1]
    ref[...] = jnp.concatenate(rows + [jnp.zeros((8 - len(rows), used), F32)], axis=0)


def over_images(z, step, init=0, unroll=2):
    px = z.H * z.W

    def one(n, carry):
        return step(n, pl.ds(pl.multiple_of(n * px, px), px), carry)

    return lax.fori_loop(0, z.n_group, one, init, unroll=unroll)


def over_halves(z, step, refs):
    px, count = z.H * z.W, z.n_group // 2
    for i, ref in enumerate(refs):

        def one(n, carry, i=i, ref=ref):
            rows = pl.ds(pl.multiple_of((i * count + n) * px, px), px)
            ref[pl.ds(pl.multiple_of(n * px, px), px), :] = step(i * count + n, rows)
            return carry

        lax.fori_loop(0, count, one, 0, unroll=2)


def hidden(z, z_ref, all_ref, hw_ref, par_ref, a_ref, b_ref, sum_ref):
    mean, inv, count = merged(z, all_ref)
    keep(sum_ref, [mean, inv, count])
    gain, shift = par_ref[0:1, :], par_ref[1:2, :]

    def step(n, rows):
        mask = image_mask(z, hw_ref[n])
        return gelu(mask * (gain * ((z_ref[rows, :] - mean) * inv) + shift)).astype(BF16)

    over_halves(z, step, (a_ref, b_ref))


def middle(z, at, z_ref, all_ref, hw_ref, par_ref, x_ref, cot_ref, *refs):
    out_ref, d_ref, sum_ref, stats_ref = refs
    mean, inv, count = merged(z, all_ref)
    keep(sum_ref, [mean, inv, count])
    gain, shift = par_ref[2:3, :], par_ref[3:4, :]
    px = z.H * z.W
    carry = (jnp.zeros((1, z.L), F32), jnp.zeros((1, z.L), F32))
    for j in range(z.Q):

        def step(n, carry, j=j):
            local = pl.ds(pl.multiple_of(n * px, px), px)
            rows = pl.ds(pl.multiple_of(j * z.own + n * px, px), px)
            mask = image_mask(z, hw_ref[j * z.n_own + n])
            normed = (z_ref[rows, :] - mean) * inv
            summed = mask * (gain * normed + shift) + x_ref[rows, :].astype(F32)
            value, slope = gelu_both(summed)
            out_ref[j, local, :] = value.astype(BF16)
            d = cot_ref[rows, :].astype(F32) * slope
            d_ref[rows, :] = d
            masked = mask * d
            return (
                carry[0] + jnp.sum(masked, 0, keepdims=True),
                carry[1] + jnp.sum(masked * normed, 0, keepdims=True),
            )

        carry = lax.fori_loop(0, z.n_own, step, carry, unroll=2)
    spread(stats_ref, list(carry))


def norm_grad(z, row, z_ref, up_ref, sum_ref, all_ref, hw_ref, par_ref, a_ref, b_ref, par_grad_ref):
    mean, inv, count = sum_ref[0:1, :], sum_ref[1:2, :], sum_ref[2:3, :]
    shift_grad = sum(all_ref[k, 0:1, : z.L] for k in range(z.S * z.Z))
    gain_grad = sum(all_ref[k, 1:2, : z.L] for k in range(z.S * z.Z))
    keep(par_grad_ref, [gain_grad, shift_grad])
    gain = par_ref[row : row + 1, :]

    def step(n, rows):
        mask = image_mask(z, hw_ref[n])
        normed = (z_ref[rows, :] - mean) * inv
        grad = inv * mask * gain * (up_ref[rows, :] - (shift_grad + normed * gain_grad) / count)
        return grad.astype(BF16)

    over_halves(z, step, (a_ref, b_ref))


def back_product(z, at, dz_ref, blocks, wcat):
    for t, block in enumerate(blocks):
        s = at[1] ^ t
        for b in range(z.Z):
            for k in range(z.K):
                rows = pl.ds(pl.multiple_of(k * z.LP + s * z.IB, z.IB), z.IB)
                if z.L % LANES == 0:
                    wcat[0, rows, b * z.L : (b + 1) * z.L] = block[b, k]
                else:
                    wcat[b, rows, :] = block[b, k]
    contract = (((1,), (1,)), ((), ()))

    def product(j):
        rows = slice(j * z.own, (j + 1) * z.own)
        if z.L % LANES == 0:
            whole = jnp.concatenate([dz_ref[i, rows, :] for i in range(z.Q)], axis=1)
            return lax.dot_general(whole, wcat[0], contract, preferred_element_type=F32)
        return sum(
            lax.dot_general(dz_ref[i, rows, :], wcat[i], contract, preferred_element_type=F32)
            for i in range(z.Q)
        )

    return product


def back_scratch(z):
    if z.L % LANES == 0:
        wide = pltpu.VMEM((1, z.K * z.LP, z.C), BF16)
    else:
        wide = pltpu.VMEM((z.Z, z.K * z.LP, z.C // z.Z), BF16)
    return [wide, pltpu.VMEM((z.own, z.K * z.LP), F32), pltpu.VMEM((z.Q, z.G, z.L), BF16)]


def hidden_grad(z, at, *refs):
    dzs, refs = refs[: 2 * z.Q], refs[2 * z.Q :]
    blocks, refs = refs[: z.S], refs[z.S :]
    z_ref, sum_ref, hw_ref, par_ref, da_ref, stats_ref, wcat, y_ref, dz_ref = refs
    gathered(z, at, dzs, dz_ref)
    conv_into(z, back_product(z, at, dz_ref, blocks, wcat), y_ref, da_ref, -1)
    mean, inv = sum_ref[0:1, :], sum_ref[1:2, :]
    gain, shift = par_ref[0:1, :], par_ref[1:2, :]

    def step(n, rows, carry):
        mask = image_mask(z, hw_ref[n])
        normed = (z_ref[rows, :] - mean) * inv
        da = da_ref[rows, :] * gelu_both(mask * (gain * normed + shift))[1]
        da_ref[rows, :] = da
        masked = mask * da
        return (
            carry[0] + jnp.sum(masked, 0, keepdims=True),
            carry[1] + jnp.sum(masked * normed, 0, keepdims=True),
        )

    zero = jnp.zeros((1, z.L), F32)
    spread(stats_ref, list(over_images(z, step, (zero, zero))))


def input_part(z, at, a_ref, b_ref, w_ref, d_ref, *refs):
    outs, (moved_ref, dx_ref) = refs[: z.Q], refs[z.Q :]
    fill_moved(z, a_ref, b_ref, moved_ref)
    contract = (((1,), (1,)), ((), ()))
    for j in range(z.Q):
        rows = slice(j * z.own, (j + 1) * z.own)
        dx_ref[j] = lax.dot_general(moved_ref[rows, :], w_ref[...], contract, preferred_element_type=F32)
    for slot in range(z.Q):

        @pl.when(at[0] == slot)
        def _(slot=slot):
            for j in range(z.Q):
                lanes = slice(slot * z.L, (slot + 1) * z.L)
                dx_ref[j, :, lanes] = dx_ref[j, :, lanes] + d_ref[j * z.own : (j + 1) * z.own, :]

    for m in range(z.Q):
        outs[m][...] = dx_ref[at[0] ^ m].astype(outs[m].dtype)


def kernel_grad(z, at, f_ref, a_ref, b_ref, mine_ref, *refs):
    theirs, (moved_ref, full_ref) = refs[:-2], refs[-2:]
    fill_moved(z, a_ref, b_ref, moved_ref)
    contract = (((0,), (0,)), ((), ()))
    if f_ref.shape[2] == z.C:
        whole = f_ref[...].reshape(z.G, z.C)
        full_ref[...] = lax.dot_general(whole, moved_ref[...], contract, preferred_element_type=F32)
    elif z.L % LANES == 0:
        whole = jnp.concatenate([f_ref[i] for i in range(z.Q)], axis=1)
        full_ref[...] = lax.dot_general(whole, moved_ref[...], contract, preferred_element_type=F32)
    else:
        for i in range(z.Q):
            full_ref[i * z.L : (i + 1) * z.L, :] = lax.dot_general(
                f_ref[i], moved_ref[...], contract, preferred_element_type=F32
            )
    for r in range(z.Q):
        for t in range(z.S):
            row = pl.multiple_of((at[0] ^ r) * z.L + (at[1] ^ t) * z.IB, z.IB)
            for k in range(z.K):
                part = full_ref[pl.ds(row, z.IB), k * z.LP : k * z.LP + z.L]
                if t == 0:
                    mine_ref[r, k] = part
                else:
                    theirs[(t - 1) * z.Q + r][k] = part.astype(BF16)


def add_sharers(z, at, *refs):
    count = 1 + z.Q * (z.S - 1)
    mine_ref, others, refs = refs[0], refs[1:count], refs[count:]
    value_ref = None
    if len(refs) > z.Q:
        value_ref, refs = refs[0], refs[1:]
    for r in range(z.Q):
        for k in range(z.K):
            total = mine_ref[r, k]
            for other in others[r :: z.Q]:
                total = total + other[k].astype(F32)
            refs[r][k * z.IB : (k + 1) * z.IB, :] = total.astype(BF16)
        if value_ref is not None:
            refs[r][z.K * z.IB :, :] = value_ref[at[0] ^ r]


def route(z, at, *refs):
    parts, refs = refs[: z.Q], refs[z.Q :]
    outs, refs = refs[: z.Z], refs[z.Z :]
    hold = refs[-1]
    for r in range(z.Q):
        hold[at[2] ^ at[0] ^ r] = parts[r][: z.K * z.IB, :]
    for m in range(z.Z):
        outs[m][...] = hold[m]
    if len(refs) == 3:
        value_ref, slots, _ = refs
        for r in range(z.Q):
            slots[at[0] ^ r] = parts[r][z.K * z.IB :, :]
        for j in range(z.Q):
            value_ref[:, j * z.L : (j + 1) * z.L] = slots[j]


def total_of(z, *refs):
    refs[-1][...] = sum(ref[...].astype(F32) for ref in refs[:-1]).astype(refs[-1].dtype)


def direction_of(grad, first, second, param, decay):
    new_first = BETA * first + (1.0 - BETA) * grad
    new_second = BETA * second + (1.0 - BETA) * grad * grad
    move = new_first / BIAS / (jnp.sqrt(new_second / BIAS) + TINY) + decay * param
    return new_first, new_second, move


def moments(z, *refs):
    parts = [refs[: z.Z], refs[z.Z : z.Z + 1]]
    refs = refs[z.Z + 1 :]
    w_ref, first_ref, second_ref, g1_ref, g2_ref, nf_ref, ns_ref, u_ref, stats_ref = refs
    rows = []
    weight_rows = []
    for j in range(2):
        total_u = jnp.zeros((1, z.L), F32)
        total_w = jnp.zeros((1, z.L), F32)
        for k in range(z.K):
            grad = sum(part[k * z.IB : (k + 1) * z.IB, :].astype(F32) for part in parts[j])
            w = w_ref[j, k]
            nf, ns, u = direction_of(grad, first_ref[j, k], second_ref[j, k], w, DECAY)
            nf_ref[j, k] = nf
            ns_ref[j, k] = ns
            u_ref[j, k] = u
            total_u = total_u + jnp.sum(u * u, 0, keepdims=True)
            total_w = total_w + jnp.sum(w * w, 0, keepdims=True)
        rows.append(total_u)
        weight_rows.append(total_w)
    spread(
        stats_ref,
        rows + weight_rows + [g1_ref[0:1, :], g1_ref[1:2, :], g2_ref[0:1, :], g2_ref[1:2, :]],
    )


def finish(z, all_ref, w_ref, u_ref, np_ref, nf_ref, ns_ref, *outs):
    nw_ref, copy_ref, nnp_ref, nnf_ref, nns_ref, trust_ref = outs
    total = all_ref[0]
    for k in range(1, z.R * z.Z):
        total = total + all_ref[k]
    tops, bottoms = [], []
    for j in range(2):
        un = jnp.sqrt(jnp.sum(total[j : j + 1, : z.L], axis=1, keepdims=True))
        wn = jnp.sqrt(jnp.sum(total[2 + j : 3 + j, : z.L], axis=1, keepdims=True))
        tops.append(wn)
        bottoms.append(un)
        scale = RATE * (wn / (un + TINY))
        for k in range(z.K):
            new = w_ref[j, k] - scale * u_ref[j, k]
            nw_ref[j, k] = new
            copy_ref[j, k] = new.astype(BF16)
    for j in range(z.Q):
        nnp_ref[:, j * z.L : (j + 1) * z.L] = all_ref[j * z.Z, 4:8, : z.L]
    param = np_ref[...]
    nf, ns, move = direction_of(nnp_ref[...], nf_ref[...], ns_ref[...], param, 0.0)
    nnf_ref[...] = nf
    nns_ref[...] = ns
    pn = jnp.sqrt(jnp.sum(param * param, axis=1, keepdims=True))
    qn = jnp.sqrt(jnp.sum(move * move, axis=1, keepdims=True))
    nnp_ref[...] = param - RATE * (pn / (qn + TINY)) * move
    for r in range(4):
        tops.append(pn[r : r + 1])
        bottoms.append(qn[r : r + 1])
    at_row = lax.broadcasted_iota(jnp.int32, (2, 6), 0)
    at_col = lax.broadcasted_iota(jnp.int32, (2, 6), 1)
    trust = jnp.zeros((2, 6), F32)
    for c in range(6):
        trust = jnp.where(at_col == c, jnp.where(at_row == 0, tops[c], bottoms[c]), trust)
    trust_ref[...] = trust


def extend(z, x_ref, valid_ref, cot_ref, out_ref):
    rows = []
    for n in range(z.n_own):
        valid = valid_ref[n].astype(F32)
        tall = jnp.sum(valid[:, 0:1], axis=0, keepdims=True)
        wide = jnp.sum(valid[0:1, :], axis=1, keepdims=True)
        rows += [tall, wide]
    rows = [jnp.broadcast_to(r, (1, z.C)) for r in rows]
    fill = z.extra - len(rows)
    extra = jnp.concatenate(rows + [jnp.zeros((fill, z.C), F32)], axis=0).astype(BF16)
    start, high = z.own + z.extra, z.own // z.Q
    for j in range(z.Q):
        out_ref[j, : z.own, :] = x_ref[...]
        out_ref[j, z.own : start, :] = extra
        for i in range(z.Q):
            out_ref[j, start:, i * z.L : (i + 1) * z.L] = cot_ref[
                i * high : (i + 1) * high, j * z.L : (j + 1) * z.L
            ]


def unpick(z, at, *refs):
    for m in range(z.Q):
        refs[z.Q][at[0] ^ m] = refs[m][...]


def pack(z, at, *refs):
    for m in range(z.Z):
        refs[z.Z][at[2] ^ m] = refs[m][0]
        refs[z.Z + 1][at[2] ^ m] = refs[m][1]


def shards(z, images, masks, cotangent, weights, first, second, params, p_first, p_second):
    q, s, b = lax.axis_index("q"), lax.axis_index("s"), lax.axis_index("z")
    at = jnp.stack([q, s, b]).astype(jnp.int32)

    def over_z(v, m):
        return lax.ppermute(v, "z", [(i, i ^ m) for i in range(z.Z)]) if m else v

    def over_s(v, m):
        return lax.ppermute(v, "s", [(i, i ^ m) for i in range(z.S)]) if m else v

    def plane(v):
        return lax.all_to_all(v, "q", 0, 0)

    def sharers(v):
        return lax.all_to_all(v, ("s", "z"), 0, 0)

    def over_q(v, m):
        return lax.ppermute(v, "q", [(i, i ^ m) for i in range(z.Q)]) if m else v

    def gather_z(w):
        return [over_z(w, m) for m in range(z.Z)]

    def fetch(w):
        own = []
        for m in range(z.Z):
            pairs = [
                ((a * z.S + c) * z.Z + e, (e * z.S + c) * z.Z + (a ^ m))
                for a in range(z.Q)
                for c in range(z.S)
                for e in range(z.Z)
            ]
            own.append(lax.ppermute(w, ("q", "s", "z"), pairs))
        return own

    def gather(a, b):
        if z.Q != 4:
            return [over_q(v, m) for v in (a, b) for m in range(z.Q)]
        a1, a2, b1, b2 = over_q(a, 1), over_q(a, 2), over_q(b, 1), over_q(b, 2)
        return [a, a1, a2, over_q(a2, 1), b, b1, b2, over_q(b1, 2)]

    def share(packed):
        return [over_s(packed, t) for t in range(z.S)]

    rows = z.own
    GL = (z.G, z.L)
    HL = (z.G // 2, z.L)
    many = z.S * z.Z
    piece = (z.K, z.IB, z.L)
    blocks = near((z.Z, *piece), BF16)
    stat = near((many, 8, LANES))
    conv_scratch = [pltpu.VMEM((z.C, z.K * z.LP), BF16), pltpu.VMEM((rows, z.K * z.LP), F32)]
    grad_scratch = [pltpu.VMEM((z.G, z.K * z.LP), BF16), pltpu.VMEM((z.C, z.K * z.LP), F32)]
    cot_rows = cotangent.reshape(rows, z.C)
    image_rows = images.reshape(rows, z.C)

    low = weights.astype(BF16)
    both = fetch(low)
    x_all = plane(
        call(
            functools.partial(extend, z),
            near((z.Q, z.sent, z.C), BF16),
            (image_rows, masks, cot_rows),
            far=(image_rows, masks, cot_rows),
        )
    )
    both, x_all = together((both, x_all))
    front_one, front_two = call(functools.partial(pack, z), [blocks] * 2, (at, *both))
    w_far = away((z.C, z.K * z.LP), BF16)
    x_far = away((z.Q, rows, z.C), BF16)
    z1, x_slice, cots, slice_params, hw, stats, w_far, x_far = call(
        functools.partial(first_conv, z),
        [
            near(GL),
            near(GL, BF16),
            near(GL, BF16),
            near((4, z.L)),
            near((z.n_group, 8, LANES)),
            stat,
            w_far,
            x_far,
        ],
        (at, params, x_all, *share(front_one)),
        conv_scratch + [pltpu.SemaphoreType.DMA((2,))],
        limit=16,
        raw=(w_far, x_far),
    )
    stats = sharers(stats)
    ha, hb, sum_one = call(
        functools.partial(hidden, z),
        [near(HL, BF16), near(HL, BF16), near((8, z.L))],
        (z1, stats, hw, slice_params),
    )
    ha, hb, front_two = together((ha, hb, front_two))
    hs = gather(ha, hb)
    h_far = away((z.Q, *GL), BF16)
    z2, stats, h_far, *back = call(
        functools.partial(second_conv, z),
        [near(GL), stat, h_far] + [near(piece, BF16)] * z.Q,
        (at, *hs, *share(front_two), hw),
        conv_scratch + [pltpu.VMEM((z.Q, *GL), BF16), pltpu.SemaphoreType.DMA],
        limit=16,
        raw=(h_far,),
    )
    stats, back = together((stats, back))
    stats, back = together((sharers(stats), [over_q(back[m], m) for m in range(z.Q)]))
    out, d, sum_two, stats = call(
        functools.partial(middle, z),
        [near((z.Q, rows, z.L), BF16), near(GL), near((8, z.L)), stat],
        (at, z2, stats, hw, slice_params, x_slice, cots),
    )
    da, db, grad_two = call(
        functools.partial(norm_grad, z, 2),
        [near(HL, BF16), near(HL, BF16), near((8, z.L))],
        (z2, d, sum_two, sharers(stats), hw, slice_params),
    )
    da, db, back = together((da, db, back))
    keep_two = call(functools.partial(unpick, z), near((z.Q, *piece), BF16), (at, *back))
    dz2s = gather(da, db)

    def kernel_gradient(feature, halves, **more):
        mine, *theirs = call(
            functools.partial(kernel_grad, z),
            [near((z.Q, *piece))] + [near(piece, BF16)] * (z.Q * (z.S - 1)),
            (at, feature, *halves),
            grad_scratch,
            limit=14,
            cost=COST_GRAD,
            far=(feature,),
            **more,
        )
        return mine, [over_s(theirs[(t - 1) * z.Q + r], t) for t in range(1, z.S) for r in range(z.Q)]

    def add_up(mine, received, *value):
        more = rows if value else 0
        return call(
            functools.partial(add_sharers, z),
            [near((z.K * z.IB + more, z.L), BF16)] * z.Q,
            (at, mine, *received, *value),
        )

    def by_plane(parts):
        return [over_q(parts[r], r) for r in range(z.Q)]

    def along(parts):
        return [over_z(parts[m], m) for m in range(z.Z)]

    parts_two = add_up(*kernel_gradient(h_far, (da, db)), out)
    da1, stats = call(
        functools.partial(hidden_grad, z),
        [near(GL), stat],
        (at, *dz2s, *share(keep_two), z1, sum_one, hw, slice_params),
        back_scratch(z),
        limit=16,
    )
    stats, parts_two = together((stats, parts_two))
    stats, parts_two = together((sharers(stats), by_plane(parts_two)))
    da, db, grad_one = call(
        functools.partial(norm_grad, z, 0),
        [near(HL, BF16), near(HL, BF16), near((8, z.L))],
        (z1, da1, sum_one, stats, hw, slice_params),
    )
    flat = near((z.K * z.IB, z.L), BF16)
    hold = pltpu.VMEM((z.Z, z.K * z.IB, z.L), BF16)
    *parts_two, values = call(
        functools.partial(route, z),
        [flat] * z.Z + [near((rows, z.C), BF16)],
        (at, *parts_two),
        [pltpu.VMEM((z.Q, rows, z.L), BF16), hold],
        after=(da,),
    )
    mine, received = kernel_gradient(x_far, (da, db))
    parts_one = add_up(mine, received)
    parts_one, parts_two = by_plane(parts_one), along(parts_two)
    parts_one, parts_two = together((parts_one, parts_two))
    dxs = call(
        functools.partial(input_part, z),
        [near((rows, z.C))] + [near((rows, z.C), BF16)] * (z.Q - 1),
        (at, da, db, w_far, d),
        [grad_scratch[0], pltpu.VMEM((z.Q, rows, z.C), F32)],
        limit=16,
        cost=COST_GRAD,
        far=(w_far,),
        after=(received[0],),
    )
    parts_one = call(functools.partial(route, z), [flat] * z.Z, (at, *parts_one), [hold], after=(dxs[0],))
    parts_one, dxs, parts_two = together((parts_one, dxs, parts_two))
    parts_one = along(parts_one)
    total_two = call(functools.partial(total_of, z), shape((z.K * z.IB, z.L)), tuple(parts_two))
    dxs = [over_q(dxs[m], m) for m in range(z.Q)]
    parts_one, dxs = together((parts_one, dxs))
    new_first, new_second, move, stats = call(
        functools.partial(moments, z),
        [shape(weights.shape)] * 2 + [near(weights.shape), near((z.R * z.Z, 8, LANES))],
        (*parts_one, total_two, weights, first, second, grad_one, grad_two),
        far=(total_two,),
    )
    stats = lax.all_to_all(stats, ("s", "q", "z"), 0, 0)
    dx = call(functools.partial(total_of, z), shape((rows, z.C), BF16), tuple(dxs))
    new_weights, copies, new_params, new_p_first, new_p_second, trust = call(
        functools.partial(finish, z),
        [shape(weights.shape), shape(weights.shape, BF16)] + [shape(params.shape)] * 3 + [shape((2, 6))],
        (stats, weights, move, params, p_first, p_second),
    )
    return (
        values.reshape(images.shape),
        dx.reshape(images.shape),
        new_weights,
        copies,
        new_first,
        new_second,
        new_params,
        new_p_first,
        new_p_second,
        trust,
    )


def solution(mesh):
    def whole(images, masks, cotangent, weights, first, second, params, p_first, p_second):
        z = Sizes(mesh, images.shape, weights.shape)
        inner = Mesh(mesh.devices.reshape(z.Q, z.S, z.Z), ("q", "s", "z"))
        pixels = P(("q", "s", "z"), None, None, None)
        kernels = P(None, None, ("q", "s"), "z")
        return jax.shard_map(
            functools.partial(shards, z),
            mesh=inner,
            in_specs=(pixels, P(("q", "s", "z"), None, None), pixels, kernels, kernels, kernels, P(), P(), P()),
            out_specs=(pixels, pixels, kernels, kernels, kernels, kernels, P(), P(), P(), P()),
            check_vma=False,
        )(images, masks, cotangent, weights, first, second, params, p_first, p_second)

    return whole
```

time: 258 us -> 184 us (0.71)
  starting transfers between devices: 98.9 us -> 59.2 us
  Pallas kernels: 53.7 us -> 30.6 us
  blocking collectives: 19.4 us -> 36.1 us
  between operations: 14.5 us -> 0.92 us
  local copies, waits for them, and re-layouts: 11.3 us -> 1.44 us
    ppermute x8 -> x4, waiting for transfers between devices: 0.02 us -> 25.7 us  [fetch(): own.append(lax.ppermute(w, ('q', 's', 'z'), pairs))]
    ppermute x8 -> x4, starting transfers between devices: 31.4 us -> 6.79 us  [fetch(): own.append(lax.ppermute(w, ('q', 's', 'z'), pairs))]
    pallas_call x17 -> x21, Pallas kernels: 53.7 us -> 30.6 us  [call(): pl.pallas_call(run, out_shape=out_shape, in_specs=[pl.BlockSpec(memory_sp...]
    ppermute x21 -> x24, waiting for transfers between devices: 31.3 us -> 10.5 us  [over_q(): return lax.ppermute(v, 'q', [(i, i ^ m) for i in range(z.Q)]) if m else v]
    all_to_all x2 -> x4, blocking collectives: 19.4 us -> 36.1 us  [sharers(): return lax.all_to_all(v, ('s', 'z'), 0, 0)]
    ppermute x21 -> x24, starting transfers between devices: 44.3 us -> 30.6 us  [over_q(): return lax.ppermute(v, 'q', [(i, i ^ m) for i in range(z.Q)]) if m else v]
    all_to_all x2 -> x1, waiting for transfers between devices: 10 us -> 0.01 us  [plane(): return lax.all_to_all(v, 'q', 0, 0)]
    unnamed x108 -> x15, local copies, waits for them, and re-layouts: 8.89 us -> 1.44 us
  transfers between devices with their start and end apart: 49 -> 47, of which waited for: 17 -> 18; matrix products, arithmetic and copies ran while one was open for 1% -> 0% of each run, Pallas kernels for 16% -> 5%
where the time goes in v2:
time: 184 us
  starting transfers between devices  59.2 us (32%)
  waiting for transfers between devices  55.3 us (30%)
  blocking collectives  36.1 us (20%)
  Pallas kernels  30.6 us (17%)
    all_to_all x4, blocking collectives, sharers(): return lax.all_to_all(v, ('s', 'z'), 0, 0)  36.1 us
    ppermute x24, starting transfers between devices, over_q(): return lax.ppermute(v, 'q', [(i, i ^ m) for i in range(z.Q)]) if m else v  30.6 us
    pallas_call x21, Pallas kernels, call(): pl.pallas_call(run, out_shape=out_shape, in_specs=[pl.BlockSpec(memory_sp...  30.6 us
    ppermute x4, waiting for transfers between devices, fetch(): own.append(lax.ppermute(w, ('q', 's', 'z'), pairs))  25.7 us
    ppermute x24, waiting for transfers between devices, over_q(): return lax.ppermute(v, 'q', [(i, i ^ m) for i in range(z.Q)]) if m else v  10.5 us
    ppermute x6, waiting for transfers between devices, over_z(): return lax.ppermute(v, 'z', [(i, i ^ m) for i in range(z.Z)]) if m else v  10.4 us
    ppermute x6, starting transfers between devices, over_z(): return lax.ppermute(v, 'z', [(i, i ^ m) for i in range(z.Z)]) if m else v  9.06 us
    ppermute x4, starting transfers between devices, fetch(): own.append(lax.ppermute(w, ('q', 's', 'z'), pairs))  6.79 us
  transfers between devices with their start and end apart: 47, of which 18 were waited for; matrix products, arithmetic and copies ran while one was open for 0% of the time, Pallas kernels for 5%

profile of v2, /device:TPU:0, one launch (start us, length us, event | category | flops | bytes accessed | tf_op | source)
XLA Modules:
  0.0 183.6 jit_solution(2104422316795026384)
XLA Ops:
  0.6 2.3 %shard_map.168 = bf16[4,336,512]{2,1,0:T(8,128)(2,1)} custom-call(bf16[256,512]{1,0:T(8,128)(2,1)} %bitcast.9, s32[4,8,8]{2,1,0:T(8,128)} %refs_1_.3, bf16[256,512]{1,0:T(8,128)(2,1)} %bitcast.10), custom_call_target="tpu_custom_call" | custom-call | flops 1 | bytes 1 | tf_op jit(solution)/shard_map/pallas_call | solution.py:68
  2.9 5.3 %all-to-all-start = ((bf16[4,336,512]{2,1,0:T(8,128)(2,1)}), bf16[4,336,512]{2,1,0:T(8,128)(2,1)S(1)}, u32[]{:S(2)}, u32[]{:S(2)}) async-start(bf16[4,336,512]{2,1,0:T(8,128)(2,1)} %shard_map.168), calls=%async_computation | async-start | bytes 2752512 | tf_op jit(solution)/shard_map/all_to_all | solution.py:630
  8.3 3.7 %collective-permute-start.3 = (bf16[2,9,64,128]{3,2,1,0:T(8,128)(2,1)S(1)}, bf16[2,9,64,128]{3,2,1,0:T(8,128)(2,1)S(1)}, u32[]{:S(2)}, u32[]{:S(2)}) collective-permute-start(bf16[2,9,64,128]{3,2,1,0:T(8,128)(2,1)S(1)} %convert_element_type.3), channel_id=1, source_target_pairs={{0,3},{1,11},{2,19},{3,27},{4,7},{5,15},{6,23},{7,31},{8,2},{9,10}... | collective-permute-start | bytes 884744 | tf_op jit(solution)/shard_map/ppermute | solution.py:650
  11.9 2.0 %collective-permute-start.2 = (bf16[2,9,64,128]{3,2,1,0:T(8,128)(2,1)S(1)}, bf16[2,9,64,128]{3,2,1,0:T(8,128)(2,1)S(1)}, u32[]{:S(2)}, u32[]{:S(2)}) collective-permute-start(bf16[2,9,64,128]{3,2,1,0:T(8,128)(2,1)S(1)} %convert_element_type.3), channel_id=1, source_target_pairs={{0,2},{1,10},{2,18},{3,26},{4,6},{5,14},{6,22},{7,30},{8,3},{9,11}... | collective-permute-start | bytes 884744 | tf_op jit(solution)/shard_map/ppermute | solution.py:650
  14.4 0.7 collective-permute-start
  15.2 23.7 %collective-permute-done.3.refs_4_ = bf16[2,9,64,128]{3,2,1,0:T(8,128)(2,1)S(1)} collective-permute-done((bf16[2,9,64,128]{3,2,1,0:T(8,128)(2,1)S(1)}, bf16[2,9,64,128]{3,2,1,0:T(8,128)(2,1)S(1)}, u32[]{:S(2)}, u32[]{:S(2)}) %collective-permute-start.3) | collective-permute-done | bytes 294944 | tf_op jit(solution)/shard_map/ppermute | solution.py:650
  38.9 1.9 %collective-permute-done.2.refs_3_ = bf16[2,9,64,128]{3,2,1,0:T(8,128)(2,1)S(1)} collective-permute-done((bf16[2,9,64,128]{3,2,1,0:T(8,128)(2,1)S(1)}, bf16[2,9,64,128]{3,2,1,0:T(8,128)(2,1)S(1)}, u32[]{:S(2)}, u32[]{:S(2)}) %collective-permute-start.2) | collective-permute-done | bytes 294944 | tf_op jit(solution)/shard_map/ppermute | solution.py:650
  40.8 0.6 shard_map.169
  41.6 2.0 %collective-permute-done.4.refs_4_ = bf16[4,9,64,128]{3,2,1,0:T(8,128)(2,1)S(1)} collective-permute-done((bf16[4,9,64,128]{3,2,1,0:T(8,128)(2,1)S(1)}, bf16[4,9,64,128]{3,2,1,0:T(8,128)(2,1)S(1)}, u32[]{:S(2)}, u32[]{:S(2)}) %collective-permute-start.4) | collective-permute-done | bytes 589856 | tf_op jit(solution)/shard_map/ppermute | solution.py:627
  43.5 2.7 %shard_map.170 = (f32[1024,128]{1,0:T(8,128)S(1)}, bf16[1024,128]{1,0:T(8,128)(2,1)S(1)}, bf16[1024,128]{1,0:T(8,128)(2,1)S(1)}, f32[4,128]{1,0:T(4,128)S(1)}, f...) custom-call(s32[3]{0:T(128)S(1)} %pad_add_fusion.refs_0_, ...), custom_call_target="tpu_custom_call" | custom-call | flops 1 | bytes 1 | tf_op jit(solution)/shard_map/pallas_call | solution.py:68
  46.3 11.7 %all_to_all.30.refs_1_ = f32[8,8,128]{2,1,0:T(8,128)S(1)} all-to-all(f32[8,8,128]{2,1,0:T(8,128)S(1)} %get-tuple-element.152), channel_id=1, replica_groups=mesh['ha'=2,'wa'=4,'ba'=4] {'wa':(2)2,'ba'}, dimensions={0} | all-to-all | bytes 65536 | tf_op jit(solution)/shard_map/all_to_all | solution.py:633
  58.6 0.8 collective-permute-start.6
  59.4 3.6 %collective-permute-start.8 = (bf16[512,128]{1,0:T(8,128)(2,1)S(1)}, bf16[512,128]{1,0:T(8,128)(2,1)S(1)}, u32[]{:S(2)}, u32[]{:S(2)}) collective-permute-start(bf16[512,128]{1,0:T(8,128)(2,1)S(1)} %get-tuple-element.159.refs_5_), channel_id=1, source_target_pairs={{0,8},{8,0},{16,24},{24,16},{1,9},{9,1},{17,25},{25,17},{2,10},{10... | collective-permute-start | bytes 393224 | tf_op jit(solution)/shard_map/ppermute | solution.py:636
  63.0 1.3 collective-permute-start.9
  64.4 4.2 %collective-permute-start.7 = (bf16[512,128]{1,0:T(8,128)(2,1)S(1)}, bf16[512,128]{1,0:T(8,128)(2,1)S(1)}, u32[]{:S(2)}, u32[]{:S(2)}) collective-permute-start(bf16[512,128]{1,0:T(8,128)(2,1)S(1)} %collective-permute-done.6.refs_3_), channel_id=1, source_target_pairs={{0,8},{8,0},{16,24},{24,16},{1,9},{9,1},{17,25},{25,17},{2,10},{10... | collective-permute-start | bytes 393224 | tf_op jit(solution)/shard_map/ppermute | solution.py:636
  69.0 1.1 collective-permute-done.5.refs_2_
  70.1 2.3 %collective-permute-done.7.refs_4_ = bf16[512,128]{1,0:T(8,128)(2,1)S(1)} collective-permute-done((bf16[512,128]{1,0:T(8,128)(2,1)S(1)}, bf16[512,128]{1,0:T(8,128)(2,1)S(1)}, u32[]{:S(2)}, u32[]{:S(2)}) %collective-permute-start.7) | collective-permute-done | bytes 131104 | tf_op jit(solution)/shard_map/ppermute | solution.py:636
  72.3 1.2 collective-permute-done.10.refs_8_
  73.6 2.7 %shard_map.172 = (f32[1024,128]{1,0:T(8,128)S(1)}, f32[8,8,128]{2,1,0:T(8,128)S(1)}, bf16[4,1024,128]{2,1,0:T(8,128)(2,1)}, bf16[9,64,128]{2,1,0:T(8,128)(2,1)S(...) custom-call(s32[3]{0:T(128)S(1)} %pad_add_fusion.refs_0_, ...), custom_call_target="tpu_custom_call" | custom-call | flops 1 | bytes 1 | tf_op jit(solution)/shard_map/pallas_call | solution.py:68
  76.3 0.8 collective-permute-start.12
  77.1 1.3 collective-permute-start.13
  78.4 1.4 collective-permute-start.14
  79.8 8.1 %all_to_all.31.refs_2_ = f32[8,8,128]{2,1,0:T(8,128)S(1)} all-to-all(f32[8,8,128]{2,1,0:T(8,128)S(1)} %get-tuple-element.167), channel_id=1, replica_groups=mesh['ha'=2,'wa'=4,'ba'=4] {'wa':(2)2,'ba'}, dimensions={0} | all-to-all | bytes 65536 | tf_op jit(solution)/shard_map/all_to_all | solution.py:633
  88.0 1.3 shard_map.173
  89.3 8.1 %all_to_all.32.refs_3_ = f32[8,8,128]{2,1,0:T(8,128)S(1)} all-to-all(f32[8,8,128]{2,1,0:T(8,128)S(1)} %get-tuple-element.177), channel_id=1, replica_groups=mesh['ha'=2,'wa'=4,'ba'=4] {'wa':(2)2,'ba'}, dimensions={0} | all-to-all | bytes 65536 | tf_op jit(solution)/shard_map/all_to_all | solution.py:633
  98.9 1.7 collective-permute-start.18
  100.6 3.1 %shard_map.177 = (f32[4,9,64,128]{3,2,1,0:T(8,128)S(1)}, bf16[9,64,128]{2,1,0:T(8,128)(2,1)S(1)}, bf16[9,64,128]{2,1,0:T(8,128)(2,1)S(1)}, bf16[9,64,128]{2,1,0:T(8,128)(2,1)S(1)}, bf16[9,64,128]{2,1,0:T(8,128)(2,1)S(1)}) custom-call(s32[3]{0:T(128)S(1)} %pad_add_fusion.refs_0_, bf16[4,1024,128]{2,1,0:T(8,128)(2,1)} %get-tuple-element.192.refs_1_, ...), custom_call_target="tpu_custom_call" | custom-call | flops 3000000000 | bytes 1 | tf_op jit(solution)/shard_map/pallas_call | solution.py:68
  105.1 1.0 collective-permute-start.15
  106.1 1.0 collective-permute-start.19
  107.1 1.0 collective-permute-start.17
  108.1 1.1 collective-permute-start.20
  109.2 0.7 shard_map.178
  109.8 1.6 collective-permute-done.15.refs_2_
  111.5 0.9 collective-permute-done.19.refs_7_
  112.4 1.1 collective-permute-done.17.refs_4_
  113.5 1.0 collective-permute-done.20.refs_8_
  114.5 3.0 %shard_map.176 = (f32[1024,128]{1,0:T(8,128)S(1)}, f32[8,8,128]{2,1,0:T(8,128)S(1)}) custom-call(s32[3]{0:T(128)S(1)} %pad_add_fusion.refs_0_, bf16[512,128]{1,0:T(8,128)(2,1)S(1)} %get-tuple-element.184.refs_1_.refs_2_, bf16[512,128]{1,0:T(8,128)(2,1)S(1)} %collective-permute-done.15.refs_2_, bf16[512,128]{1,0:T(8,128)(2,1)S(1)} %collective-permute-done.16.refs_3_, ...), custom_call_target="tpu_custom_call" | custom-call | flops 1 | bytes 1 | tf_op jit(solution)/shard_map/pallas_call | solution.py:68
  117.5 0.8 collective-permute-start.26
  118.3 1.3 collective-permute-start.27
  119.6 1.5 collective-permute-start.28
  121.1 8.1 %all_to_all.33.refs_3_ = f32[8,8,128]{2,1,0:T(8,128)S(1)} all-to-all(f32[8,8,128]{2,1,0:T(8,128)S(1)} %get-tuple-element.203), channel_id=1, replica_groups=mesh['ha'=2,'wa'=4,'ba'=4] {'wa':(2)2,'ba'}, dimensions={0} | all-to-all | bytes 65536 | tf_op jit(solution)/shard_map/all_to_all | solution.py:633
  129.2 0.7 collective-permute-done.28.refs_4_
  130.2 3.1 %shard_map.181 = (f32[4,9,64,128]{3,2,1,0:T(8,128)S(1)}, bf16[9,64,128]{2,1,0:T(8,128)(2,1)S(1)}, bf16[9,64,128]{2,1,0:T(8,128)(2,1)S(1)}, bf16[9,64,128]{2,1,0:T(8,128)(2,1)S(1)}, bf16[9,64,128]{2,1,0:T(8,128)(2,1)S(1)}) custom-call(s32[3]{0:T(128)S(1)} %pad_add_fusion.refs_0_, bf16[4,256,512]{2,1,0:T(8,128)(2,1)} %get-tuple-element.216.refs_1_, ...), custom_call_target="tpu_custom_call" | custom-call | flops 3000000000 | bytes 1 | tf_op jit(solution)/shard_map/pallas_call | solution.py:68
  134.4 0.7 shard_map.180
  136.2 3.3 %collective-permute-start.38 = (bf16[576,128]{1,0:T(8,128)(2,1)S(1)}, bf16[576,128]{1,0:T(8,128)(2,1)S(1)}, u32[]{:S(2)}, u32[]{:S(2)}) collective-permute-start(bf16[576,128]{1,0:T(8,128)(2,1)S(1)} %get-tuple-element.230), channel_id=1, source_target_pairs={{0,3},{1,2},{2,1},{3,0},{4,7},{5,6},{6,5},{7,4},{8,11},{9,10},{10,... | collective-permute-start | bytes 442376 | tf_op jit(solution)/shard_map/ppermute | solution.py:624
  139.5 0.6 shard_map.182
  140.2 0.7 collective-permute-start.33
  140.9 1.4 collective-permute-start.34
  142.2 0.7 collective-permute-done.36.refs_1_
  142.9 1.4 collective-permute-start.35
  144.3 3.0 %shard_map.183 = (f32[256,512]{1,0:T(8,128)S(1)}, bf16[256,512]{1,0:T(8,128)(2,1)S(1)}, bf16[256,512]{1,0:T(8,128)(2,1)S(1)}, bf16[256,512]{1,0:T(8,128)(2,1)S(1)}) custom-call(s32[3]{0:T(128)S(1)} %pad_add_fusion.refs_0_, bf16[512,128]{1,0:T(8,128)(2,1)S(1)} %get-tuple-element.214.refs_5_.refs_2_.refs_1_, ...), custom_call_target="tpu_custom_call" | custom-call | flops 3000000000 | bytes 1 | tf_op jit(solution)/shard_map/pallas_call | solution.py:68
  147.4 2.1 %collective-permute-done.37.refs_2_ = bf16[576,128]{1,0:T(8,128)(2,1)S(1)} collective-permute-done((bf16[576,128]{1,0:T(8,128)(2,1)S(1)}, bf16[576,128]{1,0:T(8,128)(2,1)S(1)}, u32[]{:S(2)}, u32[]{:S(2)}) %collective-permute-start.37) | collective-permute-done | bytes 147488 | tf_op jit(solution)/shard_map/ppermute | solution.py:624
  150.7 2.2 %collective-permute-start.39 = (bf16[576,128]{1,0:T(8,128)(2,1)S(1)}, bf16[576,128]{1,0:T(8,128)(2,1)S(1)}, u32[]{:S(2)}, u32[]{:S(2)}) collective-permute-start(bf16[576,128]{1,0:T(8,128)(2,1)S(1)} %get-tuple-element.249), channel_id=1, source_target_pairs={{0,1},{1,0},{2,3},{3,2},{4,5},{5,4},{6,7},{7,6},{8,9},{9,8},{10,11... | collective-permute-start | bytes 442376 | tf_op jit(solution)/shard_map/ppermute | solution.py:624
  153.5 1.4 collective-permute-start.43
  154.9 1.5 collective-permute-start.44
  156.4 2.4 %collective-permute-start.41 = (bf16[576,128]{1,0:T(8,128)(2,1)S(1)}, bf16[576,128]{1,0:T(8,128)(2,1)S(1)}, u32[]{:S(2)}, u32[]{:S(2)}) collective-permute-start(bf16[576,128]{1,0:T(8,128)(2,1)S(1)} %get-tuple-element.251), channel_id=1, source_target_pairs={{0,3},{1,2},{2,1},{3,0},{4,7},{5,6},{6,5},{7,4},{8,11},{9,10},{10,... | collective-permute-start | bytes 442376 | tf_op jit(solution)/shard_map/ppermute | solution.py:624
  158.9 0.7 copy-done.1
  159.6 7.5 %collective-permute-done.40.refs_2_ = bf16[576,128]{1,0:T(8,128)(2,1)S(1)} collective-permute-done((bf16[576,128]{1,0:T(8,128)(2,1)S(1)}, bf16[576,128]{1,0:T(8,128)(2,1)S(1)}, u32[]{:S(2)}, u32[]{:S(2)}) %collective-permute-start.40) | collective-permute-done | bytes 147488 | tf_op jit(solution)/shard_map/ppermute | solution.py:624
  167.2 2.5 %shard_map.187 = (f32[2,9,64,128]{3,2,1,0:T(8,128)}, f32[2,9,64,128]{3,2,1,0:T(8,128)}, f32[2,9,64,128]{3,2,1,0:T(8,128)S(1)}, f32[32,8,128]{2,1,0:T(8,128)}) custom-call(bf16[576,128]{1,0:T(8,128)(2,1)S(1)} %get-tuple-element.260.refs_0_, bf16[576,128]{1,0:T(8,128)(2,1)S(1)} %collective-permute-done.39.refs_1_, ...), custom_call_target="tpu_custom_call" | custom-call | flops 1 | bytes 1 | tf_op jit(solution)/shard_map/pallas_call | solution.py:68
  169.7 4.9 %all-to-all-start.5 = ((f32[32,8,128]{2,1,0:T(8,128)}), f32[32,8,128]{2,1,0:T(8,128)S(1)}, u32[]{:S(2)}, u32[]{:S(2)}) async-start(f32[32,8,128]{2,1,0:T(8,128)} %get-tuple-element.270), calls=%async_computation.5 | async-start | bytes 262144 | tf_op jit(solution)/shard_map/all_to_all | solution.py:815
  174.6 0.7 copy.19
  175.3 0.8 shard_map.185
  176.1 6.4 %all-to-all-done.5.refs_0_ = f32[32,8,128]{2,1,0:T(8,128)S(1)} async-done(((f32[32,8,128]{2,1,0:T(8,128)}), f32[32,8,128]{2,1,0:T(8,128)S(1)}, u32[]{:S(2)}, u32[]{:S(2)}) %all-to-all-start.5) | async-done | bytes 131104 | tf_op jit(solution)/shard_map/all_to_all | solution.py:815
  182.5 1.1 shard_map.188
  (72 shorter events, 8.9 us)
Async XLA Ops:
  2.9 5.3 %copy-start = (f32[2,9,64,128]{3,2,1,0:T(8,128)S(1)}, f32[2,9,64,128]{3,2,1,0:T(8,128)}, u32[]{:S(2)}) copy-start(f32[2,9,64,128]{3,2,1,0:T(8,128)} %refs_1_.5) | copy-start | bytes 1769476
  2.9 37.9 %all-to-all-start = ((bf16[4,336,512]{2,1,0:T(8,128)(2,1)}), bf16[4,336,512]{2,1,0:T(8,128)(2,1)S(1)}, u32[]{:S(2)}, u32[]{:S(2)}) async-start(bf16[4,336,512]{2,1,0:T(8,128)(2,1)} %shard_map.168), calls=%async_computation | async-start | bytes 2752512 | tf_op jit(solution)/shard_map/all_to_all | solution.py:630
  8.2 35.3 %copy-start.4 = (f32[4,512]{1,0:T(4,128)S(1)}, f32[4,512]{1,0:T(4,128)}, u32[]{:S(2)}) copy-start(f32[4,512]{1,0:T(4,128)} %refs_3_.1) | copy-start | bytes 24580
  8.3 30.6 %collective-permute-start.3 = (bf16[2,9,64,128]{3,2,1,0:T(8,128)(2,1)S(1)}, bf16[2,9,64,128]{3,2,1,0:T(8,128)(2,1)S(1)}, u32[]{:S(2)}, u32[]{:S(2)}) collective-permute-start(bf16[2,9,64,128]{3,2,1,0:T(8,128)(2,1)S(1)} %convert_element_type.3), channel_id=1, source_target_pairs={{0,3},{1,11},{2,19},{3,27},{4,7},{5,15},{6,23},{7,31},{8,2},{9,10}... | collective-permute-start | bytes 884744 | tf_op jit(solution)/shard_map/ppermute | solution.py:650
  11.9 28.9 %collective-permute-start.2 = (bf16[2,9,64,128]{3,2,1,0:T(8,128)(2,1)S(1)}, bf16[2,9,64,128]{3,2,1,0:T(8,128)(2,1)S(1)}, u32[]{:S(2)}, u32[]{:S(2)}) collective-permute-start(bf16[2,9,64,128]{3,2,1,0:T(8,128)(2,1)S(1)} %convert_element_type.3), channel_id=1, source_target_pairs={{0,2},{1,10},{2,18},{3,26},{4,6},{5,14},{6,22},{7,30},{8,3},{9,11}... | collective-permute-start | bytes 884744 | tf_op jit(solution)/shard_map/ppermute | solution.py:650
  14.0 26.9 %collective-permute-start.1 = (bf16[2,9,64,128]{3,2,1,0:T(8,128)(2,1)S(1)}, bf16[2,9,64,128]{3,2,1,0:T(8,128)(2,1)S(1)}, u32[]{:S(2)}, u32[]{:S(2)}) collective-permute-start(bf16[2,9,64,128]{3,2,1,0:T(8,128)(2,1)S(1)} %convert_element_type.3), channel_id=1, source_target_pairs={{0,1},{1,9},{2,17},{3,25},{4,5},{5,13},{6,21},{7,29},{8,0},{9,8},{... | collective-permute-start | bytes 884744 | tf_op jit(solution)/shard_map/ppermute | solution.py:650
  14.4 26.4 %collective-permute-start = (bf16[2,9,64,128]{3,2,1,0:T(8,128)(2,1)S(1)}, bf16[2,9,64,128]{3,2,1,0:T(8,128)(2,1)S(1)}, u32[]{:S(2)}, u32[]{:S(2)}) collective-permute-start(bf16[2,9,64,128]{3,2,1,0:T(8,128)(2,1)S(1)} %convert_element_type.3), channel_id=1, source_target_pairs={{0,0},{1,8},{2,16},{3,24},{4,4},{5,12},{6,20},{7,28},{8,1},{9,9},{... | collective-permute-start | bytes 884744 | tf_op jit(solution)/shard_map/ppermute | solution.py:650
  41.5 2.1 %collective-permute-start.4 = (bf16[4,9,64,128]{3,2,1,0:T(8,128)(2,1)S(1)}, bf16[4,9,64,128]{3,2,1,0:T(8,128)(2,1)S(1)}, u32[]{:S(2)}, u32[]{:S(2)}) collective-permute-start(bf16[4,9,64,128]{3,2,1,0:T(8,128)(2,1)S(1)} %get-tuple-element.150.refs_3_), channel_id=1, source_target_pairs={{0,4},{4,0},{1,5},{5,1},{2,6},{6,2},{3,7},{7,3},{8,12},{12,8},{9,1... | collective-permute-start | bytes 1769480 | tf_op jit(solution)/shard_map/ppermute | solution.py:627
  58.4 15.2 %collective-permute-start.11 = (bf16[4,9,64,128]{3,2,1,0:T(8,128)(2,1)S(1)}, bf16[4,9,64,128]{3,2,1,0:T(8,128)(2,1)S(1)}, u32[]{:S(2)}, u32[]{:S(2)}) collective-permute-start(bf16[4,9,64,128]{3,2,1,0:T(8,128)(2,1)S(1)} %get-tuple-element.160.refs_9_), channel_id=1, source_target_pairs={{0,4},{4,0},{1,5},{5,1},{2,6},{6,2},{3,7},{7,3},{8,12},{12,8},{9,1... | collective-permute-start | bytes 1769480 | tf_op jit(solution)/shard_map/ppermute | solution.py:627
  58.6 5.8 %collective-permute-start.6 = (bf16[512,128]{1,0:T(8,128)(2,1)S(1)}, bf16[512,128]{1,0:T(8,128)(2,1)S(1)}, u32[]{:S(2)}, u32[]{:S(2)}) collective-permute-start(bf16[512,128]{1,0:T(8,128)(2,1)S(1)} %get-tuple-element.158.refs_1_), channel_id=1, source_target_pairs={{0,16},{8,24},{16,0},{24,8},{1,17},{9,25},{17,1},{25,9},{2,18},{10... | collective-permute-start | bytes 393224 | tf_op jit(solution)/shard_map/ppermute | solution.py:636
  59.4 9.3 %collective-permute-start.8 = (bf16[512,128]{1,0:T(8,128)(2,1)S(1)}, bf16[512,128]{1,0:T(8,128)(2,1)S(1)}, u32[]{:S(2)}, u32[]{:S(2)}) collective-permute-start(bf16[512,128]{1,0:T(8,128)(2,1)S(1)} %get-tuple-element.159.refs_5_), channel_id=1, source_target_pairs={{0,8},{8,0},{16,24},{24,16},{1,9},{9,1},{17,25},{25,17},{2,10},{10... | collective-permute-start | bytes 393224 | tf_op jit(solution)/shard_map/ppermute | solution.py:636
  63.0 7.1 %collective-permute-start.5 = (bf16[512,128]{1,0:T(8,128)(2,1)S(1)}, bf16[512,128]{1,0:T(8,128)(2,1)S(1)}, u32[]{:S(2)}, u32[]{:S(2)}) collective-permute-start(bf16[512,128]{1,0:T(8,128)(2,1)S(1)} %get-tuple-element.158.refs_1_), channel_id=1, source_target_pairs={{0,8},{8,0},{16,24},{24,16},{1,9},{9,1},{17,25},{25,17},{2,10},{10... | collective-permute-start | bytes 393224 | tf_op jit(solution)/shard_map/ppermute | solution.py:636
  63.0 7.1 %collective-permute-start.9 = (bf16[512,128]{1,0:T(8,128)(2,1)S(1)}, bf16[512,128]{1,0:T(8,128)(2,1)S(1)}, u32[]{:S(2)}, u32[]{:S(2)}) collective-permute-start(bf16[512,128]{1,0:T(8,128)(2,1)S(1)} %get-tuple-element.159.refs_5_), channel_id=1, source_target_pairs={{0,16},{8,24},{16,0},{24,8},{1,17},{9,25},{17,1},{25,9},{2,18},{10... | collective-permute-start | bytes 393224 | tf_op jit(solution)/shard_map/ppermute | solution.py:636
  64.4 8.0 %collective-permute-start.7 = (bf16[512,128]{1,0:T(8,128)(2,1)S(1)}, bf16[512,128]{1,0:T(8,128)(2,1)S(1)}, u32[]{:S(2)}, u32[]{:S(2)}) collective-permute-start(bf16[512,128]{1,0:T(8,128)(2,1)S(1)} %collective-permute-done.6.refs_3_), channel_id=1, source_target_pairs={{0,8},{8,0},{16,24},{24,16},{1,9},{9,1},{17,25},{25,17},{2,10},{10... | collective-permute-start | bytes 393224 | tf_op jit(solution)/shard_map/ppermute | solution.py:636
  68.6 5.0 %collective-permute-start.10 = (bf16[512,128]{1,0:T(8,128)(2,1)S(1)}, bf16[512,128]{1,0:T(8,128)(2,1)S(1)}, u32[]{:S(2)}, u32[]{:S(2)}) collective-permute-start(bf16[512,128]{1,0:T(8,128)(2,1)S(1)} %collective-permute-done.8.refs_6_), channel_id=1, source_target_pairs={{0,16},{8,24},{16,0},{24,8},{1,17},{9,25},{17,1},{25,9},{2,18},{10... | collective-permute-start | bytes 393224 | tf_op jit(solution)/shard_map/ppermute | solution.py:636
  76.3 11.7 %collective-permute-start.12 = (bf16[9,64,128]{2,1,0:T(8,128)(2,1)S(1)}, bf16[9,64,128]{2,1,0:T(8,128)(2,1)S(1)}, u32[]{:S(2)}, u32[]{:S(2)}) collective-permute-start(bf16[9,64,128]{2,1,0:T(8,128)(2,1)S(1)} %get-tuple-element.169), channel_id=1, source_target_pairs={{0,8},{8,0},{16,24},{24,16},{1,9},{9,1},{17,25},{25,17},{2,10},{10... | collective-permute-start | bytes 442376 | tf_op jit(solution)/shard_map/ppermute | solution.py:636
  77.1 10.9 %collective-permute-start.13 = (bf16[9,64,128]{2,1,0:T(8,128)(2,1)S(1)}, bf16[9,64,128]{2,1,0:T(8,128)(2,1)S(1)}, u32[]{:S(2)}, u32[]{:S(2)}) collective-permute-start(bf16[9,64,128]{2,1,0:T(8,128)(2,1)S(1)} %get-tuple-element.170), channel_id=1, source_target_pairs={{0,16},{8,24},{16,0},{24,8},{1,17},{9,25},{17,1},{25,9},{2,18},{10... | collective-permute-start | bytes 442376 | tf_op jit(solution)/shard_map/ppermute | solution.py:636
  78.4 9.6 %collective-permute-start.14 = (bf16[9,64,128]{2,1,0:T(8,128)(2,1)S(1)}, bf16[9,64,128]{2,1,0:T(8,128)(2,1)S(1)}, u32[]{:S(2)}, u32[]{:S(2)}) collective-permute-start(bf16[9,64,128]{2,1,0:T(8,128)(2,1)S(1)} %get-tuple-element.171), channel_id=1, source_target_pairs={{0,24},{8,16},{16,8},{24,0},{1,25},{9,17},{17,9},{25,1},{2,26},{10... | collective-permute-start | bytes 442376 | tf_op jit(solution)/shard_map/ppermute | solution.py:636
  98.3 16.2 %collective-permute-start.21 = (bf16[4,9,64,128]{3,2,1,0:T(8,128)(2,1)S(1)}, bf16[4,9,64,128]{3,2,1,0:T(8,128)(2,1)S(1)}, u32[]{:S(2)}, u32[]{:S(2)}) collective-permute-start(bf16[4,9,64,128]{3,2,1,0:T(8,128)(2,1)S(1)} %shard_map.175.refs_9_), channel_id=1, source_target_pairs={{0,4},{4,0},{1,5},{5,1},{2,6},{6,2},{3,7},{7,3},{8,12},{12,8},{9,1... | collective-permute-start | bytes 1769480 | tf_op jit(solution)/shard_map/ppermute | solution.py:627
  98.5 5.8 %collective-permute-start.16 = (bf16[512,128]{1,0:T(8,128)(2,1)S(1)}, bf16[512,128]{1,0:T(8,128)(2,1)S(1)}, u32[]{:S(2)}, u32[]{:S(2)}) collective-permute-start(bf16[512,128]{1,0:T(8,128)(2,1)S(1)} %get-tuple-element.184.refs_1_.refs_2_), channel_id=1, source_target_pairs={{0,16},{8,24},{16,0},{24,8},{1,17},{9,25},{17,1},{25,9},{2,18},{10... | collective-permute-start | bytes 393224 | tf_op jit(solution)/shard_map/ppermute | solution.py:636
  98.9 5.5 %collective-permute-start.18 = (bf16[512,128]{1,0:T(8,128)(2,1)S(1)}, bf16[512,128]{1,0:T(8,128)(2,1)S(1)}, u32[]{:S(2)}, u32[]{:S(2)}) collective-permute-start(bf16[512,128]{1,0:T(8,128)(2,1)S(1)} %get-tuple-element.185.refs_5_.refs_3_), channel_id=1, source_target_pairs={{0,8},{8,0},{16,24},{24,16},{1,9},{9,1},{17,25},{25,17},{2,10},{10... | collective-permute-start | bytes 393224 | tf_op jit(solution)/shard_map/ppermute | solution.py:636
  103.7 1.4 collective-permute-start.22
  103.8 2.3 %collective-permute-start.23 = (bf16[9,64,128]{2,1,0:T(8,128)(2,1)S(1)}, bf16[9,64,128]{2,1,0:T(8,128)(2,1)S(1)}, u32[]{:S(2)}, u32[]{:S(2)}) collective-permute-start(bf16[9,64,128]{2,1,0:T(8,128)(2,1)S(1)} %get-tuple-element.195), channel_id=1, source_target_pairs={{0,4},{4,0},{1,5},{5,1},{2,6},{6,2},{3,7},{7,3},{8,12},{12,8},{9,1... | collective-permute-start | bytes 442376 | tf_op jit(solution)/shard_map/ppermute | solution.py:627
  104.3 2.8 %collective-permute-start.24 = (bf16[9,64,128]{2,1,0:T(8,128)(2,1)S(1)}, bf16[9,64,128]{2,1,0:T(8,128)(2,1)S(1)}, u32[]{:S(2)}, u32[]{:S(2)}) collective-permute-start(bf16[9,64,128]{2,1,0:T(8,128)(2,1)S(1)} %get-tuple-element.196), channel_id=1, source_target_pairs={{0,4},{4,0},{1,5},{5,1},{2,6},{6,2},{3,7},{7,3},{8,12},{12,8},{9,1... | collective-permute-start | bytes 442376 | tf_op jit(solution)/shard_map/ppermute | solution.py:627
  104.3 3.7 %collective-permute-start.25 = (bf16[9,64,128]{2,1,0:T(8,128)(2,1)S(1)}, bf16[9,64,128]{2,1,0:T(8,128)(2,1)S(1)}, u32[]{:S(2)}, u32[]{:S(2)}) collective-permute-start(bf16[9,64,128]{2,1,0:T(8,128)(2,1)S(1)} %get-tuple-element.197), channel_id=1, source_target_pairs={{0,4},{4,0},{1,5},{5,1},{2,6},{6,2},{3,7},{7,3},{8,12},{12,8},{9,1... | collective-permute-start | bytes 442376 | tf_op jit(solution)/shard_map/ppermute | solution.py:627
  105.1 6.3 %collective-permute-start.15 = (bf16[512,128]{1,0:T(8,128)(2,1)S(1)}, bf16[512,128]{1,0:T(8,128)(2,1)S(1)}, u32[]{:S(2)}, u32[]{:S(2)}) collective-permute-start(bf16[512,128]{1,0:T(8,128)(2,1)S(1)} %get-tuple-element.184.refs_1_.refs_2_), channel_id=1, source_target_pairs={{0,8},{8,0},{16,24},{24,16},{1,9},{9,1},{17,25},{25,17},{2,10},{10... | collective-permute-start | bytes 393224 | tf_op jit(solution)/shard_map/ppermute | solution.py:636
  106.1 6.3 %collective-permute-start.19 = (bf16[512,128]{1,0:T(8,128)(2,1)S(1)}, bf16[512,128]{1,0:T(8,128)(2,1)S(1)}, u32[]{:S(2)}, u32[]{:S(2)}) collective-permute-start(bf16[512,128]{1,0:T(8,128)(2,1)S(1)} %get-tuple-element.185.refs_5_.refs_3_), channel_id=1, source_target_pairs={{0,16},{8,24},{16,0},{24,8},{1,17},{9,25},{17,1},{25,9},{2,18},{10... | collective-permute-start | bytes 393224 | tf_op jit(solution)/shard_map/ppermute | solution.py:636
  107.1 6.4 %collective-permute-start.17 = (bf16[512,128]{1,0:T(8,128)(2,1)S(1)}, bf16[512,128]{1,0:T(8,128)(2,1)S(1)}, u32[]{:S(2)}, u32[]{:S(2)}) collective-permute-start(bf16[512,128]{1,0:T(8,128)(2,1)S(1)} %collective-permute-done.16.refs_3_), channel_id=1, source_target_pairs={{0,8},{8,0},{16,24},{24,16},{1,9},{9,1},{17,25},{25,17},{2,10},{10... | collective-permute-start | bytes 393224 | tf_op jit(solution)/shard_map/ppermute | solution.py:636
  108.1 6.4 %collective-permute-start.20 = (bf16[512,128]{1,0:T(8,128)(2,1)S(1)}, bf16[512,128]{1,0:T(8,128)(2,1)S(1)}, u32[]{:S(2)}, u32[]{:S(2)}) collective-permute-start(bf16[512,128]{1,0:T(8,128)(2,1)S(1)} %collective-permute-done.18.refs_6_), channel_id=1, source_target_pairs={{0,16},{8,24},{16,0},{24,8},{1,17},{9,25},{17,1},{25,9},{2,18},{10... | collective-permute-start | bytes 393224 | tf_op jit(solution)/shard_map/ppermute | solution.py:636
  117.5 11.7 %collective-permute-start.26 = (bf16[832,128]{1,0:T(8,128)(2,1)S(1)}, bf16[832,128]{1,0:T(8,128)(2,1)S(1)}, u32[]{:S(2)}, u32[]{:S(2)}) collective-permute-start(bf16[832,128]{1,0:T(8,128)(2,1)S(1)} %get-tuple-element.205), channel_id=1, source_target_pairs={{0,8},{8,0},{16,24},{24,16},{1,9},{9,1},{17,25},{25,17},{2,10},{10... | collective-permute-start | bytes 638984 | tf_op jit(solution)/shard_map/ppermute | solution.py:636
  118.3 10.9 %collective-permute-start.27 = (bf16[832,128]{1,0:T(8,128)(2,1)S(1)}, bf16[832,128]{1,0:T(8,128)(2,1)S(1)}, u32[]{:S(2)}, u32[]{:S(2)}) collective-permute-start(bf16[832,128]{1,0:T(8,128)(2,1)S(1)} %get-tuple-element.206), channel_id=1, source_target_pairs={{0,16},{8,24},{16,0},{24,8},{1,17},{9,25},{17,1},{25,9},{2,18},{10... | collective-permute-start | bytes 638984 | tf_op jit(solution)/shard_map/ppermute | solution.py:636
  119.6 10.3 %collective-permute-start.28 = (bf16[832,128]{1,0:T(8,128)(2,1)S(1)}, bf16[832,128]{1,0:T(8,128)(2,1)S(1)}, u32[]{:S(2)}, u32[]{:S(2)}) collective-permute-start(bf16[832,128]{1,0:T(8,128)(2,1)S(1)} %get-tuple-element.207), channel_id=1, source_target_pairs={{0,24},{8,16},{16,8},{24,0},{1,25},{9,17},{17,9},{25,1},{2,26},{10... | collective-permute-start | bytes 638984 | tf_op jit(solution)/shard_map/ppermute | solution.py:636
  133.3 2.3 %collective-permute-start.29 = (bf16[9,64,128]{2,1,0:T(8,128)(2,1)S(1)}, bf16[9,64,128]{2,1,0:T(8,128)(2,1)S(1)}, u32[]{:S(2)}, u32[]{:S(2)}) collective-permute-start(bf16[9,64,128]{2,1,0:T(8,128)(2,1)S(1)} %get-tuple-element.219), channel_id=1, source_target_pairs={{0,4},{4,0},{1,5},{5,1},{2,6},{6,2},{3,7},{7,3},{8,12},{12,8},{9,1... | collective-permute-start | bytes 442376 | tf_op jit(solution)/shard_map/ppermute | solution.py:627
  133.4 2.9 %collective-permute-start.30 = (bf16[9,64,128]{2,1,0:T(8,128)(2,1)S(1)}, bf16[9,64,128]{2,1,0:T(8,128)(2,1)S(1)}, u32[]{:S(2)}, u32[]{:S(2)}) collective-permute-start(bf16[9,64,128]{2,1,0:T(8,128)(2,1)S(1)} %get-tuple-element.220), channel_id=1, source_target_pairs={{0,4},{4,0},{1,5},{5,1},{2,6},{6,2},{3,7},{7,3},{8,12},{12,8},{9,1... | collective-permute-start | bytes 442376 | tf_op jit(solution)/shard_map/ppermute | solution.py:627
  133.9 5.7 %collective-permute-start.31 = (bf16[9,64,128]{2,1,0:T(8,128)(2,1)S(1)}, bf16[9,64,128]{2,1,0:T(8,128)(2,1)S(1)}, u32[]{:S(2)}, u32[]{:S(2)}) collective-permute-start(bf16[9,64,128]{2,1,0:T(8,128)(2,1)S(1)} %get-tuple-element.221), channel_id=1, source_target_pairs={{0,4},{4,0},{1,5},{5,1},{2,6},{6,2},{3,7},{7,3},{8,12},{12,8},{9,1... | collective-permute-start | bytes 442376 | tf_op jit(solution)/shard_map/ppermute | solution.py:627
  134.0 5.6 %collective-permute-start.32 = (bf16[9,64,128]{2,1,0:T(8,128)(2,1)S(1)}, bf16[9,64,128]{2,1,0:T(8,128)(2,1)S(1)}, u32[]{:S(2)}, u32[]{:S(2)}) collective-permute-start(bf16[9,64,128]{2,1,0:T(8,128)(2,1)S(1)} %get-tuple-element.222), channel_id=1, source_target_pairs={{0,4},{4,0},{1,5},{5,1},{2,6},{6,2},{3,7},{7,3},{8,12},{12,8},{9,1... | collective-permute-start | bytes 442376 | tf_op jit(solution)/shard_map/ppermute | solution.py:627
  135.1 7.9 %collective-permute-start.36 = (bf16[576,128]{1,0:T(8,128)(2,1)S(1)}, bf16[576,128]{1,0:T(8,128)(2,1)S(1)}, u32[]{:S(2)}, u32[]{:S(2)}) collective-permute-start(bf16[576,128]{1,0:T(8,128)(2,1)S(1)} %get-tuple-element.228), channel_id=1, source_target_pairs={{0,1},{1,0},{2,3},{3,2},{4,5},{5,4},{6,7},{7,6},{8,9},{9,8},{10,11... | collective-permute-start | bytes 442376 | tf_op jit(solution)/shard_map/ppermute | solution.py:624
  135.6 13.9 %collective-permute-start.37 = (bf16[576,128]{1,0:T(8,128)(2,1)S(1)}, bf16[576,128]{1,0:T(8,128)(2,1)S(1)}, u32[]{:S(2)}, u32[]{:S(2)}) collective-permute-start(bf16[576,128]{1,0:T(8,128)(2,1)S(1)} %get-tuple-element.229), channel_id=1, source_target_pairs={{0,2},{1,3},{2,0},{3,1},{4,6},{5,7},{6,4},{7,5},{8,10},{9,11},{10,... | collective-permute-start | bytes 442376 | tf_op jit(solution)/shard_map/ppermute | solution.py:624
  136.2 13.3 %collective-permute-start.38 = (bf16[576,128]{1,0:T(8,128)(2,1)S(1)}, bf16[576,128]{1,0:T(8,128)(2,1)S(1)}, u32[]{:S(2)}, u32[]{:S(2)}) collective-permute-start(bf16[576,128]{1,0:T(8,128)(2,1)S(1)} %get-tuple-element.230), channel_id=1, source_target_pairs={{0,3},{1,2},{2,1},{3,0},{4,7},{5,6},{6,5},{7,4},{8,11},{9,10},{10,... | collective-permute-start | bytes 442376 | tf_op jit(solution)/shard_map/ppermute | solution.py:624
  140.2 9.3 %collective-permute-start.33 = (bf16[576,128]{1,0:T(8,128)(2,1)S(1)}, bf16[576,128]{1,0:T(8,128)(2,1)S(1)}, u32[]{:S(2)}, u32[]{:S(2)}) collective-permute-start(bf16[576,128]{1,0:T(8,128)(2,1)S(1)} %get-tuple-element.224), channel_id=1, source_target_pairs={{0,8},{8,0},{16,24},{24,16},{1,9},{9,1},{17,25},{25,17},{2,10},{10... | collective-permute-start | bytes 442376 | tf_op jit(solution)/shard_map/ppermute | solution.py:636
  140.9 8.7 %collective-permute-start.34 = (bf16[576,128]{1,0:T(8,128)(2,1)S(1)}, bf16[576,128]{1,0:T(8,128)(2,1)S(1)}, u32[]{:S(2)}, u32[]{:S(2)}) collective-permute-start(bf16[576,128]{1,0:T(8,128)(2,1)S(1)} %get-tuple-element.225), channel_id=1, source_target_pairs={{0,16},{8,24},{16,0},{24,8},{1,17},{9,25},{17,1},{25,9},{2,18},{10... | collective-permute-start | bytes 442376 | tf_op jit(solution)/shard_map/ppermute | solution.py:636
  142.9 7.1 %collective-permute-start.35 = (bf16[576,128]{1,0:T(8,128)(2,1)S(1)}, bf16[576,128]{1,0:T(8,128)(2,1)S(1)}, u32[]{:S(2)}, u32[]{:S(2)}) collective-permute-start(bf16[576,128]{1,0:T(8,128)(2,1)S(1)} %get-tuple-element.226), channel_id=1, source_target_pairs={{0,24},{8,16},{16,8},{24,0},{1,25},{9,17},{17,9},{25,1},{2,26},{10... | collective-permute-start | bytes 442376 | tf_op jit(solution)/shard_map/ppermute | solution.py:636
  147.4 19.8 %copy-start.2 = (f32[2,9,64,128]{3,2,1,0:T(8,128)S(1)}, f32[2,9,64,128]{3,2,1,0:T(8,128)}, u32[]{:S(2)}) copy-start(f32[2,9,64,128]{3,2,1,0:T(8,128)} %refs_6_.1) | copy-start | bytes 1769476
  147.4 19.8 %copy-start.3 = (f32[2,9,64,128]{3,2,1,0:T(8,128)S(1)}, f32[2,9,64,128]{3,2,1,0:T(8,128)}, u32[]{:S(2)}) copy-start(f32[2,9,64,128]{3,2,1,0:T(8,128)} %refs_7_.1) | copy-start | bytes 1769476
  150.7 5.8 %collective-permute-start.39 = (bf16[576,128]{1,0:T(8,128)(2,1)S(1)}, bf16[576,128]{1,0:T(8,128)(2,1)S(1)}, u32[]{:S(2)}, u32[]{:S(2)}) collective-permute-start(bf16[576,128]{1,0:T(8,128)(2,1)S(1)} %get-tuple-element.249), channel_id=1, source_target_pairs={{0,1},{1,0},{2,3},{3,2},{4,5},{5,4},{6,7},{7,6},{8,9},{9,8},{10,11... | collective-permute-start | bytes 442376 | tf_op jit(solution)/shard_map/ppermute | solution.py:624
  152.9 14.3 %collective-permute-start.42 = (bf16[256,512]{1,0:T(8,128)(2,1)S(1)}, bf16[256,512]{1,0:T(8,128)(2,1)S(1)}, u32[]{:S(2)}, u32[]{:S(2)}) collective-permute-start(bf16[256,512]{1,0:T(8,128)(2,1)S(1)} %get-tuple-element.253), channel_id=1, source_target_pairs={{0,8},{8,0},{16,24},{24,16},{1,9},{9,1},{17,25},{25,17},{2,10},{10... | collective-permute-start | bytes 786440 | tf_op jit(solution)/shard_map/ppermute | solution.py:636
  153.5 13.7 %collective-permute-start.43 = (bf16[256,512]{1,0:T(8,128)(2,1)S(1)}, bf16[256,512]{1,0:T(8,128)(2,1)S(1)}, u32[]{:S(2)}, u32[]{:S(2)}) collective-permute-start(bf16[256,512]{1,0:T(8,128)(2,1)S(1)} %get-tuple-element.254), channel_id=1, source_target_pairs={{0,16},{8,24},{16,0},{24,8},{1,17},{9,25},{17,1},{25,9},{2,18},{10... | collective-permute-start | bytes 786440 | tf_op jit(solution)/shard_map/ppermute | solution.py:636
  154.9 12.3 %collective-permute-start.44 = (bf16[256,512]{1,0:T(8,128)(2,1)S(1)}, bf16[256,512]{1,0:T(8,128)(2,1)S(1)}, u32[]{:S(2)}, u32[]{:S(2)}) collective-permute-start(bf16[256,512]{1,0:T(8,128)(2,1)S(1)} %get-tuple-element.255), channel_id=1, source_target_pairs={{0,24},{8,16},{16,8},{24,0},{1,25},{9,17},{17,9},{25,1},{2,26},{10... | collective-permute-start | bytes 786440 | tf_op jit(solution)/shard_map/ppermute | solution.py:636
  156.4 10.8 %collective-permute-start.40 = (bf16[576,128]{1,0:T(8,128)(2,1)S(1)}, bf16[576,128]{1,0:T(8,128)(2,1)S(1)}, u32[]{:S(2)}, u32[]{:S(2)}) collective-permute-start(bf16[576,128]{1,0:T(8,128)(2,1)S(1)} %get-tuple-element.250), channel_id=1, source_target_pairs={{0,2},{1,3},{2,0},{3,1},{4,6},{5,7},{6,4},{7,5},{8,10},{9,11},{10,... | collective-permute-start | bytes 442376 | tf_op jit(solution)/shard_map/ppermute | solution.py:624
  156.4 10.7 %collective-permute-start.41 = (bf16[576,128]{1,0:T(8,128)(2,1)S(1)}, bf16[576,128]{1,0:T(8,128)(2,1)S(1)}, u32[]{:S(2)}, u32[]{:S(2)}) collective-permute-start(bf16[576,128]{1,0:T(8,128)(2,1)S(1)} %get-tuple-element.251), channel_id=1, source_target_pairs={{0,3},{1,2},{2,1},{3,0},{4,7},{5,6},{6,5},{7,4},{8,11},{9,10},{10,... | collective-permute-start | bytes 442376 | tf_op jit(solution)/shard_map/ppermute | solution.py:624
  158.9 0.7 copy-start.1
  169.7 12.8 %copy-start.5 = (f32[4,512]{1,0:T(4,128)S(1)}, f32[4,512]{1,0:T(4,128)}, u32[]{:S(2)}) copy-start(f32[4,512]{1,0:T(4,128)} %refs_4_.1) | copy-start | bytes 24580
  169.7 12.8 %copy-start.6 = (f32[4,512]{1,0:T(4,128)S(1)}, f32[4,512]{1,0:T(4,128)}, u32[]{:S(2)}) copy-start(f32[4,512]{1,0:T(4,128)} %refs_5_.3) | copy-start | bytes 24580
  169.7 12.8 %all-to-all-start.5 = ((f32[32,8,128]{2,1,0:T(8,128)}), f32[32,8,128]{2,1,0:T(8,128)S(1)}, u32[]{:S(2)}, u32[]{:S(2)}) async-start(f32[32,8,128]{2,1,0:T(8,128)} %get-tuple-element.270), calls=%async_computation.5 | async-start | bytes 262144 | tf_op jit(solution)/shard_map/all_to_all | solution.py:815

commit v3 on v2

--- a/solution.py
+++ b/solution.py
@@ -50,7 +50,7 @@
         self.IB = self.C // self.R
         self.K = weights[1]
         self.extra = 16 * ((2 * self.n_own + 15) // 16)
-        self.sent = self.own + self.extra + self.own // self.Q
+        self.sent = self.own + self.extra
 
 
 def call(body, out_shape, args, scratch=(), limit=8, far=(), after=(), cost=1, raw=()):
@@ -194,10 +194,10 @@
     spread(stats_ref, [count, mean, squares])
 
 
-def conv_into(z, product, y_ref, z_ref, sign=1):
+def conv_into(z, product, y_ref, z_ref, sign=1, at_q=0):
     for j in range(z.Q):
         y_ref[...] = product(j)
-        z_ref[j * z.own : (j + 1) * z.own, :] = shifted_sum(
+        z_ref[pl.ds(pl.multiple_of((at_q ^ j) * z.own, z.own), z.own), :] = shifted_sum(
             z, lambda k: y_ref[:, k * z.LP : k * z.LP + z.L], sign
         )
 
@@ -211,39 +211,39 @@
                 wcat[pl.ds(row, z.IB), k * z.LP : k * z.LP + z.L] = block[a, k]
 
 
-def first_conv(z, at, np_ref, x_ref, *refs):
+def first_conv(z, at, np_ref, *refs):
+    xs, refs = refs[: z.Q], refs[z.Q :]
     blocks, refs = refs[: z.S], refs[z.S :]
-    z_ref, slice_ref, cot_ref, par_ref, hw_ref, stats_ref, far_w, far_x, wcat, y_ref, sem = refs
-    start, high = z.own + z.extra, z.own // z.Q
+    z_ref, slice_ref, par_ref, hw_ref, stats_ref, far_w, far_x, wcat, y_ref, sem = refs
     fill_kernels(z, at, blocks, wcat)
-    copies = [
-        pltpu.make_async_copy(wcat, far_w, sem.at[0]),
-        pltpu.make_async_copy(x_ref.at[:, : z.own, :], far_x, sem.at[1]),
-    ]
+    copies = [pltpu.make_async_copy(wcat, far_w, sem.at[0])]
+    for m in range(z.Q):
+        copies.append(
+            pltpu.make_async_copy(xs[m].at[: z.own, :], far_x.at[at[0] ^ m], sem.at[1 + m])
+        )
     for copy in copies:
         copy.start()
-    for j in range(z.Q):
+    for m in range(z.Q):
+        j = at[0] ^ m
         for n in range(z.n_own):
             row = z.own + 2 * n
-            two = x_ref[j, row : row + 2, :LANES].astype(F32)
+            two = xs[m][row : row + 2, :LANES].astype(F32)
             hw_ref[j * z.n_own + n] = jnp.concatenate([two, jnp.zeros((6, LANES), F32)], axis=0)
-        for i in range(z.Q):
-            row = j * z.own + i * high
-            cot_ref[row : row + high, :] = x_ref[j, start:, i * z.L : (i + 1) * z.L]
     for slot in range(z.Q):
 
         @pl.when(at[0] == slot)
         def _(slot=slot):
             par_ref[...] = np_ref[:, slot * z.L : (slot + 1) * z.L]
-            for j in range(z.Q):
-                slice_ref[j * z.own : (j + 1) * z.own, :] = x_ref[
-                    j, : z.own, slot * z.L : (slot + 1) * z.L
+            for m in range(z.Q):
+                j = slot ^ m
+                slice_ref[j * z.own : (j + 1) * z.own, :] = xs[m][
+                    : z.own, slot * z.L : (slot + 1) * z.L
                 ]
 
-    def product(j):
-        return jnp.dot(x_ref[j, : z.own, :], wcat[...], preferred_element_type=F32)
-
-    conv_into(z, product, y_ref, z_ref)
+    def product(m):
+        return jnp.dot(xs[m][: z.own, :], wcat[...], preferred_element_type=F32)
+
+    conv_into(z, product, y_ref, z_ref, 1, at[0])
     local_stats(z, z_ref, hw_ref, stats_ref)
     for copy in copies:
         copy.wait()
@@ -259,10 +259,7 @@
 def second_conv(z, at, *refs):
     hs, refs = refs[: 2 * z.Q], refs[2 * z.Q :]
     blocks, refs = refs[: z.S], refs[z.S :]
-    hw_ref, z_ref, stats_ref, far_ref, refs = *refs[:4], refs[4:]
-    outs, (wcat, y_ref, h_ref, sem) = refs[: z.Q], refs[z.Q :]
-    for m in range(z.Q):
-        outs[m][...] = blocks[0][at[0] ^ m]
+    hw_ref, z_ref, stats_ref, far_ref, wcat, y_ref, h_ref, sem = refs
     gathered(z, at, hs, h_ref)
     copy = pltpu.make_async_copy(h_ref, far_ref, sem)
     copy.start()
@@ -333,8 +330,8 @@
     over_halves(z, step, (a_ref, b_ref))
 
 
-def middle(z, at, z_ref, all_ref, hw_ref, par_ref, x_ref, cot_ref, *refs):
-    out_ref, d_ref, sum_ref, stats_ref = refs
+def middle(z, at, z_ref, all_ref, hw_ref, par_ref, x_ref, *refs):
+    cot_ref, out_ref, d_ref, sum_ref, stats_ref = refs
     mean, inv, count = merged(z, all_ref)
     keep(sum_ref, [mean, inv, count])
     gain, shift = par_ref[2:3, :], par_ref[3:4, :]
@@ -585,7 +582,7 @@
     trust_ref[...] = trust
 
 
-def extend(z, x_ref, valid_ref, cot_ref, out_ref):
+def extend(z, x_ref, valid_ref, out_ref):
     rows = []
     for n in range(z.n_own):
         valid = valid_ref[n].astype(F32)
@@ -595,25 +592,46 @@
     rows = [jnp.broadcast_to(r, (1, z.C)) for r in rows]
     fill = z.extra - len(rows)
     extra = jnp.concatenate(rows + [jnp.zeros((fill, z.C), F32)], axis=0).astype(BF16)
-    start, high = z.own + z.extra, z.own // z.Q
-    for j in range(z.Q):
-        out_ref[j, : z.own, :] = x_ref[...]
-        out_ref[j, z.own : start, :] = extra
-        for i in range(z.Q):
-            out_ref[j, start:, i * z.L : (i + 1) * z.L] = cot_ref[
-                i * high : (i + 1) * high, j * z.L : (j + 1) * z.L
-            ]
+    out_ref[: z.own, :] = x_ref[...]
+    out_ref[z.own :, :] = extra
+
+
+def pick(z, more, at, *refs):
+    parts, refs = refs[: z.Z], refs[z.Z :]
+    map_ref = None
+    if more == "map":
+        map_ref, refs = refs[0], refs[1:]
+    if more == "keep":
+        far_ref, outs, (hold, sem) = refs[0], refs[1:-2], refs[-2:]
+    else:
+        outs, hold = refs[:-1], refs[-1]
+    for m in range(z.Z):
+        hold[at[2] ^ m] = parts[m][...]
+    if more == "keep":
+        copy = pltpu.make_async_copy(hold, far_ref, sem)
+        copy.start()
+    for m in range(z.Q):
+        for k in range(z.K):
+            outs[m][k * z.IB : (k + 1) * z.IB, :] = hold[at[0] ^ m, k]
+        if map_ref is not None:
+            for slot in range(z.Q):
+
+                @pl.when((at[0] ^ m) == slot)
+                def _(m=m, slot=slot):
+                    outs[m][z.K * z.IB :, :] = map_ref[:, slot * z.L : (slot + 1) * z.L]
+
+    if more == "keep":
+        copy.wait()
 
 
 def unpick(z, at, *refs):
+    parts, refs = refs[: z.Q], refs[z.Q :]
     for m in range(z.Q):
-        refs[z.Q][at[0] ^ m] = refs[m][...]
-
-
-def pack(z, at, *refs):
-    for m in range(z.Z):
-        refs[z.Z][at[2] ^ m] = refs[m][0]
-        refs[z.Z + 1][at[2] ^ m] = refs[m][1]
+        q = at[0] ^ m
+        for k in range(z.K):
+            refs[0][q, k] = parts[m][k * z.IB : (k + 1) * z.IB, :]
+        if len(refs) > 1:
+            refs[1][pl.ds(pl.multiple_of(q * z.own, z.own), z.own), :] = parts[m][z.K * z.IB :, :]
 
 
 def shards(z, images, masks, cotangent, weights, first, second, params, p_first, p_second):
@@ -626,9 +644,6 @@
     def over_s(v, m):
         return lax.ppermute(v, "s", [(i, i ^ m) for i in range(z.S)]) if m else v
 
-    def plane(v):
-        return lax.all_to_all(v, "q", 0, 0)
-
     def sharers(v):
         return lax.all_to_all(v, ("s", "z"), 0, 0)
 
@@ -637,18 +652,6 @@
 
     def gather_z(w):
         return [over_z(w, m) for m in range(z.Z)]
-
-    def fetch(w):
-        own = []
-        for m in range(z.Z):
-            pairs = [
-                ((a * z.S + c) * z.Z + e, (e * z.S + c) * z.Z + (a ^ m))
-                for a in range(z.Q)
-                for c in range(z.S)
-                for e in range(z.Z)
-            ]
-            own.append(lax.ppermute(w, ("q", "s", "z"), pairs))
-        return own
 
     def gather(a, b):
         if z.Q != 4:
@@ -671,25 +674,41 @@
     cot_rows = cotangent.reshape(rows, z.C)
     image_rows = images.reshape(rows, z.C)
 
-    low = weights.astype(BF16)
-    both = fetch(low)
-    x_all = plane(
-        call(
-            functools.partial(extend, z),
-            near((z.Q, z.sent, z.C), BF16),
-            (image_rows, masks, cot_rows),
-            far=(image_rows, masks, cot_rows),
-        )
-    )
-    both, x_all = together((both, x_all))
-    front_one, front_two = call(functools.partial(pack, z), [blocks] * 2, (at, *both))
+    low_one, low_two = (weights[j].astype(BF16) for j in range(2))
+    one = [over_z(low_one, m) for m in range(z.Z)]
+    x_sent = call(
+        functools.partial(extend, z),
+        near((z.sent, z.C), BF16),
+        (image_rows, masks),
+        far=(image_rows, masks),
+    )
+    xs = [over_q(x_sent, m) for m in range(z.Q)]
+    one, xs, low_two = together((one, xs, low_two))
+    hold = pltpu.VMEM((z.Z, *piece), BF16)
+    picked = call(
+        functools.partial(pick, z, "map"),
+        [near((z.K * z.IB + rows, z.L), BF16)] * z.Q,
+        (at, *one, cot_rows),
+        [hold],
+        far=(cot_rows,),
+    )
+    two = [over_z(low_two, m) for m in range(z.Z)]
+    picked, two = together(([over_q(picked[m], m) for m in range(z.Q)], two))
+    front_one, cots = call(functools.partial(unpick, z), [blocks, near(GL, BF16)], (at, *picked))
+    keep = away((z.Z, *piece), BF16)
+    keep_two, *picked = call(
+        functools.partial(pick, z, "keep"),
+        [keep] + [near((z.K * z.IB, z.L), BF16)] * z.Q,
+        (at, *two),
+        [hold, pltpu.SemaphoreType.DMA],
+        raw=(keep,),
+    )
     w_far = away((z.C, z.K * z.LP), BF16)
     x_far = away((z.Q, rows, z.C), BF16)
-    z1, x_slice, cots, slice_params, hw, stats, w_far, x_far = call(
+    z1, x_slice, slice_params, hw, stats, w_far, x_far = call(
         functools.partial(first_conv, z),
         [
             near(GL),
-            near(GL, BF16),
             near(GL, BF16),
             near((4, z.L)),
             near((z.n_group, 8, LANES)),
@@ -697,42 +716,41 @@
             w_far,
             x_far,
         ],
-        (at, params, x_all, *share(front_one)),
-        conv_scratch + [pltpu.SemaphoreType.DMA((2,))],
+        (at, params, *xs, *share(front_one)),
+        conv_scratch + [pltpu.SemaphoreType.DMA((1 + z.Q,))],
         limit=16,
         raw=(w_far, x_far),
     )
-    stats = sharers(stats)
+    stats, picked = together((stats, picked))
+    stats, picked = together((sharers(stats), [over_q(picked[m], m) for m in range(z.Q)]))
     ha, hb, sum_one = call(
         functools.partial(hidden, z),
         [near(HL, BF16), near(HL, BF16), near((8, z.L))],
         (z1, stats, hw, slice_params),
     )
-    ha, hb, front_two = together((ha, hb, front_two))
+    ha, hb, picked = together((ha, hb, picked))
     hs = gather(ha, hb)
+    front_two = call(functools.partial(unpick, z), [blocks], (at, *picked))[0]
     h_far = away((z.Q, *GL), BF16)
-    z2, stats, h_far, *back = call(
+    z2, stats, h_far = call(
         functools.partial(second_conv, z),
-        [near(GL), stat, h_far] + [near(piece, BF16)] * z.Q,
+        [near(GL), stat, h_far],
         (at, *hs, *share(front_two), hw),
         conv_scratch + [pltpu.VMEM((z.Q, *GL), BF16), pltpu.SemaphoreType.DMA],
         limit=16,
         raw=(h_far,),
     )
-    stats, back = together((stats, back))
-    stats, back = together((sharers(stats), [over_q(back[m], m) for m in range(z.Q)]))
     out, d, sum_two, stats = call(
         functools.partial(middle, z),
         [near((z.Q, rows, z.L), BF16), near(GL), near((8, z.L)), stat],
-        (at, z2, stats, hw, slice_params, x_slice, cots),
+        (at, z2, sharers(stats), hw, slice_params, x_slice, cots),
     )
     da, db, grad_two = call(
         functools.partial(norm_grad, z, 2),
         [near(HL, BF16), near(HL, BF16), near((8, z.L))],
         (z2, d, sum_two, sharers(stats), hw, slice_params),
     )
-    da, db, back = together((da, db, back))
-    keep_two = call(functools.partial(unpick, z), near((z.Q, *piece), BF16), (at, *back))
+    da, db, keep_two = together((da, db, keep_two))
     dz2s = gather(da, db)
 
     def kernel_gradient(feature, halves, **more):

time: 184 us -> 177 us (0.962)
  waiting for transfers between devices: 55.3 us -> 43.7 us
  starting transfers between devices: 59.2 us -> 63.4 us
  blocking collectives: 36.1 us -> 34 us
    ppermute x4 -> x0, waiting for transfers between devices: 25.7 us -> none  [fetch(): own.append(lax.ppermute(w, ('q', 's', 'z'), pairs))]
    ppermute x6 -> x12, starting transfers between devices: 9.06 us -> 21.8 us  [over_z(): return lax.ppermute(v, 'z', [(i, i ^ m) for i in range(z.Z)]) if m else v]
    ppermute x6 -> x12, waiting for transfers between devices: 10.4 us -> 22 us  [over_z(): return lax.ppermute(v, 'z', [(i, i ^ m) for i in range(z.Z)]) if m else v]
    ppermute x4 -> x0, starting transfers between devices: 6.79 us -> none  [fetch(): own.append(lax.ppermute(w, ('q', 's', 'z'), pairs))]
    all_to_all x1 -> x0, starting transfers between devices: 5.29 us -> none  [plane(): return lax.all_to_all(v, 'q', 0, 0)]
    ppermute x24 -> x30, waiting for transfers between devices: 10.5 us -> 14.7 us  [over_q(): return lax.ppermute(v, 'q', [(i, i ^ m) for i in range(z.Q)]) if m else v]
    ppermute x24 -> x30, starting transfers between devices: 30.6 us -> 34.6 us  [over_q(): return lax.ppermute(v, 'q', [(i, i ^ m) for i in range(z.Q)]) if m else v]
    all_to_all x4, blocking collectives: 36.1 us -> 34 us  [sharers(): return lax.all_to_all(v, ('s', 'z'), 0, 0)]
  transfers between devices with their start and end apart: 47 -> 54, of which waited for: 18 -> 24; matrix products, arithmetic and copies ran while one was open for 0% -> 0% of each run, Pallas kernels for 5% -> 7%
where the time goes in v3:
time: 177 us
  starting transfers between devices  63.4 us (36%)
  waiting for transfers between devices  43.7 us (25%)
  blocking collectives  34 us (19%)
  Pallas kernels  31.9 us (18%)
    ppermute x30, starting transfers between devices, over_q(): return lax.ppermute(v, 'q', [(i, i ^ m) for i in range(z.Q)]) if m else v  34.6 us
    all_to_all x4, blocking collectives, sharers(): return lax.all_to_all(v, ('s', 'z'), 0, 0)  34 us
    pallas_call x23, Pallas kernels, call(): pl.pallas_call(run, out_shape=out_shape, in_specs=[pl.BlockSpec(memory_sp...  31.9 us
    ppermute x12, waiting for transfers between devices, over_z(): return lax.ppermute(v, 'z', [(i, i ^ m) for i in range(z.Z)]) if m else v  22 us
    ppermute x12, starting transfers between devices, over_z(): return lax.ppermute(v, 'z', [(i, i ^ m) for i in range(z.Z)]) if m else v  21.8 us
    ppermute x30, waiting for transfers between devices, over_q(): return lax.ppermute(v, 'q', [(i, i ^ m) for i in range(z.Q)]) if m else v  14.7 us
    all_to_all x1, waiting for transfers between devices, shards(): stats = lax.all_to_all(stats, ('s', 'q', 'z'), 0, 0)  6.39 us
    all_to_all x1, starting transfers between devices, shards(): stats = lax.all_to_all(stats, ('s', 'q', 'z'), 0, 0)  4.9 us
  transfers between devices with their start and end apart: 54, of which 24 were waited for; matrix products, arithmetic and copies ran while one was open for 0% of the time, Pallas kernels for 7%

profile of v3, /device:TPU:0, one launch (start us, length us, event | category | flops | bytes accessed | tf_op | source)
XLA Modules:
  0.0 176.7 jit_solution(5696186752046920203)
XLA Ops:
  0.6 1.1 convert.4
  1.8 5.1 %collective-permute-start.2 = (bf16[9,64,128]{2,1,0:T(8,128)(2,1)S(1)}, bf16[9,64,128]{2,1,0:T(8,128)(2,1)S(1)}, u32[]{:S(2)}, u32[]{:S(2)}) collective-permute-start(bf16[9,64,128]{2,1,0:T(8,128)(2,1)S(1)} %get-tuple-element.165.refs_1_), channel_id=1, source_target_pairs={{0,3},{1,2},{2,1},{3,0},{4,7},{5,6},{6,5},{7,4},{8,11},{9,10},{10,... | collective-permute-start | bytes 442376 | tf_op jit(solution)/shard_map/ppermute | solution.py:642
  6.9 1.1 shard_map.168.refs_2_
  8.0 2.5 %collective-permute-start.5 = (bf16[272,512]{1,0:T(8,128)(2,1)S(1)}, bf16[272,512]{1,0:T(8,128)(2,1)S(1)}, u32[]{:S(2)}, u32[]{:S(2)}) collective-permute-start(bf16[272,512]{1,0:T(8,128)(2,1)S(1)} %shard_map.168.refs_2_), channel_id=1, source_target_pairs={{0,24},{8,16},{16,8},{24,0},{1,25},{9,17},{17,9},{25,1},{2,26},{10... | collective-permute-start | bytes 835592 | tf_op jit(solution)/shard_map/ppermute | solution.py:651
  11.5 4.9 %collective-permute-start = (bf16[9,64,128]{2,1,0:T(8,128)(2,1)S(1)}, bf16[9,64,128]{2,1,0:T(8,128)(2,1)S(1)}, u32[]{:S(2)}, u32[]{:S(2)}) collective-permute-start(bf16[9,64,128]{2,1,0:T(8,128)(2,1)S(1)} %get-tuple-element.165.refs_1_), channel_id=1, source_target_pairs={{0,1},{1,0},{2,3},{3,2},{4,5},{5,4},{6,7},{7,6},{8,9},{9,8},{10,11... | collective-permute-start | bytes 442376 | tf_op jit(solution)/shard_map/ppermute | solution.py:642
  16.5 3.0 %collective-permute-done.1.refs_3_ = bf16[9,64,128]{2,1,0:T(8,128)(2,1)S(1)} collective-permute-done((bf16[9,64,128]{2,1,0:T(8,128)(2,1)S(1)}, bf16[9,64,128]{2,1,0:T(8,128)(2,1)S(1)}, u32[]{:S(2)}, u32[]{:S(2)}) %collective-permute-start.1) | collective-permute-done | bytes 147488 | tf_op jit(solution)/shard_map/ppermute | solution.py:642
  19.4 1.4 collective-permute-done.refs_2_
  20.9 2.2 %collective-permute-done.4.refs_4_ = bf16[272,512]{1,0:T(8,128)(2,1)S(1)} collective-permute-done((bf16[272,512]{1,0:T(8,128)(2,1)S(1)}, bf16[272,512]{1,0:T(8,128)(2,1)S(1)}, u32[]{:S(2)}, u32[]{:S(2)}) %collective-permute-start.4) | collective-permute-done | bytes 278560 | tf_op jit(solution)/shard_map/ppermute | solution.py:651
  23.6 1.2 shard_map.169
  24.8 1.6 collective-permute-start.6
  26.4 1.5 collective-permute-start.7
  29.0 1.7 collective-permute-done.11.refs_4_
  30.7 1.7 collective-permute-start.9
  32.4 5.0 %collective-permute-done.10.refs_3_ = bf16[9,64,128]{2,1,0:T(8,128)(2,1)S(1)} collective-permute-done((bf16[9,64,128]{2,1,0:T(8,128)(2,1)S(1)}, bf16[9,64,128]{2,1,0:T(8,128)(2,1)S(1)}, u32[]{:S(2)}, u32[]{:S(2)}) %collective-permute-start.10) | collective-permute-done | bytes 147488 | tf_op jit(solution)/shard_map/ppermute | solution.py:642
  37.3 0.7 collective-permute-done.9.refs_2_
  38.8 1.4 shard_map.172
  40.8 2.7 %shard_map.171 = (f32[1024,128]{1,0:T(8,128)S(1)}, bf16[1024,128]{1,0:T(8,128)(2,1)S(1)}, f32[4,128]{1,0:T(4,128)S(1)}, f32[16,8,128]{2,1,0:T(8,128)S(1)}, f32[8...) custom-call(s32[3]{0:T(128)S(1)} %pad_add_fusion.refs_0_, f32[4,512]{1,0:T(4,128)S(1)} %copy-done.5, ...), custom_call_target="tpu_custom_call" | custom-call | flops 1 | bytes 1 | tf_op jit(solution)/shard_map/pallas_call | solution.py:68
  43.5 1.7 collective-permute-start.13
  45.2 1.5 collective-permute-start.14
  47.1 9.6 %all_to_all.25.refs_1_ = f32[8,8,128]{2,1,0:T(8,128)S(1)} all-to-all(f32[8,8,128]{2,1,0:T(8,128)S(1)} %get-tuple-element.189), channel_id=1, replica_groups=mesh['ha'=2,'wa'=4,'ba'=4] {'wa':(2)2,'ba'}, dimensions={0} | all-to-all | bytes 65536 | tf_op jit(solution)/shard_map/all_to_all | solution.py:648
  57.9 1.5 collective-permute-start.17
  59.4 1.5 collective-permute-start.19
  61.9 1.8 collective-permute-done.17.refs_3_
  63.7 1.5 collective-permute-start.18
  65.7 1.5 collective-permute-start.21
  67.2 1.3 collective-permute-done.16.refs_2_
  68.5 1.9 %collective-permute-done.18.refs_4_ = bf16[512,128]{1,0:T(8,128)(2,1)S(1)} collective-permute-done((bf16[512,128]{1,0:T(8,128)(2,1)S(1)}, bf16[512,128]{1,0:T(8,128)(2,1)S(1)}, u32[]{:S(2)}, u32[]{:S(2)}) %collective-permute-start.18) | collective-permute-done | bytes 131104 | tf_op jit(solution)/shard_map/ppermute | solution.py:651
  70.7 2.7 %shard_map.175 = (f32[1024,128]{1,0:T(8,128)S(1)}, f32[8,8,128]{2,1,0:T(8,128)S(1)}, bf16[4,1024,128]{2,1,0:T(8,128)(2,1)}) custom-call(s32[3]{0:T(128)S(1)} %pad_add_fusion.refs_0_, bf16[512,128]{1,0:T(8,128)(2,1)S(1)} %get-tuple-element.203.refs_1_, bf16[512,128]{1,0:T(8,128)(2,1)S(1)} %collective-permute-done.16.refs_2_, ...), custom_call_target="tpu_custom_call" | custom-call | flops 1 | bytes 1 | tf_op jit(solution)/shard_map/pallas_call | solution.py:68
  73.4 8.1 %all_to_all.26.refs_2_ = f32[8,8,128]{2,1,0:T(8,128)S(1)} all-to-all(f32[8,8,128]{2,1,0:T(8,128)S(1)} %get-tuple-element.210), channel_id=1, replica_groups=mesh['ha'=2,'wa'=4,'ba'=4] {'wa':(2)2,'ba'}, dimensions={0} | all-to-all | bytes 65536 | tf_op jit(solution)/shard_map/all_to_all | solution.py:648
  81.5 1.3 shard_map.176
  82.8 8.1 %all_to_all.27.refs_3_ = f32[8,8,128]{2,1,0:T(8,128)S(1)} all-to-all(f32[8,8,128]{2,1,0:T(8,128)S(1)} %get-tuple-element.215), channel_id=1, replica_groups=mesh['ha'=2,'wa'=4,'ba'=4] {'wa':(2)2,'ba'}, dimensions={0} | all-to-all | bytes 65536 | tf_op jit(solution)/shard_map/all_to_all | solution.py:648
  91.4 1.5 collective-permute-start.24
  93.5 3.1 %shard_map.179 = (f32[4,9,64,128]{3,2,1,0:T(8,128)S(1)}, bf16[9,64,128]{2,1,0:T(8,128)(2,1)S(1)}, bf16[9,64,128]{2,1,0:T(8,128)(2,1)S(1)}, bf16[9,64,128]{2,1,0:T(8,128)(2,1)S(1)}, bf16[9,64,128]{2,1,0:T(8,128)(2,1)S(1)}) custom-call(s32[3]{0:T(128)S(1)} %pad_add_fusion.refs_0_, bf16[4,1024,128]{2,1,0:T(8,128)(2,1)} %get-tuple-element.224.refs_1_, ...), custom_call_target="tpu_custom_call" | custom-call | flops 3000000000 | bytes 1 | tf_op jit(solution)/shard_map/pallas_call | solution.py:68
  97.3 1.2 collective-permute-done.26.refs_6_
  98.5 1.1 collective-permute-start.23
  99.5 1.0 collective-permute-start.27
  100.5 1.1 collective-permute-start.25
  101.6 0.9 collective-permute-start.28
  103.2 1.6 collective-permute-done.23.refs_2_
  104.7 1.2 collective-permute-done.27.refs_7_
  105.9 1.3 collective-permute-done.25.refs_4_
  107.6 3.0 %shard_map.178 = (f32[1024,128]{1,0:T(8,128)S(1)}, f32[8,8,128]{2,1,0:T(8,128)S(1)}) custom-call(s32[3]{0:T(128)S(1)} %pad_add_fusion.refs_0_, bf16[512,128]{1,0:T(8,128)(2,1)S(1)} %get-tuple-element.219.refs_1_.refs_2_, bf16[512,128]{1,0:T(8,128)(2,1)S(1)} %collective-permute-done.23.refs_2_, bf16[512,128]{1,0:T(8,128)(2,1)S(1)} %collective-permute-done.24.refs_3_, ...), custom_call_target="tpu_custom_call" | custom-call | flops 1 | bytes 1 | tf_op jit(solution)/shard_map/pallas_call | solution.py:68
  110.6 1.4 collective-permute-start.34
  112.0 0.7 collective-permute-start.35
  112.8 1.4 collective-permute-start.36
  114.2 8.1 %all_to_all.28.refs_3_ = f32[8,8,128]{2,1,0:T(8,128)S(1)} all-to-all(f32[8,8,128]{2,1,0:T(8,128)S(1)} %get-tuple-element.235), channel_id=1, replica_groups=mesh['ha'=2,'wa'=4,'ba'=4] {'wa':(2)2,'ba'}, dimensions={0} | all-to-all | bytes 65536 | tf_op jit(solution)/shard_map/all_to_all | solution.py:648
  123.2 3.1 %shard_map.183 = (f32[4,9,64,128]{3,2,1,0:T(8,128)S(1)}, bf16[9,64,128]{2,1,0:T(8,128)(2,1)S(1)}, bf16[9,64,128]{2,1,0:T(8,128)(2,1)S(1)}, bf16[9,64,128]{2,1,0:T(8,128)(2,1)S(1)}, bf16[9,64,128]{2,1,0:T(8,128)(2,1)S(1)}) custom-call(s32[3]{0:T(128)S(1)} %pad_add_fusion.refs_0_, bf16[4,256,512]{2,1,0:T(8,128)(2,1)} %get-tuple-element.248.refs_1_, ...), custom_call_target="tpu_custom_call" | custom-call | flops 3000000000 | bytes 1 | tf_op jit(solution)/shard_map/pallas_call | solution.py:68
  129.2 3.3 %collective-permute-start.46 = (bf16[576,128]{1,0:T(8,128)(2,1)S(1)}, bf16[576,128]{1,0:T(8,128)(2,1)S(1)}, u32[]{:S(2)}, u32[]{:S(2)}) collective-permute-start(bf16[576,128]{1,0:T(8,128)(2,1)S(1)} %get-tuple-element.262), channel_id=1, source_target_pairs={{0,3},{1,2},{2,1},{3,0},{4,7},{5,6},{6,5},{7,4},{8,11},{9,10},{10,... | collective-permute-start | bytes 442376 | tf_op jit(solution)/shard_map/ppermute | solution.py:642
  133.2 1.5 collective-permute-start.41
  135.9 1.5 collective-permute-start.43
  137.4 3.0 %shard_map.185 = (f32[256,512]{1,0:T(8,128)S(1)}, bf16[256,512]{1,0:T(8,128)(2,1)S(1)}, bf16[256,512]{1,0:T(8,128)(2,1)S(1)}, bf16[256,512]{1,0:T(8,128)(2,1)S(1)}) custom-call(s32[3]{0:T(128)S(1)} %pad_add_fusion.refs_0_, bf16[512,128]{1,0:T(8,128)(2,1)S(1)} %get-tuple-element.246.refs_5_.refs_2_.refs_1_, ...), custom_call_target="tpu_custom_call" | custom-call | flops 3000000000 | bytes 1 | tf_op jit(solution)/shard_map/pallas_call | solution.py:68
  140.5 2.0 %collective-permute-done.45.refs_2_ = bf16[576,128]{1,0:T(8,128)(2,1)S(1)} collective-permute-done((bf16[576,128]{1,0:T(8,128)(2,1)S(1)}, bf16[576,128]{1,0:T(8,128)(2,1)S(1)}, u32[]{:S(2)}, u32[]{:S(2)}) %collective-permute-start.45) | collective-permute-done | bytes 147488 | tf_op jit(solution)/shard_map/ppermute | solution.py:642
  143.6 2.2 %collective-permute-start.47 = (bf16[576,128]{1,0:T(8,128)(2,1)S(1)}, bf16[576,128]{1,0:T(8,128)(2,1)S(1)}, u32[]{:S(2)}, u32[]{:S(2)}) collective-permute-start(bf16[576,128]{1,0:T(8,128)(2,1)S(1)} %get-tuple-element.281), channel_id=1, source_target_pairs={{0,1},{1,0},{2,3},{3,2},{4,5},{5,4},{6,7},{7,6},{8,9},{9,8},{10,11... | collective-permute-start | bytes 442376 | tf_op jit(solution)/shard_map/ppermute | solution.py:642
  145.9 1.4 collective-permute-start.50
  147.9 1.4 collective-permute-start.52
  149.4 2.4 %collective-permute-start.49 = (bf16[576,128]{1,0:T(8,128)(2,1)S(1)}, bf16[576,128]{1,0:T(8,128)(2,1)S(1)}, u32[]{:S(2)}, u32[]{:S(2)}) collective-permute-start(bf16[576,128]{1,0:T(8,128)(2,1)S(1)} %get-tuple-element.283), channel_id=1, source_target_pairs={{0,3},{1,2},{2,1},{3,0},{4,7},{5,6},{6,5},{7,4},{8,11},{9,10},{10,... | collective-permute-start | bytes 442376 | tf_op jit(solution)/shard_map/ppermute | solution.py:642
  151.9 0.7 copy-done.1
  152.6 7.5 %collective-permute-done.48.refs_2_ = bf16[576,128]{1,0:T(8,128)(2,1)S(1)} collective-permute-done((bf16[576,128]{1,0:T(8,128)(2,1)S(1)}, bf16[576,128]{1,0:T(8,128)(2,1)S(1)}, u32[]{:S(2)}, u32[]{:S(2)}) %collective-permute-start.48) | collective-permute-done | bytes 147488 | tf_op jit(solution)/shard_map/ppermute | solution.py:642
  160.2 2.5 %shard_map.189 = (f32[2,9,64,128]{3,2,1,0:T(8,128)}, f32[2,9,64,128]{3,2,1,0:T(8,128)}, f32[2,9,64,128]{3,2,1,0:T(8,128)S(1)}, f32[32,8,128]{2,1,0:T(8,128)}) custom-call(bf16[576,128]{1,0:T(8,128)(2,1)S(1)} %get-tuple-element.292.refs_0_, bf16[576,128]{1,0:T(8,128)(2,1)S(1)} %collective-permute-done.47.refs_1_, ...), custom_call_target="tpu_custom_call" | custom-call | flops 1 | bytes 1 | tf_op jit(solution)/shard_map/pallas_call | solution.py:68
  162.7 4.9 %all-to-all-start.4 = ((f32[32,8,128]{2,1,0:T(8,128)}), f32[32,8,128]{2,1,0:T(8,128)S(1)}, u32[]{:S(2)}, u32[]{:S(2)}) async-start(f32[32,8,128]{2,1,0:T(8,128)} %get-tuple-element.302), calls=%async_computation.4 | async-start | bytes 262144 | tf_op jit(solution)/shard_map/all_to_all | solution.py:833
  167.6 0.7 copy.19
  168.3 0.8 shard_map.187
  169.1 6.4 %all-to-all-done.4.refs_0_ = f32[32,8,128]{2,1,0:T(8,128)S(1)} async-done(((f32[32,8,128]{2,1,0:T(8,128)}), f32[32,8,128]{2,1,0:T(8,128)S(1)}, u32[]{:S(2)}, u32[]{:S(2)}) %all-to-all-start.4) | async-done | bytes 131104 | tf_op jit(solution)/shard_map/all_to_all | solution.py:833
  175.5 1.1 shard_map.190
  (91 shorter events, 17.6 us)
Async XLA Ops:
  1.8 9.7 %collective-permute-start.2 = (bf16[9,64,128]{2,1,0:T(8,128)(2,1)S(1)}, bf16[9,64,128]{2,1,0:T(8,128)(2,1)S(1)}, u32[]{:S(2)}, u32[]{:S(2)}) collective-permute-start(bf16[9,64,128]{2,1,0:T(8,128)(2,1)S(1)} %get-tuple-element.165.refs_1_), channel_id=1, source_target_pairs={{0,3},{1,2},{2,1},{3,0},{4,7},{5,6},{6,5},{7,4},{8,11},{9,10},{10,... | collective-permute-start | bytes 442376 | tf_op jit(solution)/shard_map/ppermute | solution.py:642
  8.0 32.8 %copy-start.5 = (f32[4,512]{1,0:T(4,128)S(1)}, f32[4,512]{1,0:T(4,128)}, u32[]{:S(2)}) copy-start(f32[4,512]{1,0:T(4,128)} %refs_3_.1) | copy-start | bytes 24580
  8.0 12.9 %collective-permute-start.5 = (bf16[272,512]{1,0:T(8,128)(2,1)S(1)}, bf16[272,512]{1,0:T(8,128)(2,1)S(1)}, u32[]{:S(2)}, u32[]{:S(2)}) collective-permute-start(bf16[272,512]{1,0:T(8,128)(2,1)S(1)} %shard_map.168.refs_2_), channel_id=1, source_target_pairs={{0,24},{8,16},{16,8},{24,0},{1,25},{9,17},{17,9},{25,1},{2,26},{10... | collective-permute-start | bytes 835592 | tf_op jit(solution)/shard_map/ppermute | solution.py:651
  10.5 12.6 %collective-permute-start.4 = (bf16[272,512]{1,0:T(8,128)(2,1)S(1)}, bf16[272,512]{1,0:T(8,128)(2,1)S(1)}, u32[]{:S(2)}, u32[]{:S(2)}) collective-permute-start(bf16[272,512]{1,0:T(8,128)(2,1)S(1)} %shard_map.168.refs_2_), channel_id=1, source_target_pairs={{0,16},{8,24},{16,0},{24,8},{1,17},{9,25},{17,1},{25,9},{2,18},{10... | collective-permute-start | bytes 835592 | tf_op jit(solution)/shard_map/ppermute | solution.py:651
  11.0 12.1 %collective-permute-start.3 = (bf16[272,512]{1,0:T(8,128)(2,1)S(1)}, bf16[272,512]{1,0:T(8,128)(2,1)S(1)}, u32[]{:S(2)}, u32[]{:S(2)}) collective-permute-start(bf16[272,512]{1,0:T(8,128)(2,1)S(1)} %shard_map.168.refs_2_), channel_id=1, source_target_pairs={{0,8},{8,0},{16,24},{24,16},{1,9},{9,1},{17,25},{25,17},{2,10},{10... | collective-permute-start | bytes 835592 | tf_op jit(solution)/shard_map/ppermute | solution.py:651
  11.5 7.9 %collective-permute-start.1 = (bf16[9,64,128]{2,1,0:T(8,128)(2,1)S(1)}, bf16[9,64,128]{2,1,0:T(8,128)(2,1)S(1)}, u32[]{:S(2)}, u32[]{:S(2)}) collective-permute-start(bf16[9,64,128]{2,1,0:T(8,128)(2,1)S(1)} %get-tuple-element.165.refs_1_), channel_id=1, source_target_pairs={{0,2},{1,3},{2,0},{3,1},{4,6},{5,7},{6,4},{7,5},{8,10},{9,11},{10,... | collective-permute-start | bytes 442376 | tf_op jit(solution)/shard_map/ppermute | solution.py:642
  11.5 9.4 %collective-permute-start = (bf16[9,64,128]{2,1,0:T(8,128)(2,1)S(1)}, bf16[9,64,128]{2,1,0:T(8,128)(2,1)S(1)}, u32[]{:S(2)}, u32[]{:S(2)}) collective-permute-start(bf16[9,64,128]{2,1,0:T(8,128)(2,1)S(1)} %get-tuple-element.165.refs_1_), channel_id=1, source_target_pairs={{0,1},{1,0},{2,3},{3,2},{4,5},{5,4},{6,7},{7,6},{8,9},{9,8},{10,11... | collective-permute-start | bytes 442376 | tf_op jit(solution)/shard_map/ppermute | solution.py:642
  23.1 7.6 %collective-permute-start.11 = (bf16[9,64,128]{2,1,0:T(8,128)(2,1)S(1)}, bf16[9,64,128]{2,1,0:T(8,128)(2,1)S(1)}, u32[]{:S(2)}, u32[]{:S(2)}) collective-permute-start(bf16[9,64,128]{2,1,0:T(8,128)(2,1)S(1)} %get-tuple-element.181.refs_1_), channel_id=1, source_target_pairs={{0,3},{1,2},{2,1},{3,0},{4,7},{5,6},{6,5},{7,4},{8,11},{9,10},{10,... | collective-permute-start | bytes 442376 | tf_op jit(solution)/shard_map/ppermute | solution.py:642
  24.8 13.3 %collective-permute-start.6 = (bf16[832,128]{1,0:T(8,128)(2,1)S(1)}, bf16[832,128]{1,0:T(8,128)(2,1)S(1)}, u32[]{:S(2)}, u32[]{:S(2)}) collective-permute-start(bf16[832,128]{1,0:T(8,128)(2,1)S(1)} %get-tuple-element.170), channel_id=1, source_target_pairs={{0,8},{8,0},{16,24},{24,16},{1,9},{9,1},{17,25},{25,17},{2,10},{10... | collective-permute-start | bytes 638984 | tf_op jit(solution)/shard_map/ppermute | solution.py:651
  26.4 11.7 %collective-permute-start.7 = (bf16[832,128]{1,0:T(8,128)(2,1)S(1)}, bf16[832,128]{1,0:T(8,128)(2,1)S(1)}, u32[]{:S(2)}, u32[]{:S(2)}) collective-permute-start(bf16[832,128]{1,0:T(8,128)(2,1)S(1)} %get-tuple-element.171), channel_id=1, source_target_pairs={{0,16},{8,24},{16,0},{24,8},{1,17},{9,25},{17,1},{25,9},{2,18},{10... | collective-permute-start | bytes 638984 | tf_op jit(solution)/shard_map/ppermute | solution.py:651
  27.9 10.2 %collective-permute-start.8 = (bf16[832,128]{1,0:T(8,128)(2,1)S(1)}, bf16[832,128]{1,0:T(8,128)(2,1)S(1)}, u32[]{:S(2)}, u32[]{:S(2)}) collective-permute-start(bf16[832,128]{1,0:T(8,128)(2,1)S(1)} %get-tuple-element.172), channel_id=1, source_target_pairs={{0,24},{8,16},{16,8},{24,0},{1,25},{9,17},{17,9},{25,1},{2,26},{10... | collective-permute-start | bytes 638984 | tf_op jit(solution)/shard_map/ppermute | solution.py:651
  28.4 9.0 %collective-permute-start.10 = (bf16[9,64,128]{2,1,0:T(8,128)(2,1)S(1)}, bf16[9,64,128]{2,1,0:T(8,128)(2,1)S(1)}, u32[]{:S(2)}, u32[]{:S(2)}) collective-permute-start(bf16[9,64,128]{2,1,0:T(8,128)(2,1)S(1)} %get-tuple-element.181.refs_1_), channel_id=1, source_target_pairs={{0,2},{1,3},{2,0},{3,1},{4,6},{5,7},{6,4},{7,5},{8,10},{9,11},{10,... | collective-permute-start | bytes 442376 | tf_op jit(solution)/shard_map/ppermute | solution.py:642
  30.7 7.4 %collective-permute-start.9 = (bf16[9,64,128]{2,1,0:T(8,128)(2,1)S(1)}, bf16[9,64,128]{2,1,0:T(8,128)(2,1)S(1)}, u32[]{:S(2)}, u32[]{:S(2)}) collective-permute-start(bf16[9,64,128]{2,1,0:T(8,128)(2,1)S(1)} %get-tuple-element.181.refs_1_), channel_id=1, source_target_pairs={{0,1},{1,0},{2,3},{3,2},{4,5},{5,4},{6,7},{7,6},{8,9},{9,8},{10,11... | collective-permute-start | bytes 442376 | tf_op jit(solution)/shard_map/ppermute | solution.py:642
  38.7 2.1 %collective-permute-start.12 = (bf16[4,9,64,128]{3,2,1,0:T(8,128)(2,1)S(1)}, bf16[4,9,64,128]{3,2,1,0:T(8,128)(2,1)S(1)}, u32[]{:S(2)}, u32[]{:S(2)}) collective-permute-start(bf16[4,9,64,128]{3,2,1,0:T(8,128)(2,1)S(1)} %get-tuple-element.178.refs_6_), channel_id=1, source_target_pairs={{0,4},{4,0},{1,5},{5,1},{2,6},{6,2},{3,7},{7,3},{8,12},{12,8},{9,1... | collective-permute-start | bytes 1769480 | tf_op jit(solution)/shard_map/ppermute | solution.py:645
  43.5 13.1 %collective-permute-start.13 = (bf16[576,128]{1,0:T(8,128)(2,1)S(1)}, bf16[576,128]{1,0:T(8,128)(2,1)S(1)}, u32[]{:S(2)}, u32[]{:S(2)}) collective-permute-start(bf16[576,128]{1,0:T(8,128)(2,1)S(1)} %get-tuple-element.191), channel_id=1, source_target_pairs={{0,8},{8,0},{16,24},{24,16},{1,9},{9,1},{17,25},{25,17},{2,10},{10... | collective-permute-start | bytes 442376 | tf_op jit(solution)/shard_map/ppermute | solution.py:651
  45.2 11.5 %collective-permute-start.14 = (bf16[576,128]{1,0:T(8,128)(2,1)S(1)}, bf16[576,128]{1,0:T(8,128)(2,1)S(1)}, u32[]{:S(2)}, u32[]{:S(2)}) collective-permute-start(bf16[576,128]{1,0:T(8,128)(2,1)S(1)} %get-tuple-element.192), channel_id=1, source_target_pairs={{0,16},{8,24},{16,0},{24,8},{1,17},{9,25},{17,1},{25,9},{2,18},{10... | collective-permute-start | bytes 442376 | tf_op jit(solution)/shard_map/ppermute | solution.py:651
  46.7 10.0 %collective-permute-start.15 = (bf16[576,128]{1,0:T(8,128)(2,1)S(1)}, bf16[576,128]{1,0:T(8,128)(2,1)S(1)}, u32[]{:S(2)}, u32[]{:S(2)}) collective-permute-start(bf16[576,128]{1,0:T(8,128)(2,1)S(1)} %get-tuple-element.193), channel_id=1, source_target_pairs={{0,24},{8,16},{16,8},{24,0},{1,25},{9,17},{17,9},{25,1},{2,26},{10... | collective-permute-start | bytes 442376 | tf_op jit(solution)/shard_map/ppermute | solution.py:651
  57.7 13.0 %collective-permute-start.22 = (bf16[4,9,64,128]{3,2,1,0:T(8,128)(2,1)S(1)}, bf16[4,9,64,128]{3,2,1,0:T(8,128)(2,1)S(1)}, u32[]{:S(2)}, u32[]{:S(2)}) collective-permute-start(bf16[4,9,64,128]{3,2,1,0:T(8,128)(2,1)S(1)} %shard_map.174.refs_9_), channel_id=1, source_target_pairs={{0,4},{4,0},{1,5},{5,1},{2,6},{6,2},{3,7},{7,3},{8,12},{12,8},{9,1... | collective-permute-start | bytes 1769480 | tf_op jit(solution)/shard_map/ppermute | solution.py:645
  57.9 5.9 %collective-permute-start.17 = (bf16[512,128]{1,0:T(8,128)(2,1)S(1)}, bf16[512,128]{1,0:T(8,128)(2,1)S(1)}, u32[]{:S(2)}, u32[]{:S(2)}) collective-permute-start(bf16[512,128]{1,0:T(8,128)(2,1)S(1)} %get-tuple-element.203.refs_1_), channel_id=1, source_target_pairs={{0,16},{8,24},{16,0},{24,8},{1,17},{9,25},{17,1},{25,9},{2,18},{10... | collective-permute-start | bytes 393224 | tf_op jit(solution)/shard_map/ppermute | solution.py:651
  59.4 6.4 %collective-permute-start.19 = (bf16[512,128]{1,0:T(8,128)(2,1)S(1)}, bf16[512,128]{1,0:T(8,128)(2,1)S(1)}, u32[]{:S(2)}, u32[]{:S(2)}) collective-permute-start(bf16[512,128]{1,0:T(8,128)(2,1)S(1)} %get-tuple-element.204.refs_5_), channel_id=1, source_target_pairs={{0,8},{8,0},{16,24},{24,16},{1,9},{9,1},{17,25},{25,17},{2,10},{10... | collective-permute-start | bytes 393224 | tf_op jit(solution)/shard_map/ppermute | solution.py:651
  60.9 7.6 %collective-permute-start.16 = (bf16[512,128]{1,0:T(8,128)(2,1)S(1)}, bf16[512,128]{1,0:T(8,128)(2,1)S(1)}, u32[]{:S(2)}, u32[]{:S(2)}) collective-permute-start(bf16[512,128]{1,0:T(8,128)(2,1)S(1)} %get-tuple-element.203.refs_1_), channel_id=1, source_target_pairs={{0,8},{8,0},{16,24},{24,16},{1,9},{9,1},{17,25},{25,17},{2,10},{10... | collective-permute-start | bytes 393224 | tf_op jit(solution)/shard_map/ppermute | solution.py:651
  61.4 7.1 %collective-permute-start.20 = (bf16[512,128]{1,0:T(8,128)(2,1)S(1)}, bf16[512,128]{1,0:T(8,128)(2,1)S(1)}, u32[]{:S(2)}, u32[]{:S(2)}) collective-permute-start(bf16[512,128]{1,0:T(8,128)(2,1)S(1)} %get-tuple-element.204.refs_5_), channel_id=1, source_target_pairs={{0,16},{8,24},{16,0},{24,8},{1,17},{9,25},{17,1},{25,9},{2,18},{10... | collective-permute-start | bytes 393224 | tf_op jit(solution)/shard_map/ppermute | solution.py:651
  63.7 6.8 %collective-permute-start.18 = (bf16[512,128]{1,0:T(8,128)(2,1)S(1)}, bf16[512,128]{1,0:T(8,128)(2,1)S(1)}, u32[]{:S(2)}, u32[]{:S(2)}) collective-permute-start(bf16[512,128]{1,0:T(8,128)(2,1)S(1)} %collective-permute-done.17.refs_3_), channel_id=1, source_target_pairs={{0,8},{8,0},{16,24},{24,16},{1,9},{9,1},{17,25},{25,17},{2,10},{10... | collective-permute-start | bytes 393224 | tf_op jit(solution)/shard_map/ppermute | solution.py:651
  65.7 5.0 %collective-permute-start.21 = (bf16[512,128]{1,0:T(8,128)(2,1)S(1)}, bf16[512,128]{1,0:T(8,128)(2,1)S(1)}, u32[]{:S(2)}, u32[]{:S(2)}) collective-permute-start(bf16[512,128]{1,0:T(8,128)(2,1)S(1)} %collective-permute-done.19.refs_6_), channel_id=1, source_target_pairs={{0,16},{8,24},{16,0},{24,8},{1,17},{9,25},{17,1},{25,9},{2,18},{10... | collective-permute-start | bytes 393224 | tf_op jit(solution)/shard_map/ppermute | solution.py:651
  81.5 9.7 %copy-start.4 = (bf16[4,9,64,128]{3,2,1,0:T(8,128)(2,1)S(1)}, bf16[4,9,64,128]{3,2,1,0:T(8,128)(2,1)}, u32[]{:S(2)}) copy-start(bf16[4,9,64,128]{3,2,1,0:T(8,128)(2,1)} %get-tuple-element.221.refs_9_) | copy-start | bytes 1769476
  91.3 16.3 %collective-permute-start.29 = (bf16[4,9,64,128]{3,2,1,0:T(8,128)(2,1)S(1)}, bf16[4,9,64,128]{3,2,1,0:T(8,128)(2,1)S(1)}, u32[]{:S(2)}, u32[]{:S(2)}) collective-permute-start(bf16[4,9,64,128]{3,2,1,0:T(8,128)(2,1)S(1)} %copy-done.4), channel_id=1, source_target_pairs={{0,4},{4,0},{1,5},{5,1},{2,6},{6,2},{3,7},{7,3},{8,12},{12,8},{9,1... | collective-permute-start | bytes 1769480 | tf_op jit(solution)/shard_map/ppermute | solution.py:645
  91.4 5.8 %collective-permute-start.24 = (bf16[512,128]{1,0:T(8,128)(2,1)S(1)}, bf16[512,128]{1,0:T(8,128)(2,1)S(1)}, u32[]{:S(2)}, u32[]{:S(2)}) collective-permute-start(bf16[512,128]{1,0:T(8,128)(2,1)S(1)} %get-tuple-element.219.refs_1_.refs_2_), channel_id=1, source_target_pairs={{0,16},{8,24},{16,0},{24,8},{1,17},{9,25},{17,1},{25,9},{2,18},{10... | collective-permute-start | bytes 393224 | tf_op jit(solution)/shard_map/ppermute | solution.py:651
  93.0 5.5 %collective-permute-start.26 = (bf16[512,128]{1,0:T(8,128)(2,1)S(1)}, bf16[512,128]{1,0:T(8,128)(2,1)S(1)}, u32[]{:S(2)}, u32[]{:S(2)}) collective-permute-start(bf16[512,128]{1,0:T(8,128)(2,1)S(1)} %get-tuple-element.220.refs_5_.refs_3_), channel_id=1, source_target_pairs={{0,8},{8,0},{16,24},{24,16},{1,9},{9,1},{17,25},{25,17},{2,10},{10... | collective-permute-start | bytes 393224 | tf_op jit(solution)/shard_map/ppermute | solution.py:651
  96.6 1.8 %collective-permute-start.30 = (bf16[9,64,128]{2,1,0:T(8,128)(2,1)S(1)}, bf16[9,64,128]{2,1,0:T(8,128)(2,1)S(1)}, u32[]{:S(2)}, u32[]{:S(2)}) collective-permute-start(bf16[9,64,128]{2,1,0:T(8,128)(2,1)S(1)} %get-tuple-element.226), channel_id=1, source_target_pairs={{0,4},{4,0},{1,5},{5,1},{2,6},{6,2},{3,7},{7,3},{8,12},{12,8},{9,1... | collective-permute-start | bytes 442376 | tf_op jit(solution)/shard_map/ppermute | solution.py:645
  96.7 2.8 %collective-permute-start.31 = (bf16[9,64,128]{2,1,0:T(8,128)(2,1)S(1)}, bf16[9,64,128]{2,1,0:T(8,128)(2,1)S(1)}, u32[]{:S(2)}, u32[]{:S(2)}) collective-permute-start(bf16[9,64,128]{2,1,0:T(8,128)(2,1)S(1)} %get-tuple-element.227), channel_id=1, source_target_pairs={{0,4},{4,0},{1,5},{5,1},{2,6},{6,2},{3,7},{7,3},{8,12},{12,8},{9,1... | collective-permute-start | bytes 442376 | tf_op jit(solution)/shard_map/ppermute | solution.py:645
  97.2 3.3 %collective-permute-start.32 = (bf16[9,64,128]{2,1,0:T(8,128)(2,1)S(1)}, bf16[9,64,128]{2,1,0:T(8,128)(2,1)S(1)}, u32[]{:S(2)}, u32[]{:S(2)}) collective-permute-start(bf16[9,64,128]{2,1,0:T(8,128)(2,1)S(1)} %get-tuple-element.228), channel_id=1, source_target_pairs={{0,4},{4,0},{1,5},{5,1},{2,6},{6,2},{3,7},{7,3},{8,12},{12,8},{9,1... | collective-permute-start | bytes 442376 | tf_op jit(solution)/shard_map/ppermute | solution.py:645
  98.4 3.2 %collective-permute-start.33 = (bf16[9,64,128]{2,1,0:T(8,128)(2,1)S(1)}, bf16[9,64,128]{2,1,0:T(8,128)(2,1)S(1)}, u32[]{:S(2)}, u32[]{:S(2)}) collective-permute-start(bf16[9,64,128]{2,1,0:T(8,128)(2,1)S(1)} %get-tuple-element.229), channel_id=1, source_target_pairs={{0,4},{4,0},{1,5},{5,1},{2,6},{6,2},{3,7},{7,3},{8,12},{12,8},{9,1... | collective-permute-start | bytes 442376 | tf_op jit(solution)/shard_map/ppermute | solution.py:645
  98.5 6.3 %collective-permute-start.23 = (bf16[512,128]{1,0:T(8,128)(2,1)S(1)}, bf16[512,128]{1,0:T(8,128)(2,1)S(1)}, u32[]{:S(2)}, u32[]{:S(2)}) collective-permute-start(bf16[512,128]{1,0:T(8,128)(2,1)S(1)} %get-tuple-element.219.refs_1_.refs_2_), channel_id=1, source_target_pairs={{0,8},{8,0},{16,24},{24,16},{1,9},{9,1},{17,25},{25,17},{2,10},{10... | collective-permute-start | bytes 393224 | tf_op jit(solution)/shard_map/ppermute | solution.py:651
  99.5 6.4 %collective-permute-start.27 = (bf16[512,128]{1,0:T(8,128)(2,1)S(1)}, bf16[512,128]{1,0:T(8,128)(2,1)S(1)}, u32[]{:S(2)}, u32[]{:S(2)}) collective-permute-start(bf16[512,128]{1,0:T(8,128)(2,1)S(1)} %get-tuple-element.220.refs_5_.refs_3_), channel_id=1, source_target_pairs={{0,16},{8,24},{16,0},{24,8},{1,17},{9,25},{17,1},{25,9},{2,18},{10... | collective-permute-start | bytes 393224 | tf_op jit(solution)/shard_map/ppermute | solution.py:651
  100.5 6.6 %collective-permute-start.25 = (bf16[512,128]{1,0:T(8,128)(2,1)S(1)}, bf16[512,128]{1,0:T(8,128)(2,1)S(1)}, u32[]{:S(2)}, u32[]{:S(2)}) collective-permute-start(bf16[512,128]{1,0:T(8,128)(2,1)S(1)} %collective-permute-done.24.refs_3_), channel_id=1, source_target_pairs={{0,8},{8,0},{16,24},{24,16},{1,9},{9,1},{17,25},{25,17},{2,10},{10... | collective-permute-start | bytes 393224 | tf_op jit(solution)/shard_map/ppermute | solution.py:651
  101.6 6.0 %collective-permute-start.28 = (bf16[512,128]{1,0:T(8,128)(2,1)S(1)}, bf16[512,128]{1,0:T(8,128)(2,1)S(1)}, u32[]{:S(2)}, u32[]{:S(2)}) collective-permute-start(bf16[512,128]{1,0:T(8,128)(2,1)S(1)} %collective-permute-done.26.refs_6_), channel_id=1, source_target_pairs={{0,16},{8,24},{16,0},{24,8},{1,17},{9,25},{17,1},{25,9},{2,18},{10... | collective-permute-start | bytes 393224 | tf_op jit(solution)/shard_map/ppermute | solution.py:651
  110.6 11.7 %collective-permute-start.34 = (bf16[832,128]{1,0:T(8,128)(2,1)S(1)}, bf16[832,128]{1,0:T(8,128)(2,1)S(1)}, u32[]{:S(2)}, u32[]{:S(2)}) collective-permute-start(bf16[832,128]{1,0:T(8,128)(2,1)S(1)} %get-tuple-element.237), channel_id=1, source_target_pairs={{0,8},{8,0},{16,24},{24,16},{1,9},{9,1},{17,25},{25,17},{2,10},{10... | collective-permute-start | bytes 638984 | tf_op jit(solution)/shard_map/ppermute | solution.py:651
  112.0 10.3 %collective-permute-start.35 = (bf16[832,128]{1,0:T(8,128)(2,1)S(1)}, bf16[832,128]{1,0:T(8,128)(2,1)S(1)}, u32[]{:S(2)}, u32[]{:S(2)}) collective-permute-start(bf16[832,128]{1,0:T(8,128)(2,1)S(1)} %get-tuple-element.238), channel_id=1, source_target_pairs={{0,16},{8,24},{16,0},{24,8},{1,17},{9,25},{17,1},{25,9},{2,18},{10... | collective-permute-start | bytes 638984 | tf_op jit(solution)/shard_map/ppermute | solution.py:651
  112.8 10.1 %collective-permute-start.36 = (bf16[832,128]{1,0:T(8,128)(2,1)S(1)}, bf16[832,128]{1,0:T(8,128)(2,1)S(1)}, u32[]{:S(2)}, u32[]{:S(2)}) collective-permute-start(bf16[832,128]{1,0:T(8,128)(2,1)S(1)} %get-tuple-element.239), channel_id=1, source_target_pairs={{0,24},{8,16},{16,8},{24,0},{1,25},{9,17},{17,9},{25,1},{2,26},{10... | collective-permute-start | bytes 638984 | tf_op jit(solution)/shard_map/ppermute | solution.py:651
  126.3 2.3 %collective-permute-start.37 = (bf16[9,64,128]{2,1,0:T(8,128)(2,1)S(1)}, bf16[9,64,128]{2,1,0:T(8,128)(2,1)S(1)}, u32[]{:S(2)}, u32[]{:S(2)}) collective-permute-start(bf16[9,64,128]{2,1,0:T(8,128)(2,1)S(1)} %get-tuple-element.251), channel_id=1, source_target_pairs={{0,4},{4,0},{1,5},{5,1},{2,6},{6,2},{3,7},{7,3},{8,12},{12,8},{9,1... | collective-permute-start | bytes 442376 | tf_op jit(solution)/shard_map/ppermute | solution.py:645
  126.4 2.9 %collective-permute-start.38 = (bf16[9,64,128]{2,1,0:T(8,128)(2,1)S(1)}, bf16[9,64,128]{2,1,0:T(8,128)(2,1)S(1)}, u32[]{:S(2)}, u32[]{:S(2)}) collective-permute-start(bf16[9,64,128]{2,1,0:T(8,128)(2,1)S(1)} %get-tuple-element.252), channel_id=1, source_target_pairs={{0,4},{4,0},{1,5},{5,1},{2,6},{6,2},{3,7},{7,3},{8,12},{12,8},{9,1... | collective-permute-start | bytes 442376 | tf_op jit(solution)/shard_map/ppermute | solution.py:645
  126.9 5.7 %collective-permute-start.39 = (bf16[9,64,128]{2,1,0:T(8,128)(2,1)S(1)}, bf16[9,64,128]{2,1,0:T(8,128)(2,1)S(1)}, u32[]{:S(2)}, u32[]{:S(2)}) collective-permute-start(bf16[9,64,128]{2,1,0:T(8,128)(2,1)S(1)} %get-tuple-element.253), channel_id=1, source_target_pairs={{0,4},{4,0},{1,5},{5,1},{2,6},{6,2},{3,7},{7,3},{8,12},{12,8},{9,1... | collective-permute-start | bytes 442376 | tf_op jit(solution)/shard_map/ppermute | solution.py:645
  126.9 5.6 %collective-permute-start.40 = (bf16[9,64,128]{2,1,0:T(8,128)(2,1)S(1)}, bf16[9,64,128]{2,1,0:T(8,128)(2,1)S(1)}, u32[]{:S(2)}, u32[]{:S(2)}) collective-permute-start(bf16[9,64,128]{2,1,0:T(8,128)(2,1)S(1)} %get-tuple-element.254), channel_id=1, source_target_pairs={{0,4},{4,0},{1,5},{5,1},{2,6},{6,2},{3,7},{7,3},{8,12},{12,8},{9,1... | collective-permute-start | bytes 442376 | tf_op jit(solution)/shard_map/ppermute | solution.py:645
  128.1 7.8 %collective-permute-start.44 = (bf16[576,128]{1,0:T(8,128)(2,1)S(1)}, bf16[576,128]{1,0:T(8,128)(2,1)S(1)}, u32[]{:S(2)}, u32[]{:S(2)}) collective-permute-start(bf16[576,128]{1,0:T(8,128)(2,1)S(1)} %get-tuple-element.260), channel_id=1, source_target_pairs={{0,1},{1,0},{2,3},{3,2},{4,5},{5,4},{6,7},{7,6},{8,9},{9,8},{10,11... | collective-permute-start | bytes 442376 | tf_op jit(solution)/shard_map/ppermute | solution.py:642
  128.6 13.9 %collective-permute-start.45 = (bf16[576,128]{1,0:T(8,128)(2,1)S(1)}, bf16[576,128]{1,0:T(8,128)(2,1)S(1)}, u32[]{:S(2)}, u32[]{:S(2)}) collective-permute-start(bf16[576,128]{1,0:T(8,128)(2,1)S(1)} %get-tuple-element.261), channel_id=1, source_target_pairs={{0,2},{1,3},{2,0},{3,1},{4,6},{5,7},{6,4},{7,5},{8,10},{9,11},{10,... | collective-permute-start | bytes 442376 | tf_op jit(solution)/shard_map/ppermute | solution.py:642
  129.2 13.3 %collective-permute-start.46 = (bf16[576,128]{1,0:T(8,128)(2,1)S(1)}, bf16[576,128]{1,0:T(8,128)(2,1)S(1)}, u32[]{:S(2)}, u32[]{:S(2)}) collective-permute-start(bf16[576,128]{1,0:T(8,128)(2,1)S(1)} %get-tuple-element.262), channel_id=1, source_target_pairs={{0,3},{1,2},{2,1},{3,0},{4,7},{5,6},{6,5},{7,4},{8,11},{9,10},{10,... | collective-permute-start | bytes 442376 | tf_op jit(solution)/shard_map/ppermute | solution.py:642
  133.2 9.3 %collective-permute-start.41 = (bf16[576,128]{1,0:T(8,128)(2,1)S(1)}, bf16[576,128]{1,0:T(8,128)(2,1)S(1)}, u32[]{:S(2)}, u32[]{:S(2)}) collective-permute-start(bf16[576,128]{1,0:T(8,128)(2,1)S(1)} %get-tuple-element.256), channel_id=1, source_target_pairs={{0,8},{8,0},{16,24},{24,16},{1,9},{9,1},{17,25},{25,17},{2,10},{10... | collective-permute-start | bytes 442376 | tf_op jit(solution)/shard_map/ppermute | solution.py:651
  134.7 7.8 %collective-permute-start.42 = (bf16[576,128]{1,0:T(8,128)(2,1)S(1)}, bf16[576,128]{1,0:T(8,128)(2,1)S(1)}, u32[]{:S(2)}, u32[]{:S(2)}) collective-permute-start(bf16[576,128]{1,0:T(8,128)(2,1)S(1)} %get-tuple-element.257), channel_id=1, source_target_pairs={{0,16},{8,24},{16,0},{24,8},{1,17},{9,25},{17,1},{25,9},{2,18},{10... | collective-permute-start | bytes 442376 | tf_op jit(solution)/shard_map/ppermute | solution.py:651
  135.9 7.1 %collective-permute-start.43 = (bf16[576,128]{1,0:T(8,128)(2,1)S(1)}, bf16[576,128]{1,0:T(8,128)(2,1)S(1)}, u32[]{:S(2)}, u32[]{:S(2)}) collective-permute-start(bf16[576,128]{1,0:T(8,128)(2,1)S(1)} %get-tuple-element.258), channel_id=1, source_target_pairs={{0,24},{8,16},{16,8},{24,0},{1,25},{9,17},{17,9},{25,1},{2,26},{10... | collective-permute-start | bytes 442376 | tf_op jit(solution)/shard_map/ppermute | solution.py:651
  140.5 19.7 %copy-start = (f32[2,9,64,128]{3,2,1,0:T(8,128)S(1)}, f32[2,9,64,128]{3,2,1,0:T(8,128)}, u32[]{:S(2)}) copy-start(f32[2,9,64,128]{3,2,1,0:T(8,128)} %refs_1_.5) | copy-start | bytes 1769476
  140.5 19.7 %copy-start.2 = (f32[2,9,64,128]{3,2,1,0:T(8,128)S(1)}, f32[2,9,64,128]{3,2,1,0:T(8,128)}, u32[]{:S(2)}) copy-start(f32[2,9,64,128]{3,2,1,0:T(8,128)} %refs_6_.1) | copy-start | bytes 1769476
  140.5 19.7 %copy-start.3 = (f32[2,9,64,128]{3,2,1,0:T(8,128)S(1)}, f32[2,9,64,128]{3,2,1,0:T(8,128)}, u32[]{:S(2)}) copy-start(f32[2,9,64,128]{3,2,1,0:T(8,128)} %refs_7_.1) | copy-start | bytes 1769476
  143.6 5.8 %collective-permute-start.47 = (bf16[576,128]{1,0:T(8,128)(2,1)S(1)}, bf16[576,128]{1,0:T(8,128)(2,1)S(1)}, u32[]{:S(2)}, u32[]{:S(2)}) collective-permute-start(bf16[576,128]{1,0:T(8,128)(2,1)S(1)} %get-tuple-element.281), channel_id=1, source_target_pairs={{0,1},{1,0},{2,3},{3,2},{4,5},{5,4},{6,7},{7,6},{8,9},{9,8},{10,11... | collective-permute-start | bytes 442376 | tf_op jit(solution)/shard_map/ppermute | solution.py:642
  145.9 14.3 %collective-permute-start.50 = (bf16[256,512]{1,0:T(8,128)(2,1)S(1)}, bf16[256,512]{1,0:T(8,128)(2,1)S(1)}, u32[]{:S(2)}, u32[]{:S(2)}) collective-permute-start(bf16[256,512]{1,0:T(8,128)(2,1)S(1)} %get-tuple-element.285), channel_id=1, source_target_pairs={{0,8},{8,0},{16,24},{24,16},{1,9},{9,1},{17,25},{25,17},{2,10},{10... | collective-permute-start | bytes 786440 | tf_op jit(solution)/shard_map/ppermute | solution.py:651
  147.3 12.8 %collective-permute-start.51 = (bf16[256,512]{1,0:T(8,128)(2,1)S(1)}, bf16[256,512]{1,0:T(8,128)(2,1)S(1)}, u32[]{:S(2)}, u32[]{:S(2)}) collective-permute-start(bf16[256,512]{1,0:T(8,128)(2,1)S(1)} %get-tuple-element.286), channel_id=1, source_target_pairs={{0,16},{8,24},{16,0},{24,8},{1,17},{9,25},{17,1},{25,9},{2,18},{10... | collective-permute-start | bytes 786440 | tf_op jit(solution)/shard_map/ppermute | solution.py:651
  147.9 12.2 %collective-permute-start.52 = (bf16[256,512]{1,0:T(8,128)(2,1)S(1)}, bf16[256,512]{1,0:T(8,128)(2,1)S(1)}, u32[]{:S(2)}, u32[]{:S(2)}) collective-permute-start(bf16[256,512]{1,0:T(8,128)(2,1)S(1)} %get-tuple-element.287), channel_id=1, source_target_pairs={{0,24},{8,16},{16,8},{24,0},{1,25},{9,17},{17,9},{25,1},{2,26},{10... | collective-permute-start | bytes 786440 | tf_op jit(solution)/shard_map/ppermute | solution.py:651
  149.3 10.8 %collective-permute-start.48 = (bf16[576,128]{1,0:T(8,128)(2,1)S(1)}, bf16[576,128]{1,0:T(8,128)(2,1)S(1)}, u32[]{:S(2)}, u32[]{:S(2)}) collective-permute-start(bf16[576,128]{1,0:T(8,128)(2,1)S(1)} %get-tuple-element.282), channel_id=1, source_target_pairs={{0,2},{1,3},{2,0},{3,1},{4,6},{5,7},{6,4},{7,5},{8,10},{9,11},{10,... | collective-permute-start | bytes 442376 | tf_op jit(solution)/shard_map/ppermute | solution.py:642
  149.4 10.7 %collective-permute-start.49 = (bf16[576,128]{1,0:T(8,128)(2,1)S(1)}, bf16[576,128]{1,0:T(8,128)(2,1)S(1)}, u32[]{:S(2)}, u32[]{:S(2)}) collective-permute-start(bf16[576,128]{1,0:T(8,128)(2,1)S(1)} %get-tuple-element.283), channel_id=1, source_target_pairs={{0,3},{1,2},{2,1},{3,0},{4,7},{5,6},{6,5},{7,4},{8,11},{9,10},{10,... | collective-permute-start | bytes 442376 | tf_op jit(solution)/shard_map/ppermute | solution.py:642
  151.9 0.7 copy-start.1
  162.7 12.8 %copy-start.6 = (f32[4,512]{1,0:T(4,128)S(1)}, f32[4,512]{1,0:T(4,128)}, u32[]{:S(2)}) copy-start(f32[4,512]{1,0:T(4,128)} %refs_4_.1) | copy-start | bytes 24580
  162.7 12.8 %copy-start.7 = (f32[4,512]{1,0:T(4,128)S(1)}, f32[4,512]{1,0:T(4,128)}, u32[]{:S(2)}) copy-start(f32[4,512]{1,0:T(4,128)} %refs_5_.3) | copy-start | bytes 24580
  162.7 12.8 %all-to-all-start.4 = ((f32[32,8,128]{2,1,0:T(8,128)}), f32[32,8,128]{2,1,0:T(8,128)S(1)}, u32[]{:S(2)}, u32[]{:S(2)}) async-start(f32[32,8,128]{2,1,0:T(8,128)} %get-tuple-element.302), calls=%async_computation.4 | async-start | bytes 262144 | tf_op jit(solution)/shard_map/all_to_all | solution.py:833

commit v4 on v3

--- a/solution.py
+++ b/solution.py
@@ -50,7 +50,7 @@
         self.IB = self.C // self.R
         self.K = weights[1]
         self.extra = 16 * ((2 * self.n_own + 15) // 16)
-        self.sent = self.own + self.extra
+        self.sent = self.K * self.IB + self.own + self.extra
 
 
 def call(body, out_shape, args, scratch=(), limit=8, far=(), after=(), cost=1, raw=()):
@@ -174,24 +174,21 @@
 
 def local_stats(z, z_ref, hw_ref, stats_ref):
     px = z.H * z.W
-
-    def first(n, carry):
-        count, total = carry
+    pivot = z_ref[0:1, :]
+
+    def step(n, carry):
         mask = image_mask(z, hw_ref[n])
-        block = z_ref[pl.ds(pl.multiple_of(n * px, px), px), :]
-        return count + jnp.sum(mask, 0, keepdims=True), total + jnp.sum(mask * block, 0, keepdims=True)
+        centered = mask * (z_ref[pl.ds(pl.multiple_of(n * px, px), px), :] - pivot)
+        return (
+            carry[0] + jnp.sum(mask, 0, keepdims=True),
+            carry[1] + jnp.sum(centered, 0, keepdims=True),
+            carry[2] + jnp.sum(centered * centered, 0, keepdims=True),
+        )
 
     zero = jnp.zeros((1, z.L), F32)
-    count, total = lax.fori_loop(0, z.n_group, first, (zero, zero), unroll=4)
-    mean = total / count
-
-    def second(n, spread_sum):
-        mask = image_mask(z, hw_ref[n])
-        centered = z_ref[pl.ds(pl.multiple_of(n * px, px), px), :] - mean
-        return spread_sum + jnp.sum(mask * centered * centered, 0, keepdims=True)
-
-    squares = lax.fori_loop(0, z.n_group, second, zero, unroll=4)
-    spread(stats_ref, [count, mean, squares])
+    count, total, squares = lax.fori_loop(0, z.n_group, step, (zero, zero, zero), unroll=4)
+    offset = total / count
+    spread(stats_ref, [count, pivot + offset, jnp.maximum(squares - total * offset, 0.0)])
 
 
 def conv_into(z, product, y_ref, z_ref, sign=1, at_q=0):
@@ -214,21 +211,16 @@
 def first_conv(z, at, np_ref, *refs):
     xs, refs = refs[: z.Q], refs[z.Q :]
     blocks, refs = refs[: z.S], refs[z.S :]
-    z_ref, slice_ref, par_ref, hw_ref, stats_ref, far_w, far_x, wcat, y_ref, sem = refs
+    hw_ref, refs = refs[0], refs[1:]
+    z_ref, slice_ref, par_ref, stats_ref, far_w, far_x, wcat, y_ref, sem = refs
     fill_kernels(z, at, blocks, wcat)
     copies = [pltpu.make_async_copy(wcat, far_w, sem.at[0])]
     for m in range(z.Q):
         copies.append(
-            pltpu.make_async_copy(xs[m].at[: z.own, :], far_x.at[at[0] ^ m], sem.at[1 + m])
+            pltpu.make_async_copy(xs[m], far_x.at[at[0] ^ m], sem.at[1 + m])
         )
     for copy in copies:
         copy.start()
-    for m in range(z.Q):
-        j = at[0] ^ m
-        for n in range(z.n_own):
-            row = z.own + 2 * n
-            two = xs[m][row : row + 2, :LANES].astype(F32)
-            hw_ref[j * z.n_own + n] = jnp.concatenate([two, jnp.zeros((6, LANES), F32)], axis=0)
     for slot in range(z.Q):
 
         @pl.when(at[0] == slot)
@@ -237,11 +229,11 @@
             for m in range(z.Q):
                 j = slot ^ m
                 slice_ref[j * z.own : (j + 1) * z.own, :] = xs[m][
-                    : z.own, slot * z.L : (slot + 1) * z.L
+                    :, slot * z.L : (slot + 1) * z.L
                 ]
 
     def product(m):
-        return jnp.dot(xs[m][: z.own, :], wcat[...], preferred_element_type=F32)
+        return jnp.dot(xs[m][...], wcat[...], preferred_element_type=F32)
 
     conv_into(z, product, y_ref, z_ref, 1, at[0])
     local_stats(z, z_ref, hw_ref, stats_ref)
@@ -318,7 +310,9 @@
         lax.fori_loop(0, count, one, 0, unroll=2)
 
 
-def hidden(z, z_ref, all_ref, hw_ref, par_ref, a_ref, b_ref, sum_ref):
+def hidden(z, at, z_ref, all_ref, hw_ref, par_ref, *refs):
+    parts, (a_ref, b_ref, sum_ref, kernel_ref) = refs[: z.Q], refs[z.Q :]
+    unpick(z, at, *parts, kernel_ref)
     mean, inv, count = merged(z, all_ref)
     keep(sum_ref, [mean, inv, count])
     gain, shift = par_ref[0:1, :], par_ref[1:2, :]
@@ -477,6 +471,12 @@
                     theirs[(t - 1) * z.Q + r][k] = part.astype(BF16)
 
 
+def first_back(z, at, z_ref, up_ref, sum_ref, all_ref, hw_ref, par_ref, f_ref, *refs):
+    (a_ref, b_ref, par_grad_ref), refs = refs[:3], refs[3:]
+    norm_grad(z, 0, z_ref, up_ref, sum_ref, all_ref, hw_ref, par_ref, a_ref, b_ref, par_grad_ref)
+    kernel_grad(z, at, f_ref, a_ref, b_ref, *refs)
+
+
 def add_sharers(z, at, *refs):
     count = 1 + z.Q * (z.S - 1)
     mine_ref, others, refs = refs[0], refs[1:count], refs[count:]
@@ -520,33 +520,32 @@
     return new_first, new_second, move
 
 
-def moments(z, *refs):
-    parts = [refs[: z.Z], refs[z.Z : z.Z + 1]]
-    refs = refs[z.Z + 1 :]
-    w_ref, first_ref, second_ref, g1_ref, g2_ref, nf_ref, ns_ref, u_ref, stats_ref = refs
-    rows = []
-    weight_rows = []
-    for j in range(2):
-        total_u = jnp.zeros((1, z.L), F32)
-        total_w = jnp.zeros((1, z.L), F32)
-        for k in range(z.K):
-            grad = sum(part[k * z.IB : (k + 1) * z.IB, :].astype(F32) for part in parts[j])
-            w = w_ref[j, k]
-            nf, ns, u = direction_of(grad, first_ref[j, k], second_ref[j, k], w, DECAY)
-            nf_ref[j, k] = nf
-            ns_ref[j, k] = ns
-            u_ref[j, k] = u
-            total_u = total_u + jnp.sum(u * u, 0, keepdims=True)
-            total_w = total_w + jnp.sum(w * w, 0, keepdims=True)
-        rows.append(total_u)
-        weight_rows.append(total_w)
-    spread(
-        stats_ref,
-        rows + weight_rows + [g1_ref[0:1, :], g1_ref[1:2, :], g2_ref[0:1, :], g2_ref[1:2, :]],
-    )
-
-
-def finish(z, all_ref, w_ref, u_ref, np_ref, nf_ref, ns_ref, *outs):
+def moments(z, j, *refs):
+    count = len(refs) - (7 if j else 12)
+    parts, refs = refs[:count], refs[count:]
+    w_ref, first_ref, second_ref, refs = *refs[:3], refs[3:]
+    if j == 0:
+        other_ref, g1_ref, g2_ref, refs = refs[0], refs[1], refs[2], refs[5:]
+    nf_ref, ns_ref, u_ref, stats_ref = refs
+    total_u = jnp.zeros((1, z.L), F32)
+    total_w = jnp.zeros((1, z.L), F32)
+    for k in range(z.K):
+        grad = sum(part[k * z.IB : (k + 1) * z.IB, :].astype(F32) for part in parts)
+        w = w_ref[0, k]
+        nf, ns, u = direction_of(grad, first_ref[0, k], second_ref[0, k], w, DECAY)
+        nf_ref[0, k] = nf
+        ns_ref[0, k] = ns
+        u_ref[k] = u
+        total_u = total_u + jnp.sum(u * u, 0, keepdims=True)
+        total_w = total_w + jnp.sum(w * w, 0, keepdims=True)
+    if j:
+        keep(stats_ref, [total_u, total_w])
+    else:
+        grads = [g1_ref[0:1, :], g1_ref[1:2, :], g2_ref[0:1, :], g2_ref[1:2, :]]
+        spread(stats_ref, [total_u, other_ref[0:1, :], total_w, other_ref[1:2, :]] + grads)
+
+
+def finish(z, all_ref, w_ref, u0_ref, u1_ref, np_ref, nf_ref, ns_ref, *outs):
     nw_ref, copy_ref, nnp_ref, nnf_ref, nns_ref, trust_ref = outs
     total = all_ref[0]
     for k in range(1, z.R * z.Z):
@@ -559,7 +558,7 @@
         bottoms.append(un)
         scale = RATE * (wn / (un + TINY))
         for k in range(z.K):
-            new = w_ref[j, k] - scale * u_ref[j, k]
+            new = w_ref[j, k] - scale * (u0_ref, u1_ref)[j][k]
             nw_ref[j, k] = new
             copy_ref[j, k] = new.astype(BF16)
     for j in range(z.Q):
@@ -582,25 +581,19 @@
     trust_ref[...] = trust
 
 
-def extend(z, x_ref, valid_ref, out_ref):
-    rows = []
-    for n in range(z.n_own):
-        valid = valid_ref[n].astype(F32)
-        tall = jnp.sum(valid[:, 0:1], axis=0, keepdims=True)
-        wide = jnp.sum(valid[0:1, :], axis=1, keepdims=True)
-        rows += [tall, wide]
-    rows = [jnp.broadcast_to(r, (1, z.C)) for r in rows]
-    fill = z.extra - len(rows)
-    extra = jnp.concatenate(rows + [jnp.zeros((fill, z.C), F32)], axis=0).astype(BF16)
-    out_ref[: z.own, :] = x_ref[...]
-    out_ref[z.own :, :] = extra
-
-
 def pick(z, more, at, *refs):
     parts, refs = refs[: z.Z], refs[z.Z :]
     map_ref = None
     if more == "map":
-        map_ref, refs = refs[0], refs[1:]
+        map_ref, valid_ref, refs = refs[0], refs[1], refs[2:]
+        rows = []
+        for n in range(z.n_own):
+            valid = valid_ref[n].astype(F32)
+            tall = jnp.sum(valid[:, 0:1], axis=0, keepdims=True)
+            wide = jnp.sum(valid[0:1, :], axis=1, keepdims=True)
+            rows += [jnp.broadcast_to(tall, (1, z.L)), jnp.broadcast_to(wide, (1, z.L))]
+        rows.append(jnp.zeros((z.extra - len(rows), z.L), F32))
+        sizes = jnp.concatenate(rows, axis=0).astype(BF16)
     if more == "keep":
         far_ref, outs, (hold, sem) = refs[0], refs[1:-2], refs[-2:]
     else:
@@ -618,7 +611,9 @@
 
                 @pl.when((at[0] ^ m) == slot)
                 def _(m=m, slot=slot):
-                    outs[m][z.K * z.IB :, :] = map_ref[:, slot * z.L : (slot + 1) * z.L]
+                    outs[m][z.K * z.IB : z.K * z.IB + z.own, :] = map_ref[:, slot * z.L : (slot + 1) * z.L]
+
+            outs[m][z.K * z.IB + z.own :, :] = sizes
 
     if more == "keep":
         copy.wait()
@@ -631,7 +626,12 @@
         for k in range(z.K):
             refs[0][q, k] = parts[m][k * z.IB : (k + 1) * z.IB, :]
         if len(refs) > 1:
-            refs[1][pl.ds(pl.multiple_of(q * z.own, z.own), z.own), :] = parts[m][z.K * z.IB :, :]
+            start = z.K * z.IB
+            refs[1][pl.ds(pl.multiple_of(q * z.own, z.own), z.own), :] = parts[m][start : start + z.own, :]
+            for n in range(z.n_own):
+                row = start + z.own + 2 * n
+                two = jnp.broadcast_to(parts[m][row : row + 2, 0:1].astype(F32), (2, LANES))
+                refs[2][q * z.n_own + n] = jnp.concatenate([two, jnp.zeros((6, LANES), F32)], axis=0)
 
 
 def shards(z, images, masks, cotangent, weights, first, second, params, p_first, p_second):
@@ -676,25 +676,23 @@
 
     low_one, low_two = (weights[j].astype(BF16) for j in range(2))
     one = [over_z(low_one, m) for m in range(z.Z)]
-    x_sent = call(
-        functools.partial(extend, z),
-        near((z.sent, z.C), BF16),
-        (image_rows, masks),
-        far=(image_rows, masks),
-    )
-    xs = [over_q(x_sent, m) for m in range(z.Q)]
-    one, xs, low_two = together((one, xs, low_two))
+    xs = [over_q(image_rows, m) for m in range(z.Q)]
+    one, low_two = together((one, low_two))
     hold = pltpu.VMEM((z.Z, *piece), BF16)
     picked = call(
         functools.partial(pick, z, "map"),
-        [near((z.K * z.IB + rows, z.L), BF16)] * z.Q,
-        (at, *one, cot_rows),
+        [near((z.sent, z.L), BF16)] * z.Q,
+        (at, *one, cot_rows, masks),
         [hold],
-        far=(cot_rows,),
-    )
+    )
+    picked, xs = together((picked, xs))
     two = [over_z(low_two, m) for m in range(z.Z)]
     picked, two = together(([over_q(picked[m], m) for m in range(z.Q)], two))
-    front_one, cots = call(functools.partial(unpick, z), [blocks, near(GL, BF16)], (at, *picked))
+    front_one, cots, hw = call(
+        functools.partial(unpick, z),
+        [blocks, near(GL, BF16), near((z.n_group, 8, LANES))],
+        (at, *picked),
+    )
     keep = away((z.Z, *piece), BF16)
     keep_two, *picked = call(
         functools.partial(pick, z, "keep"),
@@ -705,32 +703,29 @@
     )
     w_far = away((z.C, z.K * z.LP), BF16)
     x_far = away((z.Q, rows, z.C), BF16)
-    z1, x_slice, slice_params, hw, stats, w_far, x_far = call(
+    z1, x_slice, slice_params, stats, w_far, x_far = call(
         functools.partial(first_conv, z),
         [
             near(GL),
             near(GL, BF16),
             near((4, z.L)),
-            near((z.n_group, 8, LANES)),
             stat,
             w_far,
             x_far,
         ],
-        (at, params, *xs, *share(front_one)),
+        (at, params, *xs, *share(front_one), hw),
         conv_scratch + [pltpu.SemaphoreType.DMA((1 + z.Q,))],
         limit=16,
         raw=(w_far, x_far),
     )
     stats, picked = together((stats, picked))
     stats, picked = together((sharers(stats), [over_q(picked[m], m) for m in range(z.Q)]))
-    ha, hb, sum_one = call(
+    ha, hb, sum_one, front_two = call(
         functools.partial(hidden, z),
-        [near(HL, BF16), near(HL, BF16), near((8, z.L))],
-        (z1, stats, hw, slice_params),
-    )
-    ha, hb, picked = together((ha, hb, picked))
+        [near(HL, BF16), near(HL, BF16), near((8, z.L)), blocks],
+        (at, z1, stats, hw, slice_params, *picked),
+    )
     hs = gather(ha, hb)
-    front_two = call(functools.partial(unpick, z), [blocks], (at, *picked))[0]
     h_far = away((z.Q, *GL), BF16)
     z2, stats, h_far = call(
         functools.partial(second_conv, z),
@@ -753,18 +748,10 @@
     da, db, keep_two = together((da, db, keep_two))
     dz2s = gather(da, db)
 
-    def kernel_gradient(feature, halves, **more):
-        mine, *theirs = call(
-            functools.partial(kernel_grad, z),
-            [near((z.Q, *piece))] + [near(piece, BF16)] * (z.Q * (z.S - 1)),
-            (at, feature, *halves),
-            grad_scratch,
-            limit=14,
-            cost=COST_GRAD,
-            far=(feature,),
-            **more,
-        )
-        return mine, [over_s(theirs[(t - 1) * z.Q + r], t) for t in range(1, z.S) for r in range(z.Q)]
+    gradient_shapes = [near((z.Q, *piece))] + [near(piece, BF16)] * (z.Q * (z.S - 1))
+
+    def to_sharers(theirs):
+        return [over_s(theirs[(t - 1) * z.Q + r], t) for t in range(1, z.S) for r in range(z.Q)]
 
     def add_up(mine, received, *value):
         more = rows if value else 0
@@ -780,7 +767,38 @@
     def along(parts):
         return [over_z(parts[m], m) for m in range(z.Z)]
 
-    parts_two = add_up(*kernel_gradient(h_far, (da, db)), out)
+    def update(j, parts, *more):
+        whole = pl.BlockSpec(memory_space=pltpu.VMEM)
+        block = pl.BlockSpec((1, *piece), lambda i: (j, 0, 0, 0))
+        held = pl.BlockSpec(memory_space=pl.ANY)
+        args = [pltpu.with_memory_space_constraint(v, pltpu.VMEM) for v in (*parts,)]
+        args += [weights, first, second]
+        specs = [whole] * len(parts) + [block] * 3
+        if more:
+            args += [pltpu.with_memory_space_constraint(v, pltpu.VMEM) for v in more[:3]] + list(more[3:])
+            specs += [whole] * 3 + [held] * 2
+        n = len(args)
+        return pl.pallas_call(
+            functools.partial(moments, z, j),
+            grid=(1,),
+            out_shape=[shape(weights.shape)] * 2
+            + [near(piece), near((8, z.L)) if j else near((z.R * z.Z, 8, LANES))],
+            in_specs=specs,
+            out_specs=[block, block, whole, whole],
+            input_output_aliases={} if j else {n - 2: 0, n - 1: 1},
+            compiler_params=pltpu.CompilerParams(vmem_limit_bytes=8 * 1024 * 1024),
+            cost_estimate=pl.CostEstimate(flops=1 if j else COST_GRAD, bytes_accessed=1, transcendentals=0),
+        )(*args)
+
+    mine, *theirs = call(
+        functools.partial(kernel_grad, z),
+        gradient_shapes,
+        (at, h_far, da, db),
+        grad_scratch,
+        limit=14,
+        cost=COST_GRAD,
+    )
+    parts_two = add_up(mine, to_sharers(theirs), out)
     da1, stats = call(
         functools.partial(hidden_grad, z),
         [near(GL), stat],
@@ -790,10 +808,13 @@
     )
     stats, parts_two = together((stats, parts_two))
     stats, parts_two = together((sharers(stats), by_plane(parts_two)))
-    da, db, grad_one = call(
-        functools.partial(norm_grad, z, 0),
-        [near(HL, BF16), near(HL, BF16), near((8, z.L))],
-        (z1, da1, sum_one, stats, hw, slice_params),
+    da, db, grad_one, mine, *theirs = call(
+        functools.partial(first_back, z),
+        [near(HL, BF16), near(HL, BF16), near((8, z.L))] + gradient_shapes,
+        (at, z1, da1, sum_one, stats, hw, slice_params, x_far),
+        grad_scratch,
+        limit=14,
+        cost=COST_GRAD,
     )
     flat = near((z.K * z.IB, z.L), BF16)
     hold = pltpu.VMEM((z.Z, z.K * z.IB, z.L), BF16)
@@ -804,7 +825,7 @@
         [pltpu.VMEM((z.Q, rows, z.L), BF16), hold],
         after=(da,),
     )
-    mine, received = kernel_gradient(x_far, (da, db))
+    received = to_sharers(theirs)
     parts_one = add_up(mine, received)
     parts_one, parts_two = by_plane(parts_one), along(parts_two)
     parts_one, parts_two = together((parts_one, parts_two))
@@ -821,21 +842,17 @@
     parts_one = call(functools.partial(route, z), [flat] * z.Z, (at, *parts_one), [hold], after=(dxs[0],))
     parts_one, dxs, parts_two = together((parts_one, dxs, parts_two))
     parts_one = along(parts_one)
-    total_two = call(functools.partial(total_of, z), shape((z.K * z.IB, z.L)), tuple(parts_two))
+    new_first, new_second, move_two, other = update(1, parts_two)
     dxs = [over_q(dxs[m], m) for m in range(z.Q)]
-    parts_one, dxs = together((parts_one, dxs))
-    new_first, new_second, move, stats = call(
-        functools.partial(moments, z),
-        [shape(weights.shape)] * 2 + [near(weights.shape), near((z.R * z.Z, 8, LANES))],
-        (*parts_one, total_two, weights, first, second, grad_one, grad_two),
-        far=(total_two,),
+    new_first, new_second, move_one, stats = update(
+        0, parts_one, other, grad_one, grad_two, new_first, new_second
     )
     stats = lax.all_to_all(stats, ("s", "q", "z"), 0, 0)
     dx = call(functools.partial(total_of, z), shape((rows, z.C), BF16), tuple(dxs))
     new_weights, copies, new_params, new_p_first, new_p_second, trust = call(
         functools.partial(finish, z),
         [shape(weights.shape), shape(weights.shape, BF16)] + [shape(params.shape)] * 3 + [shape((2, 6))],
-        (stats, weights, move, params, p_first, p_second),
+        (stats, weights, move_one, move_two, params, p_first, p_second),
     )
     return (
         values.reshape(images.shape),

time: 177 us -> 172 us (0.972)
  waiting for transfers between devices: 43.7 us -> 36.3 us
  starting transfers between devices: 63.4 us -> 67.9 us
  Pallas kernels: 31.9 us -> 29.2 us
    ppermute x12, waiting for transfers between devices: 22 us -> 16 us  [over_z(): return lax.ppermute(v, 'z', [(i, i ^ m) for i in range(z.Z)]) if m else v]
    ppermute x12, starting transfers between devices: 21.8 us -> 27.5 us  [over_z(): return lax.ppermute(v, 'z', [(i, i ^ m) for i in range(z.Z)]) if m else v]
    pallas_call x23 -> x18, Pallas kernels: 31.9 us -> 27.1 us  [call(): pl.pallas_call(run, out_shape=out_shape, in_specs=[pl.BlockSpec(memory_sp...]
    pallas_call x0 -> x2, Pallas kernels: none -> 2.11 us  [update(): pl.pallas_call(functools.partial(moments, z, j), grid=(1,), out_shape=[sh...]
  transfers between devices with their start and end apart: 54 -> 54, of which waited for: 24 -> 22; matrix products, arithmetic and copies ran while one was open for 0% -> 0% of each run, Pallas kernels for 7% -> 8%
where the time goes in v4:
time: 172 us; the launch traced here: 171 us
  starting transfers between devices  67.9 us (39%)
  waiting for transfers between devices  36.3 us (21%)
  blocking collectives  35 us (20%)
  Pallas kernels  29.2 us (17%)
    all_to_all x4, blocking collectives, sharers(): return lax.all_to_all(v, ('s', 'z'), 0, 0)  35 us
    ppermute x30, starting transfers between devices, over_q(): return lax.ppermute(v, 'q', [(i, i ^ m) for i in range(z.Q)]) if m else v  34.3 us
    ppermute x12, starting transfers between devices, over_z(): return lax.ppermute(v, 'z', [(i, i ^ m) for i in range(z.Z)]) if m else v  27.5 us
    pallas_call x18, Pallas kernels, call(): pl.pallas_call(run, out_shape=out_shape, in_specs=[pl.BlockSpec(memory_sp...  27.1 us
    ppermute x12, waiting for transfers between devices, over_z(): return lax.ppermute(v, 'z', [(i, i ^ m) for i in range(z.Z)]) if m else v  16 us
    ppermute x30, waiting for transfers between devices, over_q(): return lax.ppermute(v, 'q', [(i, i ^ m) for i in range(z.Q)]) if m else v  13.3 us
    all_to_all x1, waiting for transfers between devices, shards(): stats = lax.all_to_all(stats, ('s', 'q', 'z'), 0, 0)  6.37 us
    all_to_all x1, starting transfers between devices, shards(): stats = lax.all_to_all(stats, ('s', 'q', 'z'), 0, 0)  3.99 us
  transfers between devices with their start and end apart: 54, of which 22 were waited for; matrix products, arithmetic and copies ran while one was open for 0% of the time, Pallas kernels for 8%

profile of v4, /device:TPU:0, one launch (start us, length us, event | category | flops | bytes accessed | tf_op | source)
XLA Modules:
  0.0 171.3 jit_solution(14765824876339805886)
XLA Ops:
  0.7 1.2 convert.4
  1.9 5.1 %collective-permute-start.2 = (bf16[9,64,128]{2,1,0:T(8,128)(2,1)S(1)}, bf16[9,64,128]{2,1,0:T(8,128)(2,1)S(1)}, u32[]{:S(2)}, u32[]{:S(2)}) collective-permute-start(bf16[9,64,128]{2,1,0:T(8,128)(2,1)S(1)} %get-tuple-element.156.refs_1_), channel_id=1, source_target_pairs={{0,3},{1,2},{2,1},{3,0},{4,7},{5,6},{6,5},{7,4},{8,11},{9,10},{10,... | collective-permute-start | bytes 442376 | tf_op jit(solution)/shard_map/ppermute | solution.py:642
  7.0 2.4 %collective-permute-start.5 = (bf16[256,512]{1,0:T(8,128)(2,1)S(1)}, bf16[256,512]{1,0:T(8,128)(2,1)S(1)}, u32[]{:S(2)}, u32[]{:S(2)}) collective-permute-start(bf16[256,512]{1,0:T(8,128)(2,1)S(1)} %bitcast.13), channel_id=1, source_target_pairs={{0,24},{8,16},{16,8},{24,0},{1,25},{9,17},{17,9},{25,1},{2,26},{10... | collective-permute-start | bytes 786440 | tf_op jit(solution)/shard_map/ppermute | solution.py:651
  10.9 6.9 %collective-permute-start = (bf16[9,64,128]{2,1,0:T(8,128)(2,1)S(1)}, bf16[9,64,128]{2,1,0:T(8,128)(2,1)S(1)}, u32[]{:S(2)}, u32[]{:S(2)}) collective-permute-start(bf16[9,64,128]{2,1,0:T(8,128)(2,1)S(1)} %get-tuple-element.156.refs_1_), channel_id=1, source_target_pairs={{0,1},{1,0},{2,3},{3,2},{4,5},{5,4},{6,7},{7,6},{8,9},{9,8},{10,11... | collective-permute-start | bytes 442376 | tf_op jit(solution)/shard_map/ppermute | solution.py:642
  17.8 1.7 %collective-permute-done.1.refs_3_ = bf16[9,64,128]{2,1,0:T(8,128)(2,1)S(1)} collective-permute-done((bf16[9,64,128]{2,1,0:T(8,128)(2,1)S(1)}, bf16[9,64,128]{2,1,0:T(8,128)(2,1)S(1)}, u32[]{:S(2)}, u32[]{:S(2)}) %collective-permute-start.1) | collective-permute-done | bytes 147488 | tf_op jit(solution)/shard_map/ppermute | solution.py:642
  19.6 1.9 %collective-permute-done.refs_2_ = bf16[9,64,128]{2,1,0:T(8,128)(2,1)S(1)} collective-permute-done((bf16[9,64,128]{2,1,0:T(8,128)(2,1)S(1)}, bf16[9,64,128]{2,1,0:T(8,128)(2,1)S(1)}, u32[]{:S(2)}, u32[]{:S(2)}) %collective-permute-start) | collective-permute-done | bytes 147488 | tf_op jit(solution)/shard_map/ppermute | solution.py:642
  21.5 2.1 %collective-permute-start.11 = (bf16[9,64,128]{2,1,0:T(8,128)(2,1)S(1)}, bf16[9,64,128]{2,1,0:T(8,128)(2,1)S(1)}, u32[]{:S(2)}, u32[]{:S(2)}) collective-permute-start(bf16[9,64,128]{2,1,0:T(8,128)(2,1)S(1)} %get-tuple-element.181.refs_1_), channel_id=1, source_target_pairs={{0,3},{1,2},{2,1},{3,0},{4,7},{5,6},{6,5},{7,4},{8,11},{9,10},{10,... | collective-permute-start | bytes 442376 | tf_op jit(solution)/shard_map/ppermute | solution.py:642
  23.6 0.8 shard_map.168
  24.5 1.6 collective-permute-start.6
  26.1 1.5 collective-permute-start.7
  28.0 0.9 collective-permute-start.10
  28.9 3.5 %collective-permute-start.9 = (bf16[9,64,128]{2,1,0:T(8,128)(2,1)S(1)}, bf16[9,64,128]{2,1,0:T(8,128)(2,1)S(1)}, u32[]{:S(2)}, u32[]{:S(2)}) collective-permute-start(bf16[9,64,128]{2,1,0:T(8,128)(2,1)S(1)} %get-tuple-element.181.refs_1_), channel_id=1, source_target_pairs={{0,1},{1,0},{2,3},{3,2},{4,5},{5,4},{6,7},{7,6},{8,9},{9,8},{10,11... | collective-permute-start | bytes 442376 | tf_op jit(solution)/shard_map/ppermute | solution.py:642
  32.4 3.5 %collective-permute-done.10.refs_3_ = bf16[9,64,128]{2,1,0:T(8,128)(2,1)S(1)} collective-permute-done((bf16[9,64,128]{2,1,0:T(8,128)(2,1)S(1)}, bf16[9,64,128]{2,1,0:T(8,128)(2,1)S(1)}, u32[]{:S(2)}, u32[]{:S(2)}) %collective-permute-start.10) | collective-permute-done | bytes 147488 | tf_op jit(solution)/shard_map/ppermute | solution.py:642
  37.2 1.4 shard_map.171
  39.2 2.6 %shard_map.170 = (f32[1024,128]{1,0:T(8,128)S(1)}, bf16[1024,128]{1,0:T(8,128)(2,1)S(1)}, f32[4,128]{1,0:T(4,128)S(1)}, f32[8,8,128]{2,1,0:T(8,128)S(1)}, bf16[5...) custom-call(s32[3]{0:T(128)S(1)} %pad_add_fusion.refs_0_, f32[4,512]{1,0:T(4,128)S(1)} %copy-done.6, ...), custom_call_target="tpu_custom_call" | custom-call | flops 1 | bytes 1 | tf_op jit(solution)/shard_map/pallas_call | solution.py:68
  41.9 1.6 collective-permute-start.13
  43.4 1.5 collective-permute-start.14
  45.4 10.5 %all_to_all.25.refs_2_ = f32[8,8,128]{2,1,0:T(8,128)S(1)} all-to-all(f32[8,8,128]{2,1,0:T(8,128)S(1)} %get-tuple-element.189), channel_id=1, replica_groups=mesh['ha'=2,'wa'=4,'ba'=4] {'wa':(2)2,'ba'}, dimensions={0} | all-to-all | bytes 65536 | tf_op jit(solution)/shard_map/all_to_all | solution.py:648
  56.0 1.0 shard_map.172
  57.1 1.1 collective-permute-start.17
  58.2 1.9 %collective-permute-start.19 = (bf16[512,128]{1,0:T(8,128)(2,1)S(1)}, bf16[512,128]{1,0:T(8,128)(2,1)S(1)}, u32[]{:S(2)}, u32[]{:S(2)}) collective-permute-start(bf16[512,128]{1,0:T(8,128)(2,1)S(1)} %get-tuple-element.201.refs_5_), channel_id=1, source_target_pairs={{0,8},{8,0},{16,24},{24,16},{1,9},{9,1},{17,25},{25,17},{2,10},{10... | collective-permute-start | bytes 393224 | tf_op jit(solution)/shard_map/ppermute | solution.py:651
  60.3 1.0 collective-permute-start.20
  61.2 2.0 %collective-permute-done.17.refs_3_ = bf16[512,128]{1,0:T(8,128)(2,1)S(1)} collective-permute-done((bf16[512,128]{1,0:T(8,128)(2,1)S(1)}, bf16[512,128]{1,0:T(8,128)(2,1)S(1)}, u32[]{:S(2)}, u32[]{:S(2)}) %collective-permute-start.17) | collective-permute-done | bytes 131104 | tf_op jit(solution)/shard_map/ppermute | solution.py:651
  63.2 1.0 collective-permute-start.18
  64.6 1.9 %collective-permute-start.21 = (bf16[512,128]{1,0:T(8,128)(2,1)S(1)}, bf16[512,128]{1,0:T(8,128)(2,1)S(1)}, u32[]{:S(2)}, u32[]{:S(2)}) collective-permute-start(bf16[512,128]{1,0:T(8,128)(2,1)S(1)} %collective-permute-done.19.refs_6_), channel_id=1, source_target_pairs={{0,16},{8,24},{16,0},{24,8},{1,17},{9,25},{17,1},{25,9},{2,18},{10... | collective-permute-start | bytes 393224 | tf_op jit(solution)/shard_map/ppermute | solution.py:651
  66.5 0.9 collective-permute-done.16.refs_2_
  67.4 2.2 %collective-permute-done.18.refs_4_ = bf16[512,128]{1,0:T(8,128)(2,1)S(1)} collective-permute-done((bf16[512,128]{1,0:T(8,128)(2,1)S(1)}, bf16[512,128]{1,0:T(8,128)(2,1)S(1)}, u32[]{:S(2)}, u32[]{:S(2)}) %collective-permute-start.18) | collective-permute-done | bytes 131104 | tf_op jit(solution)/shard_map/ppermute | solution.py:651
  69.6 2.6 %shard_map.173 = (f32[1024,128]{1,0:T(8,128)S(1)}, f32[8,8,128]{2,1,0:T(8,128)S(1)}, bf16[4,1024,128]{2,1,0:T(8,128)(2,1)}) custom-call(s32[3]{0:T(128)S(1)} %pad_add_fusion.refs_0_, bf16[512,128]{1,0:T(8,128)(2,1)S(1)} %get-tuple-element.200.refs_1_, bf16[512,128]{1,0:T(8,128)(2,1)S(1)} %collective-permute-done.16.refs_2_, ...), custom_call_target="tpu_custom_call" | custom-call | flops 1 | bytes 1 | tf_op jit(solution)/shard_map/pallas_call | solution.py:68
  72.1 8.1 %all_to_all.26.refs_2_ = f32[8,8,128]{2,1,0:T(8,128)S(1)} all-to-all(f32[8,8,128]{2,1,0:T(8,128)S(1)} %get-tuple-element.204), channel_id=1, replica_groups=mesh['ha'=2,'wa'=4,'ba'=4] {'wa':(2)2,'ba'}, dimensions={0} | all-to-all | bytes 65536 | tf_op jit(solution)/shard_map/all_to_all | solution.py:648
  80.3 1.3 shard_map.174
  81.6 8.1 %all_to_all.27.refs_3_ = f32[8,8,128]{2,1,0:T(8,128)S(1)} all-to-all(f32[8,8,128]{2,1,0:T(8,128)S(1)} %get-tuple-element.209), channel_id=1, replica_groups=mesh['ha'=2,'wa'=4,'ba'=4] {'wa':(2)2,'ba'}, dimensions={0} | all-to-all | bytes 65536 | tf_op jit(solution)/shard_map/all_to_all | solution.py:648
  90.2 2.0 %collective-permute-start.24 = (bf16[512,128]{1,0:T(8,128)(2,1)S(1)}, bf16[512,128]{1,0:T(8,128)(2,1)S(1)}, u32[]{:S(2)}, u32[]{:S(2)}) collective-permute-start(bf16[512,128]{1,0:T(8,128)(2,1)S(1)} %get-tuple-element.213.refs_1_.refs_2_), channel_id=1, source_target_pairs={{0,16},{8,24},{16,0},{24,8},{1,17},{9,25},{17,1},{25,9},{2,18},{10... | collective-permute-start | bytes 393224 | tf_op jit(solution)/shard_map/ppermute | solution.py:651
  92.3 2.4 %shard_map.177 = (f32[4,9,64,128]{3,2,1,0:T(8,128)S(1)}, bf16[9,64,128]{2,1,0:T(8,128)(2,1)S(1)}, bf16[9,64,128]{2,1,0:T(8,128)(2,1)S(1)}, bf16[9,64,128]{2,1,0:T(8,128)(2,1)S(1)}, bf16[9,64,128]{2,1,0:T(8,128)(2,1)S(1)}) custom-call(s32[3]{0:T(128)S(1)} %pad_add_fusion.refs_0_, bf16[4,1024,128]{2,1,0:T(8,128)(2,1)S(1)} %copy-done.11, ...), custom_call_target="tpu_custom_call" | custom-call | flops 3000000000 | bytes 1 | tf_op jit(solution)/shard_map/pallas_call | solution.py:68
  95.2 0.9 collective-permute-done.24.refs_3_
  96.2 1.5 collective-permute-done.26.refs_6_
  97.6 0.8 collective-permute-start.23
  98.5 1.2 collective-permute-start.27
  99.7 0.8 collective-permute-start.25
  100.5 1.2 collective-permute-start.28
  102.4 1.6 collective-permute-done.23.refs_2_
  103.9 0.9 collective-permute-done.27.refs_7_
  104.9 1.5 collective-permute-done.25.refs_4_
  106.5 3.0 %shard_map.176 = (f32[1024,128]{1,0:T(8,128)S(1)}, f32[8,8,128]{2,1,0:T(8,128)S(1)}) custom-call(s32[3]{0:T(128)S(1)} %pad_add_fusion.refs_0_, bf16[512,128]{1,0:T(8,128)(2,1)S(1)} %get-tuple-element.213.refs_1_.refs_2_, bf16[512,128]{1,0:T(8,128)(2,1)S(1)} %collective-permute-done.23.refs_2_, bf16[512,128]{1,0:T(8,128)(2,1)S(1)} %collective-permute-done.24.refs_3_, ...), custom_call_target="tpu_custom_call" | custom-call | flops 1 | bytes 1 | tf_op jit(solution)/shard_map/pallas_call | solution.py:68
  109.5 1.7 collective-permute-start.34
  111.6 1.5 collective-permute-start.36
  113.1 8.1 %all_to_all.28.refs_4_ = f32[8,8,128]{2,1,0:T(8,128)S(1)} all-to-all(f32[8,8,128]{2,1,0:T(8,128)S(1)} %get-tuple-element.229), channel_id=1, replica_groups=mesh['ha'=2,'wa'=4,'ba'=4] {'wa':(2)2,'ba'}, dimensions={0} | all-to-all | bytes 65536 | tf_op jit(solution)/shard_map/all_to_all | solution.py:648
  121.2 0.9 collective-permute-done.36.refs_4_
  122.1 2.6 %shard_map.179 = (bf16[512,128]{1,0:T(8,128)(2,1)S(1)}, bf16[512,128]{1,0:T(8,128)(2,1)S(1)}, f32[8,128]{1,0:T(8,128)S(1)}, f32[4,9,64,128]{3,2,1,0:T(8,128)S(1)...) custom-call(s32[3]{0:T(128)S(1)} %pad_add_fusion.refs_0_, ...), custom_call_target="tpu_custom_call" | custom-call | flops 3000000000 | bytes 1 | tf_op jit(solution)/shard_map/pallas_call | solution.py:68
  127.7 3.3 %collective-permute-start.46 = (bf16[576,128]{1,0:T(8,128)(2,1)S(1)}, bf16[576,128]{1,0:T(8,128)(2,1)S(1)}, u32[]{:S(2)}, u32[]{:S(2)}) collective-permute-start(bf16[576,128]{1,0:T(8,128)(2,1)S(1)} %get-tuple-element.255), channel_id=1, source_target_pairs={{0,3},{1,2},{2,1},{3,0},{4,7},{5,6},{6,5},{7,4},{8,11},{9,10},{10,... | collective-permute-start | bytes 442376 | tf_op jit(solution)/shard_map/ppermute | solution.py:642
  131.7 1.5 collective-permute-start.41
  134.4 1.4 collective-permute-start.43
  135.8 3.8 %shard_map.182 = (f32[256,512]{1,0:T(8,128)S(1)}, bf16[256,512]{1,0:T(8,128)(2,1)}, bf16[256,512]{1,0:T(8,128)(2,1)S(1)}, bf16[256,512]{1,0:T(8,128)(2,1)S(1)}) custom-call(s32[3]{0:T(128)S(1)} %pad_add_fusion.refs_0_, bf16[512,128]{1,0:T(8,128)(2,1)S(1)} %get-tuple-element.241.refs_5_.refs_1_, bf16[512,128]{1,0:T(8,128)(2,1)S(1)} %get-tuple-element.260.refs_2_, ...), custom_call_target="tpu_custom_call" | custom-call | flops 3000000000 | bytes 1 | tf_op jit(solution)/shard_map/pallas_call | solution.py:68
  139.6 1.3 collective-permute-done.45.refs_2_
  142.2 2.2 %collective-permute-start.50 = (bf16[576,128]{1,0:T(8,128)(2,1)S(1)}, bf16[576,128]{1,0:T(8,128)(2,1)S(1)}, u32[]{:S(2)}, u32[]{:S(2)}) collective-permute-start(bf16[576,128]{1,0:T(8,128)(2,1)S(1)} %get-tuple-element.279), channel_id=1, source_target_pairs={{0,1},{1,0},{2,3},{3,2},{4,5},{5,4},{6,7},{7,6},{8,9},{9,8},{10,11... | collective-permute-start | bytes 442376 | tf_op jit(solution)/shard_map/ppermute | solution.py:642
  144.3 2.4 %collective-permute-start.52 = (bf16[576,128]{1,0:T(8,128)(2,1)S(1)}, bf16[576,128]{1,0:T(8,128)(2,1)S(1)}, u32[]{:S(2)}, u32[]{:S(2)}) collective-permute-start(bf16[576,128]{1,0:T(8,128)(2,1)S(1)} %get-tuple-element.281), channel_id=1, source_target_pairs={{0,3},{1,2},{2,1},{3,0},{4,7},{5,6},{6,5},{7,4},{8,11},{9,10},{10,... | collective-permute-start | bytes 442376 | tf_op jit(solution)/shard_map/ppermute | solution.py:642
  146.8 1.4 collective-permute-start.47
  148.9 1.0 shard_map.185
  149.8 1.4 collective-permute-start.49
  151.3 5.8 %collective-permute-done.51.refs_2_ = bf16[576,128]{1,0:T(8,128)(2,1)S(1)} collective-permute-done((bf16[576,128]{1,0:T(8,128)(2,1)S(1)}, bf16[576,128]{1,0:T(8,128)(2,1)S(1)}, u32[]{:S(2)}, u32[]{:S(2)}) %collective-permute-start.51) | collective-permute-done | bytes 147488 | tf_op jit(solution)/shard_map/ppermute | solution.py:642
  157.1 1.1 shard_map.186
  158.2 4.0 %all-to-all-start.4 = ((f32[32,8,128]{2,1,0:T(8,128)}), f32[32,8,128]{2,1,0:T(8,128)S(1)}, u32[]{:S(2)}, u32[]{:S(2)}) async-start(f32[32,8,128]{2,1,0:T(8,128)} %get-tuple-element.291), calls=%async_computation.4 | async-start | bytes 262144 | tf_op jit(solution)/shard_map/all_to_all | solution.py:850
  163.0 0.8 shard_map.184
  163.8 6.4 %all-to-all-done.4.refs_0_ = f32[32,8,128]{2,1,0:T(8,128)S(1)} async-done(((f32[32,8,128]{2,1,0:T(8,128)}), f32[32,8,128]{2,1,0:T(8,128)S(1)}, u32[]{:S(2)}, u32[]{:S(2)}) %all-to-all-start.4) | async-done | bytes 131104 | tf_op jit(solution)/shard_map/all_to_all | solution.py:850
  170.2 1.1 shard_map.187
  (96 shorter events, 14.9 us)
Async XLA Ops:
  0.7 23.0 %copy-start.4 = (bf16[4,8,8,512]{3,2,1,0:T(8,128)(2,1)S(1)}, bf16[4,8,8,512]{3,2,1,0:T(8,128)(2,1)}, u32[]{:S(2)}) copy-start(bf16[4,8,8,512]{3,2,1,0:T(8,128)(2,1)} %param.11) | copy-start | bytes 786436
  0.7 23.0 %copy-start.7 = (s32[4,8,8]{2,1,0:T(8,128)S(1)}, s32[4,8,8]{2,1,0:T(8,128)}, u32[]{:S(2)}) copy-start(s32[4,8,8]{2,1,0:T(8,128)} %refs_6_.4) | copy-start | bytes 3076
  1.9 9.1 %collective-permute-start.2 = (bf16[9,64,128]{2,1,0:T(8,128)(2,1)S(1)}, bf16[9,64,128]{2,1,0:T(8,128)(2,1)S(1)}, u32[]{:S(2)}, u32[]{:S(2)}) collective-permute-start(bf16[9,64,128]{2,1,0:T(8,128)(2,1)S(1)} %get-tuple-element.156.refs_1_), channel_id=1, source_target_pairs={{0,3},{1,2},{2,1},{3,0},{4,7},{5,6},{6,5},{7,4},{8,11},{9,10},{10,... | collective-permute-start | bytes 442376 | tf_op jit(solution)/shard_map/ppermute | solution.py:642
  7.0 17.4 %collective-permute-start.5 = (bf16[256,512]{1,0:T(8,128)(2,1)S(1)}, bf16[256,512]{1,0:T(8,128)(2,1)S(1)}, u32[]{:S(2)}, u32[]{:S(2)}) collective-permute-start(bf16[256,512]{1,0:T(8,128)(2,1)S(1)} %bitcast.13), channel_id=1, source_target_pairs={{0,24},{8,16},{16,8},{24,0},{1,25},{9,17},{17,9},{25,1},{2,26},{10... | collective-permute-start | bytes 786440 | tf_op jit(solution)/shard_map/ppermute | solution.py:651
  9.4 15.0 %collective-permute-start.4 = (bf16[256,512]{1,0:T(8,128)(2,1)S(1)}, bf16[256,512]{1,0:T(8,128)(2,1)S(1)}, u32[]{:S(2)}, u32[]{:S(2)}) collective-permute-start(bf16[256,512]{1,0:T(8,128)(2,1)S(1)} %bitcast.14), channel_id=1, source_target_pairs={{0,16},{8,24},{16,0},{24,8},{1,17},{9,25},{17,1},{25,9},{2,18},{10... | collective-permute-start | bytes 786440 | tf_op jit(solution)/shard_map/ppermute | solution.py:651
  10.0 14.5 %collective-permute-start.3 = (bf16[256,512]{1,0:T(8,128)(2,1)S(1)}, bf16[256,512]{1,0:T(8,128)(2,1)S(1)}, u32[]{:S(2)}, u32[]{:S(2)}) collective-permute-start(bf16[256,512]{1,0:T(8,128)(2,1)S(1)} %bitcast.15), channel_id=1, source_target_pairs={{0,8},{8,0},{16,24},{24,16},{1,9},{9,1},{17,25},{25,17},{2,10},{10... | collective-permute-start | bytes 786440 | tf_op jit(solution)/shard_map/ppermute | solution.py:651
  10.5 9.1 %collective-permute-start.1 = (bf16[9,64,128]{2,1,0:T(8,128)(2,1)S(1)}, bf16[9,64,128]{2,1,0:T(8,128)(2,1)S(1)}, u32[]{:S(2)}, u32[]{:S(2)}) collective-permute-start(bf16[9,64,128]{2,1,0:T(8,128)(2,1)S(1)} %get-tuple-element.156.refs_1_), channel_id=1, source_target_pairs={{0,2},{1,3},{2,0},{3,1},{4,6},{5,7},{6,4},{7,5},{8,10},{9,11},{10,... | collective-permute-start | bytes 442376 | tf_op jit(solution)/shard_map/ppermute | solution.py:642
  10.9 10.5 %collective-permute-start = (bf16[9,64,128]{2,1,0:T(8,128)(2,1)S(1)}, bf16[9,64,128]{2,1,0:T(8,128)(2,1)S(1)}, u32[]{:S(2)}, u32[]{:S(2)}) collective-permute-start(bf16[9,64,128]{2,1,0:T(8,128)(2,1)S(1)} %get-tuple-element.156.refs_1_), channel_id=1, source_target_pairs={{0,1},{1,0},{2,3},{3,2},{4,5},{5,4},{6,7},{7,6},{8,9},{9,8},{10,11... | collective-permute-start | bytes 442376 | tf_op jit(solution)/shard_map/ppermute | solution.py:642
  17.8 21.4 %copy-start.6 = (f32[4,512]{1,0:T(4,128)S(1)}, f32[4,512]{1,0:T(4,128)}, u32[]{:S(2)}) copy-start(f32[4,512]{1,0:T(4,128)} %refs_4_.5) | copy-start | bytes 24580
  21.5 7.4 %collective-permute-start.11 = (bf16[9,64,128]{2,1,0:T(8,128)(2,1)S(1)}, bf16[9,64,128]{2,1,0:T(8,128)(2,1)S(1)}, u32[]{:S(2)}, u32[]{:S(2)}) collective-permute-start(bf16[9,64,128]{2,1,0:T(8,128)(2,1)S(1)} %get-tuple-element.181.refs_1_), channel_id=1, source_target_pairs={{0,3},{1,2},{2,1},{3,0},{4,7},{5,6},{6,5},{7,4},{8,11},{9,10},{10,... | collective-permute-start | bytes 442376 | tf_op jit(solution)/shard_map/ppermute | solution.py:642
  24.5 12.0 %collective-permute-start.6 = (bf16[848,128]{1,0:T(8,128)(2,1)S(1)}, bf16[848,128]{1,0:T(8,128)(2,1)S(1)}, u32[]{:S(2)}, u32[]{:S(2)}) collective-permute-start(bf16[848,128]{1,0:T(8,128)(2,1)S(1)} %get-tuple-element.169), channel_id=1, source_target_pairs={{0,8},{8,0},{16,24},{24,16},{1,9},{9,1},{17,25},{25,17},{2,10},{10... | collective-permute-start | bytes 651272 | tf_op jit(solution)/shard_map/ppermute | solution.py:651
  26.1 10.4 %collective-permute-start.7 = (bf16[848,128]{1,0:T(8,128)(2,1)S(1)}, bf16[848,128]{1,0:T(8,128)(2,1)S(1)}, u32[]{:S(2)}, u32[]{:S(2)}) collective-permute-start(bf16[848,128]{1,0:T(8,128)(2,1)S(1)} %get-tuple-element.170), channel_id=1, source_target_pairs={{0,16},{8,24},{16,0},{24,8},{1,17},{9,25},{17,1},{25,9},{2,18},{10... | collective-permute-start | bytes 651272 | tf_op jit(solution)/shard_map/ppermute | solution.py:651
  27.6 9.0 %collective-permute-start.8 = (bf16[848,128]{1,0:T(8,128)(2,1)S(1)}, bf16[848,128]{1,0:T(8,128)(2,1)S(1)}, u32[]{:S(2)}, u32[]{:S(2)}) collective-permute-start(bf16[848,128]{1,0:T(8,128)(2,1)S(1)} %get-tuple-element.171), channel_id=1, source_target_pairs={{0,24},{8,16},{16,8},{24,0},{1,25},{9,17},{17,9},{25,1},{2,26},{10... | collective-permute-start | bytes 651272 | tf_op jit(solution)/shard_map/ppermute | solution.py:651
  28.0 7.8 %collective-permute-start.10 = (bf16[9,64,128]{2,1,0:T(8,128)(2,1)S(1)}, bf16[9,64,128]{2,1,0:T(8,128)(2,1)S(1)}, u32[]{:S(2)}, u32[]{:S(2)}) collective-permute-start(bf16[9,64,128]{2,1,0:T(8,128)(2,1)S(1)} %get-tuple-element.181.refs_1_), channel_id=1, source_target_pairs={{0,2},{1,3},{2,0},{3,1},{4,6},{5,7},{6,4},{7,5},{8,10},{9,11},{10,... | collective-permute-start | bytes 442376 | tf_op jit(solution)/shard_map/ppermute | solution.py:642
  28.9 7.6 %collective-permute-start.9 = (bf16[9,64,128]{2,1,0:T(8,128)(2,1)S(1)}, bf16[9,64,128]{2,1,0:T(8,128)(2,1)S(1)}, u32[]{:S(2)}, u32[]{:S(2)}) collective-permute-start(bf16[9,64,128]{2,1,0:T(8,128)(2,1)S(1)} %get-tuple-element.181.refs_1_), channel_id=1, source_target_pairs={{0,1},{1,0},{2,3},{3,2},{4,5},{5,4},{6,7},{7,6},{8,9},{9,8},{10,11... | collective-permute-start | bytes 442376 | tf_op jit(solution)/shard_map/ppermute | solution.py:642
  37.1 2.1 %collective-permute-start.12 = (bf16[4,9,64,128]{3,2,1,0:T(8,128)(2,1)S(1)}, bf16[4,9,64,128]{3,2,1,0:T(8,128)(2,1)S(1)}, u32[]{:S(2)}, u32[]{:S(2)}) collective-permute-start(bf16[4,9,64,128]{3,2,1,0:T(8,128)(2,1)S(1)} %get-tuple-element.177.refs_6_), channel_id=1, source_target_pairs={{0,4},{4,0},{1,5},{5,1},{2,6},{6,2},{3,7},{7,3},{8,12},{12,8},{9,1... | collective-permute-start | bytes 1769480 | tf_op jit(solution)/shard_map/ppermute | solution.py:645
  41.9 14.1 %collective-permute-start.13 = (bf16[576,128]{1,0:T(8,128)(2,1)S(1)}, bf16[576,128]{1,0:T(8,128)(2,1)S(1)}, u32[]{:S(2)}, u32[]{:S(2)}) collective-permute-start(bf16[576,128]{1,0:T(8,128)(2,1)S(1)} %get-tuple-element.191), channel_id=1, source_target_pairs={{0,8},{8,0},{16,24},{24,16},{1,9},{9,1},{17,25},{25,17},{2,10},{10... | collective-permute-start | bytes 442376 | tf_op jit(solution)/shard_map/ppermute | solution.py:651
  43.4 12.5 %collective-permute-start.14 = (bf16[576,128]{1,0:T(8,128)(2,1)S(1)}, bf16[576,128]{1,0:T(8,128)(2,1)S(1)}, u32[]{:S(2)}, u32[]{:S(2)}) collective-permute-start(bf16[576,128]{1,0:T(8,128)(2,1)S(1)} %get-tuple-element.192), channel_id=1, source_target_pairs={{0,16},{8,24},{16,0},{24,8},{1,17},{9,25},{17,1},{25,9},{2,18},{10... | collective-permute-start | bytes 442376 | tf_op jit(solution)/shard_map/ppermute | solution.py:651
  44.9 11.0 %collective-permute-start.15 = (bf16[576,128]{1,0:T(8,128)(2,1)S(1)}, bf16[576,128]{1,0:T(8,128)(2,1)S(1)}, u32[]{:S(2)}, u32[]{:S(2)}) collective-permute-start(bf16[576,128]{1,0:T(8,128)(2,1)S(1)} %get-tuple-element.193), channel_id=1, source_target_pairs={{0,24},{8,16},{16,8},{24,0},{1,25},{9,17},{17,9},{25,1},{2,26},{10... | collective-permute-start | bytes 442376 | tf_op jit(solution)/shard_map/ppermute | solution.py:651
  57.0 12.6 %collective-permute-start.22 = (bf16[4,9,64,128]{3,2,1,0:T(8,128)(2,1)S(1)}, bf16[4,9,64,128]{3,2,1,0:T(8,128)(2,1)S(1)}, u32[]{:S(2)}, u32[]{:S(2)}) collective-permute-start(bf16[4,9,64,128]{3,2,1,0:T(8,128)(2,1)S(1)} %get-tuple-element.202.refs_9_), channel_id=1, source_target_pairs={{0,4},{4,0},{1,5},{5,1},{2,6},{6,2},{3,7},{7,3},{8,12},{12,8},{9,1... | collective-permute-start | bytes 1769480 | tf_op jit(solution)/shard_map/ppermute | solution.py:645
  57.1 6.0 %collective-permute-start.17 = (bf16[512,128]{1,0:T(8,128)(2,1)S(1)}, bf16[512,128]{1,0:T(8,128)(2,1)S(1)}, u32[]{:S(2)}, u32[]{:S(2)}) collective-permute-start(bf16[512,128]{1,0:T(8,128)(2,1)S(1)} %get-tuple-element.200.refs_1_), channel_id=1, source_target_pairs={{0,16},{8,24},{16,0},{24,8},{1,17},{9,25},{17,1},{25,9},{2,18},{10... | collective-permute-start | bytes 393224 | tf_op jit(solution)/shard_map/ppermute | solution.py:651
  58.2 6.3 %collective-permute-start.19 = (bf16[512,128]{1,0:T(8,128)(2,1)S(1)}, bf16[512,128]{1,0:T(8,128)(2,1)S(1)}, u32[]{:S(2)}, u32[]{:S(2)}) collective-permute-start(bf16[512,128]{1,0:T(8,128)(2,1)S(1)} %get-tuple-element.201.refs_5_), channel_id=1, source_target_pairs={{0,8},{8,0},{16,24},{24,16},{1,9},{9,1},{17,25},{25,17},{2,10},{10... | collective-permute-start | bytes 393224 | tf_op jit(solution)/shard_map/ppermute | solution.py:651
  60.2 7.2 %collective-permute-start.16 = (bf16[512,128]{1,0:T(8,128)(2,1)S(1)}, bf16[512,128]{1,0:T(8,128)(2,1)S(1)}, u32[]{:S(2)}, u32[]{:S(2)}) collective-permute-start(bf16[512,128]{1,0:T(8,128)(2,1)S(1)} %get-tuple-element.200.refs_1_), channel_id=1, source_target_pairs={{0,8},{8,0},{16,24},{24,16},{1,9},{9,1},{17,25},{25,17},{2,10},{10... | collective-permute-start | bytes 393224 | tf_op jit(solution)/shard_map/ppermute | solution.py:651
  60.3 7.1 %collective-permute-start.20 = (bf16[512,128]{1,0:T(8,128)(2,1)S(1)}, bf16[512,128]{1,0:T(8,128)(2,1)S(1)}, u32[]{:S(2)}, u32[]{:S(2)}) collective-permute-start(bf16[512,128]{1,0:T(8,128)(2,1)S(1)} %get-tuple-element.201.refs_5_), channel_id=1, source_target_pairs={{0,16},{8,24},{16,0},{24,8},{1,17},{9,25},{17,1},{25,9},{2,18},{10... | collective-permute-start | bytes 393224 | tf_op jit(solution)/shard_map/ppermute | solution.py:651
  63.2 6.4 %collective-permute-start.18 = (bf16[512,128]{1,0:T(8,128)(2,1)S(1)}, bf16[512,128]{1,0:T(8,128)(2,1)S(1)}, u32[]{:S(2)}, u32[]{:S(2)}) collective-permute-start(bf16[512,128]{1,0:T(8,128)(2,1)S(1)} %collective-permute-done.17.refs_3_), channel_id=1, source_target_pairs={{0,8},{8,0},{16,24},{24,16},{1,9},{9,1},{17,25},{25,17},{2,10},{10... | collective-permute-start | bytes 393224 | tf_op jit(solution)/shard_map/ppermute | solution.py:651
  64.6 5.0 %collective-permute-start.21 = (bf16[512,128]{1,0:T(8,128)(2,1)S(1)}, bf16[512,128]{1,0:T(8,128)(2,1)S(1)}, u32[]{:S(2)}, u32[]{:S(2)}) collective-permute-start(bf16[512,128]{1,0:T(8,128)(2,1)S(1)} %collective-permute-done.19.refs_6_), channel_id=1, source_target_pairs={{0,16},{8,24},{16,0},{24,8},{1,17},{9,25},{17,1},{25,9},{2,18},{10... | collective-permute-start | bytes 393224 | tf_op jit(solution)/shard_map/ppermute | solution.py:651
  80.3 9.7 %copy-start.3 = (bf16[4,9,64,128]{3,2,1,0:T(8,128)(2,1)S(1)}, bf16[4,9,64,128]{3,2,1,0:T(8,128)(2,1)}, u32[]{:S(2)}) copy-start(bf16[4,9,64,128]{3,2,1,0:T(8,128)(2,1)} %get-tuple-element.215.refs_9_) | copy-start | bytes 1769476
  80.3 12.0 %copy-start.11 = (bf16[4,1024,128]{2,1,0:T(8,128)(2,1)S(1)}, bf16[4,1024,128]{2,1,0:T(8,128)(2,1)}, u32[]{:S(2)}) copy-start(bf16[4,1024,128]{2,1,0:T(8,128)(2,1)} %get-tuple-element.218.refs_1_) | copy-start | bytes 3145732
  90.0 16.5 %collective-permute-start.29 = (bf16[4,9,64,128]{3,2,1,0:T(8,128)(2,1)S(1)}, bf16[4,9,64,128]{3,2,1,0:T(8,128)(2,1)S(1)}, u32[]{:S(2)}, u32[]{:S(2)}) collective-permute-start(bf16[4,9,64,128]{3,2,1,0:T(8,128)(2,1)S(1)} %copy-done.3), channel_id=1, source_target_pairs={{0,4},{4,0},{1,5},{5,1},{2,6},{6,2},{3,7},{7,3},{8,12},{12,8},{9,1... | collective-permute-start | bytes 1769480 | tf_op jit(solution)/shard_map/ppermute | solution.py:645
  90.2 6.0 %collective-permute-start.24 = (bf16[512,128]{1,0:T(8,128)(2,1)S(1)}, bf16[512,128]{1,0:T(8,128)(2,1)S(1)}, u32[]{:S(2)}, u32[]{:S(2)}) collective-permute-start(bf16[512,128]{1,0:T(8,128)(2,1)S(1)} %get-tuple-element.213.refs_1_.refs_2_), channel_id=1, source_target_pairs={{0,16},{8,24},{16,0},{24,8},{1,17},{9,25},{17,1},{25,9},{2,18},{10... | collective-permute-start | bytes 393224 | tf_op jit(solution)/shard_map/ppermute | solution.py:651
  92.1 5.5 %collective-permute-start.26 = (bf16[512,128]{1,0:T(8,128)(2,1)S(1)}, bf16[512,128]{1,0:T(8,128)(2,1)S(1)}, u32[]{:S(2)}, u32[]{:S(2)}) collective-permute-start(bf16[512,128]{1,0:T(8,128)(2,1)S(1)} %get-tuple-element.214.refs_5_.refs_3_), channel_id=1, source_target_pairs={{0,8},{8,0},{16,24},{24,16},{1,9},{9,1},{17,25},{25,17},{2,10},{10... | collective-permute-start | bytes 393224 | tf_op jit(solution)/shard_map/ppermute | solution.py:651
  94.7 3.0 %collective-permute-start.30 = (bf16[9,64,128]{2,1,0:T(8,128)(2,1)S(1)}, bf16[9,64,128]{2,1,0:T(8,128)(2,1)S(1)}, u32[]{:S(2)}, u32[]{:S(2)}) collective-permute-start(bf16[9,64,128]{2,1,0:T(8,128)(2,1)S(1)} %get-tuple-element.220), channel_id=1, source_target_pairs={{0,4},{4,0},{1,5},{5,1},{2,6},{6,2},{3,7},{7,3},{8,12},{12,8},{9,1... | collective-permute-start | bytes 442376 | tf_op jit(solution)/shard_map/ppermute | solution.py:645
  94.7 3.7 %collective-permute-start.31 = (bf16[9,64,128]{2,1,0:T(8,128)(2,1)S(1)}, bf16[9,64,128]{2,1,0:T(8,128)(2,1)S(1)}, u32[]{:S(2)}, u32[]{:S(2)}) collective-permute-start(bf16[9,64,128]{2,1,0:T(8,128)(2,1)S(1)} %get-tuple-element.221), channel_id=1, source_target_pairs={{0,4},{4,0},{1,5},{5,1},{2,6},{6,2},{3,7},{7,3},{8,12},{12,8},{9,1... | collective-permute-start | bytes 442376 | tf_op jit(solution)/shard_map/ppermute | solution.py:645
  96.2 3.5 %collective-permute-start.32 = (bf16[9,64,128]{2,1,0:T(8,128)(2,1)S(1)}, bf16[9,64,128]{2,1,0:T(8,128)(2,1)S(1)}, u32[]{:S(2)}, u32[]{:S(2)}) collective-permute-start(bf16[9,64,128]{2,1,0:T(8,128)(2,1)S(1)} %get-tuple-element.222), channel_id=1, source_target_pairs={{0,4},{4,0},{1,5},{5,1},{2,6},{6,2},{3,7},{7,3},{8,12},{12,8},{9,1... | collective-permute-start | bytes 442376 | tf_op jit(solution)/shard_map/ppermute | solution.py:645
  97.6 2.8 %collective-permute-start.33 = (bf16[9,64,128]{2,1,0:T(8,128)(2,1)S(1)}, bf16[9,64,128]{2,1,0:T(8,128)(2,1)S(1)}, u32[]{:S(2)}, u32[]{:S(2)}) collective-permute-start(bf16[9,64,128]{2,1,0:T(8,128)(2,1)S(1)} %get-tuple-element.223), channel_id=1, source_target_pairs={{0,4},{4,0},{1,5},{5,1},{2,6},{6,2},{3,7},{7,3},{8,12},{12,8},{9,1... | collective-permute-start | bytes 442376 | tf_op jit(solution)/shard_map/ppermute | solution.py:645
  97.6 6.3 %collective-permute-start.23 = (bf16[512,128]{1,0:T(8,128)(2,1)S(1)}, bf16[512,128]{1,0:T(8,128)(2,1)S(1)}, u32[]{:S(2)}, u32[]{:S(2)}) collective-permute-start(bf16[512,128]{1,0:T(8,128)(2,1)S(1)} %get-tuple-element.213.refs_1_.refs_2_), channel_id=1, source_target_pairs={{0,8},{8,0},{16,24},{24,16},{1,9},{9,1},{17,25},{25,17},{2,10},{10... | collective-permute-start | bytes 393224 | tf_op jit(solution)/shard_map/ppermute | solution.py:651
  98.5 6.4 %collective-permute-start.27 = (bf16[512,128]{1,0:T(8,128)(2,1)S(1)}, bf16[512,128]{1,0:T(8,128)(2,1)S(1)}, u32[]{:S(2)}, u32[]{:S(2)}) collective-permute-start(bf16[512,128]{1,0:T(8,128)(2,1)S(1)} %get-tuple-element.214.refs_5_.refs_3_), channel_id=1, source_target_pairs={{0,16},{8,24},{16,0},{24,8},{1,17},{9,25},{17,1},{25,9},{2,18},{10... | collective-permute-start | bytes 393224 | tf_op jit(solution)/shard_map/ppermute | solution.py:651
  99.7 6.6 %collective-permute-start.25 = (bf16[512,128]{1,0:T(8,128)(2,1)S(1)}, bf16[512,128]{1,0:T(8,128)(2,1)S(1)}, u32[]{:S(2)}, u32[]{:S(2)}) collective-permute-start(bf16[512,128]{1,0:T(8,128)(2,1)S(1)} %collective-permute-done.24.refs_3_), channel_id=1, source_target_pairs={{0,8},{8,0},{16,24},{24,16},{1,9},{9,1},{17,25},{25,17},{2,10},{10... | collective-permute-start | bytes 393224 | tf_op jit(solution)/shard_map/ppermute | solution.py:651
  100.5 6.0 %collective-permute-start.28 = (bf16[512,128]{1,0:T(8,128)(2,1)S(1)}, bf16[512,128]{1,0:T(8,128)(2,1)S(1)}, u32[]{:S(2)}, u32[]{:S(2)}) collective-permute-start(bf16[512,128]{1,0:T(8,128)(2,1)S(1)} %collective-permute-done.26.refs_6_), channel_id=1, source_target_pairs={{0,16},{8,24},{16,0},{24,8},{1,17},{9,25},{17,1},{25,9},{2,18},{10... | collective-permute-start | bytes 393224 | tf_op jit(solution)/shard_map/ppermute | solution.py:651
  106.5 15.6 %copy-start.10 = (bf16[4,256,512]{2,1,0:T(8,128)(2,1)S(1)}, bf16[4,256,512]{2,1,0:T(8,128)(2,1)}, u32[]{:S(2)}) copy-start(bf16[4,256,512]{2,1,0:T(8,128)(2,1)} %get-tuple-element.240.refs_7_) | copy-start | bytes 3145732
  109.5 11.7 %collective-permute-start.34 = (bf16[832,128]{1,0:T(8,128)(2,1)S(1)}, bf16[832,128]{1,0:T(8,128)(2,1)S(1)}, u32[]{:S(2)}, u32[]{:S(2)}) collective-permute-start(bf16[832,128]{1,0:T(8,128)(2,1)S(1)} %get-tuple-element.231), channel_id=1, source_target_pairs={{0,8},{8,0},{16,24},{24,16},{1,9},{9,1},{17,25},{25,17},{2,10},{10... | collective-permute-start | bytes 638984 | tf_op jit(solution)/shard_map/ppermute | solution.py:651
  111.2 10.0 %collective-permute-start.35 = (bf16[832,128]{1,0:T(8,128)(2,1)S(1)}, bf16[832,128]{1,0:T(8,128)(2,1)S(1)}, u32[]{:S(2)}, u32[]{:S(2)}) collective-permute-start(bf16[832,128]{1,0:T(8,128)(2,1)S(1)} %get-tuple-element.232), channel_id=1, source_target_pairs={{0,16},{8,24},{16,0},{24,8},{1,17},{9,25},{17,1},{25,9},{2,18},{10... | collective-permute-start | bytes 638984 | tf_op jit(solution)/shard_map/ppermute | solution.py:651
  111.6 10.5 %collective-permute-start.36 = (bf16[832,128]{1,0:T(8,128)(2,1)S(1)}, bf16[832,128]{1,0:T(8,128)(2,1)S(1)}, u32[]{:S(2)}, u32[]{:S(2)}) collective-permute-start(bf16[832,128]{1,0:T(8,128)(2,1)S(1)} %get-tuple-element.233), channel_id=1, source_target_pairs={{0,24},{8,16},{16,8},{24,0},{1,25},{9,17},{17,9},{25,1},{2,26},{10... | collective-permute-start | bytes 638984 | tf_op jit(solution)/shard_map/ppermute | solution.py:651
  124.8 2.3 %collective-permute-start.37 = (bf16[9,64,128]{2,1,0:T(8,128)(2,1)S(1)}, bf16[9,64,128]{2,1,0:T(8,128)(2,1)S(1)}, u32[]{:S(2)}, u32[]{:S(2)}) collective-permute-start(bf16[9,64,128]{2,1,0:T(8,128)(2,1)S(1)} %get-tuple-element.244), channel_id=1, source_target_pairs={{0,4},{4,0},{1,5},{5,1},{2,6},{6,2},{3,7},{7,3},{8,12},{12,8},{9,1... | collective-permute-start | bytes 442376 | tf_op jit(solution)/shard_map/ppermute | solution.py:645
  124.8 2.9 %collective-permute-start.38 = (bf16[9,64,128]{2,1,0:T(8,128)(2,1)S(1)}, bf16[9,64,128]{2,1,0:T(8,128)(2,1)S(1)}, u32[]{:S(2)}, u32[]{:S(2)}) collective-permute-start(bf16[9,64,128]{2,1,0:T(8,128)(2,1)S(1)} %get-tuple-element.245), channel_id=1, source_target_pairs={{0,4},{4,0},{1,5},{5,1},{2,6},{6,2},{3,7},{7,3},{8,12},{12,8},{9,1... | collective-permute-start | bytes 442376 | tf_op jit(solution)/shard_map/ppermute | solution.py:645
  125.3 5.7 %collective-permute-start.39 = (bf16[9,64,128]{2,1,0:T(8,128)(2,1)S(1)}, bf16[9,64,128]{2,1,0:T(8,128)(2,1)S(1)}, u32[]{:S(2)}, u32[]{:S(2)}) collective-permute-start(bf16[9,64,128]{2,1,0:T(8,128)(2,1)S(1)} %get-tuple-element.246), channel_id=1, source_target_pairs={{0,4},{4,0},{1,5},{5,1},{2,6},{6,2},{3,7},{7,3},{8,12},{12,8},{9,1... | collective-permute-start | bytes 442376 | tf_op jit(solution)/shard_map/ppermute | solution.py:645
  125.4 5.6 %collective-permute-start.40 = (bf16[9,64,128]{2,1,0:T(8,128)(2,1)S(1)}, bf16[9,64,128]{2,1,0:T(8,128)(2,1)S(1)}, u32[]{:S(2)}, u32[]{:S(2)}) collective-permute-start(bf16[9,64,128]{2,1,0:T(8,128)(2,1)S(1)} %get-tuple-element.247), channel_id=1, source_target_pairs={{0,4},{4,0},{1,5},{5,1},{2,6},{6,2},{3,7},{7,3},{8,12},{12,8},{9,1... | collective-permute-start | bytes 442376 | tf_op jit(solution)/shard_map/ppermute | solution.py:645
  126.5 7.8 %collective-permute-start.44 = (bf16[576,128]{1,0:T(8,128)(2,1)S(1)}, bf16[576,128]{1,0:T(8,128)(2,1)S(1)}, u32[]{:S(2)}, u32[]{:S(2)}) collective-permute-start(bf16[576,128]{1,0:T(8,128)(2,1)S(1)} %get-tuple-element.253), channel_id=1, source_target_pairs={{0,1},{1,0},{2,3},{3,2},{4,5},{5,4},{6,7},{7,6},{8,9},{9,8},{10,11... | collective-permute-start | bytes 442376 | tf_op jit(solution)/shard_map/ppermute | solution.py:642
  127.1 13.9 %collective-permute-start.45 = (bf16[576,128]{1,0:T(8,128)(2,1)S(1)}, bf16[576,128]{1,0:T(8,128)(2,1)S(1)}, u32[]{:S(2)}, u32[]{:S(2)}) collective-permute-start(bf16[576,128]{1,0:T(8,128)(2,1)S(1)} %get-tuple-element.254), channel_id=1, source_target_pairs={{0,2},{1,3},{2,0},{3,1},{4,6},{5,7},{6,4},{7,5},{8,10},{9,11},{10,... | collective-permute-start | bytes 442376 | tf_op jit(solution)/shard_map/ppermute | solution.py:642
  127.7 13.3 %collective-permute-start.46 = (bf16[576,128]{1,0:T(8,128)(2,1)S(1)}, bf16[576,128]{1,0:T(8,128)(2,1)S(1)}, u32[]{:S(2)}, u32[]{:S(2)}) collective-permute-start(bf16[576,128]{1,0:T(8,128)(2,1)S(1)} %get-tuple-element.255), channel_id=1, source_target_pairs={{0,3},{1,2},{2,1},{3,0},{4,7},{5,6},{6,5},{7,4},{8,11},{9,10},{10,... | collective-permute-start | bytes 442376 | tf_op jit(solution)/shard_map/ppermute | solution.py:642
  131.7 9.3 %collective-permute-start.41 = (bf16[576,128]{1,0:T(8,128)(2,1)S(1)}, bf16[576,128]{1,0:T(8,128)(2,1)S(1)}, u32[]{:S(2)}, u32[]{:S(2)}) collective-permute-start(bf16[576,128]{1,0:T(8,128)(2,1)S(1)} %get-tuple-element.249), channel_id=1, source_target_pairs={{0,8},{8,0},{16,24},{24,16},{1,9},{9,1},{17,25},{25,17},{2,10},{10... | collective-permute-start | bytes 442376 | tf_op jit(solution)/shard_map/ppermute | solution.py:651
  133.2 7.8 %collective-permute-start.42 = (bf16[576,128]{1,0:T(8,128)(2,1)S(1)}, bf16[576,128]{1,0:T(8,128)(2,1)S(1)}, u32[]{:S(2)}, u32[]{:S(2)}) collective-permute-start(bf16[576,128]{1,0:T(8,128)(2,1)S(1)} %get-tuple-element.250), channel_id=1, source_target_pairs={{0,16},{8,24},{16,0},{24,8},{1,17},{9,25},{17,1},{25,9},{2,18},{10... | collective-permute-start | bytes 442376 | tf_op jit(solution)/shard_map/ppermute | solution.py:651
  134.4 7.1 %collective-permute-start.43 = (bf16[576,128]{1,0:T(8,128)(2,1)S(1)}, bf16[576,128]{1,0:T(8,128)(2,1)S(1)}, u32[]{:S(2)}, u32[]{:S(2)}) collective-permute-start(bf16[576,128]{1,0:T(8,128)(2,1)S(1)} %get-tuple-element.251), channel_id=1, source_target_pairs={{0,24},{8,16},{16,8},{24,0},{1,25},{9,17},{17,9},{25,1},{2,26},{10... | collective-permute-start | bytes 442376 | tf_op jit(solution)/shard_map/ppermute | solution.py:651
  135.8 13.1 %copy-start.1 = (f32[2,9,64,128]{3,2,1,0:T(8,128)S(1)}, f32[2,9,64,128]{3,2,1,0:T(8,128)}, u32[]{:S(2)}) copy-start(f32[2,9,64,128]{3,2,1,0:T(8,128)} %refs_5_.4) | copy-start | bytes 1769476
  135.8 13.1 %copy-start.2 = (f32[2,9,64,128]{3,2,1,0:T(8,128)S(1)}, f32[2,9,64,128]{3,2,1,0:T(8,128)}, u32[]{:S(2)}) copy-start(f32[2,9,64,128]{3,2,1,0:T(8,128)} %refs_6_.6) | copy-start | bytes 1769476
  142.2 7.7 %collective-permute-start.50 = (bf16[576,128]{1,0:T(8,128)(2,1)S(1)}, bf16[576,128]{1,0:T(8,128)(2,1)S(1)}, u32[]{:S(2)}, u32[]{:S(2)}) collective-permute-start(bf16[576,128]{1,0:T(8,128)(2,1)S(1)} %get-tuple-element.279), channel_id=1, source_target_pairs={{0,1},{1,0},{2,3},{3,2},{4,5},{5,4},{6,7},{7,6},{8,9},{9,8},{10,11... | collective-permute-start | bytes 442376 | tf_op jit(solution)/shard_map/ppermute | solution.py:642
  144.3 12.8 %collective-permute-start.51 = (bf16[576,128]{1,0:T(8,128)(2,1)S(1)}, bf16[576,128]{1,0:T(8,128)(2,1)S(1)}, u32[]{:S(2)}, u32[]{:S(2)}) collective-permute-start(bf16[576,128]{1,0:T(8,128)(2,1)S(1)} %get-tuple-element.280), channel_id=1, source_target_pairs={{0,2},{1,3},{2,0},{3,1},{4,6},{5,7},{6,4},{7,5},{8,10},{9,11},{10,... | collective-permute-start | bytes 442376 | tf_op jit(solution)/shard_map/ppermute | solution.py:642
  144.3 12.8 %collective-permute-start.52 = (bf16[576,128]{1,0:T(8,128)(2,1)S(1)}, bf16[576,128]{1,0:T(8,128)(2,1)S(1)}, u32[]{:S(2)}, u32[]{:S(2)}) collective-permute-start(bf16[576,128]{1,0:T(8,128)(2,1)S(1)} %get-tuple-element.281), channel_id=1, source_target_pairs={{0,3},{1,2},{2,1},{3,0},{4,7},{5,6},{6,5},{7,4},{8,11},{9,10},{10,... | collective-permute-start | bytes 442376 | tf_op jit(solution)/shard_map/ppermute | solution.py:642
  146.8 16.2 %collective-permute-start.47 = (bf16[256,512]{1,0:T(8,128)(2,1)}, bf16[256,512]{1,0:T(8,128)(2,1)S(1)}, u32[]{:S(2)}, u32[]{:S(2)}) collective-permute-start(bf16[256,512]{1,0:T(8,128)(2,1)} %get-tuple-element.275), channel_id=1, source_target_pairs={{0,8},{8,0},{16,24},{24,16},{1,9},{9,1},{17,25},{25,17},{2,10},{10... | collective-permute-start | bytes 786440 | tf_op jit(solution)/shard_map/ppermute | solution.py:651
  148.2 14.8 %collective-permute-start.48 = (bf16[256,512]{1,0:T(8,128)(2,1)S(1)}, bf16[256,512]{1,0:T(8,128)(2,1)S(1)}, u32[]{:S(2)}, u32[]{:S(2)}) collective-permute-start(bf16[256,512]{1,0:T(8,128)(2,1)S(1)} %get-tuple-element.276), channel_id=1, source_target_pairs={{0,16},{8,24},{16,0},{24,8},{1,17},{9,25},{17,1},{25,9},{2,18},{10... | collective-permute-start | bytes 786440 | tf_op jit(solution)/shard_map/ppermute | solution.py:651
  149.8 13.1 %collective-permute-start.49 = (bf16[256,512]{1,0:T(8,128)(2,1)S(1)}, bf16[256,512]{1,0:T(8,128)(2,1)S(1)}, u32[]{:S(2)}, u32[]{:S(2)}) collective-permute-start(bf16[256,512]{1,0:T(8,128)(2,1)S(1)} %get-tuple-element.277), channel_id=1, source_target_pairs={{0,24},{8,16},{16,8},{24,0},{1,25},{9,17},{17,9},{25,1},{2,26},{10... | collective-permute-start | bytes 786440 | tf_op jit(solution)/shard_map/ppermute | solution.py:651
  158.2 11.9 %copy-start.8 = (f32[4,512]{1,0:T(4,128)S(1)}, f32[4,512]{1,0:T(4,128)}, u32[]{:S(2)}) copy-start(f32[4,512]{1,0:T(4,128)} %refs_5_.5) | copy-start | bytes 24580
  158.2 11.9 %copy-start.9 = (f32[4,512]{1,0:T(4,128)S(1)}, f32[4,512]{1,0:T(4,128)}, u32[]{:S(2)}) copy-start(f32[4,512]{1,0:T(4,128)} %refs_6_.7) | copy-start | bytes 24580
  158.2 11.9 %all-to-all-start.4 = ((f32[32,8,128]{2,1,0:T(8,128)}), f32[32,8,128]{2,1,0:T(8,128)S(1)}, u32[]{:S(2)}, u32[]{:S(2)}) async-start(f32[32,8,128]{2,1,0:T(8,128)} %get-tuple-element.291), calls=%async_computation.4 | async-start | bytes 262144 | tf_op jit(solution)/shard_map/all_to_all | solution.py:850
  (2 other events, 15.6 us)

commit v5 on v4

--- a/solution.py
+++ b/solution.py
@@ -208,19 +208,28 @@
                 wcat[pl.ds(row, z.IB), k * z.LP : k * z.LP + z.L] = block[a, k]
 
 
+def split_channels(z, at, slices, outs, rows):
+    for s in range(z.S):
+
+        @pl.when(at[1] == s)
+        def _(s=s):
+            for t in range(z.S):
+                low = (s ^ t) * z.IB
+                outs[t][rows, :] = jnp.concatenate([v[:, low : low + z.IB] for v in slices], axis=1)
+
+
 def first_conv(z, at, np_ref, *refs):
     xs, refs = refs[: z.Q], refs[z.Q :]
     blocks, refs = refs[: z.S], refs[z.S :]
     hw_ref, refs = refs[0], refs[1:]
-    z_ref, slice_ref, par_ref, stats_ref, far_w, far_x, wcat, y_ref, sem = refs
+    outs, refs = refs[: z.S], refs[z.S :]
+    z_ref, slice_ref, par_ref, stats_ref, far_w, wcat, y_ref, sem = refs
     fill_kernels(z, at, blocks, wcat)
-    copies = [pltpu.make_async_copy(wcat, far_w, sem.at[0])]
+    copy = pltpu.make_async_copy(wcat, far_w, sem)
+    copy.start()
     for m in range(z.Q):
-        copies.append(
-            pltpu.make_async_copy(xs[m], far_x.at[at[0] ^ m], sem.at[1 + m])
-        )
-    for copy in copies:
-        copy.start()
+        rows = pl.ds(pl.multiple_of((at[0] ^ m) * z.own, z.own), z.own)
+        split_channels(z, at, [xs[m][:, a * z.L : (a + 1) * z.L] for a in range(z.Q)], outs, rows)
     for slot in range(z.Q):
 
         @pl.when(at[0] == slot)
@@ -237,8 +246,7 @@
 
     conv_into(z, product, y_ref, z_ref, 1, at[0])
     local_stats(z, z_ref, hw_ref, stats_ref)
-    for copy in copies:
-        copy.wait()
+    copy.wait()
 
 
 def gathered(z, at, parts, hold):
@@ -251,11 +259,12 @@
 def second_conv(z, at, *refs):
     hs, refs = refs[: 2 * z.Q], refs[2 * z.Q :]
     blocks, refs = refs[: z.S], refs[z.S :]
-    hw_ref, z_ref, stats_ref, far_ref, wcat, y_ref, h_ref, sem = refs
+    hw_ref, outs, (z_ref, stats_ref, wcat, y_ref, h_ref) = refs[0], refs[1 : 1 + z.S], refs[1 + z.S :]
     gathered(z, at, hs, h_ref)
-    copy = pltpu.make_async_copy(h_ref, far_ref, sem)
-    copy.start()
     fill_kernels(z, at, blocks, wcat)
+    for j in range(z.Q):
+        rows = slice(j * z.own, (j + 1) * z.own)
+        split_channels(z, at, [h_ref[a, rows, :] for a in range(z.Q)], outs, rows)
 
     def product(j):
         rows = slice(j * z.own, (j + 1) * z.own)
@@ -269,7 +278,6 @@
 
     conv_into(z, product, y_ref, z_ref)
     local_stats(z, z_ref, hw_ref, stats_ref)
-    copy.wait()
 
 
 def merged(z, all_ref):
@@ -353,7 +361,7 @@
     spread(stats_ref, list(carry))
 
 
-def norm_grad(z, row, z_ref, up_ref, sum_ref, all_ref, hw_ref, par_ref, a_ref, b_ref, par_grad_ref):
+def norm_grad(z, row, z_ref, up_ref, sum_ref, all_ref, hw_ref, par_ref, a_ref, b_ref, whole_ref, par_grad_ref):
     mean, inv, count = sum_ref[0:1, :], sum_ref[1:2, :], sum_ref[2:3, :]
     shift_grad = sum(all_ref[k, 0:1, : z.L] for k in range(z.S * z.Z))
     gain_grad = sum(all_ref[k, 1:2, : z.L] for k in range(z.S * z.Z))
@@ -364,7 +372,9 @@
         mask = image_mask(z, hw_ref[n])
         normed = (z_ref[rows, :] - mean) * inv
         grad = inv * mask * gain * (up_ref[rows, :] - (shift_grad + normed * gain_grad) / count)
-        return grad.astype(BF16)
+        low = grad.astype(BF16)
+        whole_ref[rows, :] = low
+        return low
 
     over_halves(z, step, (a_ref, b_ref))
 
@@ -445,52 +455,27 @@
         outs[m][...] = dx_ref[at[0] ^ m].astype(outs[m].dtype)
 
 
-def kernel_grad(z, at, f_ref, a_ref, b_ref, mine_ref, *refs):
-    theirs, (moved_ref, full_ref) = refs[:-2], refs[-2:]
-    fill_moved(z, a_ref, b_ref, moved_ref)
+def kernel_grad(z, at, *refs):
+    features, refs = refs[: z.S], refs[z.S :]
+    dzs, refs = refs[: z.S + 1], refs[z.S + 1 :]
+    value_ref = None
+    if len(refs) > z.Q + 2:
+        value_ref, refs = refs[0], refs[1:]
+    outs, (moved_ref, full_ref) = refs[: z.Q], refs[z.Q :]
     contract = (((0,), (0,)), ((), ()))
-    if f_ref.shape[2] == z.C:
-        whole = f_ref[...].reshape(z.G, z.C)
-        full_ref[...] = lax.dot_general(whole, moved_ref[...], contract, preferred_element_type=F32)
-    elif z.L % LANES == 0:
-        whole = jnp.concatenate([f_ref[i] for i in range(z.Q)], axis=1)
-        full_ref[...] = lax.dot_general(whole, moved_ref[...], contract, preferred_element_type=F32)
-    else:
-        for i in range(z.Q):
-            full_ref[i * z.L : (i + 1) * z.L, :] = lax.dot_general(
-                f_ref[i], moved_ref[...], contract, preferred_element_type=F32
-            )
+    half = z.G // 2
+    for t in range(z.S):
+        pair = (dzs[0], dzs[1]) if t == 0 else (dzs[1 + t].at[:half], dzs[1 + t].at[half:])
+        fill_moved(z, *pair, moved_ref)
+        part = lax.dot_general(features[t][...], moved_ref[...], contract, preferred_element_type=F32)
+        full_ref[...] = part if t == 0 else full_ref[...] + part
     for r in range(z.Q):
-        for t in range(z.S):
-            row = pl.multiple_of((at[0] ^ r) * z.L + (at[1] ^ t) * z.IB, z.IB)
-            for k in range(z.K):
-                part = full_ref[pl.ds(row, z.IB), k * z.LP : k * z.LP + z.L]
-                if t == 0:
-                    mine_ref[r, k] = part
-                else:
-                    theirs[(t - 1) * z.Q + r][k] = part.astype(BF16)
-
-
-def first_back(z, at, z_ref, up_ref, sum_ref, all_ref, hw_ref, par_ref, f_ref, *refs):
-    (a_ref, b_ref, par_grad_ref), refs = refs[:3], refs[3:]
-    norm_grad(z, 0, z_ref, up_ref, sum_ref, all_ref, hw_ref, par_ref, a_ref, b_ref, par_grad_ref)
-    kernel_grad(z, at, f_ref, a_ref, b_ref, *refs)
-
-
-def add_sharers(z, at, *refs):
-    count = 1 + z.Q * (z.S - 1)
-    mine_ref, others, refs = refs[0], refs[1:count], refs[count:]
-    value_ref = None
-    if len(refs) > z.Q:
-        value_ref, refs = refs[0], refs[1:]
-    for r in range(z.Q):
+        row = pl.multiple_of((at[0] ^ r) * z.IB, z.IB)
         for k in range(z.K):
-            total = mine_ref[r, k]
-            for other in others[r :: z.Q]:
-                total = total + other[k].astype(F32)
-            refs[r][k * z.IB : (k + 1) * z.IB, :] = total.astype(BF16)
+            part = full_ref[pl.ds(row, z.IB), k * z.LP : k * z.LP + z.L]
+            outs[r][k * z.IB : (k + 1) * z.IB, :] = part.astype(BF16)
         if value_ref is not None:
-            refs[r][z.K * z.IB :, :] = value_ref[at[0] ^ r]
+            outs[r][z.K * z.IB :, :] = value_ref[at[0] ^ r]
 
 
 def route(z, at, *refs):
@@ -670,7 +655,7 @@
     blocks = near((z.Z, *piece), BF16)
     stat = near((many, 8, LANES))
     conv_scratch = [pltpu.VMEM((z.C, z.K * z.LP), BF16), pltpu.VMEM((rows, z.K * z.LP), F32)]
-    grad_scratch = [pltpu.VMEM((z.G, z.K * z.LP), BF16), pltpu.VMEM((z.C, z.K * z.LP), F32)]
+    grad_scratch = [pltpu.VMEM((z.G, z.K * z.LP), BF16), pltpu.VMEM((z.Q * z.IB, z.K * z.LP), F32)]
     cot_rows = cotangent.reshape(rows, z.C)
     image_rows = images.reshape(rows, z.C)
 
@@ -702,21 +687,20 @@
         raw=(keep,),
     )
     w_far = away((z.C, z.K * z.LP), BF16)
-    x_far = away((z.Q, rows, z.C), BF16)
-    z1, x_slice, slice_params, stats, w_far, x_far = call(
+    *x_parts, z1, x_slice, slice_params, stats, w_far = call(
         functools.partial(first_conv, z),
-        [
+        [near((z.G, z.Q * z.IB), BF16)] * z.S
+        + [
             near(GL),
             near(GL, BF16),
             near((4, z.L)),
             stat,
             w_far,
-            x_far,
         ],
         (at, params, *xs, *share(front_one), hw),
-        conv_scratch + [pltpu.SemaphoreType.DMA((1 + z.Q,))],
+        conv_scratch + [pltpu.SemaphoreType.DMA],
         limit=16,
-        raw=(w_far, x_far),
+        raw=(w_far,),
     )
     stats, picked = together((stats, picked))
     stats, picked = together((sharers(stats), [over_q(picked[m], m) for m in range(z.Q)]))
@@ -726,39 +710,39 @@
         (at, z1, stats, hw, slice_params, *picked),
     )
     hs = gather(ha, hb)
-    h_far = away((z.Q, *GL), BF16)
-    z2, stats, h_far = call(
+    *h_parts, z2, stats = call(
         functools.partial(second_conv, z),
-        [near(GL), stat, h_far],
+        [near((z.G, z.Q * z.IB), BF16)] * z.S + [near(GL), stat],
         (at, *hs, *share(front_two), hw),
-        conv_scratch + [pltpu.VMEM((z.Q, *GL), BF16), pltpu.SemaphoreType.DMA],
+        conv_scratch + [pltpu.VMEM((z.Q, *GL), BF16)],
         limit=16,
-        raw=(h_far,),
-    )
+    )
+    stats, x_parts, h_parts = together((stats, x_parts, h_parts))
+    x_parts = [over_s(v, t) for t, v in enumerate(x_parts)]
+    h_parts = [over_s(v, t) for t, v in enumerate(h_parts)]
+    stats, x_parts, h_parts = together((sharers(stats), x_parts, h_parts))
     out, d, sum_two, stats = call(
         functools.partial(middle, z),
         [near((z.Q, rows, z.L), BF16), near(GL), near((8, z.L)), stat],
-        (at, z2, sharers(stats), hw, slice_params, x_slice, cots),
-    )
-    da, db, grad_two = call(
+        (at, z2, stats, hw, slice_params, x_slice, cots),
+    )
+    da, db, dz, grad_two = call(
         functools.partial(norm_grad, z, 2),
-        [near(HL, BF16), near(HL, BF16), near((8, z.L))],
+        [near(HL, BF16), near(HL, BF16), near(GL, BF16), near((8, z.L))],
         (z2, d, sum_two, sharers(stats), hw, slice_params),
     )
     da, db, keep_two = together((da, db, keep_two))
     dz2s = gather(da, db)
 
-    gradient_shapes = [near((z.Q, *piece))] + [near(piece, BF16)] * (z.Q * (z.S - 1))
-
-    def to_sharers(theirs):
-        return [over_s(theirs[(t - 1) * z.Q + r], t) for t in range(1, z.S) for r in range(z.Q)]
-
-    def add_up(mine, received, *value):
+    def gradient(features, a, b, whole, *value):
         more = rows if value else 0
         return call(
-            functools.partial(add_sharers, z),
+            functools.partial(kernel_grad, z),
             [near((z.K * z.IB + more, z.L), BF16)] * z.Q,
-            (at, mine, *received, *value),
+            (at, *features, a, b, *[over_s(whole, t) for t in range(1, z.S)], *value),
+            grad_scratch,
+            limit=14,
+            cost=COST_GRAD,
         )
 
     def by_plane(parts):
@@ -790,15 +774,7 @@
             cost_estimate=pl.CostEstimate(flops=1 if j else COST_GRAD, bytes_accessed=1, transcendentals=0),
         )(*args)
 
-    mine, *theirs = call(
-        functools.partial(kernel_grad, z),
-        gradient_shapes,
-        (at, h_far, da, db),
-        grad_scratch,
-        limit=14,
-        cost=COST_GRAD,
-    )
-    parts_two = add_up(mine, to_sharers(theirs), out)
+    parts_two = gradient(h_parts, da, db, dz, out)
     da1, stats = call(
         functools.partial(hidden_grad, z),
         [near(GL), stat],
@@ -808,13 +784,10 @@
     )
     stats, parts_two = together((stats, parts_two))
     stats, parts_two = together((sharers(stats), by_plane(parts_two)))
-    da, db, grad_one, mine, *theirs = call(
-        functools.partial(first_back, z),
-        [near(HL, BF16), near(HL, BF16), near((8, z.L))] + gradient_shapes,
-        (at, z1, da1, sum_one, stats, hw, slice_params, x_far),
-        grad_scratch,
-        limit=14,
-        cost=COST_GRAD,
+    da, db, dz, grad_one = call(
+        functools.partial(norm_grad, z, 0),
+        [near(HL, BF16), near(HL, BF16), near(GL, BF16), near((8, z.L))],
+        (z1, da1, sum_one, stats, hw, slice_params),
     )
     flat = near((z.K * z.IB, z.L), BF16)
     hold = pltpu.VMEM((z.Z, z.K * z.IB, z.L), BF16)
@@ -825,8 +798,7 @@
         [pltpu.VMEM((z.Q, rows, z.L), BF16), hold],
         after=(da,),
     )
-    received = to_sharers(theirs)
-    parts_one = add_up(mine, received)
+    parts_one = gradient(x_parts, da, db, dz)
     parts_one, parts_two = by_plane(parts_one), along(parts_two)
     parts_one, parts_two = together((parts_one, parts_two))
     dxs = call(
@@ -837,10 +809,10 @@
         limit=16,
         cost=COST_GRAD,
         far=(w_far,),
-        after=(received[0],),
-    )
-    parts_one = call(functools.partial(route, z), [flat] * z.Z, (at, *parts_one), [hold], after=(dxs[0],))
-    parts_one, dxs, parts_two = together((parts_one, dxs, parts_two))
+        after=(parts_one[0],),
+    )
+    parts_one = call(functools.partial(route, z), [flat] * z.Z, (at, *parts_one), [hold])
+    parts_one, parts_two = together((parts_one, parts_two))
     parts_one = along(parts_one)
     new_first, new_second, move_two, other = update(1, parts_two)
     dxs = [over_q(dxs[m], m) for m in range(z.Q)]

time: 172 us -> 168 us (0.977)
  waiting for transfers between devices: 36.3 us -> 30.9 us
    ppermute x12, waiting for transfers between devices: 16 us -> 13.1 us  [over_z(): return lax.ppermute(v, 'z', [(i, i ^ m) for i in range(z.Z)]) if m else v]
    pallas_call x18 -> x17, Pallas kernels: 27.1 us -> 27.6 us  [call(): pl.pallas_call(run, out_shape=out_shape, in_specs=[pl.BlockSpec(memory_sp...]
  transfers between devices with their start and end apart: 54 -> 50, of which waited for: 22 -> 20; matrix products, arithmetic and copies ran while one was open for 0% -> 0% of each run, Pallas kernels for 8% -> 9%
where the time goes in v5:
time: 168 us; the launch traced here: 167 us
  starting transfers between devices  69 us (41%)
  blocking collectives  35 us (21%)
  waiting for transfers between devices  30.9 us (18%)
  Pallas kernels  29.7 us (18%)
    ppermute x30, starting transfers between devices, over_q(): return lax.ppermute(v, 'q', [(i, i ^ m) for i in range(z.Q)]) if m else v  36 us
    all_to_all x4, blocking collectives, sharers(): return lax.all_to_all(v, ('s', 'z'), 0, 0)  35 us
    pallas_call x17, Pallas kernels, call(): pl.pallas_call(run, out_shape=out_shape, in_specs=[pl.BlockSpec(memory_sp...  27.6 us
    ppermute x12, starting transfers between devices, over_z(): return lax.ppermute(v, 'z', [(i, i ^ m) for i in range(z.Z)]) if m else v  27.3 us
    ppermute x12, waiting for transfers between devices, over_z(): return lax.ppermute(v, 'z', [(i, i ^ m) for i in range(z.Z)]) if m else v  13.1 us
    ppermute x30, waiting for transfers between devices, over_q(): return lax.ppermute(v, 'q', [(i, i ^ m) for i in range(z.Q)]) if m else v  12 us
    all_to_all x1, waiting for transfers between devices, shards(): stats = lax.all_to_all(stats, ('s', 'q', 'z'), 0, 0)  5.3 us
    all_to_all x1, starting transfers between devices, shards(): stats = lax.all_to_all(stats, ('s', 'q', 'z'), 0, 0)  4.14 us
  transfers between devices with their start and end apart: 50, of which 20 were waited for; matrix products, arithmetic and copies ran while one was open for 0% of the time, Pallas kernels for 9%

profile of v5, /device:TPU:0, one launch (start us, length us, event | category | flops | bytes accessed | tf_op | source)
XLA Modules:
  0.0 167.5 jit_solution(11399788153196446698)
XLA Ops:
  0.7 1.2 convert.4
  1.9 5.1 %collective-permute-start.2 = (bf16[9,64,128]{2,1,0:T(8,128)(2,1)S(1)}, bf16[9,64,128]{2,1,0:T(8,128)(2,1)S(1)}, u32[]{:S(2)}, u32[]{:S(2)}) collective-permute-start(bf16[9,64,128]{2,1,0:T(8,128)(2,1)S(1)} %get-tuple-element.156.refs_1_), channel_id=1, source_target_pairs={{0,3},{1,2},{2,1},{3,0},{4,7},{5,6},{6,5},{7,4},{8,11},{9,10},{10,... | collective-permute-start | bytes 442376 | tf_op jit(solution)/shard_map/ppermute | solution.py:627
  7.0 2.4 %collective-permute-start.5 = (bf16[256,512]{1,0:T(8,128)(2,1)S(1)}, bf16[256,512]{1,0:T(8,128)(2,1)S(1)}, u32[]{:S(2)}, u32[]{:S(2)}) collective-permute-start(bf16[256,512]{1,0:T(8,128)(2,1)S(1)} %bitcast.13), channel_id=1, source_target_pairs={{0,24},{8,16},{16,8},{24,0},{1,25},{9,17},{17,9},{25,1},{2,26},{10... | collective-permute-start | bytes 786440 | tf_op jit(solution)/shard_map/ppermute | solution.py:636
  10.9 6.9 %collective-permute-start = (bf16[9,64,128]{2,1,0:T(8,128)(2,1)S(1)}, bf16[9,64,128]{2,1,0:T(8,128)(2,1)S(1)}, u32[]{:S(2)}, u32[]{:S(2)}) collective-permute-start(bf16[9,64,128]{2,1,0:T(8,128)(2,1)S(1)} %get-tuple-element.156.refs_1_), channel_id=1, source_target_pairs={{0,1},{1,0},{2,3},{3,2},{4,5},{5,4},{6,7},{7,6},{8,9},{9,8},{10,11... | collective-permute-start | bytes 442376 | tf_op jit(solution)/shard_map/ppermute | solution.py:627
  17.8 1.7 %collective-permute-done.1.refs_3_ = bf16[9,64,128]{2,1,0:T(8,128)(2,1)S(1)} collective-permute-done((bf16[9,64,128]{2,1,0:T(8,128)(2,1)S(1)}, bf16[9,64,128]{2,1,0:T(8,128)(2,1)S(1)}, u32[]{:S(2)}, u32[]{:S(2)}) %collective-permute-start.1) | collective-permute-done | bytes 147488 | tf_op jit(solution)/shard_map/ppermute | solution.py:627
  19.6 1.9 %collective-permute-done.refs_2_ = bf16[9,64,128]{2,1,0:T(8,128)(2,1)S(1)} collective-permute-done((bf16[9,64,128]{2,1,0:T(8,128)(2,1)S(1)}, bf16[9,64,128]{2,1,0:T(8,128)(2,1)S(1)}, u32[]{:S(2)}, u32[]{:S(2)}) %collective-permute-start) | collective-permute-done | bytes 147488 | tf_op jit(solution)/shard_map/ppermute | solution.py:627
  21.5 2.1 %collective-permute-start.11 = (bf16[9,64,128]{2,1,0:T(8,128)(2,1)S(1)}, bf16[9,64,128]{2,1,0:T(8,128)(2,1)S(1)}, u32[]{:S(2)}, u32[]{:S(2)}) collective-permute-start(bf16[9,64,128]{2,1,0:T(8,128)(2,1)S(1)} %get-tuple-element.181.refs_1_), channel_id=1, source_target_pairs={{0,3},{1,2},{2,1},{3,0},{4,7},{5,6},{6,5},{7,4},{8,11},{9,10},{10,... | collective-permute-start | bytes 442376 | tf_op jit(solution)/shard_map/ppermute | solution.py:627
  23.6 0.8 shard_map.168
  24.5 1.6 collective-permute-start.6
  26.1 1.5 collective-permute-start.7
  28.0 0.9 collective-permute-start.10
  28.9 3.5 %collective-permute-start.9 = (bf16[9,64,128]{2,1,0:T(8,128)(2,1)S(1)}, bf16[9,64,128]{2,1,0:T(8,128)(2,1)S(1)}, u32[]{:S(2)}, u32[]{:S(2)}) collective-permute-start(bf16[9,64,128]{2,1,0:T(8,128)(2,1)S(1)} %get-tuple-element.181.refs_1_), channel_id=1, source_target_pairs={{0,1},{1,0},{2,3},{3,2},{4,5},{5,4},{6,7},{7,6},{8,9},{9,8},{10,11... | collective-permute-start | bytes 442376 | tf_op jit(solution)/shard_map/ppermute | solution.py:627
  32.4 3.5 %collective-permute-done.10.refs_3_ = bf16[9,64,128]{2,1,0:T(8,128)(2,1)S(1)} collective-permute-done((bf16[9,64,128]{2,1,0:T(8,128)(2,1)S(1)}, bf16[9,64,128]{2,1,0:T(8,128)(2,1)S(1)}, u32[]{:S(2)}, u32[]{:S(2)}) %collective-permute-start.10) | collective-permute-done | bytes 147488 | tf_op jit(solution)/shard_map/ppermute | solution.py:627
  35.8 0.7 collective-permute-done.9.refs_2_
  37.2 1.4 shard_map.171
  39.2 3.3 %shard_map.170 = (bf16[1024,256]{1,0:T(8,128)(2,1)S(1)}, bf16[1024,256]{1,0:T(8,128)(2,1)S(1)}, f32[1024,128]{1,0:T(8,128)S(1)}, bf16[1024,128]{1,0:T(8,128)(2,1...) custom-call(s32[3]{0:T(128)S(1)} %pad_add_fusion.refs_0_, ...), custom_call_target="tpu_custom_call" | custom-call | flops 1 | bytes 1 | tf_op jit(solution)/shard_map/pallas_call | solution.py:68
  42.5 1.6 collective-permute-start.13
  44.1 1.5 collective-permute-start.14
  46.1 10.5 %all_to_all.25.refs_2_ = f32[8,8,128]{2,1,0:T(8,128)S(1)} all-to-all(f32[8,8,128]{2,1,0:T(8,128)S(1)} %get-tuple-element.189), channel_id=1, replica_groups=mesh['ha'=2,'wa'=4,'ba'=4] {'wa':(2)2,'ba'}, dimensions={0} | all-to-all | bytes 65536 | tf_op jit(solution)/shard_map/all_to_all | solution.py:633
  56.6 1.0 shard_map.172
  57.8 1.1 collective-permute-start.17
  58.9 1.9 %collective-permute-start.19 = (bf16[512,128]{1,0:T(8,128)(2,1)S(1)}, bf16[512,128]{1,0:T(8,128)(2,1)S(1)}, u32[]{:S(2)}, u32[]{:S(2)}) collective-permute-start(bf16[512,128]{1,0:T(8,128)(2,1)S(1)} %get-tuple-element.201.refs_5_), channel_id=1, source_target_pairs={{0,8},{8,0},{16,24},{24,16},{1,9},{9,1},{17,25},{25,17},{2,10},{10... | collective-permute-start | bytes 393224 | tf_op jit(solution)/shard_map/ppermute | solution.py:636
  60.9 1.0 collective-permute-start.20
  61.9 2.0 %collective-permute-done.17.refs_3_ = bf16[512,128]{1,0:T(8,128)(2,1)S(1)} collective-permute-done((bf16[512,128]{1,0:T(8,128)(2,1)S(1)}, bf16[512,128]{1,0:T(8,128)(2,1)S(1)}, u32[]{:S(2)}, u32[]{:S(2)}) %collective-permute-start.17) | collective-permute-done | bytes 131104 | tf_op jit(solution)/shard_map/ppermute | solution.py:636
  63.8 1.0 collective-permute-start.18
  65.2 1.9 %collective-permute-start.21 = (bf16[512,128]{1,0:T(8,128)(2,1)S(1)}, bf16[512,128]{1,0:T(8,128)(2,1)S(1)}, u32[]{:S(2)}, u32[]{:S(2)}) collective-permute-start(bf16[512,128]{1,0:T(8,128)(2,1)S(1)} %collective-permute-done.19.refs_6_), channel_id=1, source_target_pairs={{0,16},{8,24},{16,0},{24,8},{1,17},{9,25},{17,1},{25,9},{2,18},{10... | collective-permute-start | bytes 393224 | tf_op jit(solution)/shard_map/ppermute | solution.py:636
  67.2 0.9 collective-permute-done.16.refs_2_
  68.0 2.2 %collective-permute-done.18.refs_4_ = bf16[512,128]{1,0:T(8,128)(2,1)S(1)} collective-permute-done((bf16[512,128]{1,0:T(8,128)(2,1)S(1)}, bf16[512,128]{1,0:T(8,128)(2,1)S(1)}, u32[]{:S(2)}, u32[]{:S(2)}) %collective-permute-start.18) | collective-permute-done | bytes 131104 | tf_op jit(solution)/shard_map/ppermute | solution.py:636
  70.2 3.3 %shard_map.173 = (bf16[1024,256]{1,0:T(8,128)(2,1)S(1)}, bf16[1024,256]{1,0:T(8,128)(2,1)S(1)}, f32[1024,128]{1,0:T(8,128)S(1)}, f32[8,8,128]{2,1,0:T(8,128)S(1)}) custom-call(s32[3]{0:T(128)S(1)} %pad_add_fusion.refs_0_, bf16[512,128]{1,0:T(8,128)(2,1)S(1)} %get-tuple-element.200.refs_1_, bf16[512,128]{1,0:T(8,128)(2,1)S(1)} %collective-permute-done.16.refs_2_, ...), custom_call_target="tpu_custom_call" | custom-call | flops 1 | bytes 1 | tf_op jit(solution)/shard_map/pallas_call | solution.py:68
  74.0 8.1 %all_to_all.26.refs_2_ = f32[8,8,128]{2,1,0:T(8,128)S(1)} all-to-all(f32[8,8,128]{2,1,0:T(8,128)S(1)} %get-tuple-element.209), channel_id=1, replica_groups=mesh['ha'=2,'wa'=4,'ba'=4] {'wa':(2)2,'ba'}, dimensions={0} | all-to-all | bytes 65536 | tf_op jit(solution)/shard_map/all_to_all | solution.py:633
  82.2 1.3 shard_map.174
  83.5 8.2 %all_to_all.27.refs_3_ = f32[8,8,128]{2,1,0:T(8,128)S(1)} all-to-all(f32[8,8,128]{2,1,0:T(8,128)S(1)} %get-tuple-element.219), channel_id=1, replica_groups=mesh['ha'=2,'wa'=4,'ba'=4] {'wa':(2)2,'ba'}, dimensions={0} | all-to-all | bytes 65536 | tf_op jit(solution)/shard_map/all_to_all | solution.py:633
  92.5 1.9 %collective-permute-start.26 = (bf16[512,128]{1,0:T(8,128)(2,1)S(1)}, bf16[512,128]{1,0:T(8,128)(2,1)S(1)}, u32[]{:S(2)}, u32[]{:S(2)}) collective-permute-start(bf16[512,128]{1,0:T(8,128)(2,1)S(1)} %get-tuple-element.223.refs_1_.refs_3_), channel_id=1, source_target_pairs={{0,16},{8,24},{16,0},{24,8},{1,17},{9,25},{17,1},{25,9},{2,18},{10... | collective-permute-start | bytes 393224 | tf_op jit(solution)/shard_map/ppermute | solution.py:636
  94.5 1.9 %collective-permute-start.25 = (bf16[512,128]{1,0:T(8,128)(2,1)S(1)}, bf16[512,128]{1,0:T(8,128)(2,1)S(1)}, u32[]{:S(2)}, u32[]{:S(2)}) collective-permute-start(bf16[512,128]{1,0:T(8,128)(2,1)S(1)} %get-tuple-element.223.refs_1_.refs_3_), channel_id=1, source_target_pairs={{0,8},{8,0},{16,24},{24,16},{1,9},{9,1},{17,25},{25,17},{2,10},{10... | collective-permute-start | bytes 393224 | tf_op jit(solution)/shard_map/ppermute | solution.py:636
  96.5 1.7 %collective-permute-done.26.refs_3_ = bf16[512,128]{1,0:T(8,128)(2,1)S(1)} collective-permute-done((bf16[512,128]{1,0:T(8,128)(2,1)S(1)}, bf16[512,128]{1,0:T(8,128)(2,1)S(1)}, u32[]{:S(2)}, u32[]{:S(2)}) %collective-permute-start.26) | collective-permute-done | bytes 131104 | tf_op jit(solution)/shard_map/ppermute | solution.py:636
  98.2 1.7 %collective-permute-start.29 = (bf16[512,128]{1,0:T(8,128)(2,1)S(1)}, bf16[512,128]{1,0:T(8,128)(2,1)S(1)}, u32[]{:S(2)}, u32[]{:S(2)}) collective-permute-start(bf16[512,128]{1,0:T(8,128)(2,1)S(1)} %get-tuple-element.224.refs_5_.refs_4_), channel_id=1, source_target_pairs={{0,16},{8,24},{16,0},{24,8},{1,17},{9,25},{17,1},{25,9},{2,18},{10... | collective-permute-start | bytes 393224 | tf_op jit(solution)/shard_map/ppermute | solution.py:636
  99.9 0.9 collective-permute-done.28.refs_6_
  100.9 2.0 %collective-permute-start.30 = (bf16[512,128]{1,0:T(8,128)(2,1)S(1)}, bf16[512,128]{1,0:T(8,128)(2,1)S(1)}, u32[]{:S(2)}, u32[]{:S(2)}) collective-permute-start(bf16[512,128]{1,0:T(8,128)(2,1)S(1)} %collective-permute-done.28.refs_6_), channel_id=1, source_target_pairs={{0,16},{8,24},{16,0},{24,8},{1,17},{9,25},{17,1},{25,9},{2,18},{10... | collective-permute-start | bytes 393224 | tf_op jit(solution)/shard_map/ppermute | solution.py:636
  102.9 2.6 %shard_map.177 = (bf16[832,128]{1,0:T(8,128)(2,1)S(1)}, bf16[832,128]{1,0:T(8,128)(2,1)S(1)}, bf16[832,128]{1,0:T(8,128)(2,1)S(1)}, bf16[832,128]{1,0:T(8,128)(2,1)S(1)}) custom-call(s32[3]{0:T(128)S(1)} %pad_add_fusion.refs_0_, bf16[1024,256]{1,0:T(8,128)(2,1)S(1)} %get-tuple-element.228.refs_1_, bf16[1024,256]{1,0:T(8,128)(2,1)S(1)} %collective-permute-done.24.refs_2_, ...), custom_call_target="tpu_custom_call" | custom-call | flops 3000000000 | bytes 1 | tf_op jit(solution)/shard_map/pallas_call | solution.py:68
  106.0 3.0 %shard_map.176 = (f32[1024,128]{1,0:T(8,128)S(1)}, f32[8,8,128]{2,1,0:T(8,128)S(1)}) custom-call(s32[3]{0:T(128)S(1)} %pad_add_fusion.refs_0_, bf16[512,128]{1,0:T(8,128)(2,1)S(1)} %get-tuple-element.223.refs_1_.refs_3_, bf16[512,128]{1,0:T(8,128)(2,1)S(1)} %collective-permute-done.25.refs_2_, bf16[512,128]{1,0:T(8,128)(2,1)S(1)} %collective-permute-done.26.refs_3_, ...), custom_call_target="tpu_custom_call" | custom-call | flops 1 | bytes 1 | tf_op jit(solution)/shard_map/pallas_call | solution.py:68
  109.0 1.9 %collective-permute-start.33 = (bf16[832,128]{1,0:T(8,128)(2,1)S(1)}, bf16[832,128]{1,0:T(8,128)(2,1)S(1)}, u32[]{:S(2)}, u32[]{:S(2)}) collective-permute-start(bf16[832,128]{1,0:T(8,128)(2,1)S(1)} %get-tuple-element.238), channel_id=1, source_target_pairs={{0,8},{8,0},{16,24},{24,16},{1,9},{9,1},{17,25},{25,17},{2,10},{10... | collective-permute-start | bytes 638984 | tf_op jit(solution)/shard_map/ppermute | solution.py:636
  111.1 1.5 collective-permute-start.35
  112.6 8.1 %all_to_all.28.refs_3_ = f32[8,8,128]{2,1,0:T(8,128)S(1)} all-to-all(f32[8,8,128]{2,1,0:T(8,128)S(1)} %get-tuple-element.236), channel_id=1, replica_groups=mesh['ha'=2,'wa'=4,'ba'=4] {'wa':(2)2,'ba'}, dimensions={0} | all-to-all | bytes 65536 | tf_op jit(solution)/shard_map/all_to_all | solution.py:633
  121.2 0.7 shard_map.179
  123.0 3.4 %collective-permute-start.42 = (bf16[576,128]{1,0:T(8,128)(2,1)S(1)}, bf16[576,128]{1,0:T(8,128)(2,1)S(1)}, u32[]{:S(2)}, u32[]{:S(2)}) collective-permute-start(bf16[576,128]{1,0:T(8,128)(2,1)S(1)} %get-tuple-element.261), channel_id=1, source_target_pairs={{0,3},{1,2},{2,1},{3,0},{4,7},{5,6},{6,5},{7,4},{8,11},{9,10},{10,... | collective-permute-start | bytes 442376 | tf_op jit(solution)/shard_map/ppermute | solution.py:627
  126.3 2.6 %shard_map.180 = (bf16[576,128]{1,0:T(8,128)(2,1)S(1)}, bf16[576,128]{1,0:T(8,128)(2,1)S(1)}, bf16[576,128]{1,0:T(8,128)(2,1)S(1)}, bf16[576,128]{1,0:T(8,128)(2,1)S(1)}) custom-call(s32[3]{0:T(128)S(1)} %pad_add_fusion.refs_0_, bf16[1024,256]{1,0:T(8,128)(2,1)S(1)} %get-tuple-element.251.refs_1_, bf16[1024,256]{1,0:T(8,128)(2,1)S(1)} %collective-permute-done.23.refs_2_, ...), custom_call_target="tpu_custom_call" | custom-call | flops 3000000000 | bytes 1 | tf_op jit(solution)/shard_map/pallas_call | solution.py:68
  128.9 1.9 %collective-permute-start.37 = (bf16[576,128]{1,0:T(8,128)(2,1)S(1)}, bf16[576,128]{1,0:T(8,128)(2,1)S(1)}, u32[]{:S(2)}, u32[]{:S(2)}) collective-permute-start(bf16[576,128]{1,0:T(8,128)(2,1)S(1)} %get-tuple-element.255), channel_id=1, source_target_pairs={{0,8},{8,0},{16,24},{24,16},{1,9},{9,1},{17,25},{25,17},{2,10},{10... | collective-permute-start | bytes 442376 | tf_op jit(solution)/shard_map/ppermute | solution.py:636
  131.1 1.4 collective-permute-start.39
  132.5 3.9 %collective-permute-done.41.refs_2_ = bf16[576,128]{1,0:T(8,128)(2,1)S(1)} collective-permute-done((bf16[576,128]{1,0:T(8,128)(2,1)S(1)}, bf16[576,128]{1,0:T(8,128)(2,1)S(1)}, u32[]{:S(2)}, u32[]{:S(2)}) %collective-permute-start.41) | collective-permute-done | bytes 147488 | tf_op jit(solution)/shard_map/ppermute | solution.py:627
  136.5 1.0 collective-permute-done.38.refs_3_
  137.4 1.4 collective-permute-done.39.refs_4_
  140.6 3.3 %collective-permute-start.48 = (bf16[576,128]{1,0:T(8,128)(2,1)S(1)}, bf16[576,128]{1,0:T(8,128)(2,1)S(1)}, u32[]{:S(2)}, u32[]{:S(2)}) collective-permute-start(bf16[576,128]{1,0:T(8,128)(2,1)S(1)} %get-tuple-element.281), channel_id=1, source_target_pairs={{0,3},{1,2},{2,1},{3,0},{4,7},{5,6},{6,5},{7,4},{8,11},{9,10},{10,... | collective-permute-start | bytes 442376 | tf_op jit(solution)/shard_map/ppermute | solution.py:627
  143.9 3.9 %shard_map.181 = (f32[256,512]{1,0:T(8,128)S(1)}, bf16[256,512]{1,0:T(8,128)(2,1)}, bf16[256,512]{1,0:T(8,128)(2,1)S(1)}, bf16[256,512]{1,0:T(8,128)(2,1)S(1)}) custom-call(s32[3]{0:T(128)S(1)} %pad_add_fusion.refs_0_, bf16[512,128]{1,0:T(8,128)(2,1)S(1)} %get-tuple-element.247.refs_5_.refs_3_.refs_1_, ...), custom_call_target="tpu_custom_call" | custom-call | flops 3000000000 | bytes 1 | tf_op jit(solution)/shard_map/pallas_call | solution.py:68
  147.8 1.7 %collective-permute-start.43 = (bf16[256,512]{1,0:T(8,128)(2,1)}, bf16[256,512]{1,0:T(8,128)(2,1)S(1)}, u32[]{:S(2)}, u32[]{:S(2)}) collective-permute-start(bf16[256,512]{1,0:T(8,128)(2,1)} %get-tuple-element.264), channel_id=1, source_target_pairs={{0,8},{8,0},{16,24},{24,16},{1,9},{9,1},{17,25},{25,17},{2,10},{10... | collective-permute-start | bytes 786440 | tf_op jit(solution)/shard_map/ppermute | solution.py:636
  149.9 1.0 shard_map.184
  150.9 1.4 collective-permute-start.45
  152.3 0.9 collective-permute-done.47.refs_2_
  153.2 1.1 shard_map.185
  154.3 4.1 %all-to-all-start.4 = ((f32[32,8,128]{2,1,0:T(8,128)}), f32[32,8,128]{2,1,0:T(8,128)S(1)}, u32[]{:S(2)}, u32[]{:S(2)}) async-start(f32[32,8,128]{2,1,0:T(8,128)} %get-tuple-element.291), calls=%async_computation.4 | async-start | bytes 262144 | tf_op jit(solution)/shard_map/all_to_all | solution.py:822
  158.4 0.7 copy.23
  159.2 1.1 collective-permute-done.45.refs_3_
  160.2 0.8 shard_map.182
  161.0 5.3 %all-to-all-done.4.refs_0_ = f32[32,8,128]{2,1,0:T(8,128)S(1)} async-done(((f32[32,8,128]{2,1,0:T(8,128)}), f32[32,8,128]{2,1,0:T(8,128)S(1)}, u32[]{:S(2)}, u32[]{:S(2)}) %all-to-all-start.4) | async-done | bytes 131104 | tf_op jit(solution)/shard_map/all_to_all | solution.py:822
  166.4 1.1 shard_map.186
  (83 shorter events, 10.7 us)
Async XLA Ops:
  0.6 6.3 %copy-start.5 = (bf16[4,8,8,512]{3,2,1,0:T(8,128)(2,1)S(1)}, bf16[4,8,8,512]{3,2,1,0:T(8,128)(2,1)}, u32[]{:S(2)}) copy-start(bf16[4,8,8,512]{3,2,1,0:T(8,128)(2,1)} %param.9) | copy-start | bytes 786436
  0.7 23.0 %copy-start.4 = (bf16[4,8,8,512]{3,2,1,0:T(8,128)(2,1)S(1)}, bf16[4,8,8,512]{3,2,1,0:T(8,128)(2,1)}, u32[]{:S(2)}) copy-start(bf16[4,8,8,512]{3,2,1,0:T(8,128)(2,1)} %param.11) | copy-start | bytes 786436
  0.7 23.0 %copy-start.7 = (s32[4,8,8]{2,1,0:T(8,128)S(1)}, s32[4,8,8]{2,1,0:T(8,128)}, u32[]{:S(2)}) copy-start(s32[4,8,8]{2,1,0:T(8,128)} %refs_6_.4) | copy-start | bytes 3076
  1.9 9.1 %collective-permute-start.2 = (bf16[9,64,128]{2,1,0:T(8,128)(2,1)S(1)}, bf16[9,64,128]{2,1,0:T(8,128)(2,1)S(1)}, u32[]{:S(2)}, u32[]{:S(2)}) collective-permute-start(bf16[9,64,128]{2,1,0:T(8,128)(2,1)S(1)} %get-tuple-element.156.refs_1_), channel_id=1, source_target_pairs={{0,3},{1,2},{2,1},{3,0},{4,7},{5,6},{6,5},{7,4},{8,11},{9,10},{10,... | collective-permute-start | bytes 442376 | tf_op jit(solution)/shard_map/ppermute | solution.py:627
  7.0 17.4 %collective-permute-start.5 = (bf16[256,512]{1,0:T(8,128)(2,1)S(1)}, bf16[256,512]{1,0:T(8,128)(2,1)S(1)}, u32[]{:S(2)}, u32[]{:S(2)}) collective-permute-start(bf16[256,512]{1,0:T(8,128)(2,1)S(1)} %bitcast.13), channel_id=1, source_target_pairs={{0,24},{8,16},{16,8},{24,0},{1,25},{9,17},{17,9},{25,1},{2,26},{10... | collective-permute-start | bytes 786440 | tf_op jit(solution)/shard_map/ppermute | solution.py:636
  9.4 15.0 %collective-permute-start.4 = (bf16[256,512]{1,0:T(8,128)(2,1)S(1)}, bf16[256,512]{1,0:T(8,128)(2,1)S(1)}, u32[]{:S(2)}, u32[]{:S(2)}) collective-permute-start(bf16[256,512]{1,0:T(8,128)(2,1)S(1)} %bitcast.14), channel_id=1, source_target_pairs={{0,16},{8,24},{16,0},{24,8},{1,17},{9,25},{17,1},{25,9},{2,18},{10... | collective-permute-start | bytes 786440 | tf_op jit(solution)/shard_map/ppermute | solution.py:636
  10.0 14.5 %collective-permute-start.3 = (bf16[256,512]{1,0:T(8,128)(2,1)S(1)}, bf16[256,512]{1,0:T(8,128)(2,1)S(1)}, u32[]{:S(2)}, u32[]{:S(2)}) collective-permute-start(bf16[256,512]{1,0:T(8,128)(2,1)S(1)} %bitcast.15), channel_id=1, source_target_pairs={{0,8},{8,0},{16,24},{24,16},{1,9},{9,1},{17,25},{25,17},{2,10},{10... | collective-permute-start | bytes 786440 | tf_op jit(solution)/shard_map/ppermute | solution.py:636
  10.5 9.1 %collective-permute-start.1 = (bf16[9,64,128]{2,1,0:T(8,128)(2,1)S(1)}, bf16[9,64,128]{2,1,0:T(8,128)(2,1)S(1)}, u32[]{:S(2)}, u32[]{:S(2)}) collective-permute-start(bf16[9,64,128]{2,1,0:T(8,128)(2,1)S(1)} %get-tuple-element.156.refs_1_), channel_id=1, source_target_pairs={{0,2},{1,3},{2,0},{3,1},{4,6},{5,7},{6,4},{7,5},{8,10},{9,11},{10,... | collective-permute-start | bytes 442376 | tf_op jit(solution)/shard_map/ppermute | solution.py:627
  10.9 10.5 %collective-permute-start = (bf16[9,64,128]{2,1,0:T(8,128)(2,1)S(1)}, bf16[9,64,128]{2,1,0:T(8,128)(2,1)S(1)}, u32[]{:S(2)}, u32[]{:S(2)}) collective-permute-start(bf16[9,64,128]{2,1,0:T(8,128)(2,1)S(1)} %get-tuple-element.156.refs_1_), channel_id=1, source_target_pairs={{0,1},{1,0},{2,3},{3,2},{4,5},{5,4},{6,7},{7,6},{8,9},{9,8},{10,11... | collective-permute-start | bytes 442376 | tf_op jit(solution)/shard_map/ppermute | solution.py:627
  17.8 21.4 %copy-start.6 = (f32[4,512]{1,0:T(4,128)S(1)}, f32[4,512]{1,0:T(4,128)}, u32[]{:S(2)}) copy-start(f32[4,512]{1,0:T(4,128)} %refs_4_.5) | copy-start | bytes 24580
  21.5 7.4 %collective-permute-start.11 = (bf16[9,64,128]{2,1,0:T(8,128)(2,1)S(1)}, bf16[9,64,128]{2,1,0:T(8,128)(2,1)S(1)}, u32[]{:S(2)}, u32[]{:S(2)}) collective-permute-start(bf16[9,64,128]{2,1,0:T(8,128)(2,1)S(1)} %get-tuple-element.181.refs_1_), channel_id=1, source_target_pairs={{0,3},{1,2},{2,1},{3,0},{4,7},{5,6},{6,5},{7,4},{8,11},{9,10},{10,... | collective-permute-start | bytes 442376 | tf_op jit(solution)/shard_map/ppermute | solution.py:627
  24.5 12.0 %collective-permute-start.6 = (bf16[848,128]{1,0:T(8,128)(2,1)S(1)}, bf16[848,128]{1,0:T(8,128)(2,1)S(1)}, u32[]{:S(2)}, u32[]{:S(2)}) collective-permute-start(bf16[848,128]{1,0:T(8,128)(2,1)S(1)} %get-tuple-element.169), channel_id=1, source_target_pairs={{0,8},{8,0},{16,24},{24,16},{1,9},{9,1},{17,25},{25,17},{2,10},{10... | collective-permute-start | bytes 651272 | tf_op jit(solution)/shard_map/ppermute | solution.py:636
  26.1 10.4 %collective-permute-start.7 = (bf16[848,128]{1,0:T(8,128)(2,1)S(1)}, bf16[848,128]{1,0:T(8,128)(2,1)S(1)}, u32[]{:S(2)}, u32[]{:S(2)}) collective-permute-start(bf16[848,128]{1,0:T(8,128)(2,1)S(1)} %get-tuple-element.170), channel_id=1, source_target_pairs={{0,16},{8,24},{16,0},{24,8},{1,17},{9,25},{17,1},{25,9},{2,18},{10... | collective-permute-start | bytes 651272 | tf_op jit(solution)/shard_map/ppermute | solution.py:636
  27.6 9.0 %collective-permute-start.8 = (bf16[848,128]{1,0:T(8,128)(2,1)S(1)}, bf16[848,128]{1,0:T(8,128)(2,1)S(1)}, u32[]{:S(2)}, u32[]{:S(2)}) collective-permute-start(bf16[848,128]{1,0:T(8,128)(2,1)S(1)} %get-tuple-element.171), channel_id=1, source_target_pairs={{0,24},{8,16},{16,8},{24,0},{1,25},{9,17},{17,9},{25,1},{2,26},{10... | collective-permute-start | bytes 651272 | tf_op jit(solution)/shard_map/ppermute | solution.py:636
  28.0 7.8 %collective-permute-start.10 = (bf16[9,64,128]{2,1,0:T(8,128)(2,1)S(1)}, bf16[9,64,128]{2,1,0:T(8,128)(2,1)S(1)}, u32[]{:S(2)}, u32[]{:S(2)}) collective-permute-start(bf16[9,64,128]{2,1,0:T(8,128)(2,1)S(1)} %get-tuple-element.181.refs_1_), channel_id=1, source_target_pairs={{0,2},{1,3},{2,0},{3,1},{4,6},{5,7},{6,4},{7,5},{8,10},{9,11},{10,... | collective-permute-start | bytes 442376 | tf_op jit(solution)/shard_map/ppermute | solution.py:627
  28.9 7.6 %collective-permute-start.9 = (bf16[9,64,128]{2,1,0:T(8,128)(2,1)S(1)}, bf16[9,64,128]{2,1,0:T(8,128)(2,1)S(1)}, u32[]{:S(2)}, u32[]{:S(2)}) collective-permute-start(bf16[9,64,128]{2,1,0:T(8,128)(2,1)S(1)} %get-tuple-element.181.refs_1_), channel_id=1, source_target_pairs={{0,1},{1,0},{2,3},{3,2},{4,5},{5,4},{6,7},{7,6},{8,9},{9,8},{10,11... | collective-permute-start | bytes 442376 | tf_op jit(solution)/shard_map/ppermute | solution.py:627
  37.1 2.1 %collective-permute-start.12 = (bf16[4,9,64,128]{3,2,1,0:T(8,128)(2,1)S(1)}, bf16[4,9,64,128]{3,2,1,0:T(8,128)(2,1)S(1)}, u32[]{:S(2)}, u32[]{:S(2)}) collective-permute-start(bf16[4,9,64,128]{3,2,1,0:T(8,128)(2,1)S(1)} %get-tuple-element.177.refs_6_), channel_id=1, source_target_pairs={{0,4},{4,0},{1,5},{5,1},{2,6},{6,2},{3,7},{7,3},{8,12},{12,8},{9,1... | collective-permute-start | bytes 1769480 | tf_op jit(solution)/shard_map/ppermute | solution.py:630
  42.5 14.1 %collective-permute-start.13 = (bf16[576,128]{1,0:T(8,128)(2,1)S(1)}, bf16[576,128]{1,0:T(8,128)(2,1)S(1)}, u32[]{:S(2)}, u32[]{:S(2)}) collective-permute-start(bf16[576,128]{1,0:T(8,128)(2,1)S(1)} %get-tuple-element.191), channel_id=1, source_target_pairs={{0,8},{8,0},{16,24},{24,16},{1,9},{9,1},{17,25},{25,17},{2,10},{10... | collective-permute-start | bytes 442376 | tf_op jit(solution)/shard_map/ppermute | solution.py:636
  44.1 12.5 %collective-permute-start.14 = (bf16[576,128]{1,0:T(8,128)(2,1)S(1)}, bf16[576,128]{1,0:T(8,128)(2,1)S(1)}, u32[]{:S(2)}, u32[]{:S(2)}) collective-permute-start(bf16[576,128]{1,0:T(8,128)(2,1)S(1)} %get-tuple-element.192), channel_id=1, source_target_pairs={{0,16},{8,24},{16,0},{24,8},{1,17},{9,25},{17,1},{25,9},{2,18},{10... | collective-permute-start | bytes 442376 | tf_op jit(solution)/shard_map/ppermute | solution.py:636
  45.6 11.0 %collective-permute-start.15 = (bf16[576,128]{1,0:T(8,128)(2,1)S(1)}, bf16[576,128]{1,0:T(8,128)(2,1)S(1)}, u32[]{:S(2)}, u32[]{:S(2)}) collective-permute-start(bf16[576,128]{1,0:T(8,128)(2,1)S(1)} %get-tuple-element.193), channel_id=1, source_target_pairs={{0,24},{8,16},{16,8},{24,0},{1,25},{9,17},{17,9},{25,1},{2,26},{10... | collective-permute-start | bytes 442376 | tf_op jit(solution)/shard_map/ppermute | solution.py:636
  57.6 12.6 %collective-permute-start.22 = (bf16[4,9,64,128]{3,2,1,0:T(8,128)(2,1)S(1)}, bf16[4,9,64,128]{3,2,1,0:T(8,128)(2,1)S(1)}, u32[]{:S(2)}, u32[]{:S(2)}) collective-permute-start(bf16[4,9,64,128]{3,2,1,0:T(8,128)(2,1)S(1)} %get-tuple-element.202.refs_9_), channel_id=1, source_target_pairs={{0,4},{4,0},{1,5},{5,1},{2,6},{6,2},{3,7},{7,3},{8,12},{12,8},{9,1... | collective-permute-start | bytes 1769480 | tf_op jit(solution)/shard_map/ppermute | solution.py:630
  57.8 6.0 %collective-permute-start.17 = (bf16[512,128]{1,0:T(8,128)(2,1)S(1)}, bf16[512,128]{1,0:T(8,128)(2,1)S(1)}, u32[]{:S(2)}, u32[]{:S(2)}) collective-permute-start(bf16[512,128]{1,0:T(8,128)(2,1)S(1)} %get-tuple-element.200.refs_1_), channel_id=1, source_target_pairs={{0,16},{8,24},{16,0},{24,8},{1,17},{9,25},{17,1},{25,9},{2,18},{10... | collective-permute-start | bytes 393224 | tf_op jit(solution)/shard_map/ppermute | solution.py:636
  58.9 6.3 %collective-permute-start.19 = (bf16[512,128]{1,0:T(8,128)(2,1)S(1)}, bf16[512,128]{1,0:T(8,128)(2,1)S(1)}, u32[]{:S(2)}, u32[]{:S(2)}) collective-permute-start(bf16[512,128]{1,0:T(8,128)(2,1)S(1)} %get-tuple-element.201.refs_5_), channel_id=1, source_target_pairs={{0,8},{8,0},{16,24},{24,16},{1,9},{9,1},{17,25},{25,17},{2,10},{10... | collective-permute-start | bytes 393224 | tf_op jit(solution)/shard_map/ppermute | solution.py:636
  60.8 7.2 %collective-permute-start.16 = (bf16[512,128]{1,0:T(8,128)(2,1)S(1)}, bf16[512,128]{1,0:T(8,128)(2,1)S(1)}, u32[]{:S(2)}, u32[]{:S(2)}) collective-permute-start(bf16[512,128]{1,0:T(8,128)(2,1)S(1)} %get-tuple-element.200.refs_1_), channel_id=1, source_target_pairs={{0,8},{8,0},{16,24},{24,16},{1,9},{9,1},{17,25},{25,17},{2,10},{10... | collective-permute-start | bytes 393224 | tf_op jit(solution)/shard_map/ppermute | solution.py:636
  60.9 7.1 %collective-permute-start.20 = (bf16[512,128]{1,0:T(8,128)(2,1)S(1)}, bf16[512,128]{1,0:T(8,128)(2,1)S(1)}, u32[]{:S(2)}, u32[]{:S(2)}) collective-permute-start(bf16[512,128]{1,0:T(8,128)(2,1)S(1)} %get-tuple-element.201.refs_5_), channel_id=1, source_target_pairs={{0,16},{8,24},{16,0},{24,8},{1,17},{9,25},{17,1},{25,9},{2,18},{10... | collective-permute-start | bytes 393224 | tf_op jit(solution)/shard_map/ppermute | solution.py:636
  63.8 6.4 %collective-permute-start.18 = (bf16[512,128]{1,0:T(8,128)(2,1)S(1)}, bf16[512,128]{1,0:T(8,128)(2,1)S(1)}, u32[]{:S(2)}, u32[]{:S(2)}) collective-permute-start(bf16[512,128]{1,0:T(8,128)(2,1)S(1)} %collective-permute-done.17.refs_3_), channel_id=1, source_target_pairs={{0,8},{8,0},{16,24},{24,16},{1,9},{9,1},{17,25},{25,17},{2,10},{10... | collective-permute-start | bytes 393224 | tf_op jit(solution)/shard_map/ppermute | solution.py:636
  65.2 5.0 %collective-permute-start.21 = (bf16[512,128]{1,0:T(8,128)(2,1)S(1)}, bf16[512,128]{1,0:T(8,128)(2,1)S(1)}, u32[]{:S(2)}, u32[]{:S(2)}) collective-permute-start(bf16[512,128]{1,0:T(8,128)(2,1)S(1)} %collective-permute-done.19.refs_6_), channel_id=1, source_target_pairs={{0,16},{8,24},{16,0},{24,8},{1,17},{9,25},{17,1},{25,9},{2,18},{10... | collective-permute-start | bytes 393224 | tf_op jit(solution)/shard_map/ppermute | solution.py:636
  73.5 8.7 %collective-permute-start.23 = (bf16[1024,256]{1,0:T(8,128)(2,1)S(1)}, bf16[1024,256]{1,0:T(8,128)(2,1)S(1)}, u32[]{:S(2)}, u32[]{:S(2)}) collective-permute-start(bf16[1024,256]{1,0:T(8,128)(2,1)S(1)} %get-tuple-element.211), channel_id=1, source_target_pairs={{0,4},{4,0},{1,5},{5,1},{2,6},{6,2},{3,7},{7,3},{8,12},{12,8},{9,1... | collective-permute-start | bytes 1572872 | tf_op jit(solution)/shard_map/ppermute | solution.py:630
  73.5 8.6 %collective-permute-start.24 = (bf16[1024,256]{1,0:T(8,128)(2,1)S(1)}, bf16[1024,256]{1,0:T(8,128)(2,1)S(1)}, u32[]{:S(2)}, u32[]{:S(2)}) collective-permute-start(bf16[1024,256]{1,0:T(8,128)(2,1)S(1)} %get-tuple-element.213), channel_id=1, source_target_pairs={{0,4},{4,0},{1,5},{5,1},{2,6},{6,2},{3,7},{7,3},{8,12},{12,8},{9,1... | collective-permute-start | bytes 1572872 | tf_op jit(solution)/shard_map/ppermute | solution.py:630
  82.2 9.7 %copy-start.3 = (bf16[4,9,64,128]{3,2,1,0:T(8,128)(2,1)S(1)}, bf16[4,9,64,128]{3,2,1,0:T(8,128)(2,1)}, u32[]{:S(2)}) copy-start(bf16[4,9,64,128]{3,2,1,0:T(8,128)(2,1)} %get-tuple-element.225.refs_9_) | copy-start | bytes 1769476
  91.9 14.1 %collective-permute-start.31 = (bf16[4,9,64,128]{3,2,1,0:T(8,128)(2,1)S(1)}, bf16[4,9,64,128]{3,2,1,0:T(8,128)(2,1)S(1)}, u32[]{:S(2)}, u32[]{:S(2)}) collective-permute-start(bf16[4,9,64,128]{3,2,1,0:T(8,128)(2,1)S(1)} %copy-done.3), channel_id=1, source_target_pairs={{0,4},{4,0},{1,5},{5,1},{2,6},{6,2},{3,7},{7,3},{8,12},{12,8},{9,1... | collective-permute-start | bytes 1769480 | tf_op jit(solution)/shard_map/ppermute | solution.py:630
  92.1 8.8 %collective-permute-start.32 = (bf16[1024,128]{1,0:T(8,128)(2,1)S(1)}, bf16[1024,128]{1,0:T(8,128)(2,1)S(1)}, u32[]{:S(2)}, u32[]{:S(2)}) collective-permute-start(bf16[1024,128]{1,0:T(8,128)(2,1)S(1)} %get-tuple-element.230), channel_id=1, source_target_pairs={{0,4},{4,0},{1,5},{5,1},{2,6},{6,2},{3,7},{7,3},{8,12},{12,8},{9,1... | collective-permute-start | bytes 786440 | tf_op jit(solution)/shard_map/ppermute | solution.py:630
  92.5 5.7 %collective-permute-start.26 = (bf16[512,128]{1,0:T(8,128)(2,1)S(1)}, bf16[512,128]{1,0:T(8,128)(2,1)S(1)}, u32[]{:S(2)}, u32[]{:S(2)}) collective-permute-start(bf16[512,128]{1,0:T(8,128)(2,1)S(1)} %get-tuple-element.223.refs_1_.refs_3_), channel_id=1, source_target_pairs={{0,16},{8,24},{16,0},{24,8},{1,17},{9,25},{17,1},{25,9},{2,18},{10... | collective-permute-start | bytes 393224 | tf_op jit(solution)/shard_map/ppermute | solution.py:636
  94.4 6.4 %collective-permute-start.28 = (bf16[512,128]{1,0:T(8,128)(2,1)S(1)}, bf16[512,128]{1,0:T(8,128)(2,1)S(1)}, u32[]{:S(2)}, u32[]{:S(2)}) collective-permute-start(bf16[512,128]{1,0:T(8,128)(2,1)S(1)} %get-tuple-element.224.refs_5_.refs_4_), channel_id=1, source_target_pairs={{0,8},{8,0},{16,24},{24,16},{1,9},{9,1},{17,25},{25,17},{2,10},{10... | collective-permute-start | bytes 393224 | tf_op jit(solution)/shard_map/ppermute | solution.py:636
  94.5 11.0 %collective-permute-start.25 = (bf16[512,128]{1,0:T(8,128)(2,1)S(1)}, bf16[512,128]{1,0:T(8,128)(2,1)S(1)}, u32[]{:S(2)}, u32[]{:S(2)}) collective-permute-start(bf16[512,128]{1,0:T(8,128)(2,1)S(1)} %get-tuple-element.223.refs_1_.refs_3_), channel_id=1, source_target_pairs={{0,8},{8,0},{16,24},{24,16},{1,9},{9,1},{17,25},{25,17},{2,10},{10... | collective-permute-start | bytes 393224 | tf_op jit(solution)/shard_map/ppermute | solution.py:636
  98.2 7.3 %collective-permute-start.29 = (bf16[512,128]{1,0:T(8,128)(2,1)S(1)}, bf16[512,128]{1,0:T(8,128)(2,1)S(1)}, u32[]{:S(2)}, u32[]{:S(2)}) collective-permute-start(bf16[512,128]{1,0:T(8,128)(2,1)S(1)} %get-tuple-element.224.refs_5_.refs_4_), channel_id=1, source_target_pairs={{0,16},{8,24},{16,0},{24,8},{1,17},{9,25},{17,1},{25,9},{2,18},{10... | collective-permute-start | bytes 393224 | tf_op jit(solution)/shard_map/ppermute | solution.py:636
  100.8 5.0 %collective-permute-start.27 = (bf16[512,128]{1,0:T(8,128)(2,1)S(1)}, bf16[512,128]{1,0:T(8,128)(2,1)S(1)}, u32[]{:S(2)}, u32[]{:S(2)}) collective-permute-start(bf16[512,128]{1,0:T(8,128)(2,1)S(1)} %collective-permute-done.26.refs_3_), channel_id=1, source_target_pairs={{0,8},{8,0},{16,24},{24,16},{1,9},{9,1},{17,25},{25,17},{2,10},{10... | collective-permute-start | bytes 393224 | tf_op jit(solution)/shard_map/ppermute | solution.py:636
  100.9 5.1 %collective-permute-start.30 = (bf16[512,128]{1,0:T(8,128)(2,1)S(1)}, bf16[512,128]{1,0:T(8,128)(2,1)S(1)}, u32[]{:S(2)}, u32[]{:S(2)}) collective-permute-start(bf16[512,128]{1,0:T(8,128)(2,1)S(1)} %collective-permute-done.28.refs_6_), channel_id=1, source_target_pairs={{0,16},{8,24},{16,0},{24,8},{1,17},{9,25},{17,1},{25,9},{2,18},{10... | collective-permute-start | bytes 393224 | tf_op jit(solution)/shard_map/ppermute | solution.py:636
  109.0 11.7 %collective-permute-start.33 = (bf16[832,128]{1,0:T(8,128)(2,1)S(1)}, bf16[832,128]{1,0:T(8,128)(2,1)S(1)}, u32[]{:S(2)}, u32[]{:S(2)}) collective-permute-start(bf16[832,128]{1,0:T(8,128)(2,1)S(1)} %get-tuple-element.238), channel_id=1, source_target_pairs={{0,8},{8,0},{16,24},{24,16},{1,9},{9,1},{17,25},{25,17},{2,10},{10... | collective-permute-start | bytes 638984 | tf_op jit(solution)/shard_map/ppermute | solution.py:636
  110.9 9.8 %collective-permute-start.34 = (bf16[832,128]{1,0:T(8,128)(2,1)S(1)}, bf16[832,128]{1,0:T(8,128)(2,1)S(1)}, u32[]{:S(2)}, u32[]{:S(2)}) collective-permute-start(bf16[832,128]{1,0:T(8,128)(2,1)S(1)} %get-tuple-element.239), channel_id=1, source_target_pairs={{0,16},{8,24},{16,0},{24,8},{1,17},{9,25},{17,1},{25,9},{2,18},{10... | collective-permute-start | bytes 638984 | tf_op jit(solution)/shard_map/ppermute | solution.py:636
  111.1 9.7 %collective-permute-start.35 = (bf16[832,128]{1,0:T(8,128)(2,1)S(1)}, bf16[832,128]{1,0:T(8,128)(2,1)S(1)}, u32[]{:S(2)}, u32[]{:S(2)}) collective-permute-start(bf16[832,128]{1,0:T(8,128)(2,1)S(1)} %get-tuple-element.240), channel_id=1, source_target_pairs={{0,24},{8,16},{16,8},{24,0},{1,25},{9,17},{17,9},{25,1},{2,26},{10... | collective-permute-start | bytes 638984 | tf_op jit(solution)/shard_map/ppermute | solution.py:636
  121.0 5.3 %collective-permute-start.36 = (bf16[1024,128]{1,0:T(8,128)(2,1)S(1)}, bf16[1024,128]{1,0:T(8,128)(2,1)S(1)}, u32[]{:S(2)}, u32[]{:S(2)}) collective-permute-start(bf16[1024,128]{1,0:T(8,128)(2,1)S(1)} %get-tuple-element.253), channel_id=1, source_target_pairs={{0,4},{4,0},{1,5},{5,1},{2,6},{6,2},{3,7},{7,3},{8,12},{12,8},{9,1... | collective-permute-start | bytes 786440 | tf_op jit(solution)/shard_map/ppermute | solution.py:630
  121.9 9.2 %collective-permute-start.40 = (bf16[576,128]{1,0:T(8,128)(2,1)S(1)}, bf16[576,128]{1,0:T(8,128)(2,1)S(1)}, u32[]{:S(2)}, u32[]{:S(2)}) collective-permute-start(bf16[576,128]{1,0:T(8,128)(2,1)S(1)} %get-tuple-element.259), channel_id=1, source_target_pairs={{0,1},{1,0},{2,3},{3,2},{4,5},{5,4},{6,7},{7,6},{8,9},{9,8},{10,11... | collective-permute-start | bytes 442376 | tf_op jit(solution)/shard_map/ppermute | solution.py:627
  122.5 14.0 %collective-permute-start.41 = (bf16[576,128]{1,0:T(8,128)(2,1)S(1)}, bf16[576,128]{1,0:T(8,128)(2,1)S(1)}, u32[]{:S(2)}, u32[]{:S(2)}) collective-permute-start(bf16[576,128]{1,0:T(8,128)(2,1)S(1)} %get-tuple-element.260), channel_id=1, source_target_pairs={{0,2},{1,3},{2,0},{3,1},{4,6},{5,7},{6,4},{7,5},{8,10},{9,11},{10,... | collective-permute-start | bytes 442376 | tf_op jit(solution)/shard_map/ppermute | solution.py:627
  123.0 13.5 %collective-permute-start.42 = (bf16[576,128]{1,0:T(8,128)(2,1)S(1)}, bf16[576,128]{1,0:T(8,128)(2,1)S(1)}, u32[]{:S(2)}, u32[]{:S(2)}) collective-permute-start(bf16[576,128]{1,0:T(8,128)(2,1)S(1)} %get-tuple-element.261), channel_id=1, source_target_pairs={{0,3},{1,2},{2,1},{3,0},{4,7},{5,6},{6,5},{7,4},{8,11},{9,10},{10,... | collective-permute-start | bytes 442376 | tf_op jit(solution)/shard_map/ppermute | solution.py:627
  128.9 7.5 %collective-permute-start.37 = (bf16[576,128]{1,0:T(8,128)(2,1)S(1)}, bf16[576,128]{1,0:T(8,128)(2,1)S(1)}, u32[]{:S(2)}, u32[]{:S(2)}) collective-permute-start(bf16[576,128]{1,0:T(8,128)(2,1)S(1)} %get-tuple-element.255), channel_id=1, source_target_pairs={{0,8},{8,0},{16,24},{24,16},{1,9},{9,1},{17,25},{25,17},{2,10},{10... | collective-permute-start | bytes 442376 | tf_op jit(solution)/shard_map/ppermute | solution.py:636
  130.9 6.6 %collective-permute-start.38 = (bf16[576,128]{1,0:T(8,128)(2,1)S(1)}, bf16[576,128]{1,0:T(8,128)(2,1)S(1)}, u32[]{:S(2)}, u32[]{:S(2)}) collective-permute-start(bf16[576,128]{1,0:T(8,128)(2,1)S(1)} %get-tuple-element.256), channel_id=1, source_target_pairs={{0,16},{8,24},{16,0},{24,8},{1,17},{9,25},{17,1},{25,9},{2,18},{10... | collective-permute-start | bytes 442376 | tf_op jit(solution)/shard_map/ppermute | solution.py:636
  131.1 7.8 %collective-permute-start.39 = (bf16[576,128]{1,0:T(8,128)(2,1)S(1)}, bf16[576,128]{1,0:T(8,128)(2,1)S(1)}, u32[]{:S(2)}, u32[]{:S(2)}) collective-permute-start(bf16[576,128]{1,0:T(8,128)(2,1)S(1)} %get-tuple-element.257), channel_id=1, source_target_pairs={{0,24},{8,16},{16,8},{24,0},{1,25},{9,17},{17,9},{25,1},{2,26},{10... | collective-permute-start | bytes 442376 | tf_op jit(solution)/shard_map/ppermute | solution.py:636
  139.4 11.4 %collective-permute-start.46 = (bf16[576,128]{1,0:T(8,128)(2,1)S(1)}, bf16[576,128]{1,0:T(8,128)(2,1)S(1)}, u32[]{:S(2)}, u32[]{:S(2)}) collective-permute-start(bf16[576,128]{1,0:T(8,128)(2,1)S(1)} %get-tuple-element.279), channel_id=1, source_target_pairs={{0,1},{1,0},{2,3},{3,2},{4,5},{5,4},{6,7},{7,6},{8,9},{9,8},{10,11... | collective-permute-start | bytes 442376 | tf_op jit(solution)/shard_map/ppermute | solution.py:627
  140.0 13.1 %collective-permute-start.47 = (bf16[576,128]{1,0:T(8,128)(2,1)S(1)}, bf16[576,128]{1,0:T(8,128)(2,1)S(1)}, u32[]{:S(2)}, u32[]{:S(2)}) collective-permute-start(bf16[576,128]{1,0:T(8,128)(2,1)S(1)} %get-tuple-element.280), channel_id=1, source_target_pairs={{0,2},{1,3},{2,0},{3,1},{4,6},{5,7},{6,4},{7,5},{8,10},{9,11},{10,... | collective-permute-start | bytes 442376 | tf_op jit(solution)/shard_map/ppermute | solution.py:627
  140.6 12.6 %collective-permute-start.48 = (bf16[576,128]{1,0:T(8,128)(2,1)S(1)}, bf16[576,128]{1,0:T(8,128)(2,1)S(1)}, u32[]{:S(2)}, u32[]{:S(2)}) collective-permute-start(bf16[576,128]{1,0:T(8,128)(2,1)S(1)} %get-tuple-element.281), channel_id=1, source_target_pairs={{0,3},{1,2},{2,1},{3,0},{4,7},{5,6},{6,5},{7,4},{8,11},{9,10},{10,... | collective-permute-start | bytes 442376 | tf_op jit(solution)/shard_map/ppermute | solution.py:627
  143.9 6.0 %copy-start = (f32[2,9,64,128]{3,2,1,0:T(8,128)S(1)}, f32[2,9,64,128]{3,2,1,0:T(8,128)}, u32[]{:S(2)}) copy-start(f32[2,9,64,128]{3,2,1,0:T(8,128)} %refs_1_.3) | copy-start | bytes 1769476
  143.9 6.0 %copy-start.1 = (f32[2,9,64,128]{3,2,1,0:T(8,128)S(1)}, f32[2,9,64,128]{3,2,1,0:T(8,128)}, u32[]{:S(2)}) copy-start(f32[2,9,64,128]{3,2,1,0:T(8,128)} %refs_5_.4) | copy-start | bytes 1769476
  143.9 6.0 %copy-start.2 = (f32[2,9,64,128]{3,2,1,0:T(8,128)S(1)}, f32[2,9,64,128]{3,2,1,0:T(8,128)}, u32[]{:S(2)}) copy-start(f32[2,9,64,128]{3,2,1,0:T(8,128)} %refs_6_.6) | copy-start | bytes 1769476
  147.8 11.4 %collective-permute-start.43 = (bf16[256,512]{1,0:T(8,128)(2,1)}, bf16[256,512]{1,0:T(8,128)(2,1)S(1)}, u32[]{:S(2)}, u32[]{:S(2)}) collective-permute-start(bf16[256,512]{1,0:T(8,128)(2,1)} %get-tuple-element.264), channel_id=1, source_target_pairs={{0,8},{8,0},{16,24},{24,16},{1,9},{9,1},{17,25},{25,17},{2,10},{10... | collective-permute-start | bytes 786440 | tf_op jit(solution)/shard_map/ppermute | solution.py:636
  149.5 9.7 %collective-permute-start.44 = (bf16[256,512]{1,0:T(8,128)(2,1)S(1)}, bf16[256,512]{1,0:T(8,128)(2,1)S(1)}, u32[]{:S(2)}, u32[]{:S(2)}) collective-permute-start(bf16[256,512]{1,0:T(8,128)(2,1)S(1)} %get-tuple-element.265), channel_id=1, source_target_pairs={{0,16},{8,24},{16,0},{24,8},{1,17},{9,25},{17,1},{25,9},{2,18},{10... | collective-permute-start | bytes 786440 | tf_op jit(solution)/shard_map/ppermute | solution.py:636
  150.9 9.4 %collective-permute-start.45 = (bf16[256,512]{1,0:T(8,128)(2,1)S(1)}, bf16[256,512]{1,0:T(8,128)(2,1)S(1)}, u32[]{:S(2)}, u32[]{:S(2)}) collective-permute-start(bf16[256,512]{1,0:T(8,128)(2,1)S(1)} %get-tuple-element.266), channel_id=1, source_target_pairs={{0,24},{8,16},{16,8},{24,0},{1,25},{9,17},{17,9},{25,1},{2,26},{10... | collective-permute-start | bytes 786440 | tf_op jit(solution)/shard_map/ppermute | solution.py:636
  154.3 12.1 %copy-start.8 = (f32[4,512]{1,0:T(4,128)S(1)}, f32[4,512]{1,0:T(4,128)}, u32[]{:S(2)}) copy-start(f32[4,512]{1,0:T(4,128)} %refs_5_.5) | copy-start | bytes 24580
  154.3 12.1 %copy-start.9 = (f32[4,512]{1,0:T(4,128)S(1)}, f32[4,512]{1,0:T(4,128)}, u32[]{:S(2)}) copy-start(f32[4,512]{1,0:T(4,128)} %refs_6_.7) | copy-start | bytes 24580
  154.3 12.1 %all-to-all-start.4 = ((f32[32,8,128]{2,1,0:T(8,128)}), f32[32,8,128]{2,1,0:T(8,128)S(1)}, u32[]{:S(2)}, u32[]{:S(2)}) async-start(f32[32,8,128]{2,1,0:T(8,128)} %get-tuple-element.291), calls=%async_computation.4 | async-start | bytes 262144 | tf_op jit(solution)/shard_map/all_to_all | solution.py:822

commit v6 on v5

--- a/solution.py
+++ b/solution.py
@@ -203,9 +203,11 @@
     for t, block in enumerate(blocks):
         s = at[1] ^ t
         for a in range(z.Z):
-            row = pl.multiple_of(a * z.L + s * z.IB, z.IB)
+            pieces = isinstance(block, (list, tuple))
+            row = pl.multiple_of((at[0] ^ a if pieces else a) * z.L + s * z.IB, z.IB)
             for k in range(z.K):
-                wcat[pl.ds(row, z.IB), k * z.LP : k * z.LP + z.L] = block[a, k]
+                part = block[a][k * z.IB : (k + 1) * z.IB, :] if pieces else block[a, k]
+                wcat[pl.ds(row, z.IB), k * z.LP : k * z.LP + z.L] = part
 
 
 def split_channels(z, at, slices, outs, rows):
@@ -220,10 +222,15 @@
 
 def first_conv(z, at, np_ref, *refs):
     xs, refs = refs[: z.Q], refs[z.Q :]
-    blocks, refs = refs[: z.S], refs[z.S :]
-    hw_ref, refs = refs[0], refs[1:]
+    blocks = [refs[t * z.Q : (t + 1) * z.Q] for t in range(z.S)]
+    refs = refs[z.S * z.Q :]
     outs, refs = refs[: z.S], refs[z.S :]
-    z_ref, slice_ref, par_ref, stats_ref, far_w, wcat, y_ref, sem = refs
+    z_ref, slice_ref, par_ref, hw_ref, stats_ref, far_w, wcat, y_ref, sem = refs
+    for m in range(z.Q):
+        for n in range(z.n_own):
+            row = z.K * z.IB + 2 * n
+            two = jnp.broadcast_to(blocks[0][m][row : row + 2, 0:1].astype(F32), (2, LANES))
+            hw_ref[(at[0] ^ m) * z.n_own + n] = jnp.concatenate([two, jnp.zeros((6, LANES), F32)], axis=0)
     fill_kernels(z, at, blocks, wcat)
     copy = pltpu.make_async_copy(wcat, far_w, sem)
     copy.start()
@@ -319,8 +326,8 @@
 
 
 def hidden(z, at, z_ref, all_ref, hw_ref, par_ref, *refs):
-    parts, (a_ref, b_ref, sum_ref, kernel_ref) = refs[: z.Q], refs[z.Q :]
-    unpick(z, at, *parts, kernel_ref)
+    parts, (a_ref, b_ref, sum_ref, kernel_ref, map_ref) = refs[: z.Q], refs[z.Q :]
+    unpick(z, at, *parts, kernel_ref, map_ref)
     mean, inv, count = merged(z, all_ref)
     keep(sum_ref, [mean, inv, count])
     gain, shift = par_ref[0:1, :], par_ref[1:2, :]
@@ -566,11 +573,10 @@
     trust_ref[...] = trust
 
 
-def pick(z, more, at, *refs):
+def pick(z, first, at, *refs):
     parts, refs = refs[: z.Z], refs[z.Z :]
-    map_ref = None
-    if more == "map":
-        map_ref, valid_ref, refs = refs[0], refs[1], refs[2:]
+    if first:
+        valid_ref, outs, hold = refs[0], refs[1:-1], refs[-1]
         rows = []
         for n in range(z.n_own):
             valid = valid_ref[n].astype(F32)
@@ -579,44 +585,36 @@
             rows += [jnp.broadcast_to(tall, (1, z.L)), jnp.broadcast_to(wide, (1, z.L))]
         rows.append(jnp.zeros((z.extra - len(rows), z.L), F32))
         sizes = jnp.concatenate(rows, axis=0).astype(BF16)
-    if more == "keep":
-        far_ref, outs, (hold, sem) = refs[0], refs[1:-2], refs[-2:]
     else:
-        outs, hold = refs[:-1], refs[-1]
+        map_ref, far_ref, outs, (hold, sem) = refs[0], refs[1], refs[2:-2], refs[-2:]
     for m in range(z.Z):
         hold[at[2] ^ m] = parts[m][...]
-    if more == "keep":
+    if not first:
         copy = pltpu.make_async_copy(hold, far_ref, sem)
         copy.start()
     for m in range(z.Q):
         for k in range(z.K):
             outs[m][k * z.IB : (k + 1) * z.IB, :] = hold[at[0] ^ m, k]
-        if map_ref is not None:
-            for slot in range(z.Q):
-
-                @pl.when((at[0] ^ m) == slot)
-                def _(m=m, slot=slot):
-                    outs[m][z.K * z.IB : z.K * z.IB + z.own, :] = map_ref[:, slot * z.L : (slot + 1) * z.L]
-
-            outs[m][z.K * z.IB + z.own :, :] = sizes
-
-    if more == "keep":
+        if first:
+            outs[m][z.K * z.IB :, :] = sizes
+            continue
+        for slot in range(z.Q):
+
+            @pl.when((at[0] ^ m) == slot)
+            def _(m=m, slot=slot):
+                outs[m][z.K * z.IB :, :] = map_ref[:, slot * z.L : (slot + 1) * z.L]
+
+    if not first:
         copy.wait()
 
 
 def unpick(z, at, *refs):
-    parts, refs = refs[: z.Q], refs[z.Q :]
+    parts, (out_ref, map_ref) = refs[: z.Q], refs[z.Q :]
     for m in range(z.Q):
         q = at[0] ^ m
         for k in range(z.K):
-            refs[0][q, k] = parts[m][k * z.IB : (k + 1) * z.IB, :]
-        if len(refs) > 1:
-            start = z.K * z.IB
-            refs[1][pl.ds(pl.multiple_of(q * z.own, z.own), z.own), :] = parts[m][start : start + z.own, :]
-            for n in range(z.n_own):
-                row = start + z.own + 2 * n
-                two = jnp.broadcast_to(parts[m][row : row + 2, 0:1].astype(F32), (2, LANES))
-                refs[2][q * z.n_own + n] = jnp.concatenate([two, jnp.zeros((6, LANES), F32)], axis=0)
+            out_ref[q, k] = parts[m][k * z.IB : (k + 1) * z.IB, :]
+        map_ref[pl.ds(pl.multiple_of(q * z.own, z.own), z.own), :] = parts[m][z.K * z.IB :, :]
 
 
 def shards(z, images, masks, cotangent, weights, first, second, params, p_first, p_second):
@@ -665,48 +663,44 @@
     one, low_two = together((one, low_two))
     hold = pltpu.VMEM((z.Z, *piece), BF16)
     picked = call(
-        functools.partial(pick, z, "map"),
-        [near((z.sent, z.L), BF16)] * z.Q,
-        (at, *one, cot_rows, masks),
+        functools.partial(pick, z, True),
+        [near((z.K * z.IB + z.extra, z.L), BF16)] * z.Q,
+        (at, *one, masks),
         [hold],
     )
     picked, xs = together((picked, xs))
     two = [over_z(low_two, m) for m in range(z.Z)]
-    picked, two = together(([over_q(picked[m], m) for m in range(z.Q)], two))
-    front_one, cots, hw = call(
-        functools.partial(unpick, z),
-        [blocks, near(GL, BF16), near((z.n_group, 8, LANES))],
-        (at, *picked),
-    )
+    front_one, two = together(([over_q(picked[m], m) for m in range(z.Q)], two))
     keep = away((z.Z, *piece), BF16)
     keep_two, *picked = call(
-        functools.partial(pick, z, "keep"),
-        [keep] + [near((z.K * z.IB, z.L), BF16)] * z.Q,
-        (at, *two),
+        functools.partial(pick, z, False),
+        [keep] + [near((z.K * z.IB + rows, z.L), BF16)] * z.Q,
+        (at, *two, cot_rows),
         [hold, pltpu.SemaphoreType.DMA],
         raw=(keep,),
     )
     w_far = away((z.C, z.K * z.LP), BF16)
-    *x_parts, z1, x_slice, slice_params, stats, w_far = call(
+    *x_parts, z1, x_slice, slice_params, hw, stats, w_far = call(
         functools.partial(first_conv, z),
         [near((z.G, z.Q * z.IB), BF16)] * z.S
         + [
             near(GL),
             near(GL, BF16),
             near((4, z.L)),
+            near((z.n_group, 8, LANES)),
             stat,
             w_far,
         ],
-        (at, params, *xs, *share(front_one), hw),
+        (at, params, *xs, *[over_s(v, t) for t in range(z.S) for v in front_one]),
         conv_scratch + [pltpu.SemaphoreType.DMA],
         limit=16,
         raw=(w_far,),
     )
     stats, picked = together((stats, picked))
     stats, picked = together((sharers(stats), [over_q(picked[m], m) for m in range(z.Q)]))
-    ha, hb, sum_one, front_two = call(
+    ha, hb, sum_one, front_two, cots = call(
         functools.partial(hidden, z),
-        [near(HL, BF16), near(HL, BF16), near((8, z.L)), blocks],
+        [near(HL, BF16), near(HL, BF16), near((8, z.L)), blocks, near(GL, BF16)],
         (at, z1, stats, hw, slice_params, *picked),
     )
     hs = gather(ha, hb)

time: 168 us -> 167 us (level)
  waiting for transfers between devices: 30.9 us -> 37 us
  starting transfers between devices: 69 us -> 64.7 us
  blocking collectives: 35 us -> 32.6 us
    ppermute x12, starting transfers between devices: 27.3 us -> 20.5 us  [over_z(): return lax.ppermute(v, 'z', [(i, i ^ m) for i in range(z.Z)]) if m else v]
    ppermute x12, waiting for transfers between devices: 13.1 us -> 17.7 us  [over_z(): return lax.ppermute(v, 'z', [(i, i ^ m) for i in range(z.Z)]) if m else v]
    all_to_all x4, blocking collectives: 35 us -> 32.6 us  [sharers(): return lax.all_to_all(v, ('s', 'z'), 0, 0)]
    ppermute x30, waiting for transfers between devices: 12 us -> 14.2 us  [over_q(): return lax.ppermute(v, 'q', [(i, i ^ m) for i in range(z.Q)]) if m else v]
    ppermute x30, starting transfers between devices: 36 us -> 37.8 us  [over_q(): return lax.ppermute(v, 'q', [(i, i ^ m) for i in range(z.Q)]) if m else v]
    pallas_call x17 -> x16, Pallas kernels: 27.6 us -> 26.8 us  [call(): pl.pallas_call(run, out_shape=out_shape, in_specs=[pl.BlockSpec(memory_sp...]
  transfers between devices with their start and end apart: 50 -> 53, of which waited for: 20 -> 20; matrix products, arithmetic and copies ran while one was open for 0% -> 0% of each run, Pallas kernels for 9% -> 9%
where the time goes in v6:
time: 167 us; the launch traced here: 166 us
  starting transfers between devices  64.7 us (39%)
  waiting for transfers between devices  37 us (22%)
  blocking collectives  32.6 us (20%)
  Pallas kernels  28.9 us (17%)
    ppermute x30, starting transfers between devices, over_q(): return lax.ppermute(v, 'q', [(i, i ^ m) for i in range(z.Q)]) if m else v  37.8 us
    all_to_all x4, blocking collectives, sharers(): return lax.all_to_all(v, ('s', 'z'), 0, 0)  32.6 us
    pallas_call x16, Pallas kernels, call(): pl.pallas_call(run, out_shape=out_shape, in_specs=[pl.BlockSpec(memory_sp...  26.8 us
    ppermute x12, starting transfers between devices, over_z(): return lax.ppermute(v, 'z', [(i, i ^ m) for i in range(z.Z)]) if m else v  20.5 us
    ppermute x12, waiting for transfers between devices, over_z(): return lax.ppermute(v, 'z', [(i, i ^ m) for i in range(z.Z)]) if m else v  17.7 us
    ppermute x30, waiting for transfers between devices, over_q(): return lax.ppermute(v, 'q', [(i, i ^ m) for i in range(z.Q)]) if m else v  14.2 us
    all_to_all x1, waiting for transfers between devices, shards(): stats = lax.all_to_all(stats, ('s', 'q', 'z'), 0, 0)  5.13 us
    all_to_all x1, starting transfers between devices, shards(): stats = lax.all_to_all(stats, ('s', 'q', 'z'), 0, 0)  3.9 us
  transfers between devices with their start and end apart: 53, of which 20 were waited for; matrix products, arithmetic and copies ran while one was open for 0% of the time, Pallas kernels for 9%

profile of v6, /device:TPU:0, one launch (start us, length us, event | category | flops | bytes accessed | tf_op | source)
XLA Modules:
  0.0 166.1 jit_solution(4818680037645152595)
XLA Ops:
  0.7 1.2 convert.4
  1.9 5.1 %collective-permute-start.2 = (bf16[9,64,128]{2,1,0:T(8,128)(2,1)S(1)}, bf16[9,64,128]{2,1,0:T(8,128)(2,1)S(1)}, u32[]{:S(2)}, u32[]{:S(2)}) collective-permute-start(bf16[9,64,128]{2,1,0:T(8,128)(2,1)S(1)} %get-tuple-element.155.refs_1_), channel_id=1, source_target_pairs={{0,3},{1,2},{2,1},{3,0},{4,7},{5,6},{6,5},{7,4},{8,11},{9,10},{10,... | collective-permute-start | bytes 442376 | tf_op jit(solution)/shard_map/ppermute | solution.py:625
  7.6 2.6 %collective-permute-start.5 = (bf16[256,512]{1,0:T(8,128)(2,1)S(1)}, bf16[256,512]{1,0:T(8,128)(2,1)S(1)}, u32[]{:S(2)}, u32[]{:S(2)}) collective-permute-start(bf16[256,512]{1,0:T(8,128)(2,1)S(1)} %bitcast.13), channel_id=1, source_target_pairs={{0,24},{8,16},{16,8},{24,0},{1,25},{9,17},{17,9},{25,1},{2,26},{10... | collective-permute-start | bytes 786440 | tf_op jit(solution)/shard_map/ppermute | solution.py:634
  10.8 1.0 collective-permute-done.2.refs_4_
  11.8 1.7 %collective-permute-start.3 = (bf16[256,512]{1,0:T(8,128)(2,1)S(1)}, bf16[256,512]{1,0:T(8,128)(2,1)S(1)}, u32[]{:S(2)}, u32[]{:S(2)}) collective-permute-start(bf16[256,512]{1,0:T(8,128)(2,1)S(1)} %bitcast.15), channel_id=1, source_target_pairs={{0,8},{8,0},{16,24},{24,16},{1,9},{9,1},{17,25},{25,17},{2,10},{10... | collective-permute-start | bytes 786440 | tf_op jit(solution)/shard_map/ppermute | solution.py:634
  13.5 6.0 %collective-permute-done.1.refs_3_ = bf16[9,64,128]{2,1,0:T(8,128)(2,1)S(1)} collective-permute-done((bf16[9,64,128]{2,1,0:T(8,128)(2,1)S(1)}, bf16[9,64,128]{2,1,0:T(8,128)(2,1)S(1)}, u32[]{:S(2)}, u32[]{:S(2)}) %collective-permute-start.1) | collective-permute-done | bytes 147488 | tf_op jit(solution)/shard_map/ppermute | solution.py:625
  19.5 2.8 %collective-permute-start.11 = (bf16[9,64,128]{2,1,0:T(8,128)(2,1)S(1)}, bf16[9,64,128]{2,1,0:T(8,128)(2,1)S(1)}, u32[]{:S(2)}, u32[]{:S(2)}) collective-permute-start(bf16[9,64,128]{2,1,0:T(8,128)(2,1)S(1)} %get-tuple-element.178.refs_1_), channel_id=1, source_target_pairs={{0,3},{1,2},{2,1},{3,0},{4,7},{5,6},{6,5},{7,4},{8,11},{9,10},{10,... | collective-permute-start | bytes 442376 | tf_op jit(solution)/shard_map/ppermute | solution.py:625
  22.3 0.6 shard_map.168
  23.0 1.6 collective-permute-start.6
  24.6 1.5 collective-permute-start.7
  26.6 3.0 %collective-permute-start.10 = (bf16[9,64,128]{2,1,0:T(8,128)(2,1)S(1)}, bf16[9,64,128]{2,1,0:T(8,128)(2,1)S(1)}, u32[]{:S(2)}, u32[]{:S(2)}) collective-permute-start(bf16[9,64,128]{2,1,0:T(8,128)(2,1)S(1)} %get-tuple-element.178.refs_1_), channel_id=1, source_target_pairs={{0,2},{1,3},{2,0},{3,1},{4,6},{5,7},{6,4},{7,5},{8,10},{9,11},{10,... | collective-permute-start | bytes 442376 | tf_op jit(solution)/shard_map/ppermute | solution.py:625
  29.6 4.8 %collective-permute-done.10.refs_3_ = bf16[9,64,128]{2,1,0:T(8,128)(2,1)S(1)} collective-permute-done((bf16[9,64,128]{2,1,0:T(8,128)(2,1)S(1)}, bf16[9,64,128]{2,1,0:T(8,128)(2,1)S(1)}, u32[]{:S(2)}, u32[]{:S(2)}) %collective-permute-start.10) | collective-permute-done | bytes 147488 | tf_op jit(solution)/shard_map/ppermute | solution.py:625
  34.4 1.1 collective-permute-done.9.refs_2_
  36.6 1.4 shard_map.170
  38.1 3.3 %shard_map.169 = (bf16[1024,256]{1,0:T(8,128)(2,1)S(1)}, bf16[1024,256]{1,0:T(8,128)(2,1)S(1)}, f32[1024,128]{1,0:T(8,128)S(1)}, bf16[1024,128]{1,0:T(8,128)(2,1...) custom-call(s32[3]{0:T(128)S(1)} %pad_add_fusion.refs_0_, ...), custom_call_target="tpu_custom_call" | custom-call | flops 1 | bytes 1 | tf_op jit(solution)/shard_map/pallas_call | solution.py:68
  41.4 2.5 %collective-permute-start.16 = (bf16[832,128]{1,0:T(8,128)(2,1)S(1)}, bf16[832,128]{1,0:T(8,128)(2,1)S(1)}, u32[]{:S(2)}, u32[]{:S(2)}) collective-permute-start(bf16[832,128]{1,0:T(8,128)(2,1)S(1)} %get-tuple-element.188), channel_id=1, source_target_pairs={{0,8},{8,0},{16,24},{24,16},{1,9},{9,1},{17,25},{25,17},{2,10},{10... | collective-permute-start | bytes 638984 | tf_op jit(solution)/shard_map/ppermute | solution.py:634
  43.8 1.5 collective-permute-start.17
  45.4 8.1 %all_to_all.25.refs_2_ = f32[8,8,128]{2,1,0:T(8,128)S(1)} all-to-all(f32[8,8,128]{2,1,0:T(8,128)S(1)} %get-tuple-element.186), channel_id=1, replica_groups=mesh['ha'=2,'wa'=4,'ba'=4] {'wa':(2)2,'ba'}, dimensions={0} | all-to-all | bytes 65536 | tf_op jit(solution)/shard_map/all_to_all | solution.py:631
  53.5 1.6 collective-permute-done.18.refs_8_
  55.2 1.0 shard_map.171
  56.2 1.6 collective-permute-start.20
  57.8 1.7 %collective-permute-start.22 = (bf16[512,128]{1,0:T(8,128)(2,1)S(1)}, bf16[512,128]{1,0:T(8,128)(2,1)S(1)}, u32[]{:S(2)}, u32[]{:S(2)}) collective-permute-start(bf16[512,128]{1,0:T(8,128)(2,1)S(1)} %get-tuple-element.199.refs_5_), channel_id=1, source_target_pairs={{0,8},{8,0},{16,24},{24,16},{1,9},{9,1},{17,25},{25,17},{2,10},{10... | collective-permute-start | bytes 393224 | tf_op jit(solution)/shard_map/ppermute | solution.py:634
  60.4 1.9 %collective-permute-done.20.refs_3_ = bf16[512,128]{1,0:T(8,128)(2,1)S(1)} collective-permute-done((bf16[512,128]{1,0:T(8,128)(2,1)S(1)}, bf16[512,128]{1,0:T(8,128)(2,1)S(1)}, u32[]{:S(2)}, u32[]{:S(2)}) %collective-permute-start.20) | collective-permute-done | bytes 131104 | tf_op jit(solution)/shard_map/ppermute | solution.py:634
  62.2 1.7 %collective-permute-start.21 = (bf16[512,128]{1,0:T(8,128)(2,1)S(1)}, bf16[512,128]{1,0:T(8,128)(2,1)S(1)}, u32[]{:S(2)}, u32[]{:S(2)}) collective-permute-start(bf16[512,128]{1,0:T(8,128)(2,1)S(1)} %collective-permute-done.20.refs_3_), channel_id=1, source_target_pairs={{0,8},{8,0},{16,24},{24,16},{1,9},{9,1},{17,25},{25,17},{2,10},{10... | collective-permute-start | bytes 393224 | tf_op jit(solution)/shard_map/ppermute | solution.py:634
  64.1 1.6 collective-permute-start.24
  65.8 1.2 collective-permute-done.19.refs_2_
  67.0 2.0 %collective-permute-done.21.refs_4_ = bf16[512,128]{1,0:T(8,128)(2,1)S(1)} collective-permute-done((bf16[512,128]{1,0:T(8,128)(2,1)S(1)}, bf16[512,128]{1,0:T(8,128)(2,1)S(1)}, u32[]{:S(2)}, u32[]{:S(2)}) %collective-permute-start.21) | collective-permute-done | bytes 131104 | tf_op jit(solution)/shard_map/ppermute | solution.py:634
  69.1 3.3 %shard_map.172 = (bf16[1024,256]{1,0:T(8,128)(2,1)S(1)}, bf16[1024,256]{1,0:T(8,128)(2,1)S(1)}, f32[1024,128]{1,0:T(8,128)S(1)}, f32[8,8,128]{2,1,0:T(8,128)S(1)}) custom-call(s32[3]{0:T(128)S(1)} %pad_add_fusion.refs_0_, bf16[512,128]{1,0:T(8,128)(2,1)S(1)} %get-tuple-element.198.refs_1_, bf16[512,128]{1,0:T(8,128)(2,1)S(1)} %collective-permute-done.19.refs_2_, ...), custom_call_target="tpu_custom_call" | custom-call | flops 1 | bytes 1 | tf_op jit(solution)/shard_map/pallas_call | solution.py:68
  73.0 8.1 %all_to_all.26.refs_2_ = f32[8,8,128]{2,1,0:T(8,128)S(1)} all-to-all(f32[8,8,128]{2,1,0:T(8,128)S(1)} %get-tuple-element.207), channel_id=1, replica_groups=mesh['ha'=2,'wa'=4,'ba'=4] {'wa':(2)2,'ba'}, dimensions={0} | all-to-all | bytes 65536 | tf_op jit(solution)/shard_map/all_to_all | solution.py:631
  81.1 1.3 shard_map.173
  82.4 8.2 %all_to_all.27.refs_3_ = f32[8,8,128]{2,1,0:T(8,128)S(1)} all-to-all(f32[8,8,128]{2,1,0:T(8,128)S(1)} %get-tuple-element.217), channel_id=1, replica_groups=mesh['ha'=2,'wa'=4,'ba'=4] {'wa':(2)2,'ba'}, dimensions={0} | all-to-all | bytes 65536 | tf_op jit(solution)/shard_map/all_to_all | solution.py:631
  91.4 1.6 collective-permute-start.29
  93.6 1.5 collective-permute-start.28
  95.1 1.9 %collective-permute-done.29.refs_3_ = bf16[512,128]{1,0:T(8,128)(2,1)S(1)} collective-permute-done((bf16[512,128]{1,0:T(8,128)(2,1)S(1)}, bf16[512,128]{1,0:T(8,128)(2,1)S(1)}, u32[]{:S(2)}, u32[]{:S(2)}) %collective-permute-start.29) | collective-permute-done | bytes 131104 | tf_op jit(solution)/shard_map/ppermute | solution.py:634
  96.9 1.6 collective-permute-start.32
  98.6 0.9 collective-permute-done.31.refs_6_
  100.0 1.5 collective-permute-start.33
  101.5 2.6 %shard_map.176 = (bf16[832,128]{1,0:T(8,128)(2,1)S(1)}, bf16[832,128]{1,0:T(8,128)(2,1)S(1)}, bf16[832,128]{1,0:T(8,128)(2,1)S(1)}, bf16[832,128]{1,0:T(8,128)(2,1)S(1)}) custom-call(s32[3]{0:T(128)S(1)} %pad_add_fusion.refs_0_, bf16[1024,256]{1,0:T(8,128)(2,1)S(1)} %get-tuple-element.226.refs_1_, bf16[1024,256]{1,0:T(8,128)(2,1)S(1)} %collective-permute-done.27.refs_2_, ...), custom_call_target="tpu_custom_call" | custom-call | flops 3000000000 | bytes 1 | tf_op jit(solution)/shard_map/pallas_call | solution.py:68
  105.0 3.0 %shard_map.175 = (f32[1024,128]{1,0:T(8,128)S(1)}, f32[8,8,128]{2,1,0:T(8,128)S(1)}) custom-call(s32[3]{0:T(128)S(1)} %pad_add_fusion.refs_0_, bf16[512,128]{1,0:T(8,128)(2,1)S(1)} %get-tuple-element.221.refs_1_.refs_3_, bf16[512,128]{1,0:T(8,128)(2,1)S(1)} %collective-permute-done.28.refs_2_, bf16[512,128]{1,0:T(8,128)(2,1)S(1)} %collective-permute-done.29.refs_3_, ...), custom_call_target="tpu_custom_call" | custom-call | flops 1 | bytes 1 | tf_op jit(solution)/shard_map/pallas_call | solution.py:68
  108.0 1.5 collective-permute-start.36
  109.9 1.6 collective-permute-start.38
  111.6 8.1 %all_to_all.28.refs_3_ = f32[8,8,128]{2,1,0:T(8,128)S(1)} all-to-all(f32[8,8,128]{2,1,0:T(8,128)S(1)} %get-tuple-element.234), channel_id=1, replica_groups=mesh['ha'=2,'wa'=4,'ba'=4] {'wa':(2)2,'ba'}, dimensions={0} | all-to-all | bytes 65536 | tf_op jit(solution)/shard_map/all_to_all | solution.py:631
  120.2 0.7 shard_map.178
  121.9 3.4 %collective-permute-start.45 = (bf16[576,128]{1,0:T(8,128)(2,1)S(1)}, bf16[576,128]{1,0:T(8,128)(2,1)S(1)}, u32[]{:S(2)}, u32[]{:S(2)}) collective-permute-start(bf16[576,128]{1,0:T(8,128)(2,1)S(1)} %get-tuple-element.259), channel_id=1, source_target_pairs={{0,3},{1,2},{2,1},{3,0},{4,7},{5,6},{6,5},{7,4},{8,11},{9,10},{10,... | collective-permute-start | bytes 442376 | tf_op jit(solution)/shard_map/ppermute | solution.py:625
  125.4 2.6 %shard_map.179 = (bf16[576,128]{1,0:T(8,128)(2,1)S(1)}, bf16[576,128]{1,0:T(8,128)(2,1)S(1)}, bf16[576,128]{1,0:T(8,128)(2,1)S(1)}, bf16[576,128]{1,0:T(8,128)(2,1)S(1)}) custom-call(s32[3]{0:T(128)S(1)} %pad_add_fusion.refs_0_, bf16[1024,256]{1,0:T(8,128)(2,1)S(1)} %get-tuple-element.249.refs_1_, bf16[1024,256]{1,0:T(8,128)(2,1)S(1)} %collective-permute-done.26.refs_2_, ...), custom_call_target="tpu_custom_call" | custom-call | flops 3000000000 | bytes 1 | tf_op jit(solution)/shard_map/pallas_call | solution.py:68
  128.0 1.5 collective-permute-start.40
  129.9 1.6 collective-permute-start.42
  131.5 3.9 %collective-permute-done.44.refs_2_ = bf16[576,128]{1,0:T(8,128)(2,1)S(1)} collective-permute-done((bf16[576,128]{1,0:T(8,128)(2,1)S(1)}, bf16[576,128]{1,0:T(8,128)(2,1)S(1)}, u32[]{:S(2)}, u32[]{:S(2)}) %collective-permute-start.44) | collective-permute-done | bytes 147488 | tf_op jit(solution)/shard_map/ppermute | solution.py:625
  135.4 0.7 collective-permute-done.41.refs_3_
  136.1 1.6 collective-permute-done.42.refs_4_
  138.3 0.7 collective-permute-start.49
  139.4 3.3 %collective-permute-start.51 = (bf16[576,128]{1,0:T(8,128)(2,1)S(1)}, bf16[576,128]{1,0:T(8,128)(2,1)S(1)}, u32[]{:S(2)}, u32[]{:S(2)}) collective-permute-start(bf16[576,128]{1,0:T(8,128)(2,1)S(1)} %get-tuple-element.279), channel_id=1, source_target_pairs={{0,3},{1,2},{2,1},{3,0},{4,7},{5,6},{6,5},{7,4},{8,11},{9,10},{10,... | collective-permute-start | bytes 442376 | tf_op jit(solution)/shard_map/ppermute | solution.py:625
  142.7 3.9 %shard_map.180 = (f32[256,512]{1,0:T(8,128)S(1)}, bf16[256,512]{1,0:T(8,128)(2,1)}, bf16[256,512]{1,0:T(8,128)(2,1)S(1)}, bf16[256,512]{1,0:T(8,128)(2,1)S(1)}) custom-call(s32[3]{0:T(128)S(1)} %pad_add_fusion.refs_0_, bf16[512,128]{1,0:T(8,128)(2,1)S(1)} %get-tuple-element.245.refs_5_.refs_3_.refs_1_, ...), custom_call_target="tpu_custom_call" | custom-call | flops 3000000000 | bytes 1 | tf_op jit(solution)/shard_map/pallas_call | solution.py:68
  146.6 1.5 collective-permute-start.46
  148.5 1.0 shard_map.183
  149.5 1.6 collective-permute-start.48
  151.1 0.9 collective-permute-done.50.refs_2_
  152.0 1.1 shard_map.184
  153.2 3.9 %all-to-all-start.4 = ((f32[32,8,128]{2,1,0:T(8,128)}), f32[32,8,128]{2,1,0:T(8,128)S(1)}, u32[]{:S(2)}, u32[]{:S(2)}) async-start(f32[32,8,128]{2,1,0:T(8,128)} %get-tuple-element.289), calls=%async_computation.4 | async-start | bytes 262144 | tf_op jit(solution)/shard_map/all_to_all | solution.py:816
  157.1 0.7 copy.23
  157.8 1.3 collective-permute-done.48.refs_3_
  159.0 0.8 shard_map.181
  159.8 5.1 %all-to-all-done.4.refs_0_ = f32[32,8,128]{2,1,0:T(8,128)S(1)} async-done(((f32[32,8,128]{2,1,0:T(8,128)}), f32[32,8,128]{2,1,0:T(8,128)S(1)}, u32[]{:S(2)}, u32[]{:S(2)}) %all-to-all-start.4) | async-done | bytes 131104 | tf_op jit(solution)/shard_map/all_to_all | solution.py:816
  165.0 1.1 shard_map.185
  (88 shorter events, 11.5 us)
Async XLA Ops:
  0.6 7.0 %copy-start.5 = (bf16[4,8,8,512]{3,2,1,0:T(8,128)(2,1)S(1)}, bf16[4,8,8,512]{3,2,1,0:T(8,128)(2,1)}, u32[]{:S(2)}) copy-start(bf16[4,8,8,512]{3,2,1,0:T(8,128)(2,1)} %param.9) | copy-start | bytes 786436
  0.7 21.7 %copy-start.7 = (s32[4,8,8]{2,1,0:T(8,128)S(1)}, s32[4,8,8]{2,1,0:T(8,128)}, u32[]{:S(2)}) copy-start(s32[4,8,8]{2,1,0:T(8,128)} %refs_5_.4) | copy-start | bytes 3076
  0.7 35.9 %copy-start.4 = (bf16[4,8,8,512]{3,2,1,0:T(8,128)(2,1)S(1)}, bf16[4,8,8,512]{3,2,1,0:T(8,128)(2,1)}, u32[]{:S(2)}) copy-start(bf16[4,8,8,512]{3,2,1,0:T(8,128)(2,1)} %param.11) | copy-start | bytes 786436
  1.8 36.2 %copy-start.6 = (f32[4,512]{1,0:T(4,128)S(1)}, f32[4,512]{1,0:T(4,128)}, u32[]{:S(2)}) copy-start(f32[4,512]{1,0:T(4,128)} %refs_4_.5) | copy-start | bytes 24580
  1.9 9.9 %collective-permute-start.2 = (bf16[9,64,128]{2,1,0:T(8,128)(2,1)S(1)}, bf16[9,64,128]{2,1,0:T(8,128)(2,1)S(1)}, u32[]{:S(2)}, u32[]{:S(2)}) collective-permute-start(bf16[9,64,128]{2,1,0:T(8,128)(2,1)S(1)} %get-tuple-element.155.refs_1_), channel_id=1, source_target_pairs={{0,3},{1,2},{2,1},{3,0},{4,7},{5,6},{6,5},{7,4},{8,11},{9,10},{10,... | collective-permute-start | bytes 442376 | tf_op jit(solution)/shard_map/ppermute | solution.py:625
  7.0 12.5 %collective-permute-start.1 = (bf16[9,64,128]{2,1,0:T(8,128)(2,1)S(1)}, bf16[9,64,128]{2,1,0:T(8,128)(2,1)S(1)}, u32[]{:S(2)}, u32[]{:S(2)}) collective-permute-start(bf16[9,64,128]{2,1,0:T(8,128)(2,1)S(1)} %get-tuple-element.155.refs_1_), channel_id=1, source_target_pairs={{0,2},{1,3},{2,0},{3,1},{4,6},{5,7},{6,4},{7,5},{8,10},{9,11},{10,... | collective-permute-start | bytes 442376 | tf_op jit(solution)/shard_map/ppermute | solution.py:625
  7.0 12.5 %collective-permute-start = (bf16[9,64,128]{2,1,0:T(8,128)(2,1)S(1)}, bf16[9,64,128]{2,1,0:T(8,128)(2,1)S(1)}, u32[]{:S(2)}, u32[]{:S(2)}) collective-permute-start(bf16[9,64,128]{2,1,0:T(8,128)(2,1)S(1)} %get-tuple-element.155.refs_1_), channel_id=1, source_target_pairs={{0,1},{1,0},{2,3},{3,2},{4,5},{5,4},{6,7},{7,6},{8,9},{9,8},{10,11... | collective-permute-start | bytes 442376 | tf_op jit(solution)/shard_map/ppermute | solution.py:625
  7.6 15.3 %collective-permute-start.5 = (bf16[256,512]{1,0:T(8,128)(2,1)S(1)}, bf16[256,512]{1,0:T(8,128)(2,1)S(1)}, u32[]{:S(2)}, u32[]{:S(2)}) collective-permute-start(bf16[256,512]{1,0:T(8,128)(2,1)S(1)} %bitcast.13), channel_id=1, source_target_pairs={{0,24},{8,16},{16,8},{24,0},{1,25},{9,17},{17,9},{25,1},{2,26},{10... | collective-permute-start | bytes 786440 | tf_op jit(solution)/shard_map/ppermute | solution.py:634
  10.2 12.8 %collective-permute-start.4 = (bf16[256,512]{1,0:T(8,128)(2,1)S(1)}, bf16[256,512]{1,0:T(8,128)(2,1)S(1)}, u32[]{:S(2)}, u32[]{:S(2)}) collective-permute-start(bf16[256,512]{1,0:T(8,128)(2,1)S(1)} %bitcast.14), channel_id=1, source_target_pairs={{0,16},{8,24},{16,0},{24,8},{1,17},{9,25},{17,1},{25,9},{2,18},{10... | collective-permute-start | bytes 786440 | tf_op jit(solution)/shard_map/ppermute | solution.py:634
  11.8 11.2 %collective-permute-start.3 = (bf16[256,512]{1,0:T(8,128)(2,1)S(1)}, bf16[256,512]{1,0:T(8,128)(2,1)S(1)}, u32[]{:S(2)}, u32[]{:S(2)}) collective-permute-start(bf16[256,512]{1,0:T(8,128)(2,1)S(1)} %bitcast.15), channel_id=1, source_target_pairs={{0,8},{8,0},{16,24},{24,16},{1,9},{9,1},{17,25},{25,17},{2,10},{10... | collective-permute-start | bytes 786440 | tf_op jit(solution)/shard_map/ppermute | solution.py:634
  19.5 10.1 %collective-permute-start.11 = (bf16[9,64,128]{2,1,0:T(8,128)(2,1)S(1)}, bf16[9,64,128]{2,1,0:T(8,128)(2,1)S(1)}, u32[]{:S(2)}, u32[]{:S(2)}) collective-permute-start(bf16[9,64,128]{2,1,0:T(8,128)(2,1)S(1)} %get-tuple-element.178.refs_1_), channel_id=1, source_target_pairs={{0,3},{1,2},{2,1},{3,0},{4,7},{5,6},{6,5},{7,4},{8,11},{9,10},{10,... | collective-permute-start | bytes 442376 | tf_op jit(solution)/shard_map/ppermute | solution.py:625
  23.0 12.5 %collective-permute-start.6 = (bf16[592,128]{1,0:T(8,128)(2,1)S(1)}, bf16[592,128]{1,0:T(8,128)(2,1)S(1)}, u32[]{:S(2)}, u32[]{:S(2)}) collective-permute-start(bf16[592,128]{1,0:T(8,128)(2,1)S(1)} %get-tuple-element.168), channel_id=1, source_target_pairs={{0,8},{8,0},{16,24},{24,16},{1,9},{9,1},{17,25},{25,17},{2,10},{10... | collective-permute-start | bytes 454664 | tf_op jit(solution)/shard_map/ppermute | solution.py:634
  24.6 10.9 %collective-permute-start.7 = (bf16[592,128]{1,0:T(8,128)(2,1)S(1)}, bf16[592,128]{1,0:T(8,128)(2,1)S(1)}, u32[]{:S(2)}, u32[]{:S(2)}) collective-permute-start(bf16[592,128]{1,0:T(8,128)(2,1)S(1)} %get-tuple-element.169), channel_id=1, source_target_pairs={{0,16},{8,24},{16,0},{24,8},{1,17},{9,25},{17,1},{25,9},{2,18},{10... | collective-permute-start | bytes 454664 | tf_op jit(solution)/shard_map/ppermute | solution.py:634
  26.1 9.4 %collective-permute-start.8 = (bf16[592,128]{1,0:T(8,128)(2,1)S(1)}, bf16[592,128]{1,0:T(8,128)(2,1)S(1)}, u32[]{:S(2)}, u32[]{:S(2)}) collective-permute-start(bf16[592,128]{1,0:T(8,128)(2,1)S(1)} %get-tuple-element.170), channel_id=1, source_target_pairs={{0,24},{8,16},{16,8},{24,0},{1,25},{9,17},{17,9},{25,1},{2,26},{10... | collective-permute-start | bytes 454664 | tf_op jit(solution)/shard_map/ppermute | solution.py:634
  26.6 7.8 %collective-permute-start.10 = (bf16[9,64,128]{2,1,0:T(8,128)(2,1)S(1)}, bf16[9,64,128]{2,1,0:T(8,128)(2,1)S(1)}, u32[]{:S(2)}, u32[]{:S(2)}) collective-permute-start(bf16[9,64,128]{2,1,0:T(8,128)(2,1)S(1)} %get-tuple-element.178.refs_1_), channel_id=1, source_target_pairs={{0,2},{1,3},{2,0},{3,1},{4,6},{5,7},{6,4},{7,5},{8,10},{9,11},{10,... | collective-permute-start | bytes 442376 | tf_op jit(solution)/shard_map/ppermute | solution.py:625
  29.6 5.9 %collective-permute-start.9 = (bf16[9,64,128]{2,1,0:T(8,128)(2,1)S(1)}, bf16[9,64,128]{2,1,0:T(8,128)(2,1)S(1)}, u32[]{:S(2)}, u32[]{:S(2)}) collective-permute-start(bf16[9,64,128]{2,1,0:T(8,128)(2,1)S(1)} %get-tuple-element.178.refs_1_), channel_id=1, source_target_pairs={{0,1},{1,0},{2,3},{3,2},{4,5},{5,4},{6,7},{7,6},{8,9},{9,8},{10,11... | collective-permute-start | bytes 442376 | tf_op jit(solution)/shard_map/ppermute | solution.py:625
  35.5 2.5 %collective-permute-start.12 = (bf16[592,128]{1,0:T(8,128)(2,1)S(1)}, bf16[592,128]{1,0:T(8,128)(2,1)S(1)}, u32[]{:S(2)}, u32[]{:S(2)}) collective-permute-start(bf16[592,128]{1,0:T(8,128)(2,1)S(1)} %get-tuple-element.172.refs_6_), channel_id=1, source_target_pairs={{0,4},{4,0},{1,5},{5,1},{2,6},{6,2},{3,7},{7,3},{8,12},{12,8},{9,1... | collective-permute-start | bytes 454664 | tf_op jit(solution)/shard_map/ppermute | solution.py:628
  35.6 2.4 %collective-permute-start.13 = (bf16[592,128]{1,0:T(8,128)(2,1)S(1)}, bf16[592,128]{1,0:T(8,128)(2,1)S(1)}, u32[]{:S(2)}, u32[]{:S(2)}) collective-permute-start(bf16[592,128]{1,0:T(8,128)(2,1)S(1)} %collective-permute-done.6.refs_7_), channel_id=1, source_target_pairs={{0,4},{4,0},{1,5},{5,1},{2,6},{6,2},{3,7},{7,3},{8,12},{12,8},{9,1... | collective-permute-start | bytes 454664 | tf_op jit(solution)/shard_map/ppermute | solution.py:628
  36.1 2.0 %collective-permute-start.14 = (bf16[592,128]{1,0:T(8,128)(2,1)S(1)}, bf16[592,128]{1,0:T(8,128)(2,1)S(1)}, u32[]{:S(2)}, u32[]{:S(2)}) collective-permute-start(bf16[592,128]{1,0:T(8,128)(2,1)S(1)} %collective-permute-done.7.refs_8_), channel_id=1, source_target_pairs={{0,4},{4,0},{1,5},{5,1},{2,6},{6,2},{3,7},{7,3},{8,12},{12,8},{9,1... | collective-permute-start | bytes 454664 | tf_op jit(solution)/shard_map/ppermute | solution.py:628
  36.2 1.9 %collective-permute-start.15 = (bf16[592,128]{1,0:T(8,128)(2,1)S(1)}, bf16[592,128]{1,0:T(8,128)(2,1)S(1)}, u32[]{:S(2)}, u32[]{:S(2)}) collective-permute-start(bf16[592,128]{1,0:T(8,128)(2,1)S(1)} %collective-permute-done.8.refs_9_), channel_id=1, source_target_pairs={{0,4},{4,0},{1,5},{5,1},{2,6},{6,2},{3,7},{7,3},{8,12},{12,8},{9,1... | collective-permute-start | bytes 454664 | tf_op jit(solution)/shard_map/ppermute | solution.py:628
  41.4 12.2 %collective-permute-start.16 = (bf16[832,128]{1,0:T(8,128)(2,1)S(1)}, bf16[832,128]{1,0:T(8,128)(2,1)S(1)}, u32[]{:S(2)}, u32[]{:S(2)}) collective-permute-start(bf16[832,128]{1,0:T(8,128)(2,1)S(1)} %get-tuple-element.188), channel_id=1, source_target_pairs={{0,8},{8,0},{16,24},{24,16},{1,9},{9,1},{17,25},{25,17},{2,10},{10... | collective-permute-start | bytes 638984 | tf_op jit(solution)/shard_map/ppermute | solution.py:634
  43.8 9.7 %collective-permute-start.17 = (bf16[832,128]{1,0:T(8,128)(2,1)S(1)}, bf16[832,128]{1,0:T(8,128)(2,1)S(1)}, u32[]{:S(2)}, u32[]{:S(2)}) collective-permute-start(bf16[832,128]{1,0:T(8,128)(2,1)S(1)} %get-tuple-element.189), channel_id=1, source_target_pairs={{0,16},{8,24},{16,0},{24,8},{1,17},{9,25},{17,1},{25,9},{2,18},{10... | collective-permute-start | bytes 638984 | tf_op jit(solution)/shard_map/ppermute | solution.py:634
  45.3 9.8 %collective-permute-start.18 = (bf16[832,128]{1,0:T(8,128)(2,1)S(1)}, bf16[832,128]{1,0:T(8,128)(2,1)S(1)}, u32[]{:S(2)}, u32[]{:S(2)}) collective-permute-start(bf16[832,128]{1,0:T(8,128)(2,1)S(1)} %get-tuple-element.190), channel_id=1, source_target_pairs={{0,24},{8,16},{16,8},{24,0},{1,25},{9,17},{17,9},{25,1},{2,26},{10... | collective-permute-start | bytes 638984 | tf_op jit(solution)/shard_map/ppermute | solution.py:634
  56.2 13.0 %collective-permute-start.25 = (bf16[4,9,64,128]{3,2,1,0:T(8,128)(2,1)S(1)}, bf16[4,9,64,128]{3,2,1,0:T(8,128)(2,1)S(1)}, u32[]{:S(2)}, u32[]{:S(2)}) collective-permute-start(bf16[4,9,64,128]{3,2,1,0:T(8,128)(2,1)S(1)} %get-tuple-element.200.refs_9_), channel_id=1, source_target_pairs={{0,4},{4,0},{1,5},{5,1},{2,6},{6,2},{3,7},{7,3},{8,12},{12,8},{9,1... | collective-permute-start | bytes 1769480 | tf_op jit(solution)/shard_map/ppermute | solution.py:628
  56.2 6.0 %collective-permute-start.20 = (bf16[512,128]{1,0:T(8,128)(2,1)S(1)}, bf16[512,128]{1,0:T(8,128)(2,1)S(1)}, u32[]{:S(2)}, u32[]{:S(2)}) collective-permute-start(bf16[512,128]{1,0:T(8,128)(2,1)S(1)} %get-tuple-element.198.refs_1_), channel_id=1, source_target_pairs={{0,16},{8,24},{16,0},{24,8},{1,17},{9,25},{17,1},{25,9},{2,18},{10... | collective-permute-start | bytes 393224 | tf_op jit(solution)/shard_map/ppermute | solution.py:634
  57.8 6.3 %collective-permute-start.22 = (bf16[512,128]{1,0:T(8,128)(2,1)S(1)}, bf16[512,128]{1,0:T(8,128)(2,1)S(1)}, u32[]{:S(2)}, u32[]{:S(2)}) collective-permute-start(bf16[512,128]{1,0:T(8,128)(2,1)S(1)} %get-tuple-element.199.refs_5_), channel_id=1, source_target_pairs={{0,8},{8,0},{16,24},{24,16},{1,9},{9,1},{17,25},{25,17},{2,10},{10... | collective-permute-start | bytes 393224 | tf_op jit(solution)/shard_map/ppermute | solution.py:634
  59.5 7.5 %collective-permute-start.19 = (bf16[512,128]{1,0:T(8,128)(2,1)S(1)}, bf16[512,128]{1,0:T(8,128)(2,1)S(1)}, u32[]{:S(2)}, u32[]{:S(2)}) collective-permute-start(bf16[512,128]{1,0:T(8,128)(2,1)S(1)} %get-tuple-element.198.refs_1_), channel_id=1, source_target_pairs={{0,8},{8,0},{16,24},{24,16},{1,9},{9,1},{17,25},{25,17},{2,10},{10... | collective-permute-start | bytes 393224 | tf_op jit(solution)/shard_map/ppermute | solution.py:634
  59.8 7.1 %collective-permute-start.23 = (bf16[512,128]{1,0:T(8,128)(2,1)S(1)}, bf16[512,128]{1,0:T(8,128)(2,1)S(1)}, u32[]{:S(2)}, u32[]{:S(2)}) collective-permute-start(bf16[512,128]{1,0:T(8,128)(2,1)S(1)} %get-tuple-element.199.refs_5_), channel_id=1, source_target_pairs={{0,16},{8,24},{16,0},{24,8},{1,17},{9,25},{17,1},{25,9},{2,18},{10... | collective-permute-start | bytes 393224 | tf_op jit(solution)/shard_map/ppermute | solution.py:634
  62.2 6.8 %collective-permute-start.21 = (bf16[512,128]{1,0:T(8,128)(2,1)S(1)}, bf16[512,128]{1,0:T(8,128)(2,1)S(1)}, u32[]{:S(2)}, u32[]{:S(2)}) collective-permute-start(bf16[512,128]{1,0:T(8,128)(2,1)S(1)} %collective-permute-done.20.refs_3_), channel_id=1, source_target_pairs={{0,8},{8,0},{16,24},{24,16},{1,9},{9,1},{17,25},{25,17},{2,10},{10... | collective-permute-start | bytes 393224 | tf_op jit(solution)/shard_map/ppermute | solution.py:634
  64.1 5.0 %collective-permute-start.24 = (bf16[512,128]{1,0:T(8,128)(2,1)S(1)}, bf16[512,128]{1,0:T(8,128)(2,1)S(1)}, u32[]{:S(2)}, u32[]{:S(2)}) collective-permute-start(bf16[512,128]{1,0:T(8,128)(2,1)S(1)} %collective-permute-done.22.refs_6_), channel_id=1, source_target_pairs={{0,16},{8,24},{16,0},{24,8},{1,17},{9,25},{17,1},{25,9},{2,18},{10... | collective-permute-start | bytes 393224 | tf_op jit(solution)/shard_map/ppermute | solution.py:634
  72.4 8.7 %collective-permute-start.26 = (bf16[1024,256]{1,0:T(8,128)(2,1)S(1)}, bf16[1024,256]{1,0:T(8,128)(2,1)S(1)}, u32[]{:S(2)}, u32[]{:S(2)}) collective-permute-start(bf16[1024,256]{1,0:T(8,128)(2,1)S(1)} %get-tuple-element.209), channel_id=1, source_target_pairs={{0,4},{4,0},{1,5},{5,1},{2,6},{6,2},{3,7},{7,3},{8,12},{12,8},{9,1... | collective-permute-start | bytes 1572872 | tf_op jit(solution)/shard_map/ppermute | solution.py:628
  72.5 8.6 %collective-permute-start.27 = (bf16[1024,256]{1,0:T(8,128)(2,1)S(1)}, bf16[1024,256]{1,0:T(8,128)(2,1)S(1)}, u32[]{:S(2)}, u32[]{:S(2)}) collective-permute-start(bf16[1024,256]{1,0:T(8,128)(2,1)S(1)} %get-tuple-element.211), channel_id=1, source_target_pairs={{0,4},{4,0},{1,5},{5,1},{2,6},{6,2},{3,7},{7,3},{8,12},{12,8},{9,1... | collective-permute-start | bytes 1572872 | tf_op jit(solution)/shard_map/ppermute | solution.py:628
  81.1 9.7 %copy-start.3 = (bf16[4,9,64,128]{3,2,1,0:T(8,128)(2,1)S(1)}, bf16[4,9,64,128]{3,2,1,0:T(8,128)(2,1)}, u32[]{:S(2)}) copy-start(bf16[4,9,64,128]{3,2,1,0:T(8,128)(2,1)} %get-tuple-element.223.refs_9_) | copy-start | bytes 1769476
  90.8 14.1 %collective-permute-start.34 = (bf16[4,9,64,128]{3,2,1,0:T(8,128)(2,1)S(1)}, bf16[4,9,64,128]{3,2,1,0:T(8,128)(2,1)S(1)}, u32[]{:S(2)}, u32[]{:S(2)}) collective-permute-start(bf16[4,9,64,128]{3,2,1,0:T(8,128)(2,1)S(1)} %copy-done.3), channel_id=1, source_target_pairs={{0,4},{4,0},{1,5},{5,1},{2,6},{6,2},{3,7},{7,3},{8,12},{12,8},{9,1... | collective-permute-start | bytes 1769480 | tf_op jit(solution)/shard_map/ppermute | solution.py:628
  91.0 9.0 %collective-permute-start.35 = (bf16[1024,128]{1,0:T(8,128)(2,1)S(1)}, bf16[1024,128]{1,0:T(8,128)(2,1)S(1)}, u32[]{:S(2)}, u32[]{:S(2)}) collective-permute-start(bf16[1024,128]{1,0:T(8,128)(2,1)S(1)} %get-tuple-element.228), channel_id=1, source_target_pairs={{0,4},{4,0},{1,5},{5,1},{2,6},{6,2},{3,7},{7,3},{8,12},{12,8},{9,1... | collective-permute-start | bytes 786440 | tf_op jit(solution)/shard_map/ppermute | solution.py:628
  91.4 5.5 %collective-permute-start.29 = (bf16[512,128]{1,0:T(8,128)(2,1)S(1)}, bf16[512,128]{1,0:T(8,128)(2,1)S(1)}, u32[]{:S(2)}, u32[]{:S(2)}) collective-permute-start(bf16[512,128]{1,0:T(8,128)(2,1)S(1)} %get-tuple-element.221.refs_1_.refs_3_), channel_id=1, source_target_pairs={{0,16},{8,24},{16,0},{24,8},{1,17},{9,25},{17,1},{25,9},{2,18},{10... | collective-permute-start | bytes 393224 | tf_op jit(solution)/shard_map/ppermute | solution.py:634
  93.0 6.4 %collective-permute-start.31 = (bf16[512,128]{1,0:T(8,128)(2,1)S(1)}, bf16[512,128]{1,0:T(8,128)(2,1)S(1)}, u32[]{:S(2)}, u32[]{:S(2)}) collective-permute-start(bf16[512,128]{1,0:T(8,128)(2,1)S(1)} %get-tuple-element.222.refs_5_.refs_4_), channel_id=1, source_target_pairs={{0,8},{8,0},{16,24},{24,16},{1,9},{9,1},{17,25},{25,17},{2,10},{10... | collective-permute-start | bytes 393224 | tf_op jit(solution)/shard_map/ppermute | solution.py:634
  93.6 10.5 %collective-permute-start.28 = (bf16[512,128]{1,0:T(8,128)(2,1)S(1)}, bf16[512,128]{1,0:T(8,128)(2,1)S(1)}, u32[]{:S(2)}, u32[]{:S(2)}) collective-permute-start(bf16[512,128]{1,0:T(8,128)(2,1)S(1)} %get-tuple-element.221.refs_1_.refs_3_), channel_id=1, source_target_pairs={{0,8},{8,0},{16,24},{24,16},{1,9},{9,1},{17,25},{25,17},{2,10},{10... | collective-permute-start | bytes 393224 | tf_op jit(solution)/shard_map/ppermute | solution.py:634
  96.9 7.2 %collective-permute-start.32 = (bf16[512,128]{1,0:T(8,128)(2,1)S(1)}, bf16[512,128]{1,0:T(8,128)(2,1)S(1)}, u32[]{:S(2)}, u32[]{:S(2)}) collective-permute-start(bf16[512,128]{1,0:T(8,128)(2,1)S(1)} %get-tuple-element.222.refs_5_.refs_4_), channel_id=1, source_target_pairs={{0,16},{8,24},{16,0},{24,8},{1,17},{9,25},{17,1},{25,9},{2,18},{10... | collective-permute-start | bytes 393224 | tf_op jit(solution)/shard_map/ppermute | solution.py:634
  99.4 5.0 %collective-permute-start.30 = (bf16[512,128]{1,0:T(8,128)(2,1)S(1)}, bf16[512,128]{1,0:T(8,128)(2,1)S(1)}, u32[]{:S(2)}, u32[]{:S(2)}) collective-permute-start(bf16[512,128]{1,0:T(8,128)(2,1)S(1)} %collective-permute-done.29.refs_3_), channel_id=1, source_target_pairs={{0,8},{8,0},{16,24},{24,16},{1,9},{9,1},{17,25},{25,17},{2,10},{10... | collective-permute-start | bytes 393224 | tf_op jit(solution)/shard_map/ppermute | solution.py:634
  100.0 5.0 %collective-permute-start.33 = (bf16[512,128]{1,0:T(8,128)(2,1)S(1)}, bf16[512,128]{1,0:T(8,128)(2,1)S(1)}, u32[]{:S(2)}, u32[]{:S(2)}) collective-permute-start(bf16[512,128]{1,0:T(8,128)(2,1)S(1)} %collective-permute-done.31.refs_6_), channel_id=1, source_target_pairs={{0,16},{8,24},{16,0},{24,8},{1,17},{9,25},{17,1},{25,9},{2,18},{10... | collective-permute-start | bytes 393224 | tf_op jit(solution)/shard_map/ppermute | solution.py:634
  108.0 11.7 %collective-permute-start.36 = (bf16[832,128]{1,0:T(8,128)(2,1)S(1)}, bf16[832,128]{1,0:T(8,128)(2,1)S(1)}, u32[]{:S(2)}, u32[]{:S(2)}) collective-permute-start(bf16[832,128]{1,0:T(8,128)(2,1)S(1)} %get-tuple-element.236), channel_id=1, source_target_pairs={{0,8},{8,0},{16,24},{24,16},{1,9},{9,1},{17,25},{25,17},{2,10},{10... | collective-permute-start | bytes 638984 | tf_op jit(solution)/shard_map/ppermute | solution.py:634
  109.5 10.2 %collective-permute-start.37 = (bf16[832,128]{1,0:T(8,128)(2,1)S(1)}, bf16[832,128]{1,0:T(8,128)(2,1)S(1)}, u32[]{:S(2)}, u32[]{:S(2)}) collective-permute-start(bf16[832,128]{1,0:T(8,128)(2,1)S(1)} %get-tuple-element.237), channel_id=1, source_target_pairs={{0,16},{8,24},{16,0},{24,8},{1,17},{9,25},{17,1},{25,9},{2,18},{10... | collective-permute-start | bytes 638984 | tf_op jit(solution)/shard_map/ppermute | solution.py:634
  109.9 9.8 %collective-permute-start.38 = (bf16[832,128]{1,0:T(8,128)(2,1)S(1)}, bf16[832,128]{1,0:T(8,128)(2,1)S(1)}, u32[]{:S(2)}, u32[]{:S(2)}) collective-permute-start(bf16[832,128]{1,0:T(8,128)(2,1)S(1)} %get-tuple-element.238), channel_id=1, source_target_pairs={{0,24},{8,16},{16,8},{24,0},{1,25},{9,17},{17,9},{25,1},{2,26},{10... | collective-permute-start | bytes 638984 | tf_op jit(solution)/shard_map/ppermute | solution.py:634
  120.0 5.4 %collective-permute-start.39 = (bf16[1024,128]{1,0:T(8,128)(2,1)S(1)}, bf16[1024,128]{1,0:T(8,128)(2,1)S(1)}, u32[]{:S(2)}, u32[]{:S(2)}) collective-permute-start(bf16[1024,128]{1,0:T(8,128)(2,1)S(1)} %get-tuple-element.251), channel_id=1, source_target_pairs={{0,4},{4,0},{1,5},{5,1},{2,6},{6,2},{3,7},{7,3},{8,12},{12,8},{9,1... | collective-permute-start | bytes 786440 | tf_op jit(solution)/shard_map/ppermute | solution.py:628
  120.9 9.0 %collective-permute-start.43 = (bf16[576,128]{1,0:T(8,128)(2,1)S(1)}, bf16[576,128]{1,0:T(8,128)(2,1)S(1)}, u32[]{:S(2)}, u32[]{:S(2)}) collective-permute-start(bf16[576,128]{1,0:T(8,128)(2,1)S(1)} %get-tuple-element.257), channel_id=1, source_target_pairs={{0,1},{1,0},{2,3},{3,2},{4,5},{5,4},{6,7},{7,6},{8,9},{9,8},{10,11... | collective-permute-start | bytes 442376 | tf_op jit(solution)/shard_map/ppermute | solution.py:625
  121.4 14.0 %collective-permute-start.44 = (bf16[576,128]{1,0:T(8,128)(2,1)S(1)}, bf16[576,128]{1,0:T(8,128)(2,1)S(1)}, u32[]{:S(2)}, u32[]{:S(2)}) collective-permute-start(bf16[576,128]{1,0:T(8,128)(2,1)S(1)} %get-tuple-element.258), channel_id=1, source_target_pairs={{0,2},{1,3},{2,0},{3,1},{4,6},{5,7},{6,4},{7,5},{8,10},{9,11},{10,... | collective-permute-start | bytes 442376 | tf_op jit(solution)/shard_map/ppermute | solution.py:625
  121.9 13.5 %collective-permute-start.45 = (bf16[576,128]{1,0:T(8,128)(2,1)S(1)}, bf16[576,128]{1,0:T(8,128)(2,1)S(1)}, u32[]{:S(2)}, u32[]{:S(2)}) collective-permute-start(bf16[576,128]{1,0:T(8,128)(2,1)S(1)} %get-tuple-element.259), channel_id=1, source_target_pairs={{0,3},{1,2},{2,1},{3,0},{4,7},{5,6},{6,5},{7,4},{8,11},{9,10},{10,... | collective-permute-start | bytes 442376 | tf_op jit(solution)/shard_map/ppermute | solution.py:625
  128.0 7.4 %collective-permute-start.40 = (bf16[576,128]{1,0:T(8,128)(2,1)S(1)}, bf16[576,128]{1,0:T(8,128)(2,1)S(1)}, u32[]{:S(2)}, u32[]{:S(2)}) collective-permute-start(bf16[576,128]{1,0:T(8,128)(2,1)S(1)} %get-tuple-element.253), channel_id=1, source_target_pairs={{0,8},{8,0},{16,24},{24,16},{1,9},{9,1},{17,25},{25,17},{2,10},{10... | collective-permute-start | bytes 442376 | tf_op jit(solution)/shard_map/ppermute | solution.py:634
  129.5 6.6 %collective-permute-start.41 = (bf16[576,128]{1,0:T(8,128)(2,1)S(1)}, bf16[576,128]{1,0:T(8,128)(2,1)S(1)}, u32[]{:S(2)}, u32[]{:S(2)}) collective-permute-start(bf16[576,128]{1,0:T(8,128)(2,1)S(1)} %get-tuple-element.254), channel_id=1, source_target_pairs={{0,16},{8,24},{16,0},{24,8},{1,17},{9,25},{17,1},{25,9},{2,18},{10... | collective-permute-start | bytes 442376 | tf_op jit(solution)/shard_map/ppermute | solution.py:634
  129.9 7.8 %collective-permute-start.42 = (bf16[576,128]{1,0:T(8,128)(2,1)S(1)}, bf16[576,128]{1,0:T(8,128)(2,1)S(1)}, u32[]{:S(2)}, u32[]{:S(2)}) collective-permute-start(bf16[576,128]{1,0:T(8,128)(2,1)S(1)} %get-tuple-element.255), channel_id=1, source_target_pairs={{0,24},{8,16},{16,8},{24,0},{1,25},{9,17},{17,9},{25,1},{2,26},{10... | collective-permute-start | bytes 442376 | tf_op jit(solution)/shard_map/ppermute | solution.py:634
  138.3 11.2 %collective-permute-start.49 = (bf16[576,128]{1,0:T(8,128)(2,1)S(1)}, bf16[576,128]{1,0:T(8,128)(2,1)S(1)}, u32[]{:S(2)}, u32[]{:S(2)}) collective-permute-start(bf16[576,128]{1,0:T(8,128)(2,1)S(1)} %get-tuple-element.277), channel_id=1, source_target_pairs={{0,1},{1,0},{2,3},{3,2},{4,5},{5,4},{6,7},{7,6},{8,9},{9,8},{10,11... | collective-permute-start | bytes 442376 | tf_op jit(solution)/shard_map/ppermute | solution.py:625
  139.0 13.0 %collective-permute-start.50 = (bf16[576,128]{1,0:T(8,128)(2,1)S(1)}, bf16[576,128]{1,0:T(8,128)(2,1)S(1)}, u32[]{:S(2)}, u32[]{:S(2)}) collective-permute-start(bf16[576,128]{1,0:T(8,128)(2,1)S(1)} %get-tuple-element.278), channel_id=1, source_target_pairs={{0,2},{1,3},{2,0},{3,1},{4,6},{5,7},{6,4},{7,5},{8,10},{9,11},{10,... | collective-permute-start | bytes 442376 | tf_op jit(solution)/shard_map/ppermute | solution.py:625
  139.4 12.6 %collective-permute-start.51 = (bf16[576,128]{1,0:T(8,128)(2,1)S(1)}, bf16[576,128]{1,0:T(8,128)(2,1)S(1)}, u32[]{:S(2)}, u32[]{:S(2)}) collective-permute-start(bf16[576,128]{1,0:T(8,128)(2,1)S(1)} %get-tuple-element.279), channel_id=1, source_target_pairs={{0,3},{1,2},{2,1},{3,0},{4,7},{5,6},{6,5},{7,4},{8,11},{9,10},{10,... | collective-permute-start | bytes 442376 | tf_op jit(solution)/shard_map/ppermute | solution.py:625
  142.7 5.8 %copy-start = (f32[2,9,64,128]{3,2,1,0:T(8,128)S(1)}, f32[2,9,64,128]{3,2,1,0:T(8,128)}, u32[]{:S(2)}) copy-start(f32[2,9,64,128]{3,2,1,0:T(8,128)} %refs_1_.3) | copy-start | bytes 1769476
  142.7 5.8 %copy-start.1 = (f32[2,9,64,128]{3,2,1,0:T(8,128)S(1)}, f32[2,9,64,128]{3,2,1,0:T(8,128)}, u32[]{:S(2)}) copy-start(f32[2,9,64,128]{3,2,1,0:T(8,128)} %refs_5_.6) | copy-start | bytes 1769476
  142.7 5.8 %copy-start.2 = (f32[2,9,64,128]{3,2,1,0:T(8,128)S(1)}, f32[2,9,64,128]{3,2,1,0:T(8,128)}, u32[]{:S(2)}) copy-start(f32[2,9,64,128]{3,2,1,0:T(8,128)} %refs_6_.4) | copy-start | bytes 1769476
  146.6 11.2 %collective-permute-start.46 = (bf16[256,512]{1,0:T(8,128)(2,1)}, bf16[256,512]{1,0:T(8,128)(2,1)S(1)}, u32[]{:S(2)}, u32[]{:S(2)}) collective-permute-start(bf16[256,512]{1,0:T(8,128)(2,1)} %get-tuple-element.262), channel_id=1, source_target_pairs={{0,8},{8,0},{16,24},{24,16},{1,9},{9,1},{17,25},{25,17},{2,10},{10... | collective-permute-start | bytes 786440 | tf_op jit(solution)/shard_map/ppermute | solution.py:634
  148.1 9.7 %collective-permute-start.47 = (bf16[256,512]{1,0:T(8,128)(2,1)S(1)}, bf16[256,512]{1,0:T(8,128)(2,1)S(1)}, u32[]{:S(2)}, u32[]{:S(2)}) collective-permute-start(bf16[256,512]{1,0:T(8,128)(2,1)S(1)} %get-tuple-element.263), channel_id=1, source_target_pairs={{0,16},{8,24},{16,0},{24,8},{1,17},{9,25},{17,1},{25,9},{2,18},{10... | collective-permute-start | bytes 786440 | tf_op jit(solution)/shard_map/ppermute | solution.py:634
  149.5 9.6 %collective-permute-start.48 = (bf16[256,512]{1,0:T(8,128)(2,1)S(1)}, bf16[256,512]{1,0:T(8,128)(2,1)S(1)}, u32[]{:S(2)}, u32[]{:S(2)}) collective-permute-start(bf16[256,512]{1,0:T(8,128)(2,1)S(1)} %get-tuple-element.264), channel_id=1, source_target_pairs={{0,24},{8,16},{16,8},{24,0},{1,25},{9,17},{17,9},{25,1},{2,26},{10... | collective-permute-start | bytes 786440 | tf_op jit(solution)/shard_map/ppermute | solution.py:634
  153.2 11.8 %copy-start.8 = (f32[4,512]{1,0:T(4,128)S(1)}, f32[4,512]{1,0:T(4,128)}, u32[]{:S(2)}) copy-start(f32[4,512]{1,0:T(4,128)} %refs_5_.7) | copy-start | bytes 24580
  153.2 11.8 %copy-start.9 = (f32[4,512]{1,0:T(4,128)S(1)}, f32[4,512]{1,0:T(4,128)}, u32[]{:S(2)}) copy-start(f32[4,512]{1,0:T(4,128)} %refs_6_.5) | copy-start | bytes 24580
  153.2 11.8 %all-to-all-start.4 = ((f32[32,8,128]{2,1,0:T(8,128)}), f32[32,8,128]{2,1,0:T(8,128)S(1)}, u32[]{:S(2)}, u32[]{:S(2)}) async-start(f32[32,8,128]{2,1,0:T(8,128)} %get-tuple-element.289), calls=%async_computation.4 | async-start | bytes 262144 | tf_op jit(solution)/shard_map/all_to_all | solution.py:816

commit v7 on v6

--- a/solution.py
+++ b/solution.py
@@ -162,12 +162,12 @@
 
 
 def spread(ref, rows):
-    used = rows[0].shape[1]
-    if len(rows) < 8:
-        rows = rows + [jnp.zeros((8 - len(rows), used), F32)]
+    used, many = rows[0].shape[1], ref.shape[1]
+    if len(rows) < many:
+        rows = rows + [jnp.zeros((many - len(rows), used), F32)]
     stat = jnp.concatenate(rows, axis=0)
     if used < LANES:
-        stat = jnp.concatenate([stat, jnp.zeros((8, LANES - used), F32)], axis=1)
+        stat = jnp.concatenate([stat, jnp.zeros((many, LANES - used), F32)], axis=1)
     for k in range(ref.shape[0]):
         ref[k] = stat
 
@@ -220,12 +220,28 @@
                 outs[t][rows, :] = jnp.concatenate([v[:, low : low + z.IB] for v in slices], axis=1)
 
 
-def first_conv(z, at, np_ref, *refs):
+def split_images(z, at, np_ref, *refs):
+    xs, outs, (slice_ref, par_ref) = refs[: z.Q], refs[z.Q : -2], refs[-2:]
+    for m in range(z.Q):
+        rows = pl.ds(pl.multiple_of((at[0] ^ m) * z.own, z.own), z.own)
+        split_channels(z, at, [xs[m][:, a * z.L : (a + 1) * z.L] for a in range(z.Q)], outs, rows)
+    for slot in range(z.Q):
+
+        @pl.when(at[0] == slot)
+        def _(slot=slot):
+            par_ref[...] = np_ref[:, slot * z.L : (slot + 1) * z.L]
+            for m in range(z.Q):
+                j = slot ^ m
+                slice_ref[j * z.own : (j + 1) * z.own, :] = xs[m][
+                    :, slot * z.L : (slot + 1) * z.L
+                ]
+
+
+def first_conv(z, at, *refs):
     xs, refs = refs[: z.Q], refs[z.Q :]
     blocks = [refs[t * z.Q : (t + 1) * z.Q] for t in range(z.S)]
     refs = refs[z.S * z.Q :]
-    outs, refs = refs[: z.S], refs[z.S :]
-    z_ref, slice_ref, par_ref, hw_ref, stats_ref, far_w, wcat, y_ref, sem = refs
+    z_ref, hw_ref, stats_ref, far_w, wcat, y_ref, sem = refs
     for m in range(z.Q):
         for n in range(z.n_own):
             row = z.K * z.IB + 2 * n
@@ -234,19 +250,6 @@
     fill_kernels(z, at, blocks, wcat)
     copy = pltpu.make_async_copy(wcat, far_w, sem)
     copy.start()
-    for m in range(z.Q):
-        rows = pl.ds(pl.multiple_of((at[0] ^ m) * z.own, z.own), z.own)
-        split_channels(z, at, [xs[m][:, a * z.L : (a + 1) * z.L] for a in range(z.Q)], outs, rows)
-    for slot in range(z.Q):
-
-        @pl.when(at[0] == slot)
-        def _(slot=slot):
-            par_ref[...] = np_ref[:, slot * z.L : (slot + 1) * z.L]
-            for m in range(z.Q):
-                j = slot ^ m
-                slice_ref[j * z.own : (j + 1) * z.own, :] = xs[m][
-                    :, slot * z.L : (slot + 1) * z.L
-                ]
 
     def product(m):
         return jnp.dot(xs[m][...], wcat[...], preferred_element_type=F32)
@@ -386,7 +389,8 @@
     over_halves(z, step, (a_ref, b_ref))
 
 
-def back_product(z, at, dz_ref, blocks, wcat):
+def hidden_slope(z, at, *refs):
+    blocks, (z_ref, sum_ref, hw_ref, par_ref, wcat, slope_ref) = refs[: z.S], refs[z.S :]
     for t, block in enumerate(blocks):
         s = at[1] ^ t
         for b in range(z.Z):
@@ -396,6 +400,18 @@
                     wcat[0, rows, b * z.L : (b + 1) * z.L] = block[b, k]
                 else:
                     wcat[b, rows, :] = block[b, k]
+    mean, inv = sum_ref[0:1, :], sum_ref[1:2, :]
+    gain, shift = par_ref[0:1, :], par_ref[1:2, :]
+
+    def step(n, rows, carry):
+        normed = (z_ref[rows, :] - mean) * inv
+        slope_ref[rows, :] = gelu_both(image_mask(z, hw_ref[n]) * (gain * normed + shift))[1]
+        return carry
+
+    over_images(z, step)
+
+
+def back_product(z, dz_ref, wcat):
     contract = (((1,), (1,)), ((), ()))
 
     def product(j):
@@ -411,27 +427,23 @@
     return product
 
 
-def back_scratch(z):
+def back_wide(z):
     if z.L % LANES == 0:
-        wide = pltpu.VMEM((1, z.K * z.LP, z.C), BF16)
-    else:
-        wide = pltpu.VMEM((z.Z, z.K * z.LP, z.C // z.Z), BF16)
-    return [wide, pltpu.VMEM((z.own, z.K * z.LP), F32), pltpu.VMEM((z.Q, z.G, z.L), BF16)]
+        return near((1, z.K * z.LP, z.C), BF16)
+    return near((z.Z, z.K * z.LP, z.C // z.Z), BF16)
 
 
 def hidden_grad(z, at, *refs):
     dzs, refs = refs[: 2 * z.Q], refs[2 * z.Q :]
-    blocks, refs = refs[: z.S], refs[z.S :]
-    z_ref, sum_ref, hw_ref, par_ref, da_ref, stats_ref, wcat, y_ref, dz_ref = refs
+    wcat, slope_ref, z_ref, sum_ref, hw_ref, da_ref, stats_ref, y_ref, dz_ref = refs
     gathered(z, at, dzs, dz_ref)
-    conv_into(z, back_product(z, at, dz_ref, blocks, wcat), y_ref, da_ref, -1)
+    conv_into(z, back_product(z, dz_ref, wcat), y_ref, da_ref, -1)
     mean, inv = sum_ref[0:1, :], sum_ref[1:2, :]
-    gain, shift = par_ref[0:1, :], par_ref[1:2, :]
 
     def step(n, rows, carry):
         mask = image_mask(z, hw_ref[n])
         normed = (z_ref[rows, :] - mean) * inv
-        da = da_ref[rows, :] * gelu_both(mask * (gain * normed + shift))[1]
+        da = da_ref[rows, :] * slope_ref[rows, :]
         da_ref[rows, :] = da
         masked = mask * da
         return (
@@ -513,11 +525,13 @@
 
 
 def moments(z, j, *refs):
-    count = len(refs) - (7 if j else 12)
+    count = len(refs) - 10
     parts, refs = refs[:count], refs[count:]
     w_ref, first_ref, second_ref, refs = *refs[:3], refs[3:]
-    if j == 0:
-        other_ref, g1_ref, g2_ref, refs = refs[0], refs[1], refs[2], refs[5:]
+    if j:
+        g1_ref, g2_ref, at, refs = *refs[:3], refs[3:]
+    else:
+        other_ref, refs = refs[0], refs[3:]
     nf_ref, ns_ref, u_ref, stats_ref = refs
     total_u = jnp.zeros((1, z.L), F32)
     total_w = jnp.zeros((1, z.L), F32)
@@ -530,22 +544,28 @@
         u_ref[k] = u
         total_u = total_u + jnp.sum(u * u, 0, keepdims=True)
         total_w = total_w + jnp.sum(w * w, 0, keepdims=True)
+    lane = lax.broadcasted_iota(jnp.int32, (1, z.L), 1)
+    sums = jnp.zeros((1, z.L), F32) if j else other_ref[0:1, :]
+    for c, v in enumerate([total_u, total_w]):
+        sums = jnp.where(lane == 2 * c + j, jnp.sum(v, axis=1, keepdims=True), sums)
     if j:
-        keep(stats_ref, [total_u, total_w])
+        own = jnp.zeros((1, z.L), F32)
+        for r, v in enumerate([g1_ref[0:1, :], g1_ref[1:2, :], g2_ref[0:1, :], g2_ref[1:2, :]]):
+            own = jnp.where(at[2] == r, v, own)
+        keep(stats_ref, [sums, own])
     else:
-        grads = [g1_ref[0:1, :], g1_ref[1:2, :], g2_ref[0:1, :], g2_ref[1:2, :]]
-        spread(stats_ref, [total_u, other_ref[0:1, :], total_w, other_ref[1:2, :]] + grads)
+        spread(stats_ref, [sums, other_ref[1:2, :]])
 
 
 def finish(z, all_ref, w_ref, u0_ref, u1_ref, np_ref, nf_ref, ns_ref, *outs):
     nw_ref, copy_ref, nnp_ref, nnf_ref, nns_ref, trust_ref = outs
-    total = all_ref[0]
+    total = all_ref[0, 0:1, :]
     for k in range(1, z.R * z.Z):
-        total = total + all_ref[k]
+        total = total + all_ref[k, 0:1, :]
     tops, bottoms = [], []
     for j in range(2):
-        un = jnp.sqrt(jnp.sum(total[j : j + 1, : z.L], axis=1, keepdims=True))
-        wn = jnp.sqrt(jnp.sum(total[2 + j : 3 + j, : z.L], axis=1, keepdims=True))
+        un = jnp.sqrt(total[:, j : j + 1])
+        wn = jnp.sqrt(total[:, 2 + j : 3 + j])
         tops.append(wn)
         bottoms.append(un)
         scale = RATE * (wn / (un + TINY))
@@ -554,7 +574,8 @@
             nw_ref[j, k] = new
             copy_ref[j, k] = new.astype(BF16)
     for j in range(z.Q):
-        nnp_ref[:, j * z.L : (j + 1) * z.L] = all_ref[j * z.Z, 4:8, : z.L]
+        for r in range(4):
+            nnp_ref[r : r + 1, j * z.L : (j + 1) * z.L] = all_ref[j * z.Z + r, 1:2, : z.L]
     param = np_ref[...]
     nf, ns, move = direction_of(nnp_ref[...], nf_ref[...], ns_ref[...], param, 0.0)
     nnf_ref[...] = nf
@@ -651,7 +672,7 @@
     many = z.S * z.Z
     piece = (z.K, z.IB, z.L)
     blocks = near((z.Z, *piece), BF16)
-    stat = near((many, 8, LANES))
+    stat, pair = near((many, 4, LANES)), near((many, 2, LANES))
     conv_scratch = [pltpu.VMEM((z.C, z.K * z.LP), BF16), pltpu.VMEM((rows, z.K * z.LP), F32)]
     grad_scratch = [pltpu.VMEM((z.G, z.K * z.LP), BF16), pltpu.VMEM((z.Q * z.IB, z.K * z.LP), F32)]
     cot_rows = cotangent.reshape(rows, z.C)
@@ -670,7 +691,13 @@
     )
     picked, xs = together((picked, xs))
     two = [over_z(low_two, m) for m in range(z.Z)]
-    front_one, two = together(([over_q(picked[m], m) for m in range(z.Q)], two))
+    *x_parts, x_slice, slice_params = call(
+        functools.partial(split_images, z),
+        [near((z.G, z.Q * z.IB), BF16)] * z.S + [near(GL, BF16), near((4, z.L))],
+        (at, params, *xs),
+    )
+    front_one = [over_q(picked[m], m) for m in range(z.Q)]
+    front_one, x_parts, two = together((front_one, x_parts, two))
     keep = away((z.Z, *piece), BF16)
     keep_two, *picked = call(
         functools.partial(pick, z, False),
@@ -680,18 +707,10 @@
         raw=(keep,),
     )
     w_far = away((z.C, z.K * z.LP), BF16)
-    *x_parts, z1, x_slice, slice_params, hw, stats, w_far = call(
+    z1, hw, stats, w_far = call(
         functools.partial(first_conv, z),
-        [near((z.G, z.Q * z.IB), BF16)] * z.S
-        + [
-            near(GL),
-            near(GL, BF16),
-            near((4, z.L)),
-            near((z.n_group, 8, LANES)),
-            stat,
-            w_far,
-        ],
-        (at, params, *xs, *[over_s(v, t) for t in range(z.S) for v in front_one]),
+        [near(GL), near((z.n_group, 8, LANES)), stat, w_far],
+        (at, *xs, *[over_s(v, t) for t in range(z.S) for v in front_one]),
         conv_scratch + [pltpu.SemaphoreType.DMA],
         limit=16,
         raw=(w_far,),
@@ -717,7 +736,7 @@
     stats, x_parts, h_parts = together((sharers(stats), x_parts, h_parts))
     out, d, sum_two, stats = call(
         functools.partial(middle, z),
-        [near((z.Q, rows, z.L), BF16), near(GL), near((8, z.L)), stat],
+        [near((z.Q, rows, z.L), BF16), near(GL), near((8, z.L)), pair],
         (at, z2, stats, hw, slice_params, x_slice, cots),
     )
     da, db, dz, grad_two = call(
@@ -749,18 +768,20 @@
         whole = pl.BlockSpec(memory_space=pltpu.VMEM)
         block = pl.BlockSpec((1, *piece), lambda i: (j, 0, 0, 0))
         held = pl.BlockSpec(memory_space=pl.ANY)
-        args = [pltpu.with_memory_space_constraint(v, pltpu.VMEM) for v in (*parts,)]
-        args += [weights, first, second]
+        args = [pltpu.with_memory_space_constraint(v, pltpu.VMEM) for v in parts] + [weights, first, second]
         specs = [whole] * len(parts) + [block] * 3
-        if more:
-            args += [pltpu.with_memory_space_constraint(v, pltpu.VMEM) for v in more[:3]] + list(more[3:])
-            specs += [whole] * 3 + [held] * 2
+        if j:
+            args += [pltpu.with_memory_space_constraint(v, pltpu.VMEM) for v in more] + [at]
+            specs += [whole] * 2 + [pl.BlockSpec(memory_space=pltpu.SMEM)]
+        else:
+            args += [pltpu.with_memory_space_constraint(more[0], pltpu.VMEM), *more[1:]]
+            specs += [whole] + [held] * 2
         n = len(args)
         return pl.pallas_call(
             functools.partial(moments, z, j),
             grid=(1,),
             out_shape=[shape(weights.shape)] * 2
-            + [near(piece), near((8, z.L)) if j else near((z.R * z.Z, 8, LANES))],
+            + [near(piece), near((8, z.L)) if j else near((z.R * z.Z, 2, LANES))],
             in_specs=specs,
             out_specs=[block, block, whole, whole],
             input_output_aliases={} if j else {n - 2: 0, n - 1: 1},
@@ -769,11 +790,16 @@
         )(*args)
 
     parts_two = gradient(h_parts, da, db, dz, out)
+    wide, slope = call(
+        functools.partial(hidden_slope, z),
+        [back_wide(z), near(GL)],
+        (at, *share(keep_two), z1, sum_one, hw, slice_params),
+    )
     da1, stats = call(
         functools.partial(hidden_grad, z),
-        [near(GL), stat],
-        (at, *dz2s, *share(keep_two), z1, sum_one, hw, slice_params),
-        back_scratch(z),
+        [near(GL), pair],
+        (at, *dz2s, wide, slope, z1, sum_one, hw),
+        [pltpu.VMEM((rows, z.K * z.LP), F32), pltpu.VMEM((z.Q, *GL), BF16)],
         limit=16,
     )
     stats, parts_two = together((stats, parts_two))
@@ -808,13 +834,12 @@
     parts_one = call(functools.partial(route, z), [flat] * z.Z, (at, *parts_one), [hold])
     parts_one, parts_two = together((parts_one, parts_two))
     parts_one = along(parts_one)
-    new_first, new_second, move_two, other = update(1, parts_two)
+    new_first, new_second, move_two, other = update(1, parts_two, grad_one, grad_two)
     dxs = [over_q(dxs[m], m) for m in range(z.Q)]
-    new_first, new_second, move_one, stats = update(
-        0, parts_one, other, grad_one, grad_two, new_first, new_second
-    )
+    new_first, new_second, move_one, stats = update(0, parts_one, other, new_first, new_second)
     stats = lax.all_to_all(stats, ("s", "q", "z"), 0, 0)
     dx = call(functools.partial(total_of, z), shape((rows, z.C), BF16), tuple(dxs))
+    stats, dx = together((stats, dx))
     new_weights, copies, new_params, new_p_first, new_p_second, trust = call(
         functools.partial(finish, z),
         [shape(weights.shape), shape(weights.shape, BF16)] + [shape(params.shape)] * 3 + [shape((2, 6))],

time: 167 us -> 165 us (0.988)
  waiting for transfers between devices: 37 us -> 33.1 us
  Pallas kernels: 28.9 us -> 30.8 us
    ppermute x12, waiting for transfers between devices: 17.7 us -> 15.7 us  [over_z(): return lax.ppermute(v, 'z', [(i, i ^ m) for i in range(z.Z)]) if m else v]
    pallas_call x16 -> x18, Pallas kernels: 26.8 us -> 28 us  [call(): pl.pallas_call(run, out_shape=out_shape, in_specs=[pl.BlockSpec(memory_sp...]
  transfers between devices with their start and end apart: 53 -> 53, of which waited for: 20 -> 18; matrix products, arithmetic and copies ran while one was open for 0% -> 0% of each run, Pallas kernels for 9% -> 11%
where the time goes in v7:
time: 165 us; the launch traced here: 164 us
  starting transfers between devices  64.3 us (39%)
  blocking collectives  33.2 us (20%)
  waiting for transfers between devices  33.1 us (20%)
  Pallas kernels  30.8 us (19%)
    ppermute x30, starting transfers between devices, over_q(): return lax.ppermute(v, 'q', [(i, i ^ m) for i in range(z.Q)]) if m else v  37.8 us
    all_to_all x4, blocking collectives, sharers(): return lax.all_to_all(v, ('s', 'z'), 0, 0)  33.2 us
    pallas_call x18, Pallas kernels, call(): pl.pallas_call(run, out_shape=out_shape, in_specs=[pl.BlockSpec(memory_sp...  28 us
    ppermute x12, starting transfers between devices, over_z(): return lax.ppermute(v, 'z', [(i, i ^ m) for i in range(z.Z)]) if m else v  20.2 us
    ppermute x12, waiting for transfers between devices, over_z(): return lax.ppermute(v, 'z', [(i, i ^ m) for i in range(z.Z)]) if m else v  15.7 us
    ppermute x30, waiting for transfers between devices, over_q(): return lax.ppermute(v, 'q', [(i, i ^ m) for i in range(z.Q)]) if m else v  13 us
    all_to_all x1, waiting for transfers between devices, shards(): stats = lax.all_to_all(stats, ('s', 'q', 'z'), 0, 0)  4.3 us
    all_to_all x1, starting transfers between devices, shards(): stats = lax.all_to_all(stats, ('s', 'q', 'z'), 0, 0)  3.79 us
  transfers between devices with their start and end apart: 53, of which 18 were waited for; matrix products, arithmetic and copies ran while one was open for 0% of the time, Pallas kernels for 11%

profile of v7, /device:TPU:0, one launch (start us, length us, event | category | flops | bytes accessed | tf_op | source)
XLA Modules:
  0.0 164.4 jit_solution(13255420245428380953)
XLA Ops:
  0.7 1.2 convert.4
  1.9 3.1 %collective-permute-start = (bf16[9,64,128]{2,1,0:T(8,128)(2,1)S(1)}, bf16[9,64,128]{2,1,0:T(8,128)(2,1)S(1)}, u32[]{:S(2)}, u32[]{:S(2)}) collective-permute-start(bf16[9,64,128]{2,1,0:T(8,128)(2,1)S(1)} %get-tuple-element.161.refs_1_), channel_id=1, source_target_pairs={{0,1},{1,0},{2,3},{3,2},{4,5},{5,4},{6,7},{7,6},{8,9},{9,8},{10,11... | collective-permute-start | bytes 442376 | tf_op jit(solution)/shard_map/ppermute | solution.py:646
  5.0 2.6 %collective-permute-start.1 = (bf16[9,64,128]{2,1,0:T(8,128)(2,1)S(1)}, bf16[9,64,128]{2,1,0:T(8,128)(2,1)S(1)}, u32[]{:S(2)}, u32[]{:S(2)}) collective-permute-start(bf16[9,64,128]{2,1,0:T(8,128)(2,1)S(1)} %get-tuple-element.161.refs_1_), channel_id=1, source_target_pairs={{0,2},{1,3},{2,0},{3,1},{4,6},{5,7},{6,4},{7,5},{8,10},{9,11},{10,... | collective-permute-start | bytes 442376 | tf_op jit(solution)/shard_map/ppermute | solution.py:646
  7.6 1.7 %collective-permute-start.3 = (bf16[256,512]{1,0:T(8,128)(2,1)S(1)}, bf16[256,512]{1,0:T(8,128)(2,1)S(1)}, u32[]{:S(2)}, u32[]{:S(2)}) collective-permute-start(bf16[256,512]{1,0:T(8,128)(2,1)S(1)} %bitcast.12), channel_id=1, source_target_pairs={{0,8},{8,0},{16,24},{24,16},{1,9},{9,1},{17,25},{25,17},{2,10},{10... | collective-permute-start | bytes 786440 | tf_op jit(solution)/shard_map/ppermute | solution.py:655
  9.3 1.5 collective-permute-start.4
  10.8 2.7 %collective-permute-start.5 = (bf16[256,512]{1,0:T(8,128)(2,1)S(1)}, bf16[256,512]{1,0:T(8,128)(2,1)S(1)}, u32[]{:S(2)}, u32[]{:S(2)}) collective-permute-start(bf16[256,512]{1,0:T(8,128)(2,1)S(1)} %bitcast.14), channel_id=1, source_target_pairs={{0,24},{8,16},{16,8},{24,0},{1,25},{9,17},{17,9},{25,1},{2,26},{10... | collective-permute-start | bytes 786440 | tf_op jit(solution)/shard_map/ppermute | solution.py:655
  13.5 5.5 %collective-permute-done.1.refs_3_ = bf16[9,64,128]{2,1,0:T(8,128)(2,1)S(1)} collective-permute-done((bf16[9,64,128]{2,1,0:T(8,128)(2,1)S(1)}, bf16[9,64,128]{2,1,0:T(8,128)(2,1)S(1)}, u32[]{:S(2)}, u32[]{:S(2)}) %collective-permute-start.1) | collective-permute-done | bytes 147488 | tf_op jit(solution)/shard_map/ppermute | solution.py:646
  19.0 3.3 %collective-permute-start.10 = (bf16[9,64,128]{2,1,0:T(8,128)(2,1)S(1)}, bf16[9,64,128]{2,1,0:T(8,128)(2,1)S(1)}, u32[]{:S(2)}, u32[]{:S(2)}) collective-permute-start(bf16[9,64,128]{2,1,0:T(8,128)(2,1)S(1)} %get-tuple-element.186.refs_1_), channel_id=1, source_target_pairs={{0,2},{1,3},{2,0},{3,1},{4,6},{5,7},{6,4},{7,5},{8,10},{9,11},{10,... | collective-permute-start | bytes 442376 | tf_op jit(solution)/shard_map/ppermute | solution.py:646
  23.0 1.6 collective-permute-start.6
  24.6 1.5 collective-permute-start.7
  26.6 2.3 %collective-permute-start.11 = (bf16[9,64,128]{2,1,0:T(8,128)(2,1)S(1)}, bf16[9,64,128]{2,1,0:T(8,128)(2,1)S(1)}, u32[]{:S(2)}, u32[]{:S(2)}) collective-permute-start(bf16[9,64,128]{2,1,0:T(8,128)(2,1)S(1)} %get-tuple-element.186.refs_1_), channel_id=1, source_target_pairs={{0,3},{1,2},{2,1},{3,0},{4,7},{5,6},{6,5},{7,4},{8,11},{9,10},{10,... | collective-permute-start | bytes 442376 | tf_op jit(solution)/shard_map/ppermute | solution.py:646
  28.9 2.1 %collective-permute-done.10.refs_3_ = bf16[9,64,128]{2,1,0:T(8,128)(2,1)S(1)} collective-permute-done((bf16[9,64,128]{2,1,0:T(8,128)(2,1)S(1)}, bf16[9,64,128]{2,1,0:T(8,128)(2,1)S(1)}, u32[]{:S(2)}, u32[]{:S(2)}) %collective-permute-start.10) | collective-permute-done | bytes 147488 | tf_op jit(solution)/shard_map/ppermute | solution.py:646
  30.9 1.3 shard_map.169
  32.3 1.4 collective-permute-done.11.refs_4_
  33.7 2.4 %collective-permute-done.9.refs_2_ = bf16[9,64,128]{2,1,0:T(8,128)(2,1)S(1)} collective-permute-done((bf16[9,64,128]{2,1,0:T(8,128)(2,1)S(1)}, bf16[9,64,128]{2,1,0:T(8,128)(2,1)S(1)}, u32[]{:S(2)}, u32[]{:S(2)}) %collective-permute-start.9) | collective-permute-done | bytes 147488 | tf_op jit(solution)/shard_map/ppermute | solution.py:646
  37.2 1.4 shard_map.171
  38.6 2.5 %shard_map.170 = (f32[1024,128]{1,0:T(8,128)S(1)}, f32[16,8,128]{2,1,0:T(8,128)S(1)}, f32[8,4,128]{2,1,0:T(4,128)S(1)}, bf16[512,1152]{1,0:T(8,128)(2,1)}) custom-call(s32[3]{0:T(128)S(1)} %pad_add_fusion.refs_0_.refs_9_, bf16[256,512]{1,0:T(8,128)(2,1)S(1)} %bitcast.16, bf16[256,512]{1,0:T(8,128)(2,1)S(1)} %collective-permute-done.3.refs_3_.refs_2_, ...), custom_call_target="tpu_custom_call" | custom-call | flops 1 | bytes 1 | tf_op jit(solution)/shard_map/pallas_call | solution.py:68
  41.2 1.6 collective-permute-start.16
  42.8 1.5 collective-permute-start.17
  44.7 8.7 %all_to_all.25.refs_2_ = f32[8,4,128]{2,1,0:T(4,128)S(1)} all-to-all(f32[8,4,128]{2,1,0:T(4,128)S(1)} %get-tuple-element.194), channel_id=1, replica_groups=mesh['ha'=2,'wa'=4,'ba'=4] {'wa':(2)2,'ba'}, dimensions={0} | all-to-all | bytes 32768 | tf_op jit(solution)/shard_map/all_to_all | solution.py:652
  53.4 0.8 collective-permute-done.18.refs_8_
  54.2 1.0 shard_map.172
  55.3 1.6 collective-permute-start.20
  56.8 1.6 collective-permute-start.22
  59.4 1.9 %collective-permute-done.20.refs_3_ = bf16[512,128]{1,0:T(8,128)(2,1)S(1)} collective-permute-done((bf16[512,128]{1,0:T(8,128)(2,1)S(1)}, bf16[512,128]{1,0:T(8,128)(2,1)S(1)}, u32[]{:S(2)}, u32[]{:S(2)}) %collective-permute-start.20) | collective-permute-done | bytes 131104 | tf_op jit(solution)/shard_map/ppermute | solution.py:655
  61.3 1.5 collective-permute-start.21
  63.2 1.5 collective-permute-start.24
  64.7 1.3 collective-permute-done.19.refs_2_
  66.0 2.0 %collective-permute-done.21.refs_4_ = bf16[512,128]{1,0:T(8,128)(2,1)S(1)} collective-permute-done((bf16[512,128]{1,0:T(8,128)(2,1)S(1)}, bf16[512,128]{1,0:T(8,128)(2,1)S(1)}, u32[]{:S(2)}, u32[]{:S(2)}) %collective-permute-start.21) | collective-permute-done | bytes 131104 | tf_op jit(solution)/shard_map/ppermute | solution.py:655
  68.2 3.3 %shard_map.173 = (bf16[1024,256]{1,0:T(8,128)(2,1)S(1)}, bf16[1024,256]{1,0:T(8,128)(2,1)S(1)}, f32[1024,128]{1,0:T(8,128)S(1)}, f32[8,4,128]{2,1,0:T(4,128)S(1)}) custom-call(s32[3]{0:T(128)S(1)} %pad_add_fusion.refs_0_.refs_9_, bf16[512,128]{1,0:T(8,128)(2,1)S(1)} %get-tuple-element.206.refs_1_, bf16[512,128]{1,0:T(8,128)(2,1)S(1)} %collective-permute-done.19.refs_2_, ...), custom_call_target="tpu_custom_call" | custom-call | flops 1 | bytes 1 | tf_op jit(solution)/shard_map/pallas_call | solution.py:68
  72.0 8.7 %all_to_all.26.refs_2_ = f32[8,4,128]{2,1,0:T(4,128)S(1)} all-to-all(f32[8,4,128]{2,1,0:T(4,128)S(1)} %get-tuple-element.215), channel_id=1, replica_groups=mesh['ha'=2,'wa'=4,'ba'=4] {'wa':(2)2,'ba'}, dimensions={0} | all-to-all | bytes 32768 | tf_op jit(solution)/shard_map/all_to_all | solution.py:652
  80.7 1.3 shard_map.174
  82.0 8.0 %all_to_all.27.refs_3_ = f32[8,2,128]{2,1,0:T(2,128)S(1)} all-to-all(f32[8,2,128]{2,1,0:T(2,128)S(1)} %get-tuple-element.225), channel_id=1, replica_groups=mesh['ha'=2,'wa'=4,'ba'=4] {'wa':(2)2,'ba'}, dimensions={0} | all-to-all | bytes 16384 | tf_op jit(solution)/shard_map/all_to_all | solution.py:652
  90.8 1.5 collective-permute-start.29
  92.9 1.4 collective-permute-start.28
  94.3 2.0 %collective-permute-done.29.refs_3_ = bf16[512,128]{1,0:T(8,128)(2,1)S(1)} collective-permute-done((bf16[512,128]{1,0:T(8,128)(2,1)S(1)}, bf16[512,128]{1,0:T(8,128)(2,1)S(1)}, u32[]{:S(2)}, u32[]{:S(2)}) %collective-permute-start.29) | collective-permute-done | bytes 131104 | tf_op jit(solution)/shard_map/ppermute | solution.py:655
  96.3 1.5 collective-permute-start.32
  97.8 0.9 collective-permute-done.31.refs_6_
  99.3 1.5 collective-permute-start.33
  100.8 2.6 %shard_map.178 = (bf16[832,128]{1,0:T(8,128)(2,1)S(1)}, bf16[832,128]{1,0:T(8,128)(2,1)S(1)}, bf16[832,128]{1,0:T(8,128)(2,1)S(1)}, bf16[832,128]{1,0:T(8,128)(2,1)S(1)}) custom-call(s32[3]{0:T(128)S(1)} %pad_add_fusion.refs_0_.refs_9_, bf16[1024,256]{1,0:T(8,128)(2,1)S(1)} %get-tuple-element.236.refs_1_, ...), custom_call_target="tpu_custom_call" | custom-call | flops 3000000000 | bytes 1 | tf_op jit(solution)/shard_map/pallas_call | solution.py:68
  103.4 1.3 shard_map.176
  104.7 2.4 %shard_map.177 = (f32[1024,128]{1,0:T(8,128)S(1)}, f32[8,2,128]{2,1,0:T(2,128)S(1)}) custom-call(s32[3]{0:T(128)S(1)} %pad_add_fusion.refs_0_.refs_9_, bf16[512,128]{1,0:T(8,128)(2,1)S(1)} %get-tuple-element.229.refs_1_.refs_3_, bf16[512,128]{1,0:T(8,128)(2,1)S(1)} %collective-permute-done.28.refs_2_, bf16[512,128]{1,0:T(8,128)(2,1)S(1)} %collective-permute-done.29.refs_3_, ...), custom_call_target="tpu_custom_call" | custom-call | flops 1 | bytes 1 | tf_op jit(solution)/shard_map/pallas_call | solution.py:68
  107.1 1.0 collective-permute-start.36
  108.2 1.0 collective-permute-start.37
  109.2 1.5 collective-permute-start.38
  110.7 8.0 %all_to_all.28.refs_3_ = f32[8,2,128]{2,1,0:T(2,128)S(1)} all-to-all(f32[8,2,128]{2,1,0:T(2,128)S(1)} %get-tuple-element.244), channel_id=1, replica_groups=mesh['ha'=2,'wa'=4,'ba'=4] {'wa':(2)2,'ba'}, dimensions={0} | all-to-all | bytes 16384 | tf_op jit(solution)/shard_map/all_to_all | solution.py:652
  121.0 3.3 %collective-permute-start.45 = (bf16[576,128]{1,0:T(8,128)(2,1)S(1)}, bf16[576,128]{1,0:T(8,128)(2,1)S(1)}, u32[]{:S(2)}, u32[]{:S(2)}) collective-permute-start(bf16[576,128]{1,0:T(8,128)(2,1)S(1)} %get-tuple-element.268), channel_id=1, source_target_pairs={{0,3},{1,2},{2,1},{3,0},{4,7},{5,6},{6,5},{7,4},{8,11},{9,10},{10,... | collective-permute-start | bytes 442376 | tf_op jit(solution)/shard_map/ppermute | solution.py:646
  124.3 2.6 %shard_map.181 = (bf16[576,128]{1,0:T(8,128)(2,1)S(1)}, bf16[576,128]{1,0:T(8,128)(2,1)S(1)}, bf16[576,128]{1,0:T(8,128)(2,1)S(1)}, bf16[576,128]{1,0:T(8,128)(2,1)S(1)}) custom-call(s32[3]{0:T(128)S(1)} %pad_add_fusion.refs_0_.refs_9_, bf16[1024,256]{1,0:T(8,128)(2,1)S(1)} %get-tuple-element.257.refs_1_, ...), custom_call_target="tpu_custom_call" | custom-call | flops 3000000000 | bytes 1 | tf_op jit(solution)/shard_map/pallas_call | solution.py:68
  126.9 1.0 collective-permute-start.40
  127.9 1.0 collective-permute-start.41
  128.9 1.5 collective-permute-start.42
  130.5 3.9 %collective-permute-done.44.refs_2_ = bf16[576,128]{1,0:T(8,128)(2,1)S(1)} collective-permute-done((bf16[576,128]{1,0:T(8,128)(2,1)S(1)}, bf16[576,128]{1,0:T(8,128)(2,1)S(1)}, u32[]{:S(2)}, u32[]{:S(2)}) %collective-permute-start.44) | collective-permute-done | bytes 147488 | tf_op jit(solution)/shard_map/ppermute | solution.py:646
  134.5 2.1 %collective-permute-done.42.refs_4_ = bf16[576,128]{1,0:T(8,128)(2,1)S(1)} collective-permute-done((bf16[576,128]{1,0:T(8,128)(2,1)S(1)}, bf16[576,128]{1,0:T(8,128)(2,1)S(1)}, u32[]{:S(2)}, u32[]{:S(2)}) %collective-permute-start.42) | collective-permute-done | bytes 147488 | tf_op jit(solution)/shard_map/ppermute | solution.py:655
  138.4 3.3 %collective-permute-start.48 = (bf16[576,128]{1,0:T(8,128)(2,1)S(1)}, bf16[576,128]{1,0:T(8,128)(2,1)S(1)}, u32[]{:S(2)}, u32[]{:S(2)}) collective-permute-start(bf16[576,128]{1,0:T(8,128)(2,1)S(1)} %get-tuple-element.284), channel_id=1, source_target_pairs={{0,3},{1,2},{2,1},{3,0},{4,7},{5,6},{6,5},{7,4},{8,11},{9,10},{10,... | collective-permute-start | bytes 442376 | tf_op jit(solution)/shard_map/ppermute | solution.py:646
  141.7 3.9 %shard_map.185 = (f32[256,512]{1,0:T(8,128)S(1)}, bf16[256,512]{1,0:T(8,128)(2,1)}, bf16[256,512]{1,0:T(8,128)(2,1)S(1)}, bf16[256,512]{1,0:T(8,128)(2,1)S(1)}) custom-call(s32[3]{0:T(128)S(1)} %pad_add_fusion.refs_0_.refs_9_, bf16[512,128]{1,0:T(8,128)(2,1)S(1)} %get-tuple-element.255.refs_5_.refs_3_.refs_1_, ...), custom_call_target="tpu_custom_call" | custom-call | flops 3000000000 | bytes 1 | tf_op jit(solution)/shard_map/pallas_call | solution.py:68
  145.6 1.0 collective-permute-start.49
  146.5 1.0 collective-permute-start.50
  147.5 1.6 shard_map.183
  149.2 1.5 collective-permute-start.51
  151.1 1.1 shard_map.184
  152.2 3.8 %all-to-all-start.4 = ((f32[32,2,128]{2,1,0:T(2,128)}), f32[32,2,128]{2,1,0:T(2,128)S(1)}, u32[]{:S(2)}, u32[]{:S(2)}) async-start(f32[32,2,128]{2,1,0:T(2,128)} %get-tuple-element.294), calls=%async_computation.4 | async-start | bytes 65536 | tf_op jit(solution)/shard_map/all_to_all | solution.py:840
  156.7 1.4 collective-permute-done.51.refs_3_
  158.9 4.3 %all-to-all-done.4.refs_0_ = f32[32,2,128]{2,1,0:T(2,128)S(1)} async-done(((f32[32,2,128]{2,1,0:T(2,128)}), f32[32,2,128]{2,1,0:T(2,128)S(1)}, u32[]{:S(2)}, u32[]{:S(2)}) %all-to-all-start.4) | async-done | bytes 32800 | tf_op jit(solution)/shard_map/all_to_all | solution.py:840
  163.2 1.2 shard_map.187
  (90 shorter events, 13.2 us)
Async XLA Ops:
  0.6 6.9 %copy-start.1 = (bf16[4,8,8,512]{3,2,1,0:T(8,128)(2,1)S(1)}, bf16[4,8,8,512]{3,2,1,0:T(8,128)(2,1)}, u32[]{:S(2)}) copy-start(bf16[4,8,8,512]{3,2,1,0:T(8,128)(2,1)} %param.9) | copy-start | bytes 786436
  0.7 21.7 %copy-start.7 = (s32[4,8,8]{2,1,0:T(8,128)S(1)}, s32[4,8,8]{2,1,0:T(8,128)}, u32[]{:S(2)}) copy-start(s32[4,8,8]{2,1,0:T(8,128)} %refs_5_.4) | copy-start | bytes 3076
  0.7 30.3 %copy-start.6 = (f32[4,512]{1,0:T(4,128)S(1)}, f32[4,512]{1,0:T(4,128)}, u32[]{:S(2)}) copy-start(f32[4,512]{1,0:T(4,128)} %refs_4_.5) | copy-start | bytes 24580
  1.8 35.4 %copy-start.5 = (bf16[4,8,8,512]{3,2,1,0:T(8,128)(2,1)S(1)}, bf16[4,8,8,512]{3,2,1,0:T(8,128)(2,1)}, u32[]{:S(2)}) copy-start(bf16[4,8,8,512]{3,2,1,0:T(8,128)(2,1)} %param.11) | copy-start | bytes 786436
  1.9 8.9 %collective-permute-start = (bf16[9,64,128]{2,1,0:T(8,128)(2,1)S(1)}, bf16[9,64,128]{2,1,0:T(8,128)(2,1)S(1)}, u32[]{:S(2)}, u32[]{:S(2)}) collective-permute-start(bf16[9,64,128]{2,1,0:T(8,128)(2,1)S(1)} %get-tuple-element.161.refs_1_), channel_id=1, source_target_pairs={{0,1},{1,0},{2,3},{3,2},{4,5},{5,4},{6,7},{7,6},{8,9},{9,8},{10,11... | collective-permute-start | bytes 442376 | tf_op jit(solution)/shard_map/ppermute | solution.py:646
  5.0 14.0 %collective-permute-start.1 = (bf16[9,64,128]{2,1,0:T(8,128)(2,1)S(1)}, bf16[9,64,128]{2,1,0:T(8,128)(2,1)S(1)}, u32[]{:S(2)}, u32[]{:S(2)}) collective-permute-start(bf16[9,64,128]{2,1,0:T(8,128)(2,1)S(1)} %get-tuple-element.161.refs_1_), channel_id=1, source_target_pairs={{0,2},{1,3},{2,0},{3,1},{4,6},{5,7},{6,4},{7,5},{8,10},{9,11},{10,... | collective-permute-start | bytes 442376 | tf_op jit(solution)/shard_map/ppermute | solution.py:646
  7.6 11.4 %collective-permute-start.2 = (bf16[9,64,128]{2,1,0:T(8,128)(2,1)S(1)}, bf16[9,64,128]{2,1,0:T(8,128)(2,1)S(1)}, u32[]{:S(2)}, u32[]{:S(2)}) collective-permute-start(bf16[9,64,128]{2,1,0:T(8,128)(2,1)S(1)} %get-tuple-element.161.refs_1_), channel_id=1, source_target_pairs={{0,3},{1,2},{2,1},{3,0},{4,7},{5,6},{6,5},{7,4},{8,11},{9,10},{10,... | collective-permute-start | bytes 442376 | tf_op jit(solution)/shard_map/ppermute | solution.py:646
  7.6 15.4 %collective-permute-start.3 = (bf16[256,512]{1,0:T(8,128)(2,1)S(1)}, bf16[256,512]{1,0:T(8,128)(2,1)S(1)}, u32[]{:S(2)}, u32[]{:S(2)}) collective-permute-start(bf16[256,512]{1,0:T(8,128)(2,1)S(1)} %bitcast.12), channel_id=1, source_target_pairs={{0,8},{8,0},{16,24},{24,16},{1,9},{9,1},{17,25},{25,17},{2,10},{10... | collective-permute-start | bytes 786440 | tf_op jit(solution)/shard_map/ppermute | solution.py:655
  9.3 13.7 %collective-permute-start.4 = (bf16[256,512]{1,0:T(8,128)(2,1)S(1)}, bf16[256,512]{1,0:T(8,128)(2,1)S(1)}, u32[]{:S(2)}, u32[]{:S(2)}) collective-permute-start(bf16[256,512]{1,0:T(8,128)(2,1)S(1)} %bitcast.13), channel_id=1, source_target_pairs={{0,16},{8,24},{16,0},{24,8},{1,17},{9,25},{17,1},{25,9},{2,18},{10... | collective-permute-start | bytes 786440 | tf_op jit(solution)/shard_map/ppermute | solution.py:655
  10.8 12.2 %collective-permute-start.5 = (bf16[256,512]{1,0:T(8,128)(2,1)S(1)}, bf16[256,512]{1,0:T(8,128)(2,1)S(1)}, u32[]{:S(2)}, u32[]{:S(2)}) collective-permute-start(bf16[256,512]{1,0:T(8,128)(2,1)S(1)} %bitcast.14), channel_id=1, source_target_pairs={{0,24},{8,16},{16,8},{24,0},{1,25},{9,17},{17,9},{25,1},{2,26},{10... | collective-permute-start | bytes 786440 | tf_op jit(solution)/shard_map/ppermute | solution.py:655
  19.0 12.0 %collective-permute-start.10 = (bf16[9,64,128]{2,1,0:T(8,128)(2,1)S(1)}, bf16[9,64,128]{2,1,0:T(8,128)(2,1)S(1)}, u32[]{:S(2)}, u32[]{:S(2)}) collective-permute-start(bf16[9,64,128]{2,1,0:T(8,128)(2,1)S(1)} %get-tuple-element.186.refs_1_), channel_id=1, source_target_pairs={{0,2},{1,3},{2,0},{3,1},{4,6},{5,7},{6,4},{7,5},{8,10},{9,11},{10,... | collective-permute-start | bytes 442376 | tf_op jit(solution)/shard_map/ppermute | solution.py:646
  23.0 13.1 %collective-permute-start.6 = (bf16[592,128]{1,0:T(8,128)(2,1)S(1)}, bf16[592,128]{1,0:T(8,128)(2,1)S(1)}, u32[]{:S(2)}, u32[]{:S(2)}) collective-permute-start(bf16[592,128]{1,0:T(8,128)(2,1)S(1)} %get-tuple-element.174), channel_id=1, source_target_pairs={{0,8},{8,0},{16,24},{24,16},{1,9},{9,1},{17,25},{25,17},{2,10},{10... | collective-permute-start | bytes 454664 | tf_op jit(solution)/shard_map/ppermute | solution.py:655
  24.6 11.5 %collective-permute-start.7 = (bf16[592,128]{1,0:T(8,128)(2,1)S(1)}, bf16[592,128]{1,0:T(8,128)(2,1)S(1)}, u32[]{:S(2)}, u32[]{:S(2)}) collective-permute-start(bf16[592,128]{1,0:T(8,128)(2,1)S(1)} %get-tuple-element.175), channel_id=1, source_target_pairs={{0,16},{8,24},{16,0},{24,8},{1,17},{9,25},{17,1},{25,9},{2,18},{10... | collective-permute-start | bytes 454664 | tf_op jit(solution)/shard_map/ppermute | solution.py:655
  26.1 10.0 %collective-permute-start.8 = (bf16[592,128]{1,0:T(8,128)(2,1)S(1)}, bf16[592,128]{1,0:T(8,128)(2,1)S(1)}, u32[]{:S(2)}, u32[]{:S(2)}) collective-permute-start(bf16[592,128]{1,0:T(8,128)(2,1)S(1)} %get-tuple-element.176), channel_id=1, source_target_pairs={{0,24},{8,16},{16,8},{24,0},{1,25},{9,17},{17,9},{25,1},{2,26},{10... | collective-permute-start | bytes 454664 | tf_op jit(solution)/shard_map/ppermute | solution.py:655
  26.6 7.1 %collective-permute-start.11 = (bf16[9,64,128]{2,1,0:T(8,128)(2,1)S(1)}, bf16[9,64,128]{2,1,0:T(8,128)(2,1)S(1)}, u32[]{:S(2)}, u32[]{:S(2)}) collective-permute-start(bf16[9,64,128]{2,1,0:T(8,128)(2,1)S(1)} %get-tuple-element.186.refs_1_), channel_id=1, source_target_pairs={{0,3},{1,2},{2,1},{3,0},{4,7},{5,6},{6,5},{7,4},{8,11},{9,10},{10,... | collective-permute-start | bytes 442376 | tf_op jit(solution)/shard_map/ppermute | solution.py:646
  30.9 5.1 %collective-permute-start.9 = (bf16[9,64,128]{2,1,0:T(8,128)(2,1)S(1)}, bf16[9,64,128]{2,1,0:T(8,128)(2,1)S(1)}, u32[]{:S(2)}, u32[]{:S(2)}) collective-permute-start(bf16[9,64,128]{2,1,0:T(8,128)(2,1)S(1)} %get-tuple-element.186.refs_1_), channel_id=1, source_target_pairs={{0,1},{1,0},{2,3},{3,2},{4,5},{5,4},{6,7},{7,6},{8,9},{9,8},{10,11... | collective-permute-start | bytes 442376 | tf_op jit(solution)/shard_map/ppermute | solution.py:646
  36.1 2.5 %collective-permute-start.12 = (bf16[592,128]{1,0:T(8,128)(2,1)S(1)}, bf16[592,128]{1,0:T(8,128)(2,1)S(1)}, u32[]{:S(2)}, u32[]{:S(2)}) collective-permute-start(bf16[592,128]{1,0:T(8,128)(2,1)S(1)} %get-tuple-element.180.refs_5_), channel_id=1, source_target_pairs={{0,4},{4,0},{1,5},{5,1},{2,6},{6,2},{3,7},{7,3},{8,12},{12,8},{9,1... | collective-permute-start | bytes 454664 | tf_op jit(solution)/shard_map/ppermute | solution.py:649
  36.2 2.4 %collective-permute-start.13 = (bf16[592,128]{1,0:T(8,128)(2,1)S(1)}, bf16[592,128]{1,0:T(8,128)(2,1)S(1)}, u32[]{:S(2)}, u32[]{:S(2)}) collective-permute-start(bf16[592,128]{1,0:T(8,128)(2,1)S(1)} %collective-permute-done.6.refs_6_), channel_id=1, source_target_pairs={{0,4},{4,0},{1,5},{5,1},{2,6},{6,2},{3,7},{7,3},{8,12},{12,8},{9,1... | collective-permute-start | bytes 454664 | tf_op jit(solution)/shard_map/ppermute | solution.py:649
  36.7 1.9 %collective-permute-start.14 = (bf16[592,128]{1,0:T(8,128)(2,1)S(1)}, bf16[592,128]{1,0:T(8,128)(2,1)S(1)}, u32[]{:S(2)}, u32[]{:S(2)}) collective-permute-start(bf16[592,128]{1,0:T(8,128)(2,1)S(1)} %collective-permute-done.7.refs_7_), channel_id=1, source_target_pairs={{0,4},{4,0},{1,5},{5,1},{2,6},{6,2},{3,7},{7,3},{8,12},{12,8},{9,1... | collective-permute-start | bytes 454664 | tf_op jit(solution)/shard_map/ppermute | solution.py:649
  36.8 1.9 %collective-permute-start.15 = (bf16[592,128]{1,0:T(8,128)(2,1)S(1)}, bf16[592,128]{1,0:T(8,128)(2,1)S(1)}, u32[]{:S(2)}, u32[]{:S(2)}) collective-permute-start(bf16[592,128]{1,0:T(8,128)(2,1)S(1)} %collective-permute-done.8.refs_8_), channel_id=1, source_target_pairs={{0,4},{4,0},{1,5},{5,1},{2,6},{6,2},{3,7},{7,3},{8,12},{12,8},{9,1... | collective-permute-start | bytes 454664 | tf_op jit(solution)/shard_map/ppermute | solution.py:649
  41.2 12.2 %collective-permute-start.16 = (bf16[832,128]{1,0:T(8,128)(2,1)S(1)}, bf16[832,128]{1,0:T(8,128)(2,1)S(1)}, u32[]{:S(2)}, u32[]{:S(2)}) collective-permute-start(bf16[832,128]{1,0:T(8,128)(2,1)S(1)} %get-tuple-element.196), channel_id=1, source_target_pairs={{0,8},{8,0},{16,24},{24,16},{1,9},{9,1},{17,25},{25,17},{2,10},{10... | collective-permute-start | bytes 638984 | tf_op jit(solution)/shard_map/ppermute | solution.py:655
  42.8 10.6 %collective-permute-start.17 = (bf16[832,128]{1,0:T(8,128)(2,1)S(1)}, bf16[832,128]{1,0:T(8,128)(2,1)S(1)}, u32[]{:S(2)}, u32[]{:S(2)}) collective-permute-start(bf16[832,128]{1,0:T(8,128)(2,1)S(1)} %get-tuple-element.197), channel_id=1, source_target_pairs={{0,16},{8,24},{16,0},{24,8},{1,17},{9,25},{17,1},{25,9},{2,18},{10... | collective-permute-start | bytes 638984 | tf_op jit(solution)/shard_map/ppermute | solution.py:655
  44.2 10.0 %collective-permute-start.18 = (bf16[832,128]{1,0:T(8,128)(2,1)S(1)}, bf16[832,128]{1,0:T(8,128)(2,1)S(1)}, u32[]{:S(2)}, u32[]{:S(2)}) collective-permute-start(bf16[832,128]{1,0:T(8,128)(2,1)S(1)} %get-tuple-element.198), channel_id=1, source_target_pairs={{0,24},{8,16},{16,8},{24,0},{1,25},{9,17},{17,9},{25,1},{2,26},{10... | collective-permute-start | bytes 638984 | tf_op jit(solution)/shard_map/ppermute | solution.py:655
  55.2 12.9 %collective-permute-start.25 = (bf16[4,9,64,128]{3,2,1,0:T(8,128)(2,1)S(1)}, bf16[4,9,64,128]{3,2,1,0:T(8,128)(2,1)S(1)}, u32[]{:S(2)}, u32[]{:S(2)}) collective-permute-start(bf16[4,9,64,128]{3,2,1,0:T(8,128)(2,1)S(1)} %get-tuple-element.208.refs_9_), channel_id=1, source_target_pairs={{0,4},{4,0},{1,5},{5,1},{2,6},{6,2},{3,7},{7,3},{8,12},{12,8},{9,1... | collective-permute-start | bytes 1769480 | tf_op jit(solution)/shard_map/ppermute | solution.py:649
  55.3 6.0 %collective-permute-start.20 = (bf16[512,128]{1,0:T(8,128)(2,1)S(1)}, bf16[512,128]{1,0:T(8,128)(2,1)S(1)}, u32[]{:S(2)}, u32[]{:S(2)}) collective-permute-start(bf16[512,128]{1,0:T(8,128)(2,1)S(1)} %get-tuple-element.206.refs_1_), channel_id=1, source_target_pairs={{0,16},{8,24},{16,0},{24,8},{1,17},{9,25},{17,1},{25,9},{2,18},{10... | collective-permute-start | bytes 393224 | tf_op jit(solution)/shard_map/ppermute | solution.py:655
  56.8 6.3 %collective-permute-start.22 = (bf16[512,128]{1,0:T(8,128)(2,1)S(1)}, bf16[512,128]{1,0:T(8,128)(2,1)S(1)}, u32[]{:S(2)}, u32[]{:S(2)}) collective-permute-start(bf16[512,128]{1,0:T(8,128)(2,1)S(1)} %get-tuple-element.207.refs_5_), channel_id=1, source_target_pairs={{0,8},{8,0},{16,24},{24,16},{1,9},{9,1},{17,25},{25,17},{2,10},{10... | collective-permute-start | bytes 393224 | tf_op jit(solution)/shard_map/ppermute | solution.py:655
  58.4 7.6 %collective-permute-start.19 = (bf16[512,128]{1,0:T(8,128)(2,1)S(1)}, bf16[512,128]{1,0:T(8,128)(2,1)S(1)}, u32[]{:S(2)}, u32[]{:S(2)}) collective-permute-start(bf16[512,128]{1,0:T(8,128)(2,1)S(1)} %get-tuple-element.206.refs_1_), channel_id=1, source_target_pairs={{0,8},{8,0},{16,24},{24,16},{1,9},{9,1},{17,25},{25,17},{2,10},{10... | collective-permute-start | bytes 393224 | tf_op jit(solution)/shard_map/ppermute | solution.py:655
  58.9 7.1 %collective-permute-start.23 = (bf16[512,128]{1,0:T(8,128)(2,1)S(1)}, bf16[512,128]{1,0:T(8,128)(2,1)S(1)}, u32[]{:S(2)}, u32[]{:S(2)}) collective-permute-start(bf16[512,128]{1,0:T(8,128)(2,1)S(1)} %get-tuple-element.207.refs_5_), channel_id=1, source_target_pairs={{0,16},{8,24},{16,0},{24,8},{1,17},{9,25},{17,1},{25,9},{2,18},{10... | collective-permute-start | bytes 393224 | tf_op jit(solution)/shard_map/ppermute | solution.py:655
  61.3 6.8 %collective-permute-start.21 = (bf16[512,128]{1,0:T(8,128)(2,1)S(1)}, bf16[512,128]{1,0:T(8,128)(2,1)S(1)}, u32[]{:S(2)}, u32[]{:S(2)}) collective-permute-start(bf16[512,128]{1,0:T(8,128)(2,1)S(1)} %collective-permute-done.20.refs_3_), channel_id=1, source_target_pairs={{0,8},{8,0},{16,24},{24,16},{1,9},{9,1},{17,25},{25,17},{2,10},{10... | collective-permute-start | bytes 393224 | tf_op jit(solution)/shard_map/ppermute | solution.py:655
  63.2 5.0 %collective-permute-start.24 = (bf16[512,128]{1,0:T(8,128)(2,1)S(1)}, bf16[512,128]{1,0:T(8,128)(2,1)S(1)}, u32[]{:S(2)}, u32[]{:S(2)}) collective-permute-start(bf16[512,128]{1,0:T(8,128)(2,1)S(1)} %collective-permute-done.22.refs_6_), channel_id=1, source_target_pairs={{0,16},{8,24},{16,0},{24,8},{1,17},{9,25},{17,1},{25,9},{2,18},{10... | collective-permute-start | bytes 393224 | tf_op jit(solution)/shard_map/ppermute | solution.py:655
  71.4 18.8 %copy-start.2 = (bf16[4,9,64,128]{3,2,1,0:T(8,128)(2,1)S(1)}, bf16[4,9,64,128]{3,2,1,0:T(8,128)(2,1)}, u32[]{:S(2)}) copy-start(bf16[4,9,64,128]{3,2,1,0:T(8,128)(2,1)} %get-tuple-element.231.refs_1_) | copy-start | bytes 1769476
  71.4 9.2 %collective-permute-start.26 = (bf16[1024,256]{1,0:T(8,128)(2,1)S(1)}, bf16[1024,256]{1,0:T(8,128)(2,1)S(1)}, u32[]{:S(2)}, u32[]{:S(2)}) collective-permute-start(bf16[1024,256]{1,0:T(8,128)(2,1)S(1)} %get-tuple-element.217), channel_id=1, source_target_pairs={{0,4},{4,0},{1,5},{5,1},{2,6},{6,2},{3,7},{7,3},{8,12},{12,8},{9,1... | collective-permute-start | bytes 1572872 | tf_op jit(solution)/shard_map/ppermute | solution.py:649
  71.5 9.2 %collective-permute-start.27 = (bf16[1024,256]{1,0:T(8,128)(2,1)S(1)}, bf16[1024,256]{1,0:T(8,128)(2,1)S(1)}, u32[]{:S(2)}, u32[]{:S(2)}) collective-permute-start(bf16[1024,256]{1,0:T(8,128)(2,1)S(1)} %get-tuple-element.219), channel_id=1, source_target_pairs={{0,4},{4,0},{1,5},{5,1},{2,6},{6,2},{3,7},{7,3},{8,12},{12,8},{9,1... | collective-permute-start | bytes 1572872 | tf_op jit(solution)/shard_map/ppermute | solution.py:649
  90.2 13.2 %collective-permute-start.34 = (bf16[4,9,64,128]{3,2,1,0:T(8,128)(2,1)S(1)}, bf16[4,9,64,128]{3,2,1,0:T(8,128)(2,1)S(1)}, u32[]{:S(2)}, u32[]{:S(2)}) collective-permute-start(bf16[4,9,64,128]{3,2,1,0:T(8,128)(2,1)S(1)} %copy-done.2), channel_id=1, source_target_pairs={{0,4},{4,0},{1,5},{5,1},{2,6},{6,2},{3,7},{7,3},{8,12},{12,8},{9,1... | collective-permute-start | bytes 1769480 | tf_op jit(solution)/shard_map/ppermute | solution.py:649
  90.4 8.9 %collective-permute-start.35 = (bf16[1024,128]{1,0:T(8,128)(2,1)S(1)}, bf16[1024,128]{1,0:T(8,128)(2,1)S(1)}, u32[]{:S(2)}, u32[]{:S(2)}) collective-permute-start(bf16[1024,128]{1,0:T(8,128)(2,1)S(1)} %get-tuple-element.238), channel_id=1, source_target_pairs={{0,4},{4,0},{1,5},{5,1},{2,6},{6,2},{3,7},{7,3},{8,12},{12,8},{9,1... | collective-permute-start | bytes 786440 | tf_op jit(solution)/shard_map/ppermute | solution.py:649
  90.8 5.5 %collective-permute-start.29 = (bf16[512,128]{1,0:T(8,128)(2,1)S(1)}, bf16[512,128]{1,0:T(8,128)(2,1)S(1)}, u32[]{:S(2)}, u32[]{:S(2)}) collective-permute-start(bf16[512,128]{1,0:T(8,128)(2,1)S(1)} %get-tuple-element.229.refs_1_.refs_3_), channel_id=1, source_target_pairs={{0,16},{8,24},{16,0},{24,8},{1,17},{9,25},{17,1},{25,9},{2,18},{10... | collective-permute-start | bytes 393224 | tf_op jit(solution)/shard_map/ppermute | solution.py:655
  92.3 6.4 %collective-permute-start.31 = (bf16[512,128]{1,0:T(8,128)(2,1)S(1)}, bf16[512,128]{1,0:T(8,128)(2,1)S(1)}, u32[]{:S(2)}, u32[]{:S(2)}) collective-permute-start(bf16[512,128]{1,0:T(8,128)(2,1)S(1)} %get-tuple-element.230.refs_5_.refs_4_), channel_id=1, source_target_pairs={{0,8},{8,0},{16,24},{24,16},{1,9},{9,1},{17,25},{25,17},{2,10},{10... | collective-permute-start | bytes 393224 | tf_op jit(solution)/shard_map/ppermute | solution.py:655
  92.9 11.8 %collective-permute-start.28 = (bf16[512,128]{1,0:T(8,128)(2,1)S(1)}, bf16[512,128]{1,0:T(8,128)(2,1)S(1)}, u32[]{:S(2)}, u32[]{:S(2)}) collective-permute-start(bf16[512,128]{1,0:T(8,128)(2,1)S(1)} %get-tuple-element.229.refs_1_.refs_3_), channel_id=1, source_target_pairs={{0,8},{8,0},{16,24},{24,16},{1,9},{9,1},{17,25},{25,17},{2,10},{10... | collective-permute-start | bytes 393224 | tf_op jit(solution)/shard_map/ppermute | solution.py:655
  96.3 8.3 %collective-permute-start.32 = (bf16[512,128]{1,0:T(8,128)(2,1)S(1)}, bf16[512,128]{1,0:T(8,128)(2,1)S(1)}, u32[]{:S(2)}, u32[]{:S(2)}) collective-permute-start(bf16[512,128]{1,0:T(8,128)(2,1)S(1)} %get-tuple-element.230.refs_5_.refs_4_), channel_id=1, source_target_pairs={{0,16},{8,24},{16,0},{24,8},{1,17},{9,25},{17,1},{25,9},{2,18},{10... | collective-permute-start | bytes 393224 | tf_op jit(solution)/shard_map/ppermute | solution.py:655
  98.7 6.0 %collective-permute-start.30 = (bf16[512,128]{1,0:T(8,128)(2,1)S(1)}, bf16[512,128]{1,0:T(8,128)(2,1)S(1)}, u32[]{:S(2)}, u32[]{:S(2)}) collective-permute-start(bf16[512,128]{1,0:T(8,128)(2,1)S(1)} %collective-permute-done.29.refs_3_), channel_id=1, source_target_pairs={{0,8},{8,0},{16,24},{24,16},{1,9},{9,1},{17,25},{25,17},{2,10},{10... | collective-permute-start | bytes 393224 | tf_op jit(solution)/shard_map/ppermute | solution.py:655
  99.3 5.4 %collective-permute-start.33 = (bf16[512,128]{1,0:T(8,128)(2,1)S(1)}, bf16[512,128]{1,0:T(8,128)(2,1)S(1)}, u32[]{:S(2)}, u32[]{:S(2)}) collective-permute-start(bf16[512,128]{1,0:T(8,128)(2,1)S(1)} %collective-permute-done.31.refs_6_), channel_id=1, source_target_pairs={{0,16},{8,24},{16,0},{24,8},{1,17},{9,25},{17,1},{25,9},{2,18},{10... | collective-permute-start | bytes 393224 | tf_op jit(solution)/shard_map/ppermute | solution.py:655
  107.1 11.5 %collective-permute-start.36 = (bf16[832,128]{1,0:T(8,128)(2,1)S(1)}, bf16[832,128]{1,0:T(8,128)(2,1)S(1)}, u32[]{:S(2)}, u32[]{:S(2)}) collective-permute-start(bf16[832,128]{1,0:T(8,128)(2,1)S(1)} %get-tuple-element.246), channel_id=1, source_target_pairs={{0,8},{8,0},{16,24},{24,16},{1,9},{9,1},{17,25},{25,17},{2,10},{10... | collective-permute-start | bytes 638984 | tf_op jit(solution)/shard_map/ppermute | solution.py:655
  108.2 10.5 %collective-permute-start.37 = (bf16[832,128]{1,0:T(8,128)(2,1)S(1)}, bf16[832,128]{1,0:T(8,128)(2,1)S(1)}, u32[]{:S(2)}, u32[]{:S(2)}) collective-permute-start(bf16[832,128]{1,0:T(8,128)(2,1)S(1)} %get-tuple-element.247), channel_id=1, source_target_pairs={{0,16},{8,24},{16,0},{24,8},{1,17},{9,25},{17,1},{25,9},{2,18},{10... | collective-permute-start | bytes 638984 | tf_op jit(solution)/shard_map/ppermute | solution.py:655
  109.2 9.5 %collective-permute-start.38 = (bf16[832,128]{1,0:T(8,128)(2,1)S(1)}, bf16[832,128]{1,0:T(8,128)(2,1)S(1)}, u32[]{:S(2)}, u32[]{:S(2)}) collective-permute-start(bf16[832,128]{1,0:T(8,128)(2,1)S(1)} %get-tuple-element.248), channel_id=1, source_target_pairs={{0,24},{8,16},{16,8},{24,0},{1,25},{9,17},{17,9},{25,1},{2,26},{10... | collective-permute-start | bytes 638984 | tf_op jit(solution)/shard_map/ppermute | solution.py:655
  118.9 5.4 %collective-permute-start.39 = (bf16[1024,128]{1,0:T(8,128)(2,1)S(1)}, bf16[1024,128]{1,0:T(8,128)(2,1)S(1)}, u32[]{:S(2)}, u32[]{:S(2)}) collective-permute-start(bf16[1024,128]{1,0:T(8,128)(2,1)S(1)} %get-tuple-element.260), channel_id=1, source_target_pairs={{0,4},{4,0},{1,5},{5,1},{2,6},{6,2},{3,7},{7,3},{8,12},{12,8},{9,1... | collective-permute-start | bytes 786440 | tf_op jit(solution)/shard_map/ppermute | solution.py:649
  119.8 9.1 %collective-permute-start.43 = (bf16[576,128]{1,0:T(8,128)(2,1)S(1)}, bf16[576,128]{1,0:T(8,128)(2,1)S(1)}, u32[]{:S(2)}, u32[]{:S(2)}) collective-permute-start(bf16[576,128]{1,0:T(8,128)(2,1)S(1)} %get-tuple-element.266), channel_id=1, source_target_pairs={{0,1},{1,0},{2,3},{3,2},{4,5},{5,4},{6,7},{7,6},{8,9},{9,8},{10,11... | collective-permute-start | bytes 442376 | tf_op jit(solution)/shard_map/ppermute | solution.py:646
  120.4 14.0 %collective-permute-start.44 = (bf16[576,128]{1,0:T(8,128)(2,1)S(1)}, bf16[576,128]{1,0:T(8,128)(2,1)S(1)}, u32[]{:S(2)}, u32[]{:S(2)}) collective-permute-start(bf16[576,128]{1,0:T(8,128)(2,1)S(1)} %get-tuple-element.267), channel_id=1, source_target_pairs={{0,2},{1,3},{2,0},{3,1},{4,6},{5,7},{6,4},{7,5},{8,10},{9,11},{10,... | collective-permute-start | bytes 442376 | tf_op jit(solution)/shard_map/ppermute | solution.py:646
  121.0 13.5 %collective-permute-start.45 = (bf16[576,128]{1,0:T(8,128)(2,1)S(1)}, bf16[576,128]{1,0:T(8,128)(2,1)S(1)}, u32[]{:S(2)}, u32[]{:S(2)}) collective-permute-start(bf16[576,128]{1,0:T(8,128)(2,1)S(1)} %get-tuple-element.268), channel_id=1, source_target_pairs={{0,3},{1,2},{2,1},{3,0},{4,7},{5,6},{6,5},{7,4},{8,11},{9,10},{10,... | collective-permute-start | bytes 442376 | tf_op jit(solution)/shard_map/ppermute | solution.py:646
  126.9 7.5 %collective-permute-start.40 = (bf16[576,128]{1,0:T(8,128)(2,1)S(1)}, bf16[576,128]{1,0:T(8,128)(2,1)S(1)}, u32[]{:S(2)}, u32[]{:S(2)}) collective-permute-start(bf16[576,128]{1,0:T(8,128)(2,1)S(1)} %get-tuple-element.262), channel_id=1, source_target_pairs={{0,8},{8,0},{16,24},{24,16},{1,9},{9,1},{17,25},{25,17},{2,10},{10... | collective-permute-start | bytes 442376 | tf_op jit(solution)/shard_map/ppermute | solution.py:655
  127.9 6.6 %collective-permute-start.41 = (bf16[576,128]{1,0:T(8,128)(2,1)S(1)}, bf16[576,128]{1,0:T(8,128)(2,1)S(1)}, u32[]{:S(2)}, u32[]{:S(2)}) collective-permute-start(bf16[576,128]{1,0:T(8,128)(2,1)S(1)} %get-tuple-element.263), channel_id=1, source_target_pairs={{0,16},{8,24},{16,0},{24,8},{1,17},{9,25},{17,1},{25,9},{2,18},{10... | collective-permute-start | bytes 442376 | tf_op jit(solution)/shard_map/ppermute | solution.py:655
  128.9 7.7 %collective-permute-start.42 = (bf16[576,128]{1,0:T(8,128)(2,1)S(1)}, bf16[576,128]{1,0:T(8,128)(2,1)S(1)}, u32[]{:S(2)}, u32[]{:S(2)}) collective-permute-start(bf16[576,128]{1,0:T(8,128)(2,1)S(1)} %get-tuple-element.264), channel_id=1, source_target_pairs={{0,24},{8,16},{16,8},{24,0},{1,25},{9,17},{17,9},{25,1},{2,26},{10... | collective-permute-start | bytes 442376 | tf_op jit(solution)/shard_map/ppermute | solution.py:655
  137.2 12.0 %collective-permute-start.46 = (bf16[576,128]{1,0:T(8,128)(2,1)S(1)}, bf16[576,128]{1,0:T(8,128)(2,1)S(1)}, u32[]{:S(2)}, u32[]{:S(2)}) collective-permute-start(bf16[576,128]{1,0:T(8,128)(2,1)S(1)} %get-tuple-element.282), channel_id=1, source_target_pairs={{0,1},{1,0},{2,3},{3,2},{4,5},{5,4},{6,7},{7,6},{8,9},{9,8},{10,11... | collective-permute-start | bytes 442376 | tf_op jit(solution)/shard_map/ppermute | solution.py:646
  138.0 13.1 %collective-permute-start.47 = (bf16[576,128]{1,0:T(8,128)(2,1)S(1)}, bf16[576,128]{1,0:T(8,128)(2,1)S(1)}, u32[]{:S(2)}, u32[]{:S(2)}) collective-permute-start(bf16[576,128]{1,0:T(8,128)(2,1)S(1)} %get-tuple-element.283), channel_id=1, source_target_pairs={{0,2},{1,3},{2,0},{3,1},{4,6},{5,7},{6,4},{7,5},{8,10},{9,11},{10,... | collective-permute-start | bytes 442376 | tf_op jit(solution)/shard_map/ppermute | solution.py:646
  138.4 12.7 %collective-permute-start.48 = (bf16[576,128]{1,0:T(8,128)(2,1)S(1)}, bf16[576,128]{1,0:T(8,128)(2,1)S(1)}, u32[]{:S(2)}, u32[]{:S(2)}) collective-permute-start(bf16[576,128]{1,0:T(8,128)(2,1)S(1)} %get-tuple-element.284), channel_id=1, source_target_pairs={{0,3},{1,2},{2,1},{3,0},{4,7},{5,6},{6,5},{7,4},{8,11},{9,10},{10,... | collective-permute-start | bytes 442376 | tf_op jit(solution)/shard_map/ppermute | solution.py:646
  141.7 5.9 %copy-start = (f32[2,9,64,128]{3,2,1,0:T(8,128)S(1)}, f32[2,9,64,128]{3,2,1,0:T(8,128)}, u32[]{:S(2)}) copy-start(f32[2,9,64,128]{3,2,1,0:T(8,128)} %refs_1_.3) | copy-start | bytes 1769476
  141.7 5.9 %copy-start.3 = (f32[2,9,64,128]{3,2,1,0:T(8,128)S(1)}, f32[2,9,64,128]{3,2,1,0:T(8,128)}, u32[]{:S(2)}) copy-start(f32[2,9,64,128]{3,2,1,0:T(8,128)} %refs_5_.6) | copy-start | bytes 1769476
  141.7 5.9 %copy-start.4 = (f32[2,9,64,128]{3,2,1,0:T(8,128)S(1)}, f32[2,9,64,128]{3,2,1,0:T(8,128)}, u32[]{:S(2)}) copy-start(f32[2,9,64,128]{3,2,1,0:T(8,128)} %refs_6_.4) | copy-start | bytes 1769476
  145.6 11.1 %collective-permute-start.49 = (bf16[256,512]{1,0:T(8,128)(2,1)}, bf16[256,512]{1,0:T(8,128)(2,1)S(1)}, u32[]{:S(2)}, u32[]{:S(2)}) collective-permute-start(bf16[256,512]{1,0:T(8,128)(2,1)} %get-tuple-element.297), channel_id=1, source_target_pairs={{0,8},{8,0},{16,24},{24,16},{1,9},{9,1},{17,25},{25,17},{2,10},{10... | collective-permute-start | bytes 786440 | tf_op jit(solution)/shard_map/ppermute | solution.py:655
  146.5 10.1 %collective-permute-start.50 = (bf16[256,512]{1,0:T(8,128)(2,1)S(1)}, bf16[256,512]{1,0:T(8,128)(2,1)S(1)}, u32[]{:S(2)}, u32[]{:S(2)}) collective-permute-start(bf16[256,512]{1,0:T(8,128)(2,1)S(1)} %get-tuple-element.298), channel_id=1, source_target_pairs={{0,16},{8,24},{16,0},{24,8},{1,17},{9,25},{17,1},{25,9},{2,18},{10... | collective-permute-start | bytes 786440 | tf_op jit(solution)/shard_map/ppermute | solution.py:655
  149.2 8.9 %collective-permute-start.51 = (bf16[256,512]{1,0:T(8,128)(2,1)S(1)}, bf16[256,512]{1,0:T(8,128)(2,1)S(1)}, u32[]{:S(2)}, u32[]{:S(2)}) collective-permute-start(bf16[256,512]{1,0:T(8,128)(2,1)S(1)} %get-tuple-element.299), channel_id=1, source_target_pairs={{0,24},{8,16},{16,8},{24,0},{1,25},{9,17},{17,9},{25,1},{2,26},{10... | collective-permute-start | bytes 786440 | tf_op jit(solution)/shard_map/ppermute | solution.py:655
  152.2 11.0 %copy-start.8 = (f32[4,512]{1,0:T(4,128)S(1)}, f32[4,512]{1,0:T(4,128)}, u32[]{:S(2)}) copy-start(f32[4,512]{1,0:T(4,128)} %refs_5_.7) | copy-start | bytes 24580
  152.2 11.0 %copy-start.9 = (f32[4,512]{1,0:T(4,128)S(1)}, f32[4,512]{1,0:T(4,128)}, u32[]{:S(2)}) copy-start(f32[4,512]{1,0:T(4,128)} %refs_6_.5) | copy-start | bytes 24580
  152.2 11.0 %all-to-all-start.4 = ((f32[32,2,128]{2,1,0:T(2,128)}), f32[32,2,128]{2,1,0:T(2,128)S(1)}, u32[]{:S(2)}, u32[]{:S(2)}) async-start(f32[32,2,128]{2,1,0:T(2,128)} %get-tuple-element.294), calls=%async_computation.4 | async-start | bytes 65536 | tf_op jit(solution)/shard_map/all_to_all | solution.py:840

commit v8 on v7

--- a/solution.py
+++ b/solution.py
@@ -202,22 +202,21 @@
 def fill_kernels(z, at, blocks, wcat):
     for t, block in enumerate(blocks):
         s = at[1] ^ t
-        for a in range(z.Z):
+        for m in range(z.Z):
             pieces = isinstance(block, (list, tuple))
-            row = pl.multiple_of((at[0] ^ a if pieces else a) * z.L + s * z.IB, z.IB)
+            row = pl.multiple_of((at[0] ^ m if pieces else m) * z.L + s * z.IB, z.IB)
             for k in range(z.K):
-                part = block[a][k * z.IB : (k + 1) * z.IB, :] if pieces else block[a, k]
+                part = block[m][k * z.IB : (k + 1) * z.IB, :] if pieces else block[at[0] ^ m, k]
                 wcat[pl.ds(row, z.IB), k * z.LP : k * z.LP + z.L] = part
 
 
 def split_channels(z, at, slices, outs, rows):
-    for s in range(z.S):
-
-        @pl.when(at[1] == s)
-        def _(s=s):
-            for t in range(z.S):
-                low = (s ^ t) * z.IB
-                outs[t][rows, :] = jnp.concatenate([v[:, low : low + z.IB] for v in slices], axis=1)
+    parts = [jnp.concatenate([v[:, s * z.IB : (s + 1) * z.IB] for v in slices], axis=1) for s in range(z.S)]
+    for t in range(z.S):
+        part = parts[t]
+        for s in range(1, z.S):
+            part = jnp.where(at[1] == s, parts[s ^ t], part)
+        outs[t][rows, :] = part
 
 
 def split_images(z, at, np_ref, *refs):
@@ -259,31 +258,26 @@
     copy.wait()
 
 
-def gathered(z, at, parts, hold):
-    half = z.G // 2
-    for m in range(z.Q):
-        hold[at[0] ^ m, :half] = parts[m][...]
-        hold[at[0] ^ m, half:] = parts[z.Q + m][...]
+def gathered(z, parts, j):
+    half = z.Q // 2
+    at_part, row = (0, j) if j < half else (z.Q, j - half)
+    return [parts[at_part + m][row * z.own : (row + 1) * z.own, :] for m in range(z.Q)]
 
 
 def second_conv(z, at, *refs):
     hs, refs = refs[: 2 * z.Q], refs[2 * z.Q :]
     blocks, refs = refs[: z.S], refs[z.S :]
-    hw_ref, outs, (z_ref, stats_ref, wcat, y_ref, h_ref) = refs[0], refs[1 : 1 + z.S], refs[1 + z.S :]
-    gathered(z, at, hs, h_ref)
+    hw_ref, outs, (z_ref, stats_ref, wcat, y_ref) = refs[0], refs[1 : 1 + z.S], refs[1 + z.S :]
     fill_kernels(z, at, blocks, wcat)
-    for j in range(z.Q):
-        rows = slice(j * z.own, (j + 1) * z.own)
-        split_channels(z, at, [h_ref[a, rows, :] for a in range(z.Q)], outs, rows)
 
     def product(j):
-        rows = slice(j * z.own, (j + 1) * z.own)
+        slices = gathered(z, hs, j)
+        split_channels(z, at, slices, outs, slice(j * z.own, (j + 1) * z.own))
         if z.L % LANES == 0:
-            whole = jnp.concatenate([h_ref[i, rows, :] for i in range(z.Q)], axis=1)
-            return jnp.dot(whole, wcat[...], preferred_element_type=F32)
+            return jnp.dot(jnp.concatenate(slices, axis=1), wcat[...], preferred_element_type=F32)
         return sum(
-            jnp.dot(h_ref[i, rows, :], wcat[i * z.L : (i + 1) * z.L, :], preferred_element_type=F32)
-            for i in range(z.Q)
+            jnp.dot(v, wcat[m * z.L : (m + 1) * z.L, :], preferred_element_type=F32)
+            for m, v in enumerate(slices)
         )
 
     conv_into(z, product, y_ref, z_ref)
@@ -393,13 +387,13 @@
     blocks, (z_ref, sum_ref, hw_ref, par_ref, wcat, slope_ref) = refs[: z.S], refs[z.S :]
     for t, block in enumerate(blocks):
         s = at[1] ^ t
-        for b in range(z.Z):
+        for m in range(z.Z):
             for k in range(z.K):
                 rows = pl.ds(pl.multiple_of(k * z.LP + s * z.IB, z.IB), z.IB)
                 if z.L % LANES == 0:
-                    wcat[0, rows, b * z.L : (b + 1) * z.L] = block[b, k]
+                    wcat[0, rows, m * z.L : (m + 1) * z.L] = block[at[0] ^ m, k]
                 else:
-                    wcat[b, rows, :] = block[b, k]
+                    wcat[m, rows, :] = block[at[0] ^ m, k]
     mean, inv = sum_ref[0:1, :], sum_ref[1:2, :]
     gain, shift = par_ref[0:1, :], par_ref[1:2, :]
 
@@ -411,17 +405,16 @@
     over_images(z, step)
 
 
-def back_product(z, dz_ref, wcat):
+def back_product(z, dzs, wcat):
     contract = (((1,), (1,)), ((), ()))
 
     def product(j):
-        rows = slice(j * z.own, (j + 1) * z.own)
+        slices = gathered(z, dzs, j)
         if z.L % LANES == 0:
-            whole = jnp.concatenate([dz_ref[i, rows, :] for i in range(z.Q)], axis=1)
+            whole = jnp.concatenate(slices, axis=1)
             return lax.dot_general(whole, wcat[0], contract, preferred_element_type=F32)
         return sum(
-            lax.dot_general(dz_ref[i, rows, :], wcat[i], contract, preferred_element_type=F32)
-            for i in range(z.Q)
+            lax.dot_general(v, wcat[m], contract, preferred_element_type=F32) for m, v in enumerate(slices)
         )
 
     return product
@@ -435,9 +428,8 @@
 
 def hidden_grad(z, at, *refs):
     dzs, refs = refs[: 2 * z.Q], refs[2 * z.Q :]
-    wcat, slope_ref, z_ref, sum_ref, hw_ref, da_ref, stats_ref, y_ref, dz_ref = refs
-    gathered(z, at, dzs, dz_ref)
-    conv_into(z, back_product(z, dz_ref, wcat), y_ref, da_ref, -1)
+    wcat, slope_ref, z_ref, sum_ref, hw_ref, da_ref, stats_ref, y_ref = refs
+    conv_into(z, back_product(z, dzs, wcat), y_ref, da_ref, -1)
     mean, inv = sum_ref[0:1, :], sum_ref[1:2, :]
 
     def step(n, rows, carry):
@@ -456,25 +448,18 @@
 
 
 def input_part(z, at, a_ref, b_ref, w_ref, d_ref, *refs):
-    outs, (moved_ref, dx_ref) = refs[: z.Q], refs[z.Q :]
+    outs, moved_ref = refs[: z.Q], refs[z.Q]
     fill_moved(z, a_ref, b_ref, moved_ref)
     contract = (((1,), (1,)), ((), ()))
-    for j in range(z.Q):
-        rows = slice(j * z.own, (j + 1) * z.own)
-        dx_ref[j] = lax.dot_general(moved_ref[rows, :], w_ref[...], contract, preferred_element_type=F32)
-    for slot in range(z.Q):
-
-        @pl.when(at[0] == slot)
-        def _(slot=slot):
-            for j in range(z.Q):
-                lanes = slice(slot * z.L, (slot + 1) * z.L)
-                dx_ref[j, :, lanes] = dx_ref[j, :, lanes] + d_ref[j * z.own : (j + 1) * z.own, :]
-
     for m in range(z.Q):
-        outs[m][...] = dx_ref[at[0] ^ m].astype(outs[m].dtype)
-
-
-def kernel_grad(z, at, *refs):
+        rows = pl.ds(pl.multiple_of((at[0] ^ m) * z.own, z.own), z.own)
+        part = lax.dot_general(moved_ref[rows, :], w_ref[...], contract, preferred_element_type=F32)
+        d = d_ref[rows, :]
+        own = jnp.concatenate([jnp.where(at[0] == slot, d, 0.0) for slot in range(z.Q)], axis=1)
+        outs[m][...] = (part + own).astype(outs[m].dtype)
+
+
+def kernel_grad(z, ordered, at, *refs):
     features, refs = refs[: z.S], refs[z.S :]
     dzs, refs = refs[: z.S + 1], refs[z.S + 1 :]
     value_ref = None
@@ -485,11 +470,12 @@
     half = z.G // 2
     for t in range(z.S):
         pair = (dzs[0], dzs[1]) if t == 0 else (dzs[1 + t].at[:half], dzs[1 + t].at[half:])
-        fill_moved(z, *pair, moved_ref)
-        part = lax.dot_general(features[t][...], moved_ref[...], contract, preferred_element_type=F32)
+        moved = moved_ref.at[t % 2]
+        fill_moved(z, *pair, moved)
+        part = lax.dot_general(features[t][...], moved[...], contract, preferred_element_type=F32)
         full_ref[...] = part if t == 0 else full_ref[...] + part
     for r in range(z.Q):
-        row = pl.multiple_of((at[0] ^ r) * z.IB, z.IB)
+        row = pl.multiple_of((at[0] ^ r if ordered else r) * z.IB, z.IB)
         for k in range(z.K):
             part = full_ref[pl.ds(row, z.IB), k * z.LP : k * z.LP + z.L]
             outs[r][k * z.IB : (k + 1) * z.IB, :] = part.astype(BF16)
@@ -674,7 +660,8 @@
     blocks = near((z.Z, *piece), BF16)
     stat, pair = near((many, 4, LANES)), near((many, 2, LANES))
     conv_scratch = [pltpu.VMEM((z.C, z.K * z.LP), BF16), pltpu.VMEM((rows, z.K * z.LP), F32)]
-    grad_scratch = [pltpu.VMEM((z.G, z.K * z.LP), BF16), pltpu.VMEM((z.Q * z.IB, z.K * z.LP), F32)]
+    moved = (z.G, z.K * z.LP)
+    grad_scratch = [pltpu.VMEM((2, *moved), BF16), pltpu.VMEM((z.Q * z.IB, z.K * z.LP), F32)]
     cot_rows = cotangent.reshape(rows, z.C)
     image_rows = images.reshape(rows, z.C)
 
@@ -727,7 +714,7 @@
         functools.partial(second_conv, z),
         [near((z.G, z.Q * z.IB), BF16)] * z.S + [near(GL), stat],
         (at, *hs, *share(front_two), hw),
-        conv_scratch + [pltpu.VMEM((z.Q, *GL), BF16)],
+        conv_scratch,
         limit=16,
     )
     stats, x_parts, h_parts = together((stats, x_parts, h_parts))
@@ -750,11 +737,11 @@
     def gradient(features, a, b, whole, *value):
         more = rows if value else 0
         return call(
-            functools.partial(kernel_grad, z),
+            functools.partial(kernel_grad, z, not value),
             [near((z.K * z.IB + more, z.L), BF16)] * z.Q,
             (at, *features, a, b, *[over_s(whole, t) for t in range(1, z.S)], *value),
             grad_scratch,
-            limit=14,
+            limit=18,
             cost=COST_GRAD,
         )
 
@@ -799,7 +786,7 @@
         functools.partial(hidden_grad, z),
         [near(GL), pair],
         (at, *dz2s, wide, slope, z1, sum_one, hw),
-        [pltpu.VMEM((rows, z.K * z.LP), F32), pltpu.VMEM((z.Q, *GL), BF16)],
+        [pltpu.VMEM((rows, z.K * z.LP), F32)],
         limit=16,
     )
     stats, parts_two = together((stats, parts_two))
@@ -819,13 +806,14 @@
         after=(da,),
     )
     parts_one = gradient(x_parts, da, db, dz)
+    parts_one, parts_two[3] = together((parts_one, parts_two[3]))
     parts_one, parts_two = by_plane(parts_one), along(parts_two)
     parts_one, parts_two = together((parts_one, parts_two))
     dxs = call(
         functools.partial(input_part, z),
         [near((rows, z.C))] + [near((rows, z.C), BF16)] * (z.Q - 1),
         (at, da, db, w_far, d),
-        [grad_scratch[0], pltpu.VMEM((z.Q, rows, z.C), F32)],
+        [pltpu.VMEM(moved, BF16)],
         limit=16,
         cost=COST_GRAD,
         far=(w_far,),

time: 165 us -> 163 us (0.988)
  transfers between devices with their start and end apart: 53 -> 53, of which waited for: 18 -> 20; matrix products, arithmetic and copies ran while one was open for 0% -> 0% of each run, Pallas kernels for 11% -> 10%
where the time goes in v8:
time: 163 us
  starting transfers between devices  63.7 us (39%)
  waiting for transfers between devices  33.9 us (21%)
  blocking collectives  33.2 us (20%)
  Pallas kernels  29.2 us (18%)
    ppermute x30, starting transfers between devices, over_q(): return lax.ppermute(v, 'q', [(i, i ^ m) for i in range(z.Q)]) if m else v  37.8 us
    all_to_all x4, blocking collectives, sharers(): return lax.all_to_all(v, ('s', 'z'), 0, 0)  33.2 us
    pallas_call x18, Pallas kernels, call(): pl.pallas_call(run, out_shape=out_shape, in_specs=[pl.BlockSpec(memory_sp...  26.5 us
    ppermute x12, starting transfers between devices, over_z(): return lax.ppermute(v, 'z', [(i, i ^ m) for i in range(z.Z)]) if m else v  19.2 us
    ppermute x12, waiting for transfers between devices, over_z(): return lax.ppermute(v, 'z', [(i, i ^ m) for i in range(z.Z)]) if m else v  16.5 us
    ppermute x30, waiting for transfers between devices, over_q(): return lax.ppermute(v, 'q', [(i, i ^ m) for i in range(z.Q)]) if m else v  13.1 us
    all_to_all x1, waiting for transfers between devices, shards(): stats = lax.all_to_all(stats, ('s', 'q', 'z'), 0, 0)  4.22 us
    all_to_all x1, starting transfers between devices, shards(): stats = lax.all_to_all(stats, ('s', 'q', 'z'), 0, 0)  4.21 us
  transfers between devices with their start and end apart: 53, of which 20 were waited for; matrix products, arithmetic and copies ran while one was open for 0% of the time, Pallas kernels for 10%

profile of v8, /device:TPU:0, one launch (start us, length us, event | category | flops | bytes accessed | tf_op | source)
XLA Modules:
  0.0 163.0 jit_solution(1617057781990578518)
XLA Ops:
  0.7 1.2 convert.4
  1.9 3.1 %collective-permute-start = (bf16[9,64,128]{2,1,0:T(8,128)(2,1)S(1)}, bf16[9,64,128]{2,1,0:T(8,128)(2,1)S(1)}, u32[]{:S(2)}, u32[]{:S(2)}) collective-permute-start(bf16[9,64,128]{2,1,0:T(8,128)(2,1)S(1)} %get-tuple-element.166.refs_1_), channel_id=1, source_target_pairs={{0,1},{1,0},{2,3},{3,2},{4,5},{5,4},{6,7},{7,6},{8,9},{9,8},{10,11... | collective-permute-start | bytes 442376 | tf_op jit(solution)/shard_map/ppermute | solution.py:632
  5.0 2.6 %collective-permute-start.1 = (bf16[9,64,128]{2,1,0:T(8,128)(2,1)S(1)}, bf16[9,64,128]{2,1,0:T(8,128)(2,1)S(1)}, u32[]{:S(2)}, u32[]{:S(2)}) collective-permute-start(bf16[9,64,128]{2,1,0:T(8,128)(2,1)S(1)} %get-tuple-element.166.refs_1_), channel_id=1, source_target_pairs={{0,2},{1,3},{2,0},{3,1},{4,6},{5,7},{6,4},{7,5},{8,10},{9,11},{10,... | collective-permute-start | bytes 442376 | tf_op jit(solution)/shard_map/ppermute | solution.py:632
  7.6 1.7 %collective-permute-start.3 = (bf16[256,512]{1,0:T(8,128)(2,1)S(1)}, bf16[256,512]{1,0:T(8,128)(2,1)S(1)}, u32[]{:S(2)}, u32[]{:S(2)}) collective-permute-start(bf16[256,512]{1,0:T(8,128)(2,1)S(1)} %bitcast.12), channel_id=1, source_target_pairs={{0,8},{8,0},{16,24},{24,16},{1,9},{9,1},{17,25},{25,17},{2,10},{10... | collective-permute-start | bytes 786440 | tf_op jit(solution)/shard_map/ppermute | solution.py:641
  9.3 1.5 collective-permute-start.4
  10.8 2.7 %collective-permute-start.5 = (bf16[256,512]{1,0:T(8,128)(2,1)S(1)}, bf16[256,512]{1,0:T(8,128)(2,1)S(1)}, u32[]{:S(2)}, u32[]{:S(2)}) collective-permute-start(bf16[256,512]{1,0:T(8,128)(2,1)S(1)} %bitcast.14), channel_id=1, source_target_pairs={{0,24},{8,16},{16,8},{24,0},{1,25},{9,17},{17,9},{25,1},{2,26},{10... | collective-permute-start | bytes 786440 | tf_op jit(solution)/shard_map/ppermute | solution.py:641
  13.5 5.5 %collective-permute-done.1.refs_3_ = bf16[9,64,128]{2,1,0:T(8,128)(2,1)S(1)} collective-permute-done((bf16[9,64,128]{2,1,0:T(8,128)(2,1)S(1)}, bf16[9,64,128]{2,1,0:T(8,128)(2,1)S(1)}, u32[]{:S(2)}, u32[]{:S(2)}) %collective-permute-start.1) | collective-permute-done | bytes 147488 | tf_op jit(solution)/shard_map/ppermute | solution.py:632
  19.0 3.3 %collective-permute-start.10 = (bf16[9,64,128]{2,1,0:T(8,128)(2,1)S(1)}, bf16[9,64,128]{2,1,0:T(8,128)(2,1)S(1)}, u32[]{:S(2)}, u32[]{:S(2)}) collective-permute-start(bf16[9,64,128]{2,1,0:T(8,128)(2,1)S(1)} %get-tuple-element.191.refs_1_), channel_id=1, source_target_pairs={{0,2},{1,3},{2,0},{3,1},{4,6},{5,7},{6,4},{7,5},{8,10},{9,11},{10,... | collective-permute-start | bytes 442376 | tf_op jit(solution)/shard_map/ppermute | solution.py:632
  23.0 1.6 collective-permute-start.6
  24.6 1.5 collective-permute-start.7
  26.6 2.3 %collective-permute-start.11 = (bf16[9,64,128]{2,1,0:T(8,128)(2,1)S(1)}, bf16[9,64,128]{2,1,0:T(8,128)(2,1)S(1)}, u32[]{:S(2)}, u32[]{:S(2)}) collective-permute-start(bf16[9,64,128]{2,1,0:T(8,128)(2,1)S(1)} %get-tuple-element.191.refs_1_), channel_id=1, source_target_pairs={{0,3},{1,2},{2,1},{3,0},{4,7},{5,6},{6,5},{7,4},{8,11},{9,10},{10,... | collective-permute-start | bytes 442376 | tf_op jit(solution)/shard_map/ppermute | solution.py:632
  28.9 2.1 %collective-permute-done.10.refs_3_ = bf16[9,64,128]{2,1,0:T(8,128)(2,1)S(1)} collective-permute-done((bf16[9,64,128]{2,1,0:T(8,128)(2,1)S(1)}, bf16[9,64,128]{2,1,0:T(8,128)(2,1)S(1)}, u32[]{:S(2)}, u32[]{:S(2)}) %collective-permute-start.10) | collective-permute-done | bytes 147488 | tf_op jit(solution)/shard_map/ppermute | solution.py:632
  30.9 0.9 shard_map.169
  31.9 1.8 %collective-permute-done.11.refs_4_ = bf16[9,64,128]{2,1,0:T(8,128)(2,1)S(1)} collective-permute-done((bf16[9,64,128]{2,1,0:T(8,128)(2,1)S(1)}, bf16[9,64,128]{2,1,0:T(8,128)(2,1)S(1)}, u32[]{:S(2)}, u32[]{:S(2)}) %collective-permute-start.11) | collective-permute-done | bytes 147488 | tf_op jit(solution)/shard_map/ppermute | solution.py:632
  33.7 2.4 %collective-permute-done.9.refs_2_ = bf16[9,64,128]{2,1,0:T(8,128)(2,1)S(1)} collective-permute-done((bf16[9,64,128]{2,1,0:T(8,128)(2,1)S(1)}, bf16[9,64,128]{2,1,0:T(8,128)(2,1)S(1)}, u32[]{:S(2)}, u32[]{:S(2)}) %collective-permute-start.9) | collective-permute-done | bytes 147488 | tf_op jit(solution)/shard_map/ppermute | solution.py:632
  37.2 1.4 shard_map.171
  38.6 2.5 %shard_map.170 = (f32[1024,128]{1,0:T(8,128)S(1)}, f32[16,8,128]{2,1,0:T(8,128)S(1)}, f32[8,4,128]{2,1,0:T(4,128)S(1)}, bf16[512,1152]{1,0:T(8,128)(2,1)}) custom-call(s32[3]{0:T(128)S(1)} %pad_add_fusion.refs_0_.refs_9_, bf16[256,512]{1,0:T(8,128)(2,1)S(1)} %bitcast.16, bf16[256,512]{1,0:T(8,128)(2,1)S(1)} %collective-permute-done.3.refs_3_.refs_2_, ...), custom_call_target="tpu_custom_call" | custom-call | flops 1 | bytes 1 | tf_op jit(solution)/shard_map/pallas_call | solution.py:68
  41.2 1.6 collective-permute-start.16
  42.8 1.5 collective-permute-start.17
  44.7 8.7 %all_to_all.25.refs_2_ = f32[8,4,128]{2,1,0:T(4,128)S(1)} all-to-all(f32[8,4,128]{2,1,0:T(4,128)S(1)} %get-tuple-element.199), channel_id=1, replica_groups=mesh['ha'=2,'wa'=4,'ba'=4] {'wa':(2)2,'ba'}, dimensions={0} | all-to-all | bytes 32768 | tf_op jit(solution)/shard_map/all_to_all | solution.py:638
  53.4 0.8 collective-permute-done.18.refs_8_
  54.2 1.0 shard_map.172
  55.3 1.6 collective-permute-start.20
  56.8 1.6 collective-permute-start.22
  59.4 1.9 %collective-permute-done.20.refs_3_ = bf16[512,128]{1,0:T(8,128)(2,1)S(1)} collective-permute-done((bf16[512,128]{1,0:T(8,128)(2,1)S(1)}, bf16[512,128]{1,0:T(8,128)(2,1)S(1)}, u32[]{:S(2)}, u32[]{:S(2)}) %collective-permute-start.20) | collective-permute-done | bytes 131104 | tf_op jit(solution)/shard_map/ppermute | solution.py:641
  61.3 1.5 collective-permute-start.21
  63.2 1.5 collective-permute-start.24
  64.7 1.3 collective-permute-done.19.refs_2_
  66.0 2.0 %collective-permute-done.21.refs_4_ = bf16[512,128]{1,0:T(8,128)(2,1)S(1)} collective-permute-done((bf16[512,128]{1,0:T(8,128)(2,1)S(1)}, bf16[512,128]{1,0:T(8,128)(2,1)S(1)}, u32[]{:S(2)}, u32[]{:S(2)}) %collective-permute-start.21) | collective-permute-done | bytes 131104 | tf_op jit(solution)/shard_map/ppermute | solution.py:641
  68.2 2.6 %shard_map.173 = (bf16[1024,256]{1,0:T(8,128)(2,1)S(1)}, bf16[1024,256]{1,0:T(8,128)(2,1)S(1)}, f32[1024,128]{1,0:T(8,128)S(1)}, f32[8,4,128]{2,1,0:T(4,128)S(1)}) custom-call(s32[3]{0:T(128)S(1)} %pad_add_fusion.refs_0_.refs_9_, bf16[512,128]{1,0:T(8,128)(2,1)S(1)} %get-tuple-element.211.refs_1_, bf16[512,128]{1,0:T(8,128)(2,1)S(1)} %collective-permute-done.19.refs_2_, ...), custom_call_target="tpu_custom_call" | custom-call | flops 1 | bytes 1 | tf_op jit(solution)/shard_map/pallas_call | solution.py:68
  71.3 8.7 %all_to_all.26.refs_2_ = f32[8,4,128]{2,1,0:T(4,128)S(1)} all-to-all(f32[8,4,128]{2,1,0:T(4,128)S(1)} %get-tuple-element.220), channel_id=1, replica_groups=mesh['ha'=2,'wa'=4,'ba'=4] {'wa':(2)2,'ba'}, dimensions={0} | all-to-all | bytes 32768 | tf_op jit(solution)/shard_map/all_to_all | solution.py:638
  80.0 1.3 shard_map.174
  81.3 8.0 %all_to_all.27.refs_3_ = f32[8,2,128]{2,1,0:T(2,128)S(1)} all-to-all(f32[8,2,128]{2,1,0:T(2,128)S(1)} %get-tuple-element.230), channel_id=1, replica_groups=mesh['ha'=2,'wa'=4,'ba'=4] {'wa':(2)2,'ba'}, dimensions={0} | all-to-all | bytes 16384 | tf_op jit(solution)/shard_map/all_to_all | solution.py:638
  90.1 1.5 collective-permute-start.29
  92.2 1.4 collective-permute-start.28
  93.6 2.0 %collective-permute-done.29.refs_3_ = bf16[512,128]{1,0:T(8,128)(2,1)S(1)} collective-permute-done((bf16[512,128]{1,0:T(8,128)(2,1)S(1)}, bf16[512,128]{1,0:T(8,128)(2,1)S(1)}, u32[]{:S(2)}, u32[]{:S(2)}) %collective-permute-start.29) | collective-permute-done | bytes 131104 | tf_op jit(solution)/shard_map/ppermute | solution.py:641
  95.6 1.5 collective-permute-start.32
  97.1 0.9 collective-permute-done.31.refs_6_
  98.6 1.5 collective-permute-start.33
  100.1 2.3 %shard_map.178 = (bf16[832,128]{1,0:T(8,128)(2,1)S(1)}, bf16[832,128]{1,0:T(8,128)(2,1)S(1)}, bf16[832,128]{1,0:T(8,128)(2,1)S(1)}, bf16[832,128]{1,0:T(8,128)(2,1)S(1)}) custom-call(s32[3]{0:T(128)S(1)} %pad_add_fusion.refs_0_.refs_9_, bf16[1024,256]{1,0:T(8,128)(2,1)S(1)} %get-tuple-element.241.refs_1_, ...), custom_call_target="tpu_custom_call" | custom-call | flops 3000000000 | bytes 1 | tf_op jit(solution)/shard_map/pallas_call | solution.py:68
  102.5 1.3 shard_map.176
  103.8 2.5 %shard_map.177 = (f32[1024,128]{1,0:T(8,128)S(1)}, f32[8,2,128]{2,1,0:T(2,128)S(1)}) custom-call(s32[3]{0:T(128)S(1)} %pad_add_fusion.refs_0_.refs_9_, bf16[512,128]{1,0:T(8,128)(2,1)S(1)} %get-tuple-element.234.refs_1_.refs_3_, bf16[512,128]{1,0:T(8,128)(2,1)S(1)} %collective-permute-done.28.refs_2_, bf16[512,128]{1,0:T(8,128)(2,1)S(1)} %collective-permute-done.29.refs_3_, ...), custom_call_target="tpu_custom_call" | custom-call | flops 1 | bytes 1 | tf_op jit(solution)/shard_map/pallas_call | solution.py:68
  106.2 1.3 collective-permute-start.36
  108.2 1.5 collective-permute-start.38
  109.8 8.0 %all_to_all.28.refs_3_ = f32[8,2,128]{2,1,0:T(2,128)S(1)} all-to-all(f32[8,2,128]{2,1,0:T(2,128)S(1)} %get-tuple-element.249), channel_id=1, replica_groups=mesh['ha'=2,'wa'=4,'ba'=4] {'wa':(2)2,'ba'}, dimensions={0} | all-to-all | bytes 16384 | tf_op jit(solution)/shard_map/all_to_all | solution.py:638
  120.1 2.4 %shard_map.181 = (bf16[576,128]{1,0:T(8,128)(2,1)S(1)}, bf16[576,128]{1,0:T(8,128)(2,1)S(1)}, bf16[576,128]{1,0:T(8,128)(2,1)S(1)}, bf16[576,128]{1,0:T(8,128)(2,1)S(1)}) custom-call(s32[3]{0:T(128)S(1)} %pad_add_fusion.refs_0_.refs_9_, bf16[1024,256]{1,0:T(8,128)(2,1)S(1)} %get-tuple-element.262.refs_1_, ...), custom_call_target="tpu_custom_call" | custom-call | flops 3000000000 | bytes 1 | tf_op jit(solution)/shard_map/pallas_call | solution.py:68
  122.5 1.3 collective-permute-start.40
  124.5 1.5 collective-permute-start.42
  126.0 1.1 collective-permute-done.43.refs_1_
  127.1 2.2 %collective-permute-start.45 = (bf16[576,128]{1,0:T(8,128)(2,1)S(1)}, bf16[576,128]{1,0:T(8,128)(2,1)S(1)}, u32[]{:S(2)}, u32[]{:S(2)}) collective-permute-start(bf16[576,128]{1,0:T(8,128)(2,1)S(1)} %get-tuple-element.278), channel_id=1, source_target_pairs={{0,3},{1,2},{2,1},{3,0},{4,7},{5,6},{6,5},{7,4},{8,11},{9,10},{10,... | collective-permute-start | bytes 442376 | tf_op jit(solution)/shard_map/ppermute | solution.py:632
  129.4 1.0 collective-permute-done.44.refs_2_
  130.5 2.0 %collective-permute-done.42.refs_4_ = bf16[576,128]{1,0:T(8,128)(2,1)S(1)} collective-permute-done((bf16[576,128]{1,0:T(8,128)(2,1)S(1)}, bf16[576,128]{1,0:T(8,128)(2,1)S(1)}, u32[]{:S(2)}, u32[]{:S(2)}) %collective-permute-start.42) | collective-permute-done | bytes 147488 | tf_op jit(solution)/shard_map/ppermute | solution.py:641
  132.5 1.9 %collective-permute-done.45.refs_3_ = bf16[576,128]{1,0:T(8,128)(2,1)S(1)} collective-permute-done((bf16[576,128]{1,0:T(8,128)(2,1)S(1)}, bf16[576,128]{1,0:T(8,128)(2,1)S(1)}, u32[]{:S(2)}, u32[]{:S(2)}) %collective-permute-start.45) | collective-permute-done | bytes 147488 | tf_op jit(solution)/shard_map/ppermute | solution.py:632
  135.0 2.1 %collective-permute-start.46 = (bf16[576,128]{1,0:T(8,128)(2,1)S(1)}, bf16[576,128]{1,0:T(8,128)(2,1)S(1)}, u32[]{:S(2)}, u32[]{:S(2)}) collective-permute-start(bf16[576,128]{1,0:T(8,128)(2,1)S(1)} %get-tuple-element.292), channel_id=1, source_target_pairs={{0,1},{1,0},{2,3},{3,2},{4,5},{5,4},{6,7},{7,6},{8,9},{9,8},{10,11... | collective-permute-start | bytes 442376 | tf_op jit(solution)/shard_map/ppermute | solution.py:632
  137.6 1.9 %collective-permute-start.48 = (bf16[576,128]{1,0:T(8,128)(2,1)S(1)}, bf16[576,128]{1,0:T(8,128)(2,1)S(1)}, u32[]{:S(2)}, u32[]{:S(2)}) collective-permute-start(bf16[576,128]{1,0:T(8,128)(2,1)S(1)} %get-tuple-element.294), channel_id=1, source_target_pairs={{0,3},{1,2},{2,1},{3,0},{4,7},{5,6},{6,5},{7,4},{8,11},{9,10},{10,... | collective-permute-start | bytes 442376 | tf_op jit(solution)/shard_map/ppermute | solution.py:632
  139.5 3.8 %shard_map.185 = (f32[256,512]{1,0:T(8,128)S(1)}, bf16[256,512]{1,0:T(8,128)(2,1)}, bf16[256,512]{1,0:T(8,128)(2,1)S(1)}, bf16[256,512]{1,0:T(8,128)(2,1)S(1)}) custom-call(s32[3]{0:T(128)S(1)} %pad_add_fusion.refs_0_.refs_9_, bf16[512,128]{1,0:T(8,128)(2,1)S(1)} %get-tuple-element.260.refs_5_.refs_3_.refs_1_, ...), custom_call_target="tpu_custom_call" | custom-call | flops 3000000000 | bytes 1 | tf_op jit(solution)/shard_map/pallas_call | solution.py:68
  143.3 1.2 collective-permute-start.49
  145.2 1.6 %shard_map.183 = (f32[2,9,64,128]{3,2,1,0:T(8,128)}, f32[2,9,64,128]{3,2,1,0:T(8,128)}, f32[9,64,128]{2,1,0:T(8,128)S(1)}, f32[8,128]{1,0:T(8,128)S(1)}) custom-call(bf16[576,128]{1,0:T(8,128)(2,1)S(1)} %get-tuple-element.295.refs_0_, bf16[576,128]{1,0:T(8,128)(2,1)S(1)} %collective-permute-done.43.refs_1_, ...), custom_call_target="tpu_custom_call" | custom-call | flops 1 | bytes 1 | tf_op jit(solution)/shard_map/pallas_call | solution.py:767
  146.9 1.5 collective-permute-start.51
  149.3 1.1 shard_map.184
  150.4 4.2 %all-to-all-start.4 = ((f32[32,2,128]{2,1,0:T(2,128)}), f32[32,2,128]{2,1,0:T(2,128)S(1)}, u32[]{:S(2)}, u32[]{:S(2)}) async-start(f32[32,2,128]{2,1,0:T(2,128)} %get-tuple-element.304), calls=%async_computation.4 | async-start | bytes 65536 | tf_op jit(solution)/shard_map/all_to_all | solution.py:828
  155.3 1.5 collective-permute-done.51.refs_3_
  157.6 4.2 %all-to-all-done.4.refs_0_ = f32[32,2,128]{2,1,0:T(2,128)S(1)} async-done(((f32[32,2,128]{2,1,0:T(2,128)}), f32[32,2,128]{2,1,0:T(2,128)S(1)}, u32[]{:S(2)}, u32[]{:S(2)}) %all-to-all-start.4) | async-done | bytes 32800 | tf_op jit(solution)/shard_map/all_to_all | solution.py:828
  161.8 1.2 shard_map.187
  (90 shorter events, 15.3 us)
Async XLA Ops:
  0.6 6.9 %copy-start.1 = (bf16[4,8,8,512]{3,2,1,0:T(8,128)(2,1)S(1)}, bf16[4,8,8,512]{3,2,1,0:T(8,128)(2,1)}, u32[]{:S(2)}) copy-start(bf16[4,8,8,512]{3,2,1,0:T(8,128)(2,1)} %param.9) | copy-start | bytes 786436
  0.7 21.7 %copy-start.7 = (s32[4,8,8]{2,1,0:T(8,128)S(1)}, s32[4,8,8]{2,1,0:T(8,128)}, u32[]{:S(2)}) copy-start(s32[4,8,8]{2,1,0:T(8,128)} %refs_5_.4) | copy-start | bytes 3076
  0.7 30.3 %copy-start.6 = (f32[4,512]{1,0:T(4,128)S(1)}, f32[4,512]{1,0:T(4,128)}, u32[]{:S(2)}) copy-start(f32[4,512]{1,0:T(4,128)} %refs_4_.5) | copy-start | bytes 24580
  1.8 35.4 %copy-start.5 = (bf16[4,8,8,512]{3,2,1,0:T(8,128)(2,1)S(1)}, bf16[4,8,8,512]{3,2,1,0:T(8,128)(2,1)}, u32[]{:S(2)}) copy-start(bf16[4,8,8,512]{3,2,1,0:T(8,128)(2,1)} %param.11) | copy-start | bytes 786436
  1.9 8.9 %collective-permute-start = (bf16[9,64,128]{2,1,0:T(8,128)(2,1)S(1)}, bf16[9,64,128]{2,1,0:T(8,128)(2,1)S(1)}, u32[]{:S(2)}, u32[]{:S(2)}) collective-permute-start(bf16[9,64,128]{2,1,0:T(8,128)(2,1)S(1)} %get-tuple-element.166.refs_1_), channel_id=1, source_target_pairs={{0,1},{1,0},{2,3},{3,2},{4,5},{5,4},{6,7},{7,6},{8,9},{9,8},{10,11... | collective-permute-start | bytes 442376 | tf_op jit(solution)/shard_map/ppermute | solution.py:632
  5.0 14.0 %collective-permute-start.1 = (bf16[9,64,128]{2,1,0:T(8,128)(2,1)S(1)}, bf16[9,64,128]{2,1,0:T(8,128)(2,1)S(1)}, u32[]{:S(2)}, u32[]{:S(2)}) collective-permute-start(bf16[9,64,128]{2,1,0:T(8,128)(2,1)S(1)} %get-tuple-element.166.refs_1_), channel_id=1, source_target_pairs={{0,2},{1,3},{2,0},{3,1},{4,6},{5,7},{6,4},{7,5},{8,10},{9,11},{10,... | collective-permute-start | bytes 442376 | tf_op jit(solution)/shard_map/ppermute | solution.py:632
  7.6 11.4 %collective-permute-start.2 = (bf16[9,64,128]{2,1,0:T(8,128)(2,1)S(1)}, bf16[9,64,128]{2,1,0:T(8,128)(2,1)S(1)}, u32[]{:S(2)}, u32[]{:S(2)}) collective-permute-start(bf16[9,64,128]{2,1,0:T(8,128)(2,1)S(1)} %get-tuple-element.166.refs_1_), channel_id=1, source_target_pairs={{0,3},{1,2},{2,1},{3,0},{4,7},{5,6},{6,5},{7,4},{8,11},{9,10},{10,... | collective-permute-start | bytes 442376 | tf_op jit(solution)/shard_map/ppermute | solution.py:632
  7.6 15.4 %collective-permute-start.3 = (bf16[256,512]{1,0:T(8,128)(2,1)S(1)}, bf16[256,512]{1,0:T(8,128)(2,1)S(1)}, u32[]{:S(2)}, u32[]{:S(2)}) collective-permute-start(bf16[256,512]{1,0:T(8,128)(2,1)S(1)} %bitcast.12), channel_id=1, source_target_pairs={{0,8},{8,0},{16,24},{24,16},{1,9},{9,1},{17,25},{25,17},{2,10},{10... | collective-permute-start | bytes 786440 | tf_op jit(solution)/shard_map/ppermute | solution.py:641
  9.3 13.7 %collective-permute-start.4 = (bf16[256,512]{1,0:T(8,128)(2,1)S(1)}, bf16[256,512]{1,0:T(8,128)(2,1)S(1)}, u32[]{:S(2)}, u32[]{:S(2)}) collective-permute-start(bf16[256,512]{1,0:T(8,128)(2,1)S(1)} %bitcast.13), channel_id=1, source_target_pairs={{0,16},{8,24},{16,0},{24,8},{1,17},{9,25},{17,1},{25,9},{2,18},{10... | collective-permute-start | bytes 786440 | tf_op jit(solution)/shard_map/ppermute | solution.py:641
  10.8 12.2 %collective-permute-start.5 = (bf16[256,512]{1,0:T(8,128)(2,1)S(1)}, bf16[256,512]{1,0:T(8,128)(2,1)S(1)}, u32[]{:S(2)}, u32[]{:S(2)}) collective-permute-start(bf16[256,512]{1,0:T(8,128)(2,1)S(1)} %bitcast.14), channel_id=1, source_target_pairs={{0,24},{8,16},{16,8},{24,0},{1,25},{9,17},{17,9},{25,1},{2,26},{10... | collective-permute-start | bytes 786440 | tf_op jit(solution)/shard_map/ppermute | solution.py:641
  19.0 12.0 %collective-permute-start.10 = (bf16[9,64,128]{2,1,0:T(8,128)(2,1)S(1)}, bf16[9,64,128]{2,1,0:T(8,128)(2,1)S(1)}, u32[]{:S(2)}, u32[]{:S(2)}) collective-permute-start(bf16[9,64,128]{2,1,0:T(8,128)(2,1)S(1)} %get-tuple-element.191.refs_1_), channel_id=1, source_target_pairs={{0,2},{1,3},{2,0},{3,1},{4,6},{5,7},{6,4},{7,5},{8,10},{9,11},{10,... | collective-permute-start | bytes 442376 | tf_op jit(solution)/shard_map/ppermute | solution.py:632
  23.0 13.1 %collective-permute-start.6 = (bf16[592,128]{1,0:T(8,128)(2,1)S(1)}, bf16[592,128]{1,0:T(8,128)(2,1)S(1)}, u32[]{:S(2)}, u32[]{:S(2)}) collective-permute-start(bf16[592,128]{1,0:T(8,128)(2,1)S(1)} %get-tuple-element.179), channel_id=1, source_target_pairs={{0,8},{8,0},{16,24},{24,16},{1,9},{9,1},{17,25},{25,17},{2,10},{10... | collective-permute-start | bytes 454664 | tf_op jit(solution)/shard_map/ppermute | solution.py:641
  24.6 11.5 %collective-permute-start.7 = (bf16[592,128]{1,0:T(8,128)(2,1)S(1)}, bf16[592,128]{1,0:T(8,128)(2,1)S(1)}, u32[]{:S(2)}, u32[]{:S(2)}) collective-permute-start(bf16[592,128]{1,0:T(8,128)(2,1)S(1)} %get-tuple-element.180), channel_id=1, source_target_pairs={{0,16},{8,24},{16,0},{24,8},{1,17},{9,25},{17,1},{25,9},{2,18},{10... | collective-permute-start | bytes 454664 | tf_op jit(solution)/shard_map/ppermute | solution.py:641
  26.1 10.0 %collective-permute-start.8 = (bf16[592,128]{1,0:T(8,128)(2,1)S(1)}, bf16[592,128]{1,0:T(8,128)(2,1)S(1)}, u32[]{:S(2)}, u32[]{:S(2)}) collective-permute-start(bf16[592,128]{1,0:T(8,128)(2,1)S(1)} %get-tuple-element.181), channel_id=1, source_target_pairs={{0,24},{8,16},{16,8},{24,0},{1,25},{9,17},{17,9},{25,1},{2,26},{10... | collective-permute-start | bytes 454664 | tf_op jit(solution)/shard_map/ppermute | solution.py:641
  26.6 7.1 %collective-permute-start.11 = (bf16[9,64,128]{2,1,0:T(8,128)(2,1)S(1)}, bf16[9,64,128]{2,1,0:T(8,128)(2,1)S(1)}, u32[]{:S(2)}, u32[]{:S(2)}) collective-permute-start(bf16[9,64,128]{2,1,0:T(8,128)(2,1)S(1)} %get-tuple-element.191.refs_1_), channel_id=1, source_target_pairs={{0,3},{1,2},{2,1},{3,0},{4,7},{5,6},{6,5},{7,4},{8,11},{9,10},{10,... | collective-permute-start | bytes 442376 | tf_op jit(solution)/shard_map/ppermute | solution.py:632
  30.9 5.1 %collective-permute-start.9 = (bf16[9,64,128]{2,1,0:T(8,128)(2,1)S(1)}, bf16[9,64,128]{2,1,0:T(8,128)(2,1)S(1)}, u32[]{:S(2)}, u32[]{:S(2)}) collective-permute-start(bf16[9,64,128]{2,1,0:T(8,128)(2,1)S(1)} %get-tuple-element.191.refs_1_), channel_id=1, source_target_pairs={{0,1},{1,0},{2,3},{3,2},{4,5},{5,4},{6,7},{7,6},{8,9},{9,8},{10,11... | collective-permute-start | bytes 442376 | tf_op jit(solution)/shard_map/ppermute | solution.py:632
  36.1 2.5 %collective-permute-start.12 = (bf16[592,128]{1,0:T(8,128)(2,1)S(1)}, bf16[592,128]{1,0:T(8,128)(2,1)S(1)}, u32[]{:S(2)}, u32[]{:S(2)}) collective-permute-start(bf16[592,128]{1,0:T(8,128)(2,1)S(1)} %get-tuple-element.185.refs_5_), channel_id=1, source_target_pairs={{0,4},{4,0},{1,5},{5,1},{2,6},{6,2},{3,7},{7,3},{8,12},{12,8},{9,1... | collective-permute-start | bytes 454664 | tf_op jit(solution)/shard_map/ppermute | solution.py:635
  36.2 2.4 %collective-permute-start.13 = (bf16[592,128]{1,0:T(8,128)(2,1)S(1)}, bf16[592,128]{1,0:T(8,128)(2,1)S(1)}, u32[]{:S(2)}, u32[]{:S(2)}) collective-permute-start(bf16[592,128]{1,0:T(8,128)(2,1)S(1)} %collective-permute-done.6.refs_6_), channel_id=1, source_target_pairs={{0,4},{4,0},{1,5},{5,1},{2,6},{6,2},{3,7},{7,3},{8,12},{12,8},{9,1... | collective-permute-start | bytes 454664 | tf_op jit(solution)/shard_map/ppermute | solution.py:635
  36.7 1.9 %collective-permute-start.14 = (bf16[592,128]{1,0:T(8,128)(2,1)S(1)}, bf16[592,128]{1,0:T(8,128)(2,1)S(1)}, u32[]{:S(2)}, u32[]{:S(2)}) collective-permute-start(bf16[592,128]{1,0:T(8,128)(2,1)S(1)} %collective-permute-done.7.refs_7_), channel_id=1, source_target_pairs={{0,4},{4,0},{1,5},{5,1},{2,6},{6,2},{3,7},{7,3},{8,12},{12,8},{9,1... | collective-permute-start | bytes 454664 | tf_op jit(solution)/shard_map/ppermute | solution.py:635
  36.8 1.9 %collective-permute-start.15 = (bf16[592,128]{1,0:T(8,128)(2,1)S(1)}, bf16[592,128]{1,0:T(8,128)(2,1)S(1)}, u32[]{:S(2)}, u32[]{:S(2)}) collective-permute-start(bf16[592,128]{1,0:T(8,128)(2,1)S(1)} %collective-permute-done.8.refs_8_), channel_id=1, source_target_pairs={{0,4},{4,0},{1,5},{5,1},{2,6},{6,2},{3,7},{7,3},{8,12},{12,8},{9,1... | collective-permute-start | bytes 454664 | tf_op jit(solution)/shard_map/ppermute | solution.py:635
  41.2 12.2 %collective-permute-start.16 = (bf16[832,128]{1,0:T(8,128)(2,1)S(1)}, bf16[832,128]{1,0:T(8,128)(2,1)S(1)}, u32[]{:S(2)}, u32[]{:S(2)}) collective-permute-start(bf16[832,128]{1,0:T(8,128)(2,1)S(1)} %get-tuple-element.201), channel_id=1, source_target_pairs={{0,8},{8,0},{16,24},{24,16},{1,9},{9,1},{17,25},{25,17},{2,10},{10... | collective-permute-start | bytes 638984 | tf_op jit(solution)/shard_map/ppermute | solution.py:641
  42.8 10.6 %collective-permute-start.17 = (bf16[832,128]{1,0:T(8,128)(2,1)S(1)}, bf16[832,128]{1,0:T(8,128)(2,1)S(1)}, u32[]{:S(2)}, u32[]{:S(2)}) collective-permute-start(bf16[832,128]{1,0:T(8,128)(2,1)S(1)} %get-tuple-element.202), channel_id=1, source_target_pairs={{0,16},{8,24},{16,0},{24,8},{1,17},{9,25},{17,1},{25,9},{2,18},{10... | collective-permute-start | bytes 638984 | tf_op jit(solution)/shard_map/ppermute | solution.py:641
  44.2 10.0 %collective-permute-start.18 = (bf16[832,128]{1,0:T(8,128)(2,1)S(1)}, bf16[832,128]{1,0:T(8,128)(2,1)S(1)}, u32[]{:S(2)}, u32[]{:S(2)}) collective-permute-start(bf16[832,128]{1,0:T(8,128)(2,1)S(1)} %get-tuple-element.203), channel_id=1, source_target_pairs={{0,24},{8,16},{16,8},{24,0},{1,25},{9,17},{17,9},{25,1},{2,26},{10... | collective-permute-start | bytes 638984 | tf_op jit(solution)/shard_map/ppermute | solution.py:641
  55.2 12.9 %collective-permute-start.25 = (bf16[4,9,64,128]{3,2,1,0:T(8,128)(2,1)S(1)}, bf16[4,9,64,128]{3,2,1,0:T(8,128)(2,1)S(1)}, u32[]{:S(2)}, u32[]{:S(2)}) collective-permute-start(bf16[4,9,64,128]{3,2,1,0:T(8,128)(2,1)S(1)} %get-tuple-element.213.refs_9_), channel_id=1, source_target_pairs={{0,4},{4,0},{1,5},{5,1},{2,6},{6,2},{3,7},{7,3},{8,12},{12,8},{9,1... | collective-permute-start | bytes 1769480 | tf_op jit(solution)/shard_map/ppermute | solution.py:635
  55.3 6.0 %collective-permute-start.20 = (bf16[512,128]{1,0:T(8,128)(2,1)S(1)}, bf16[512,128]{1,0:T(8,128)(2,1)S(1)}, u32[]{:S(2)}, u32[]{:S(2)}) collective-permute-start(bf16[512,128]{1,0:T(8,128)(2,1)S(1)} %get-tuple-element.211.refs_1_), channel_id=1, source_target_pairs={{0,16},{8,24},{16,0},{24,8},{1,17},{9,25},{17,1},{25,9},{2,18},{10... | collective-permute-start | bytes 393224 | tf_op jit(solution)/shard_map/ppermute | solution.py:641
  56.8 6.3 %collective-permute-start.22 = (bf16[512,128]{1,0:T(8,128)(2,1)S(1)}, bf16[512,128]{1,0:T(8,128)(2,1)S(1)}, u32[]{:S(2)}, u32[]{:S(2)}) collective-permute-start(bf16[512,128]{1,0:T(8,128)(2,1)S(1)} %get-tuple-element.212.refs_5_), channel_id=1, source_target_pairs={{0,8},{8,0},{16,24},{24,16},{1,9},{9,1},{17,25},{25,17},{2,10},{10... | collective-permute-start | bytes 393224 | tf_op jit(solution)/shard_map/ppermute | solution.py:641
  58.4 7.6 %collective-permute-start.19 = (bf16[512,128]{1,0:T(8,128)(2,1)S(1)}, bf16[512,128]{1,0:T(8,128)(2,1)S(1)}, u32[]{:S(2)}, u32[]{:S(2)}) collective-permute-start(bf16[512,128]{1,0:T(8,128)(2,1)S(1)} %get-tuple-element.211.refs_1_), channel_id=1, source_target_pairs={{0,8},{8,0},{16,24},{24,16},{1,9},{9,1},{17,25},{25,17},{2,10},{10... | collective-permute-start | bytes 393224 | tf_op jit(solution)/shard_map/ppermute | solution.py:641
  58.9 7.1 %collective-permute-start.23 = (bf16[512,128]{1,0:T(8,128)(2,1)S(1)}, bf16[512,128]{1,0:T(8,128)(2,1)S(1)}, u32[]{:S(2)}, u32[]{:S(2)}) collective-permute-start(bf16[512,128]{1,0:T(8,128)(2,1)S(1)} %get-tuple-element.212.refs_5_), channel_id=1, source_target_pairs={{0,16},{8,24},{16,0},{24,8},{1,17},{9,25},{17,1},{25,9},{2,18},{10... | collective-permute-start | bytes 393224 | tf_op jit(solution)/shard_map/ppermute | solution.py:641
  61.3 6.8 %collective-permute-start.21 = (bf16[512,128]{1,0:T(8,128)(2,1)S(1)}, bf16[512,128]{1,0:T(8,128)(2,1)S(1)}, u32[]{:S(2)}, u32[]{:S(2)}) collective-permute-start(bf16[512,128]{1,0:T(8,128)(2,1)S(1)} %collective-permute-done.20.refs_3_), channel_id=1, source_target_pairs={{0,8},{8,0},{16,24},{24,16},{1,9},{9,1},{17,25},{25,17},{2,10},{10... | collective-permute-start | bytes 393224 | tf_op jit(solution)/shard_map/ppermute | solution.py:641
  63.2 5.0 %collective-permute-start.24 = (bf16[512,128]{1,0:T(8,128)(2,1)S(1)}, bf16[512,128]{1,0:T(8,128)(2,1)S(1)}, u32[]{:S(2)}, u32[]{:S(2)}) collective-permute-start(bf16[512,128]{1,0:T(8,128)(2,1)S(1)} %collective-permute-done.22.refs_6_), channel_id=1, source_target_pairs={{0,16},{8,24},{16,0},{24,8},{1,17},{9,25},{17,1},{25,9},{2,18},{10... | collective-permute-start | bytes 393224 | tf_op jit(solution)/shard_map/ppermute | solution.py:641
  70.7 18.8 %copy-start.2 = (bf16[4,9,64,128]{3,2,1,0:T(8,128)(2,1)S(1)}, bf16[4,9,64,128]{3,2,1,0:T(8,128)(2,1)}, u32[]{:S(2)}) copy-start(bf16[4,9,64,128]{3,2,1,0:T(8,128)(2,1)} %get-tuple-element.236.refs_1_) | copy-start | bytes 1769476
  70.8 9.2 %collective-permute-start.26 = (bf16[1024,256]{1,0:T(8,128)(2,1)S(1)}, bf16[1024,256]{1,0:T(8,128)(2,1)S(1)}, u32[]{:S(2)}, u32[]{:S(2)}) collective-permute-start(bf16[1024,256]{1,0:T(8,128)(2,1)S(1)} %get-tuple-element.222), channel_id=1, source_target_pairs={{0,4},{4,0},{1,5},{5,1},{2,6},{6,2},{3,7},{7,3},{8,12},{12,8},{9,1... | collective-permute-start | bytes 1572872 | tf_op jit(solution)/shard_map/ppermute | solution.py:635
  70.8 9.2 %collective-permute-start.27 = (bf16[1024,256]{1,0:T(8,128)(2,1)S(1)}, bf16[1024,256]{1,0:T(8,128)(2,1)S(1)}, u32[]{:S(2)}, u32[]{:S(2)}) collective-permute-start(bf16[1024,256]{1,0:T(8,128)(2,1)S(1)} %get-tuple-element.224), channel_id=1, source_target_pairs={{0,4},{4,0},{1,5},{5,1},{2,6},{6,2},{3,7},{7,3},{8,12},{12,8},{9,1... | collective-permute-start | bytes 1572872 | tf_op jit(solution)/shard_map/ppermute | solution.py:635
  89.5 12.9 %collective-permute-start.34 = (bf16[4,9,64,128]{3,2,1,0:T(8,128)(2,1)S(1)}, bf16[4,9,64,128]{3,2,1,0:T(8,128)(2,1)S(1)}, u32[]{:S(2)}, u32[]{:S(2)}) collective-permute-start(bf16[4,9,64,128]{3,2,1,0:T(8,128)(2,1)S(1)} %copy-done.2), channel_id=1, source_target_pairs={{0,4},{4,0},{1,5},{5,1},{2,6},{6,2},{3,7},{7,3},{8,12},{12,8},{9,1... | collective-permute-start | bytes 1769480 | tf_op jit(solution)/shard_map/ppermute | solution.py:635
  89.7 8.9 %collective-permute-start.35 = (bf16[1024,128]{1,0:T(8,128)(2,1)S(1)}, bf16[1024,128]{1,0:T(8,128)(2,1)S(1)}, u32[]{:S(2)}, u32[]{:S(2)}) collective-permute-start(bf16[1024,128]{1,0:T(8,128)(2,1)S(1)} %get-tuple-element.243), channel_id=1, source_target_pairs={{0,4},{4,0},{1,5},{5,1},{2,6},{6,2},{3,7},{7,3},{8,12},{12,8},{9,1... | collective-permute-start | bytes 786440 | tf_op jit(solution)/shard_map/ppermute | solution.py:635
  90.1 5.5 %collective-permute-start.29 = (bf16[512,128]{1,0:T(8,128)(2,1)S(1)}, bf16[512,128]{1,0:T(8,128)(2,1)S(1)}, u32[]{:S(2)}, u32[]{:S(2)}) collective-permute-start(bf16[512,128]{1,0:T(8,128)(2,1)S(1)} %get-tuple-element.234.refs_1_.refs_3_), channel_id=1, source_target_pairs={{0,16},{8,24},{16,0},{24,8},{1,17},{9,25},{17,1},{25,9},{2,18},{10... | collective-permute-start | bytes 393224 | tf_op jit(solution)/shard_map/ppermute | solution.py:641
  91.6 6.4 %collective-permute-start.31 = (bf16[512,128]{1,0:T(8,128)(2,1)S(1)}, bf16[512,128]{1,0:T(8,128)(2,1)S(1)}, u32[]{:S(2)}, u32[]{:S(2)}) collective-permute-start(bf16[512,128]{1,0:T(8,128)(2,1)S(1)} %get-tuple-element.235.refs_5_.refs_4_), channel_id=1, source_target_pairs={{0,8},{8,0},{16,24},{24,16},{1,9},{9,1},{17,25},{25,17},{2,10},{10... | collective-permute-start | bytes 393224 | tf_op jit(solution)/shard_map/ppermute | solution.py:641
  92.2 11.5 %collective-permute-start.28 = (bf16[512,128]{1,0:T(8,128)(2,1)S(1)}, bf16[512,128]{1,0:T(8,128)(2,1)S(1)}, u32[]{:S(2)}, u32[]{:S(2)}) collective-permute-start(bf16[512,128]{1,0:T(8,128)(2,1)S(1)} %get-tuple-element.234.refs_1_.refs_3_), channel_id=1, source_target_pairs={{0,8},{8,0},{16,24},{24,16},{1,9},{9,1},{17,25},{25,17},{2,10},{10... | collective-permute-start | bytes 393224 | tf_op jit(solution)/shard_map/ppermute | solution.py:641
  95.6 8.1 %collective-permute-start.32 = (bf16[512,128]{1,0:T(8,128)(2,1)S(1)}, bf16[512,128]{1,0:T(8,128)(2,1)S(1)}, u32[]{:S(2)}, u32[]{:S(2)}) collective-permute-start(bf16[512,128]{1,0:T(8,128)(2,1)S(1)} %get-tuple-element.235.refs_5_.refs_4_), channel_id=1, source_target_pairs={{0,16},{8,24},{16,0},{24,8},{1,17},{9,25},{17,1},{25,9},{2,18},{10... | collective-permute-start | bytes 393224 | tf_op jit(solution)/shard_map/ppermute | solution.py:641
  98.0 5.8 %collective-permute-start.30 = (bf16[512,128]{1,0:T(8,128)(2,1)S(1)}, bf16[512,128]{1,0:T(8,128)(2,1)S(1)}, u32[]{:S(2)}, u32[]{:S(2)}) collective-permute-start(bf16[512,128]{1,0:T(8,128)(2,1)S(1)} %collective-permute-done.29.refs_3_), channel_id=1, source_target_pairs={{0,8},{8,0},{16,24},{24,16},{1,9},{9,1},{17,25},{25,17},{2,10},{10... | collective-permute-start | bytes 393224 | tf_op jit(solution)/shard_map/ppermute | solution.py:641
  98.6 5.2 %collective-permute-start.33 = (bf16[512,128]{1,0:T(8,128)(2,1)S(1)}, bf16[512,128]{1,0:T(8,128)(2,1)S(1)}, u32[]{:S(2)}, u32[]{:S(2)}) collective-permute-start(bf16[512,128]{1,0:T(8,128)(2,1)S(1)} %collective-permute-done.31.refs_6_), channel_id=1, source_target_pairs={{0,16},{8,24},{16,0},{24,8},{1,17},{9,25},{17,1},{25,9},{2,18},{10... | collective-permute-start | bytes 393224 | tf_op jit(solution)/shard_map/ppermute | solution.py:641
  106.2 11.5 %collective-permute-start.36 = (bf16[832,128]{1,0:T(8,128)(2,1)S(1)}, bf16[832,128]{1,0:T(8,128)(2,1)S(1)}, u32[]{:S(2)}, u32[]{:S(2)}) collective-permute-start(bf16[832,128]{1,0:T(8,128)(2,1)S(1)} %get-tuple-element.251), channel_id=1, source_target_pairs={{0,8},{8,0},{16,24},{24,16},{1,9},{9,1},{17,25},{25,17},{2,10},{10... | collective-permute-start | bytes 638984 | tf_op jit(solution)/shard_map/ppermute | solution.py:641
  107.5 10.2 %collective-permute-start.37 = (bf16[832,128]{1,0:T(8,128)(2,1)S(1)}, bf16[832,128]{1,0:T(8,128)(2,1)S(1)}, u32[]{:S(2)}, u32[]{:S(2)}) collective-permute-start(bf16[832,128]{1,0:T(8,128)(2,1)S(1)} %get-tuple-element.252), channel_id=1, source_target_pairs={{0,16},{8,24},{16,0},{24,8},{1,17},{9,25},{17,1},{25,9},{2,18},{10... | collective-permute-start | bytes 638984 | tf_op jit(solution)/shard_map/ppermute | solution.py:641
  108.2 9.5 %collective-permute-start.38 = (bf16[832,128]{1,0:T(8,128)(2,1)S(1)}, bf16[832,128]{1,0:T(8,128)(2,1)S(1)}, u32[]{:S(2)}, u32[]{:S(2)}) collective-permute-start(bf16[832,128]{1,0:T(8,128)(2,1)S(1)} %get-tuple-element.253), channel_id=1, source_target_pairs={{0,24},{8,16},{16,8},{24,0},{1,25},{9,17},{17,9},{25,1},{2,26},{10... | collective-permute-start | bytes 638984 | tf_op jit(solution)/shard_map/ppermute | solution.py:641
  118.0 2.0 %collective-permute-start.39 = (bf16[1024,128]{1,0:T(8,128)(2,1)S(1)}, bf16[1024,128]{1,0:T(8,128)(2,1)S(1)}, u32[]{:S(2)}, u32[]{:S(2)}) collective-permute-start(bf16[1024,128]{1,0:T(8,128)(2,1)S(1)} %get-tuple-element.265), channel_id=1, source_target_pairs={{0,4},{4,0},{1,5},{5,1},{2,6},{6,2},{3,7},{7,3},{8,12},{12,8},{9,1... | collective-permute-start | bytes 786440 | tf_op jit(solution)/shard_map/ppermute | solution.py:635
  118.9 8.2 %collective-permute-start.43 = (bf16[576,128]{1,0:T(8,128)(2,1)S(1)}, bf16[576,128]{1,0:T(8,128)(2,1)S(1)}, u32[]{:S(2)}, u32[]{:S(2)}) collective-permute-start(bf16[576,128]{1,0:T(8,128)(2,1)S(1)} %get-tuple-element.276), channel_id=1, source_target_pairs={{0,1},{1,0},{2,3},{3,2},{4,5},{5,4},{6,7},{7,6},{8,9},{9,8},{10,11... | collective-permute-start | bytes 442376 | tf_op jit(solution)/shard_map/ppermute | solution.py:632
  119.5 10.8 %collective-permute-start.44 = (bf16[576,128]{1,0:T(8,128)(2,1)S(1)}, bf16[576,128]{1,0:T(8,128)(2,1)S(1)}, u32[]{:S(2)}, u32[]{:S(2)}) collective-permute-start(bf16[576,128]{1,0:T(8,128)(2,1)S(1)} %get-tuple-element.277), channel_id=1, source_target_pairs={{0,2},{1,3},{2,0},{3,1},{4,6},{5,7},{6,4},{7,5},{8,10},{9,11},{10,... | collective-permute-start | bytes 442376 | tf_op jit(solution)/shard_map/ppermute | solution.py:632
  122.5 7.9 %collective-permute-start.40 = (bf16[576,128]{1,0:T(8,128)(2,1)S(1)}, bf16[576,128]{1,0:T(8,128)(2,1)S(1)}, u32[]{:S(2)}, u32[]{:S(2)}) collective-permute-start(bf16[576,128]{1,0:T(8,128)(2,1)S(1)} %get-tuple-element.272), channel_id=1, source_target_pairs={{0,8},{8,0},{16,24},{24,16},{1,9},{9,1},{17,25},{25,17},{2,10},{10... | collective-permute-start | bytes 442376 | tf_op jit(solution)/shard_map/ppermute | solution.py:641
  123.7 6.8 %collective-permute-start.41 = (bf16[576,128]{1,0:T(8,128)(2,1)S(1)}, bf16[576,128]{1,0:T(8,128)(2,1)S(1)}, u32[]{:S(2)}, u32[]{:S(2)}) collective-permute-start(bf16[576,128]{1,0:T(8,128)(2,1)S(1)} %get-tuple-element.273), channel_id=1, source_target_pairs={{0,16},{8,24},{16,0},{24,8},{1,17},{9,25},{17,1},{25,9},{2,18},{10... | collective-permute-start | bytes 442376 | tf_op jit(solution)/shard_map/ppermute | solution.py:641
  124.5 8.0 %collective-permute-start.42 = (bf16[576,128]{1,0:T(8,128)(2,1)S(1)}, bf16[576,128]{1,0:T(8,128)(2,1)S(1)}, u32[]{:S(2)}, u32[]{:S(2)}) collective-permute-start(bf16[576,128]{1,0:T(8,128)(2,1)S(1)} %get-tuple-element.274), channel_id=1, source_target_pairs={{0,24},{8,16},{16,8},{24,0},{1,25},{9,17},{17,9},{25,1},{2,26},{10... | collective-permute-start | bytes 442376 | tf_op jit(solution)/shard_map/ppermute | solution.py:641
  127.1 7.2 %collective-permute-start.45 = (bf16[576,128]{1,0:T(8,128)(2,1)S(1)}, bf16[576,128]{1,0:T(8,128)(2,1)S(1)}, u32[]{:S(2)}, u32[]{:S(2)}) collective-permute-start(bf16[576,128]{1,0:T(8,128)(2,1)S(1)} %get-tuple-element.278), channel_id=1, source_target_pairs={{0,3},{1,2},{2,1},{3,0},{4,7},{5,6},{6,5},{7,4},{8,11},{9,10},{10,... | collective-permute-start | bytes 442376 | tf_op jit(solution)/shard_map/ppermute | solution.py:632
  135.0 11.9 %collective-permute-start.46 = (bf16[576,128]{1,0:T(8,128)(2,1)S(1)}, bf16[576,128]{1,0:T(8,128)(2,1)S(1)}, u32[]{:S(2)}, u32[]{:S(2)}) collective-permute-start(bf16[576,128]{1,0:T(8,128)(2,1)S(1)} %get-tuple-element.292), channel_id=1, source_target_pairs={{0,1},{1,0},{2,3},{3,2},{4,5},{5,4},{6,7},{7,6},{8,9},{9,8},{10,11... | collective-permute-start | bytes 442376 | tf_op jit(solution)/shard_map/ppermute | solution.py:632
  137.1 12.2 %collective-permute-start.47 = (bf16[576,128]{1,0:T(8,128)(2,1)S(1)}, bf16[576,128]{1,0:T(8,128)(2,1)S(1)}, u32[]{:S(2)}, u32[]{:S(2)}) collective-permute-start(bf16[576,128]{1,0:T(8,128)(2,1)S(1)} %get-tuple-element.293), channel_id=1, source_target_pairs={{0,2},{1,3},{2,0},{3,1},{4,6},{5,7},{6,4},{7,5},{8,10},{9,11},{10,... | collective-permute-start | bytes 442376 | tf_op jit(solution)/shard_map/ppermute | solution.py:632
  137.6 11.6 %collective-permute-start.48 = (bf16[576,128]{1,0:T(8,128)(2,1)S(1)}, bf16[576,128]{1,0:T(8,128)(2,1)S(1)}, u32[]{:S(2)}, u32[]{:S(2)}) collective-permute-start(bf16[576,128]{1,0:T(8,128)(2,1)S(1)} %get-tuple-element.294), channel_id=1, source_target_pairs={{0,3},{1,2},{2,1},{3,0},{4,7},{5,6},{6,5},{7,4},{8,11},{9,10},{10,... | collective-permute-start | bytes 442376 | tf_op jit(solution)/shard_map/ppermute | solution.py:632
  139.5 5.7 %copy-start = (f32[2,9,64,128]{3,2,1,0:T(8,128)S(1)}, f32[2,9,64,128]{3,2,1,0:T(8,128)}, u32[]{:S(2)}) copy-start(f32[2,9,64,128]{3,2,1,0:T(8,128)} %refs_1_.3) | copy-start | bytes 1769476
  139.5 5.7 %copy-start.3 = (f32[2,9,64,128]{3,2,1,0:T(8,128)S(1)}, f32[2,9,64,128]{3,2,1,0:T(8,128)}, u32[]{:S(2)}) copy-start(f32[2,9,64,128]{3,2,1,0:T(8,128)} %refs_5_.6) | copy-start | bytes 1769476
  139.5 5.7 %copy-start.4 = (f32[2,9,64,128]{3,2,1,0:T(8,128)S(1)}, f32[2,9,64,128]{3,2,1,0:T(8,128)}, u32[]{:S(2)}) copy-start(f32[2,9,64,128]{3,2,1,0:T(8,128)} %refs_6_.4) | copy-start | bytes 1769476
  143.3 12.0 %collective-permute-start.49 = (bf16[256,512]{1,0:T(8,128)(2,1)}, bf16[256,512]{1,0:T(8,128)(2,1)S(1)}, u32[]{:S(2)}, u32[]{:S(2)}) collective-permute-start(bf16[256,512]{1,0:T(8,128)(2,1)} %get-tuple-element.307), channel_id=1, source_target_pairs={{0,8},{8,0},{16,24},{24,16},{1,9},{9,1},{17,25},{25,17},{2,10},{10... | collective-permute-start | bytes 786440 | tf_op jit(solution)/shard_map/ppermute | solution.py:641
  144.5 10.8 %collective-permute-start.50 = (bf16[256,512]{1,0:T(8,128)(2,1)S(1)}, bf16[256,512]{1,0:T(8,128)(2,1)S(1)}, u32[]{:S(2)}, u32[]{:S(2)}) collective-permute-start(bf16[256,512]{1,0:T(8,128)(2,1)S(1)} %get-tuple-element.308), channel_id=1, source_target_pairs={{0,16},{8,24},{16,0},{24,8},{1,17},{9,25},{17,1},{25,9},{2,18},{10... | collective-permute-start | bytes 786440 | tf_op jit(solution)/shard_map/ppermute | solution.py:641
  146.9 9.9 %collective-permute-start.51 = (bf16[256,512]{1,0:T(8,128)(2,1)S(1)}, bf16[256,512]{1,0:T(8,128)(2,1)S(1)}, u32[]{:S(2)}, u32[]{:S(2)}) collective-permute-start(bf16[256,512]{1,0:T(8,128)(2,1)S(1)} %get-tuple-element.309), channel_id=1, source_target_pairs={{0,24},{8,16},{16,8},{24,0},{1,25},{9,17},{17,9},{25,1},{2,26},{10... | collective-permute-start | bytes 786440 | tf_op jit(solution)/shard_map/ppermute | solution.py:641
  150.4 11.4 %copy-start.8 = (f32[4,512]{1,0:T(4,128)S(1)}, f32[4,512]{1,0:T(4,128)}, u32[]{:S(2)}) copy-start(f32[4,512]{1,0:T(4,128)} %refs_5_.7) | copy-start | bytes 24580
  150.4 11.4 %copy-start.9 = (f32[4,512]{1,0:T(4,128)S(1)}, f32[4,512]{1,0:T(4,128)}, u32[]{:S(2)}) copy-start(f32[4,512]{1,0:T(4,128)} %refs_6_.5) | copy-start | bytes 24580
  150.4 11.4 %all-to-all-start.4 = ((f32[32,2,128]{2,1,0:T(2,128)}), f32[32,2,128]{2,1,0:T(2,128)S(1)}, u32[]{:S(2)}, u32[]{:S(2)}) async-start(f32[32,2,128]{2,1,0:T(2,128)} %get-tuple-element.304), calls=%async_computation.4 | async-start | bytes 65536 | tf_op jit(solution)/shard_map/all_to_all | solution.py:828

commit v9 on v8

--- a/solution.py
+++ b/solution.py
@@ -605,11 +605,10 @@
         if first:
             outs[m][z.K * z.IB :, :] = sizes
             continue
-        for slot in range(z.Q):
-
-            @pl.when((at[0] ^ m) == slot)
-            def _(m=m, slot=slot):
-                outs[m][z.K * z.IB :, :] = map_ref[:, slot * z.L : (slot + 1) * z.L]
+        part = map_ref[:, : z.L]
+        for slot in range(1, z.Q):
+            part = jnp.where((at[0] ^ m) == slot, map_ref[:, slot * z.L : (slot + 1) * z.L], part)
+        outs[m][z.K * z.IB :, :] = part
 
     if not first:
         copy.wait()

time: 163 us -> 163 us (level)
  no operation moved by 1% of the time
where the time goes in v9:
time: 163 us
  starting transfers between devices  63.7 us (39%)
  waiting for transfers between devices  33.9 us (21%)
  blocking collectives  33.2 us (20%)
  Pallas kernels  29.2 us (18%)
    ppermute x30, starting transfers between devices, over_q(): return lax.ppermute(v, 'q', [(i, i ^ m) for i in range(z.Q)]) if m else v  37.8 us
    all_to_all x4, blocking collectives, sharers(): return lax.all_to_all(v, ('s', 'z'), 0, 0)  33.2 us
    pallas_call x18, Pallas kernels, call(): pl.pallas_call(run, out_shape=out_shape, in_specs=[pl.BlockSpec(memory_sp...  26.5 us
    ppermute x12, starting transfers between devices, over_z(): return lax.ppermute(v, 'z', [(i, i ^ m) for i in range(z.Z)]) if m else v  19.2 us
    ppermute x12, waiting for transfers between devices, over_z(): return lax.ppermute(v, 'z', [(i, i ^ m) for i in range(z.Z)]) if m else v  16.5 us
    ppermute x30, waiting for transfers between devices, over_q(): return lax.ppermute(v, 'q', [(i, i ^ m) for i in range(z.Q)]) if m else v  13.1 us
    all_to_all x1, waiting for transfers between devices, shards(): stats = lax.all_to_all(stats, ('s', 'q', 'z'), 0, 0)  4.22 us
    all_to_all x1, starting transfers between devices, shards(): stats = lax.all_to_all(stats, ('s', 'q', 'z'), 0, 0)  4.21 us
  transfers between devices with their start and end apart: 53, of which 20 were waited for; matrix products, arithmetic and copies ran while one was open for 0% of the time, Pallas kernels for 10%

profile of v9, /device:TPU:0, one launch (start us, length us, event | category | flops | bytes accessed | tf_op | source)
XLA Modules:
  0.0 163.0 jit_solution(14799594627952065877)
XLA Ops:
  0.7 1.2 convert.4
  1.9 3.1 %collective-permute-start = (bf16[9,64,128]{2,1,0:T(8,128)(2,1)S(1)}, bf16[9,64,128]{2,1,0:T(8,128)(2,1)S(1)}, u32[]{:S(2)}, u32[]{:S(2)}) collective-permute-start(bf16[9,64,128]{2,1,0:T(8,128)(2,1)S(1)} %get-tuple-element.166.refs_1_), channel_id=1, source_target_pairs={{0,1},{1,0},{2,3},{3,2},{4,5},{5,4},{6,7},{7,6},{8,9},{9,8},{10,11... | collective-permute-start | bytes 442376 | tf_op jit(solution)/shard_map/ppermute | solution.py:631
  5.0 2.6 %collective-permute-start.1 = (bf16[9,64,128]{2,1,0:T(8,128)(2,1)S(1)}, bf16[9,64,128]{2,1,0:T(8,128)(2,1)S(1)}, u32[]{:S(2)}, u32[]{:S(2)}) collective-permute-start(bf16[9,64,128]{2,1,0:T(8,128)(2,1)S(1)} %get-tuple-element.166.refs_1_), channel_id=1, source_target_pairs={{0,2},{1,3},{2,0},{3,1},{4,6},{5,7},{6,4},{7,5},{8,10},{9,11},{10,... | collective-permute-start | bytes 442376 | tf_op jit(solution)/shard_map/ppermute | solution.py:631
  7.6 1.7 %collective-permute-start.3 = (bf16[256,512]{1,0:T(8,128)(2,1)S(1)}, bf16[256,512]{1,0:T(8,128)(2,1)S(1)}, u32[]{:S(2)}, u32[]{:S(2)}) collective-permute-start(bf16[256,512]{1,0:T(8,128)(2,1)S(1)} %bitcast.12), channel_id=1, source_target_pairs={{0,8},{8,0},{16,24},{24,16},{1,9},{9,1},{17,25},{25,17},{2,10},{10... | collective-permute-start | bytes 786440 | tf_op jit(solution)/shard_map/ppermute | solution.py:640
  9.3 1.5 collective-permute-start.4
  10.8 2.7 %collective-permute-start.5 = (bf16[256,512]{1,0:T(8,128)(2,1)S(1)}, bf16[256,512]{1,0:T(8,128)(2,1)S(1)}, u32[]{:S(2)}, u32[]{:S(2)}) collective-permute-start(bf16[256,512]{1,0:T(8,128)(2,1)S(1)} %bitcast.14), channel_id=1, source_target_pairs={{0,24},{8,16},{16,8},{24,0},{1,25},{9,17},{17,9},{25,1},{2,26},{10... | collective-permute-start | bytes 786440 | tf_op jit(solution)/shard_map/ppermute | solution.py:640
  13.5 5.5 %collective-permute-done.1.refs_3_ = bf16[9,64,128]{2,1,0:T(8,128)(2,1)S(1)} collective-permute-done((bf16[9,64,128]{2,1,0:T(8,128)(2,1)S(1)}, bf16[9,64,128]{2,1,0:T(8,128)(2,1)S(1)}, u32[]{:S(2)}, u32[]{:S(2)}) %collective-permute-start.1) | collective-permute-done | bytes 147488 | tf_op jit(solution)/shard_map/ppermute | solution.py:631
  19.0 3.3 %collective-permute-start.10 = (bf16[9,64,128]{2,1,0:T(8,128)(2,1)S(1)}, bf16[9,64,128]{2,1,0:T(8,128)(2,1)S(1)}, u32[]{:S(2)}, u32[]{:S(2)}) collective-permute-start(bf16[9,64,128]{2,1,0:T(8,128)(2,1)S(1)} %get-tuple-element.191.refs_1_), channel_id=1, source_target_pairs={{0,2},{1,3},{2,0},{3,1},{4,6},{5,7},{6,4},{7,5},{8,10},{9,11},{10,... | collective-permute-start | bytes 442376 | tf_op jit(solution)/shard_map/ppermute | solution.py:631
  23.0 1.6 collective-permute-start.6
  24.6 1.5 collective-permute-start.7
  26.6 2.3 %collective-permute-start.11 = (bf16[9,64,128]{2,1,0:T(8,128)(2,1)S(1)}, bf16[9,64,128]{2,1,0:T(8,128)(2,1)S(1)}, u32[]{:S(2)}, u32[]{:S(2)}) collective-permute-start(bf16[9,64,128]{2,1,0:T(8,128)(2,1)S(1)} %get-tuple-element.191.refs_1_), channel_id=1, source_target_pairs={{0,3},{1,2},{2,1},{3,0},{4,7},{5,6},{6,5},{7,4},{8,11},{9,10},{10,... | collective-permute-start | bytes 442376 | tf_op jit(solution)/shard_map/ppermute | solution.py:631
  28.9 2.1 %collective-permute-done.10.refs_3_ = bf16[9,64,128]{2,1,0:T(8,128)(2,1)S(1)} collective-permute-done((bf16[9,64,128]{2,1,0:T(8,128)(2,1)S(1)}, bf16[9,64,128]{2,1,0:T(8,128)(2,1)S(1)}, u32[]{:S(2)}, u32[]{:S(2)}) %collective-permute-start.10) | collective-permute-done | bytes 147488 | tf_op jit(solution)/shard_map/ppermute | solution.py:631
  30.9 0.9 shard_map.169
  31.9 1.8 %collective-permute-done.11.refs_4_ = bf16[9,64,128]{2,1,0:T(8,128)(2,1)S(1)} collective-permute-done((bf16[9,64,128]{2,1,0:T(8,128)(2,1)S(1)}, bf16[9,64,128]{2,1,0:T(8,128)(2,1)S(1)}, u32[]{:S(2)}, u32[]{:S(2)}) %collective-permute-start.11) | collective-permute-done | bytes 147488 | tf_op jit(solution)/shard_map/ppermute | solution.py:631
  33.7 2.4 %collective-permute-done.9.refs_2_ = bf16[9,64,128]{2,1,0:T(8,128)(2,1)S(1)} collective-permute-done((bf16[9,64,128]{2,1,0:T(8,128)(2,1)S(1)}, bf16[9,64,128]{2,1,0:T(8,128)(2,1)S(1)}, u32[]{:S(2)}, u32[]{:S(2)}) %collective-permute-start.9) | collective-permute-done | bytes 147488 | tf_op jit(solution)/shard_map/ppermute | solution.py:631
  37.2 1.4 shard_map.171
  38.6 2.5 %shard_map.170 = (f32[1024,128]{1,0:T(8,128)S(1)}, f32[16,8,128]{2,1,0:T(8,128)S(1)}, f32[8,4,128]{2,1,0:T(4,128)S(1)}, bf16[512,1152]{1,0:T(8,128)(2,1)}) custom-call(s32[3]{0:T(128)S(1)} %pad_add_fusion.refs_0_.refs_9_, bf16[256,512]{1,0:T(8,128)(2,1)S(1)} %bitcast.16, bf16[256,512]{1,0:T(8,128)(2,1)S(1)} %collective-permute-done.3.refs_3_.refs_2_, ...), custom_call_target="tpu_custom_call" | custom-call | flops 1 | bytes 1 | tf_op jit(solution)/shard_map/pallas_call | solution.py:68
  41.2 1.6 collective-permute-start.16
  42.8 1.5 collective-permute-start.17
  44.7 8.7 %all_to_all.25.refs_2_ = f32[8,4,128]{2,1,0:T(4,128)S(1)} all-to-all(f32[8,4,128]{2,1,0:T(4,128)S(1)} %get-tuple-element.199), channel_id=1, replica_groups=mesh['ha'=2,'wa'=4,'ba'=4] {'wa':(2)2,'ba'}, dimensions={0} | all-to-all | bytes 32768 | tf_op jit(solution)/shard_map/all_to_all | solution.py:637
  53.4 0.8 collective-permute-done.18.refs_8_
  54.2 1.0 shard_map.172
  55.3 1.6 collective-permute-start.20
  56.8 1.6 collective-permute-start.22
  59.4 1.9 %collective-permute-done.20.refs_3_ = bf16[512,128]{1,0:T(8,128)(2,1)S(1)} collective-permute-done((bf16[512,128]{1,0:T(8,128)(2,1)S(1)}, bf16[512,128]{1,0:T(8,128)(2,1)S(1)}, u32[]{:S(2)}, u32[]{:S(2)}) %collective-permute-start.20) | collective-permute-done | bytes 131104 | tf_op jit(solution)/shard_map/ppermute | solution.py:640
  61.3 1.5 collective-permute-start.21
  63.2 1.5 collective-permute-start.24
  64.7 1.3 collective-permute-done.19.refs_2_
  66.0 2.0 %collective-permute-done.21.refs_4_ = bf16[512,128]{1,0:T(8,128)(2,1)S(1)} collective-permute-done((bf16[512,128]{1,0:T(8,128)(2,1)S(1)}, bf16[512,128]{1,0:T(8,128)(2,1)S(1)}, u32[]{:S(2)}, u32[]{:S(2)}) %collective-permute-start.21) | collective-permute-done | bytes 131104 | tf_op jit(solution)/shard_map/ppermute | solution.py:640
  68.2 2.6 %shard_map.173 = (bf16[1024,256]{1,0:T(8,128)(2,1)S(1)}, bf16[1024,256]{1,0:T(8,128)(2,1)S(1)}, f32[1024,128]{1,0:T(8,128)S(1)}, f32[8,4,128]{2,1,0:T(4,128)S(1)}) custom-call(s32[3]{0:T(128)S(1)} %pad_add_fusion.refs_0_.refs_9_, bf16[512,128]{1,0:T(8,128)(2,1)S(1)} %get-tuple-element.211.refs_1_, bf16[512,128]{1,0:T(8,128)(2,1)S(1)} %collective-permute-done.19.refs_2_, ...), custom_call_target="tpu_custom_call" | custom-call | flops 1 | bytes 1 | tf_op jit(solution)/shard_map/pallas_call | solution.py:68
  71.3 8.7 %all_to_all.26.refs_2_ = f32[8,4,128]{2,1,0:T(4,128)S(1)} all-to-all(f32[8,4,128]{2,1,0:T(4,128)S(1)} %get-tuple-element.220), channel_id=1, replica_groups=mesh['ha'=2,'wa'=4,'ba'=4] {'wa':(2)2,'ba'}, dimensions={0} | all-to-all | bytes 32768 | tf_op jit(solution)/shard_map/all_to_all | solution.py:637
  80.0 1.3 shard_map.174
  81.3 8.0 %all_to_all.27.refs_3_ = f32[8,2,128]{2,1,0:T(2,128)S(1)} all-to-all(f32[8,2,128]{2,1,0:T(2,128)S(1)} %get-tuple-element.230), channel_id=1, replica_groups=mesh['ha'=2,'wa'=4,'ba'=4] {'wa':(2)2,'ba'}, dimensions={0} | all-to-all | bytes 16384 | tf_op jit(solution)/shard_map/all_to_all | solution.py:637
  90.1 1.5 collective-permute-start.29
  92.2 1.4 collective-permute-start.28
  93.6 2.0 %collective-permute-done.29.refs_3_ = bf16[512,128]{1,0:T(8,128)(2,1)S(1)} collective-permute-done((bf16[512,128]{1,0:T(8,128)(2,1)S(1)}, bf16[512,128]{1,0:T(8,128)(2,1)S(1)}, u32[]{:S(2)}, u32[]{:S(2)}) %collective-permute-start.29) | collective-permute-done | bytes 131104 | tf_op jit(solution)/shard_map/ppermute | solution.py:640
  95.6 1.5 collective-permute-start.32
  97.1 0.9 collective-permute-done.31.refs_6_
  98.6 1.5 collective-permute-start.33
  100.1 2.3 %shard_map.178 = (bf16[832,128]{1,0:T(8,128)(2,1)S(1)}, bf16[832,128]{1,0:T(8,128)(2,1)S(1)}, bf16[832,128]{1,0:T(8,128)(2,1)S(1)}, bf16[832,128]{1,0:T(8,128)(2,1)S(1)}) custom-call(s32[3]{0:T(128)S(1)} %pad_add_fusion.refs_0_.refs_9_, bf16[1024,256]{1,0:T(8,128)(2,1)S(1)} %get-tuple-element.241.refs_1_, ...), custom_call_target="tpu_custom_call" | custom-call | flops 3000000000 | bytes 1 | tf_op jit(solution)/shard_map/pallas_call | solution.py:68
  102.5 1.3 shard_map.176
  103.8 2.5 %shard_map.177 = (f32[1024,128]{1,0:T(8,128)S(1)}, f32[8,2,128]{2,1,0:T(2,128)S(1)}) custom-call(s32[3]{0:T(128)S(1)} %pad_add_fusion.refs_0_.refs_9_, bf16[512,128]{1,0:T(8,128)(2,1)S(1)} %get-tuple-element.234.refs_1_.refs_3_, bf16[512,128]{1,0:T(8,128)(2,1)S(1)} %collective-permute-done.28.refs_2_, bf16[512,128]{1,0:T(8,128)(2,1)S(1)} %collective-permute-done.29.refs_3_, ...), custom_call_target="tpu_custom_call" | custom-call | flops 1 | bytes 1 | tf_op jit(solution)/shard_map/pallas_call | solution.py:68
  106.2 1.3 collective-permute-start.36
  108.2 1.5 collective-permute-start.38
  109.8 8.0 %all_to_all.28.refs_3_ = f32[8,2,128]{2,1,0:T(2,128)S(1)} all-to-all(f32[8,2,128]{2,1,0:T(2,128)S(1)} %get-tuple-element.249), channel_id=1, replica_groups=mesh['ha'=2,'wa'=4,'ba'=4] {'wa':(2)2,'ba'}, dimensions={0} | all-to-all | bytes 16384 | tf_op jit(solution)/shard_map/all_to_all | solution.py:637
  120.1 2.4 %shard_map.181 = (bf16[576,128]{1,0:T(8,128)(2,1)S(1)}, bf16[576,128]{1,0:T(8,128)(2,1)S(1)}, bf16[576,128]{1,0:T(8,128)(2,1)S(1)}, bf16[576,128]{1,0:T(8,128)(2,1)S(1)}) custom-call(s32[3]{0:T(128)S(1)} %pad_add_fusion.refs_0_.refs_9_, bf16[1024,256]{1,0:T(8,128)(2,1)S(1)} %get-tuple-element.262.refs_1_, ...), custom_call_target="tpu_custom_call" | custom-call | flops 3000000000 | bytes 1 | tf_op jit(solution)/shard_map/pallas_call | solution.py:68
  122.5 1.3 collective-permute-start.40
  124.5 1.5 collective-permute-start.42
  126.0 1.1 collective-permute-done.43.refs_1_
  127.1 2.2 %collective-permute-start.45 = (bf16[576,128]{1,0:T(8,128)(2,1)S(1)}, bf16[576,128]{1,0:T(8,128)(2,1)S(1)}, u32[]{:S(2)}, u32[]{:S(2)}) collective-permute-start(bf16[576,128]{1,0:T(8,128)(2,1)S(1)} %get-tuple-element.278), channel_id=1, source_target_pairs={{0,3},{1,2},{2,1},{3,0},{4,7},{5,6},{6,5},{7,4},{8,11},{9,10},{10,... | collective-permute-start | bytes 442376 | tf_op jit(solution)/shard_map/ppermute | solution.py:631
  129.4 1.0 collective-permute-done.44.refs_2_
  130.5 2.0 %collective-permute-done.42.refs_4_ = bf16[576,128]{1,0:T(8,128)(2,1)S(1)} collective-permute-done((bf16[576,128]{1,0:T(8,128)(2,1)S(1)}, bf16[576,128]{1,0:T(8,128)(2,1)S(1)}, u32[]{:S(2)}, u32[]{:S(2)}) %collective-permute-start.42) | collective-permute-done | bytes 147488 | tf_op jit(solution)/shard_map/ppermute | solution.py:640
  132.5 1.9 %collective-permute-done.45.refs_3_ = bf16[576,128]{1,0:T(8,128)(2,1)S(1)} collective-permute-done((bf16[576,128]{1,0:T(8,128)(2,1)S(1)}, bf16[576,128]{1,0:T(8,128)(2,1)S(1)}, u32[]{:S(2)}, u32[]{:S(2)}) %collective-permute-start.45) | collective-permute-done | bytes 147488 | tf_op jit(solution)/shard_map/ppermute | solution.py:631
  135.0 2.1 %collective-permute-start.46 = (bf16[576,128]{1,0:T(8,128)(2,1)S(1)}, bf16[576,128]{1,0:T(8,128)(2,1)S(1)}, u32[]{:S(2)}, u32[]{:S(2)}) collective-permute-start(bf16[576,128]{1,0:T(8,128)(2,1)S(1)} %get-tuple-element.292), channel_id=1, source_target_pairs={{0,1},{1,0},{2,3},{3,2},{4,5},{5,4},{6,7},{7,6},{8,9},{9,8},{10,11... | collective-permute-start | bytes 442376 | tf_op jit(solution)/shard_map/ppermute | solution.py:631
  137.6 1.9 %collective-permute-start.48 = (bf16[576,128]{1,0:T(8,128)(2,1)S(1)}, bf16[576,128]{1,0:T(8,128)(2,1)S(1)}, u32[]{:S(2)}, u32[]{:S(2)}) collective-permute-start(bf16[576,128]{1,0:T(8,128)(2,1)S(1)} %get-tuple-element.294), channel_id=1, source_target_pairs={{0,3},{1,2},{2,1},{3,0},{4,7},{5,6},{6,5},{7,4},{8,11},{9,10},{10,... | collective-permute-start | bytes 442376 | tf_op jit(solution)/shard_map/ppermute | solution.py:631
  139.5 3.8 %shard_map.185 = (f32[256,512]{1,0:T(8,128)S(1)}, bf16[256,512]{1,0:T(8,128)(2,1)}, bf16[256,512]{1,0:T(8,128)(2,1)S(1)}, bf16[256,512]{1,0:T(8,128)(2,1)S(1)}) custom-call(s32[3]{0:T(128)S(1)} %pad_add_fusion.refs_0_.refs_9_, bf16[512,128]{1,0:T(8,128)(2,1)S(1)} %get-tuple-element.260.refs_5_.refs_3_.refs_1_, ...), custom_call_target="tpu_custom_call" | custom-call | flops 3000000000 | bytes 1 | tf_op jit(solution)/shard_map/pallas_call | solution.py:68
  143.3 1.2 collective-permute-start.49
  145.2 1.6 %shard_map.183 = (f32[2,9,64,128]{3,2,1,0:T(8,128)}, f32[2,9,64,128]{3,2,1,0:T(8,128)}, f32[9,64,128]{2,1,0:T(8,128)S(1)}, f32[8,128]{1,0:T(8,128)S(1)}) custom-call(bf16[576,128]{1,0:T(8,128)(2,1)S(1)} %get-tuple-element.295.refs_0_, bf16[576,128]{1,0:T(8,128)(2,1)S(1)} %collective-permute-done.43.refs_1_, ...), custom_call_target="tpu_custom_call" | custom-call | flops 1 | bytes 1 | tf_op jit(solution)/shard_map/pallas_call | solution.py:766
  146.9 1.5 collective-permute-start.51
  149.3 1.1 shard_map.184
  150.4 4.2 %all-to-all-start.4 = ((f32[32,2,128]{2,1,0:T(2,128)}), f32[32,2,128]{2,1,0:T(2,128)S(1)}, u32[]{:S(2)}, u32[]{:S(2)}) async-start(f32[32,2,128]{2,1,0:T(2,128)} %get-tuple-element.304), calls=%async_computation.4 | async-start | bytes 65536 | tf_op jit(solution)/shard_map/all_to_all | solution.py:827
  155.3 1.5 collective-permute-done.51.refs_3_
  157.6 4.2 %all-to-all-done.4.refs_0_ = f32[32,2,128]{2,1,0:T(2,128)S(1)} async-done(((f32[32,2,128]{2,1,0:T(2,128)}), f32[32,2,128]{2,1,0:T(2,128)S(1)}, u32[]{:S(2)}, u32[]{:S(2)}) %all-to-all-start.4) | async-done | bytes 32800 | tf_op jit(solution)/shard_map/all_to_all | solution.py:827
  161.8 1.2 shard_map.187
  (90 shorter events, 15.3 us)
Async XLA Ops:
  0.6 6.9 %copy-start.1 = (bf16[4,8,8,512]{3,2,1,0:T(8,128)(2,1)S(1)}, bf16[4,8,8,512]{3,2,1,0:T(8,128)(2,1)}, u32[]{:S(2)}) copy-start(bf16[4,8,8,512]{3,2,1,0:T(8,128)(2,1)} %param.9) | copy-start | bytes 786436
  0.7 21.7 %copy-start.7 = (s32[4,8,8]{2,1,0:T(8,128)S(1)}, s32[4,8,8]{2,1,0:T(8,128)}, u32[]{:S(2)}) copy-start(s32[4,8,8]{2,1,0:T(8,128)} %refs_5_.4) | copy-start | bytes 3076
  0.7 30.3 %copy-start.6 = (f32[4,512]{1,0:T(4,128)S(1)}, f32[4,512]{1,0:T(4,128)}, u32[]{:S(2)}) copy-start(f32[4,512]{1,0:T(4,128)} %refs_4_.5) | copy-start | bytes 24580
  1.8 35.4 %copy-start.5 = (bf16[4,8,8,512]{3,2,1,0:T(8,128)(2,1)S(1)}, bf16[4,8,8,512]{3,2,1,0:T(8,128)(2,1)}, u32[]{:S(2)}) copy-start(bf16[4,8,8,512]{3,2,1,0:T(8,128)(2,1)} %param.11) | copy-start | bytes 786436
  1.9 8.9 %collective-permute-start = (bf16[9,64,128]{2,1,0:T(8,128)(2,1)S(1)}, bf16[9,64,128]{2,1,0:T(8,128)(2,1)S(1)}, u32[]{:S(2)}, u32[]{:S(2)}) collective-permute-start(bf16[9,64,128]{2,1,0:T(8,128)(2,1)S(1)} %get-tuple-element.166.refs_1_), channel_id=1, source_target_pairs={{0,1},{1,0},{2,3},{3,2},{4,5},{5,4},{6,7},{7,6},{8,9},{9,8},{10,11... | collective-permute-start | bytes 442376 | tf_op jit(solution)/shard_map/ppermute | solution.py:631
  5.0 14.0 %collective-permute-start.1 = (bf16[9,64,128]{2,1,0:T(8,128)(2,1)S(1)}, bf16[9,64,128]{2,1,0:T(8,128)(2,1)S(1)}, u32[]{:S(2)}, u32[]{:S(2)}) collective-permute-start(bf16[9,64,128]{2,1,0:T(8,128)(2,1)S(1)} %get-tuple-element.166.refs_1_), channel_id=1, source_target_pairs={{0,2},{1,3},{2,0},{3,1},{4,6},{5,7},{6,4},{7,5},{8,10},{9,11},{10,... | collective-permute-start | bytes 442376 | tf_op jit(solution)/shard_map/ppermute | solution.py:631
  7.6 11.4 %collective-permute-start.2 = (bf16[9,64,128]{2,1,0:T(8,128)(2,1)S(1)}, bf16[9,64,128]{2,1,0:T(8,128)(2,1)S(1)}, u32[]{:S(2)}, u32[]{:S(2)}) collective-permute-start(bf16[9,64,128]{2,1,0:T(8,128)(2,1)S(1)} %get-tuple-element.166.refs_1_), channel_id=1, source_target_pairs={{0,3},{1,2},{2,1},{3,0},{4,7},{5,6},{6,5},{7,4},{8,11},{9,10},{10,... | collective-permute-start | bytes 442376 | tf_op jit(solution)/shard_map/ppermute | solution.py:631
  7.6 15.4 %collective-permute-start.3 = (bf16[256,512]{1,0:T(8,128)(2,1)S(1)}, bf16[256,512]{1,0:T(8,128)(2,1)S(1)}, u32[]{:S(2)}, u32[]{:S(2)}) collective-permute-start(bf16[256,512]{1,0:T(8,128)(2,1)S(1)} %bitcast.12), channel_id=1, source_target_pairs={{0,8},{8,0},{16,24},{24,16},{1,9},{9,1},{17,25},{25,17},{2,10},{10... | collective-permute-start | bytes 786440 | tf_op jit(solution)/shard_map/ppermute | solution.py:640
  9.3 13.7 %collective-permute-start.4 = (bf16[256,512]{1,0:T(8,128)(2,1)S(1)}, bf16[256,512]{1,0:T(8,128)(2,1)S(1)}, u32[]{:S(2)}, u32[]{:S(2)}) collective-permute-start(bf16[256,512]{1,0:T(8,128)(2,1)S(1)} %bitcast.13), channel_id=1, source_target_pairs={{0,16},{8,24},{16,0},{24,8},{1,17},{9,25},{17,1},{25,9},{2,18},{10... | collective-permute-start | bytes 786440 | tf_op jit(solution)/shard_map/ppermute | solution.py:640
  10.8 12.2 %collective-permute-start.5 = (bf16[256,512]{1,0:T(8,128)(2,1)S(1)}, bf16[256,512]{1,0:T(8,128)(2,1)S(1)}, u32[]{:S(2)}, u32[]{:S(2)}) collective-permute-start(bf16[256,512]{1,0:T(8,128)(2,1)S(1)} %bitcast.14), channel_id=1, source_target_pairs={{0,24},{8,16},{16,8},{24,0},{1,25},{9,17},{17,9},{25,1},{2,26},{10... | collective-permute-start | bytes 786440 | tf_op jit(solution)/shard_map/ppermute | solution.py:640
  19.0 12.0 %collective-permute-start.10 = (bf16[9,64,128]{2,1,0:T(8,128)(2,1)S(1)}, bf16[9,64,128]{2,1,0:T(8,128)(2,1)S(1)}, u32[]{:S(2)}, u32[]{:S(2)}) collective-permute-start(bf16[9,64,128]{2,1,0:T(8,128)(2,1)S(1)} %get-tuple-element.191.refs_1_), channel_id=1, source_target_pairs={{0,2},{1,3},{2,0},{3,1},{4,6},{5,7},{6,4},{7,5},{8,10},{9,11},{10,... | collective-permute-start | bytes 442376 | tf_op jit(solution)/shard_map/ppermute | solution.py:631
  23.0 13.1 %collective-permute-start.6 = (bf16[592,128]{1,0:T(8,128)(2,1)S(1)}, bf16[592,128]{1,0:T(8,128)(2,1)S(1)}, u32[]{:S(2)}, u32[]{:S(2)}) collective-permute-start(bf16[592,128]{1,0:T(8,128)(2,1)S(1)} %get-tuple-element.179), channel_id=1, source_target_pairs={{0,8},{8,0},{16,24},{24,16},{1,9},{9,1},{17,25},{25,17},{2,10},{10... | collective-permute-start | bytes 454664 | tf_op jit(solution)/shard_map/ppermute | solution.py:640
  24.6 11.5 %collective-permute-start.7 = (bf16[592,128]{1,0:T(8,128)(2,1)S(1)}, bf16[592,128]{1,0:T(8,128)(2,1)S(1)}, u32[]{:S(2)}, u32[]{:S(2)}) collective-permute-start(bf16[592,128]{1,0:T(8,128)(2,1)S(1)} %get-tuple-element.180), channel_id=1, source_target_pairs={{0,16},{8,24},{16,0},{24,8},{1,17},{9,25},{17,1},{25,9},{2,18},{10... | collective-permute-start | bytes 454664 | tf_op jit(solution)/shard_map/ppermute | solution.py:640
  26.1 10.0 %collective-permute-start.8 = (bf16[592,128]{1,0:T(8,128)(2,1)S(1)}, bf16[592,128]{1,0:T(8,128)(2,1)S(1)}, u32[]{:S(2)}, u32[]{:S(2)}) collective-permute-start(bf16[592,128]{1,0:T(8,128)(2,1)S(1)} %get-tuple-element.181), channel_id=1, source_target_pairs={{0,24},{8,16},{16,8},{24,0},{1,25},{9,17},{17,9},{25,1},{2,26},{10... | collective-permute-start | bytes 454664 | tf_op jit(solution)/shard_map/ppermute | solution.py:640
  26.6 7.1 %collective-permute-start.11 = (bf16[9,64,128]{2,1,0:T(8,128)(2,1)S(1)}, bf16[9,64,128]{2,1,0:T(8,128)(2,1)S(1)}, u32[]{:S(2)}, u32[]{:S(2)}) collective-permute-start(bf16[9,64,128]{2,1,0:T(8,128)(2,1)S(1)} %get-tuple-element.191.refs_1_), channel_id=1, source_target_pairs={{0,3},{1,2},{2,1},{3,0},{4,7},{5,6},{6,5},{7,4},{8,11},{9,10},{10,... | collective-permute-start | bytes 442376 | tf_op jit(solution)/shard_map/ppermute | solution.py:631
  30.9 5.1 %collective-permute-start.9 = (bf16[9,64,128]{2,1,0:T(8,128)(2,1)S(1)}, bf16[9,64,128]{2,1,0:T(8,128)(2,1)S(1)}, u32[]{:S(2)}, u32[]{:S(2)}) collective-permute-start(bf16[9,64,128]{2,1,0:T(8,128)(2,1)S(1)} %get-tuple-element.191.refs_1_), channel_id=1, source_target_pairs={{0,1},{1,0},{2,3},{3,2},{4,5},{5,4},{6,7},{7,6},{8,9},{9,8},{10,11... | collective-permute-start | bytes 442376 | tf_op jit(solution)/shard_map/ppermute | solution.py:631
  36.1 2.5 %collective-permute-start.12 = (bf16[592,128]{1,0:T(8,128)(2,1)S(1)}, bf16[592,128]{1,0:T(8,128)(2,1)S(1)}, u32[]{:S(2)}, u32[]{:S(2)}) collective-permute-start(bf16[592,128]{1,0:T(8,128)(2,1)S(1)} %get-tuple-element.185.refs_5_), channel_id=1, source_target_pairs={{0,4},{4,0},{1,5},{5,1},{2,6},{6,2},{3,7},{7,3},{8,12},{12,8},{9,1... | collective-permute-start | bytes 454664 | tf_op jit(solution)/shard_map/ppermute | solution.py:634
  36.2 2.4 %collective-permute-start.13 = (bf16[592,128]{1,0:T(8,128)(2,1)S(1)}, bf16[592,128]{1,0:T(8,128)(2,1)S(1)}, u32[]{:S(2)}, u32[]{:S(2)}) collective-permute-start(bf16[592,128]{1,0:T(8,128)(2,1)S(1)} %collective-permute-done.6.refs_6_), channel_id=1, source_target_pairs={{0,4},{4,0},{1,5},{5,1},{2,6},{6,2},{3,7},{7,3},{8,12},{12,8},{9,1... | collective-permute-start | bytes 454664 | tf_op jit(solution)/shard_map/ppermute | solution.py:634
  36.7 1.9 %collective-permute-start.14 = (bf16[592,128]{1,0:T(8,128)(2,1)S(1)}, bf16[592,128]{1,0:T(8,128)(2,1)S(1)}, u32[]{:S(2)}, u32[]{:S(2)}) collective-permute-start(bf16[592,128]{1,0:T(8,128)(2,1)S(1)} %collective-permute-done.7.refs_7_), channel_id=1, source_target_pairs={{0,4},{4,0},{1,5},{5,1},{2,6},{6,2},{3,7},{7,3},{8,12},{12,8},{9,1... | collective-permute-start | bytes 454664 | tf_op jit(solution)/shard_map/ppermute | solution.py:634
  36.8 1.9 %collective-permute-start.15 = (bf16[592,128]{1,0:T(8,128)(2,1)S(1)}, bf16[592,128]{1,0:T(8,128)(2,1)S(1)}, u32[]{:S(2)}, u32[]{:S(2)}) collective-permute-start(bf16[592,128]{1,0:T(8,128)(2,1)S(1)} %collective-permute-done.8.refs_8_), channel_id=1, source_target_pairs={{0,4},{4,0},{1,5},{5,1},{2,6},{6,2},{3,7},{7,3},{8,12},{12,8},{9,1... | collective-permute-start | bytes 454664 | tf_op jit(solution)/shard_map/ppermute | solution.py:634
  41.2 12.2 %collective-permute-start.16 = (bf16[832,128]{1,0:T(8,128)(2,1)S(1)}, bf16[832,128]{1,0:T(8,128)(2,1)S(1)}, u32[]{:S(2)}, u32[]{:S(2)}) collective-permute-start(bf16[832,128]{1,0:T(8,128)(2,1)S(1)} %get-tuple-element.201), channel_id=1, source_target_pairs={{0,8},{8,0},{16,24},{24,16},{1,9},{9,1},{17,25},{25,17},{2,10},{10... | collective-permute-start | bytes 638984 | tf_op jit(solution)/shard_map/ppermute | solution.py:640
  42.8 10.6 %collective-permute-start.17 = (bf16[832,128]{1,0:T(8,128)(2,1)S(1)}, bf16[832,128]{1,0:T(8,128)(2,1)S(1)}, u32[]{:S(2)}, u32[]{:S(2)}) collective-permute-start(bf16[832,128]{1,0:T(8,128)(2,1)S(1)} %get-tuple-element.202), channel_id=1, source_target_pairs={{0,16},{8,24},{16,0},{24,8},{1,17},{9,25},{17,1},{25,9},{2,18},{10... | collective-permute-start | bytes 638984 | tf_op jit(solution)/shard_map/ppermute | solution.py:640
  44.2 10.0 %collective-permute-start.18 = (bf16[832,128]{1,0:T(8,128)(2,1)S(1)}, bf16[832,128]{1,0:T(8,128)(2,1)S(1)}, u32[]{:S(2)}, u32[]{:S(2)}) collective-permute-start(bf16[832,128]{1,0:T(8,128)(2,1)S(1)} %get-tuple-element.203), channel_id=1, source_target_pairs={{0,24},{8,16},{16,8},{24,0},{1,25},{9,17},{17,9},{25,1},{2,26},{10... | collective-permute-start | bytes 638984 | tf_op jit(solution)/shard_map/ppermute | solution.py:640
  55.2 12.9 %collective-permute-start.25 = (bf16[4,9,64,128]{3,2,1,0:T(8,128)(2,1)S(1)}, bf16[4,9,64,128]{3,2,1,0:T(8,128)(2,1)S(1)}, u32[]{:S(2)}, u32[]{:S(2)}) collective-permute-start(bf16[4,9,64,128]{3,2,1,0:T(8,128)(2,1)S(1)} %get-tuple-element.213.refs_9_), channel_id=1, source_target_pairs={{0,4},{4,0},{1,5},{5,1},{2,6},{6,2},{3,7},{7,3},{8,12},{12,8},{9,1... | collective-permute-start | bytes 1769480 | tf_op jit(solution)/shard_map/ppermute | solution.py:634
  55.3 6.0 %collective-permute-start.20 = (bf16[512,128]{1,0:T(8,128)(2,1)S(1)}, bf16[512,128]{1,0:T(8,128)(2,1)S(1)}, u32[]{:S(2)}, u32[]{:S(2)}) collective-permute-start(bf16[512,128]{1,0:T(8,128)(2,1)S(1)} %get-tuple-element.211.refs_1_), channel_id=1, source_target_pairs={{0,16},{8,24},{16,0},{24,8},{1,17},{9,25},{17,1},{25,9},{2,18},{10... | collective-permute-start | bytes 393224 | tf_op jit(solution)/shard_map/ppermute | solution.py:640
  56.8 6.3 %collective-permute-start.22 = (bf16[512,128]{1,0:T(8,128)(2,1)S(1)}, bf16[512,128]{1,0:T(8,128)(2,1)S(1)}, u32[]{:S(2)}, u32[]{:S(2)}) collective-permute-start(bf16[512,128]{1,0:T(8,128)(2,1)S(1)} %get-tuple-element.212.refs_5_), channel_id=1, source_target_pairs={{0,8},{8,0},{16,24},{24,16},{1,9},{9,1},{17,25},{25,17},{2,10},{10... | collective-permute-start | bytes 393224 | tf_op jit(solution)/shard_map/ppermute | solution.py:640
  58.4 7.6 %collective-permute-start.19 = (bf16[512,128]{1,0:T(8,128)(2,1)S(1)}, bf16[512,128]{1,0:T(8,128)(2,1)S(1)}, u32[]{:S(2)}, u32[]{:S(2)}) collective-permute-start(bf16[512,128]{1,0:T(8,128)(2,1)S(1)} %get-tuple-element.211.refs_1_), channel_id=1, source_target_pairs={{0,8},{8,0},{16,24},{24,16},{1,9},{9,1},{17,25},{25,17},{2,10},{10... | collective-permute-start | bytes 393224 | tf_op jit(solution)/shard_map/ppermute | solution.py:640
  58.9 7.1 %collective-permute-start.23 = (bf16[512,128]{1,0:T(8,128)(2,1)S(1)}, bf16[512,128]{1,0:T(8,128)(2,1)S(1)}, u32[]{:S(2)}, u32[]{:S(2)}) collective-permute-start(bf16[512,128]{1,0:T(8,128)(2,1)S(1)} %get-tuple-element.212.refs_5_), channel_id=1, source_target_pairs={{0,16},{8,24},{16,0},{24,8},{1,17},{9,25},{17,1},{25,9},{2,18},{10... | collective-permute-start | bytes 393224 | tf_op jit(solution)/shard_map/ppermute | solution.py:640
  61.3 6.8 %collective-permute-start.21 = (bf16[512,128]{1,0:T(8,128)(2,1)S(1)}, bf16[512,128]{1,0:T(8,128)(2,1)S(1)}, u32[]{:S(2)}, u32[]{:S(2)}) collective-permute-start(bf16[512,128]{1,0:T(8,128)(2,1)S(1)} %collective-permute-done.20.refs_3_), channel_id=1, source_target_pairs={{0,8},{8,0},{16,24},{24,16},{1,9},{9,1},{17,25},{25,17},{2,10},{10... | collective-permute-start | bytes 393224 | tf_op jit(solution)/shard_map/ppermute | solution.py:640
  63.2 5.0 %collective-permute-start.24 = (bf16[512,128]{1,0:T(8,128)(2,1)S(1)}, bf16[512,128]{1,0:T(8,128)(2,1)S(1)}, u32[]{:S(2)}, u32[]{:S(2)}) collective-permute-start(bf16[512,128]{1,0:T(8,128)(2,1)S(1)} %collective-permute-done.22.refs_6_), channel_id=1, source_target_pairs={{0,16},{8,24},{16,0},{24,8},{1,17},{9,25},{17,1},{25,9},{2,18},{10... | collective-permute-start | bytes 393224 | tf_op jit(solution)/shard_map/ppermute | solution.py:640
  70.7 18.8 %copy-start.2 = (bf16[4,9,64,128]{3,2,1,0:T(8,128)(2,1)S(1)}, bf16[4,9,64,128]{3,2,1,0:T(8,128)(2,1)}, u32[]{:S(2)}) copy-start(bf16[4,9,64,128]{3,2,1,0:T(8,128)(2,1)} %get-tuple-element.236.refs_1_) | copy-start | bytes 1769476
  70.8 9.2 %collective-permute-start.26 = (bf16[1024,256]{1,0:T(8,128)(2,1)S(1)}, bf16[1024,256]{1,0:T(8,128)(2,1)S(1)}, u32[]{:S(2)}, u32[]{:S(2)}) collective-permute-start(bf16[1024,256]{1,0:T(8,128)(2,1)S(1)} %get-tuple-element.222), channel_id=1, source_target_pairs={{0,4},{4,0},{1,5},{5,1},{2,6},{6,2},{3,7},{7,3},{8,12},{12,8},{9,1... | collective-permute-start | bytes 1572872 | tf_op jit(solution)/shard_map/ppermute | solution.py:634
  70.8 9.2 %collective-permute-start.27 = (bf16[1024,256]{1,0:T(8,128)(2,1)S(1)}, bf16[1024,256]{1,0:T(8,128)(2,1)S(1)}, u32[]{:S(2)}, u32[]{:S(2)}) collective-permute-start(bf16[1024,256]{1,0:T(8,128)(2,1)S(1)} %get-tuple-element.224), channel_id=1, source_target_pairs={{0,4},{4,0},{1,5},{5,1},{2,6},{6,2},{3,7},{7,3},{8,12},{12,8},{9,1... | collective-permute-start | bytes 1572872 | tf_op jit(solution)/shard_map/ppermute | solution.py:634
  89.5 12.9 %collective-permute-start.34 = (bf16[4,9,64,128]{3,2,1,0:T(8,128)(2,1)S(1)}, bf16[4,9,64,128]{3,2,1,0:T(8,128)(2,1)S(1)}, u32[]{:S(2)}, u32[]{:S(2)}) collective-permute-start(bf16[4,9,64,128]{3,2,1,0:T(8,128)(2,1)S(1)} %copy-done.2), channel_id=1, source_target_pairs={{0,4},{4,0},{1,5},{5,1},{2,6},{6,2},{3,7},{7,3},{8,12},{12,8},{9,1... | collective-permute-start | bytes 1769480 | tf_op jit(solution)/shard_map/ppermute | solution.py:634
  89.7 8.9 %collective-permute-start.35 = (bf16[1024,128]{1,0:T(8,128)(2,1)S(1)}, bf16[1024,128]{1,0:T(8,128)(2,1)S(1)}, u32[]{:S(2)}, u32[]{:S(2)}) collective-permute-start(bf16[1024,128]{1,0:T(8,128)(2,1)S(1)} %get-tuple-element.243), channel_id=1, source_target_pairs={{0,4},{4,0},{1,5},{5,1},{2,6},{6,2},{3,7},{7,3},{8,12},{12,8},{9,1... | collective-permute-start | bytes 786440 | tf_op jit(solution)/shard_map/ppermute | solution.py:634
  90.1 5.5 %collective-permute-start.29 = (bf16[512,128]{1,0:T(8,128)(2,1)S(1)}, bf16[512,128]{1,0:T(8,128)(2,1)S(1)}, u32[]{:S(2)}, u32[]{:S(2)}) collective-permute-start(bf16[512,128]{1,0:T(8,128)(2,1)S(1)} %get-tuple-element.234.refs_1_.refs_3_), channel_id=1, source_target_pairs={{0,16},{8,24},{16,0},{24,8},{1,17},{9,25},{17,1},{25,9},{2,18},{10... | collective-permute-start | bytes 393224 | tf_op jit(solution)/shard_map/ppermute | solution.py:640
  91.6 6.4 %collective-permute-start.31 = (bf16[512,128]{1,0:T(8,128)(2,1)S(1)}, bf16[512,128]{1,0:T(8,128)(2,1)S(1)}, u32[]{:S(2)}, u32[]{:S(2)}) collective-permute-start(bf16[512,128]{1,0:T(8,128)(2,1)S(1)} %get-tuple-element.235.refs_5_.refs_4_), channel_id=1, source_target_pairs={{0,8},{8,0},{16,24},{24,16},{1,9},{9,1},{17,25},{25,17},{2,10},{10... | collective-permute-start | bytes 393224 | tf_op jit(solution)/shard_map/ppermute | solution.py:640
  92.2 11.5 %collective-permute-start.28 = (bf16[512,128]{1,0:T(8,128)(2,1)S(1)}, bf16[512,128]{1,0:T(8,128)(2,1)S(1)}, u32[]{:S(2)}, u32[]{:S(2)}) collective-permute-start(bf16[512,128]{1,0:T(8,128)(2,1)S(1)} %get-tuple-element.234.refs_1_.refs_3_), channel_id=1, source_target_pairs={{0,8},{8,0},{16,24},{24,16},{1,9},{9,1},{17,25},{25,17},{2,10},{10... | collective-permute-start | bytes 393224 | tf_op jit(solution)/shard_map/ppermute | solution.py:640
  95.6 8.1 %collective-permute-start.32 = (bf16[512,128]{1,0:T(8,128)(2,1)S(1)}, bf16[512,128]{1,0:T(8,128)(2,1)S(1)}, u32[]{:S(2)}, u32[]{:S(2)}) collective-permute-start(bf16[512,128]{1,0:T(8,128)(2,1)S(1)} %get-tuple-element.235.refs_5_.refs_4_), channel_id=1, source_target_pairs={{0,16},{8,24},{16,0},{24,8},{1,17},{9,25},{17,1},{25,9},{2,18},{10... | collective-permute-start | bytes 393224 | tf_op jit(solution)/shard_map/ppermute | solution.py:640
  98.0 5.8 %collective-permute-start.30 = (bf16[512,128]{1,0:T(8,128)(2,1)S(1)}, bf16[512,128]{1,0:T(8,128)(2,1)S(1)}, u32[]{:S(2)}, u32[]{:S(2)}) collective-permute-start(bf16[512,128]{1,0:T(8,128)(2,1)S(1)} %collective-permute-done.29.refs_3_), channel_id=1, source_target_pairs={{0,8},{8,0},{16,24},{24,16},{1,9},{9,1},{17,25},{25,17},{2,10},{10... | collective-permute-start | bytes 393224 | tf_op jit(solution)/shard_map/ppermute | solution.py:640
  98.6 5.2 %collective-permute-start.33 = (bf16[512,128]{1,0:T(8,128)(2,1)S(1)}, bf16[512,128]{1,0:T(8,128)(2,1)S(1)}, u32[]{:S(2)}, u32[]{:S(2)}) collective-permute-start(bf16[512,128]{1,0:T(8,128)(2,1)S(1)} %collective-permute-done.31.refs_6_), channel_id=1, source_target_pairs={{0,16},{8,24},{16,0},{24,8},{1,17},{9,25},{17,1},{25,9},{2,18},{10... | collective-permute-start | bytes 393224 | tf_op jit(solution)/shard_map/ppermute | solution.py:640
  106.2 11.5 %collective-permute-start.36 = (bf16[832,128]{1,0:T(8,128)(2,1)S(1)}, bf16[832,128]{1,0:T(8,128)(2,1)S(1)}, u32[]{:S(2)}, u32[]{:S(2)}) collective-permute-start(bf16[832,128]{1,0:T(8,128)(2,1)S(1)} %get-tuple-element.251), channel_id=1, source_target_pairs={{0,8},{8,0},{16,24},{24,16},{1,9},{9,1},{17,25},{25,17},{2,10},{10... | collective-permute-start | bytes 638984 | tf_op jit(solution)/shard_map/ppermute | solution.py:640
  107.5 10.2 %collective-permute-start.37 = (bf16[832,128]{1,0:T(8,128)(2,1)S(1)}, bf16[832,128]{1,0:T(8,128)(2,1)S(1)}, u32[]{:S(2)}, u32[]{:S(2)}) collective-permute-start(bf16[832,128]{1,0:T(8,128)(2,1)S(1)} %get-tuple-element.252), channel_id=1, source_target_pairs={{0,16},{8,24},{16,0},{24,8},{1,17},{9,25},{17,1},{25,9},{2,18},{10... | collective-permute-start | bytes 638984 | tf_op jit(solution)/shard_map/ppermute | solution.py:640
  108.2 9.5 %collective-permute-start.38 = (bf16[832,128]{1,0:T(8,128)(2,1)S(1)}, bf16[832,128]{1,0:T(8,128)(2,1)S(1)}, u32[]{:S(2)}, u32[]{:S(2)}) collective-permute-start(bf16[832,128]{1,0:T(8,128)(2,1)S(1)} %get-tuple-element.253), channel_id=1, source_target_pairs={{0,24},{8,16},{16,8},{24,0},{1,25},{9,17},{17,9},{25,1},{2,26},{10... | collective-permute-start | bytes 638984 | tf_op jit(solution)/shard_map/ppermute | solution.py:640
  118.0 2.0 %collective-permute-start.39 = (bf16[1024,128]{1,0:T(8,128)(2,1)S(1)}, bf16[1024,128]{1,0:T(8,128)(2,1)S(1)}, u32[]{:S(2)}, u32[]{:S(2)}) collective-permute-start(bf16[1024,128]{1,0:T(8,128)(2,1)S(1)} %get-tuple-element.265), channel_id=1, source_target_pairs={{0,4},{4,0},{1,5},{5,1},{2,6},{6,2},{3,7},{7,3},{8,12},{12,8},{9,1... | collective-permute-start | bytes 786440 | tf_op jit(solution)/shard_map/ppermute | solution.py:634
  118.9 8.2 %collective-permute-start.43 = (bf16[576,128]{1,0:T(8,128)(2,1)S(1)}, bf16[576,128]{1,0:T(8,128)(2,1)S(1)}, u32[]{:S(2)}, u32[]{:S(2)}) collective-permute-start(bf16[576,128]{1,0:T(8,128)(2,1)S(1)} %get-tuple-element.276), channel_id=1, source_target_pairs={{0,1},{1,0},{2,3},{3,2},{4,5},{5,4},{6,7},{7,6},{8,9},{9,8},{10,11... | collective-permute-start | bytes 442376 | tf_op jit(solution)/shard_map/ppermute | solution.py:631
  119.5 10.8 %collective-permute-start.44 = (bf16[576,128]{1,0:T(8,128)(2,1)S(1)}, bf16[576,128]{1,0:T(8,128)(2,1)S(1)}, u32[]{:S(2)}, u32[]{:S(2)}) collective-permute-start(bf16[576,128]{1,0:T(8,128)(2,1)S(1)} %get-tuple-element.277), channel_id=1, source_target_pairs={{0,2},{1,3},{2,0},{3,1},{4,6},{5,7},{6,4},{7,5},{8,10},{9,11},{10,... | collective-permute-start | bytes 442376 | tf_op jit(solution)/shard_map/ppermute | solution.py:631
  122.5 7.9 %collective-permute-start.40 = (bf16[576,128]{1,0:T(8,128)(2,1)S(1)}, bf16[576,128]{1,0:T(8,128)(2,1)S(1)}, u32[]{:S(2)}, u32[]{:S(2)}) collective-permute-start(bf16[576,128]{1,0:T(8,128)(2,1)S(1)} %get-tuple-element.272), channel_id=1, source_target_pairs={{0,8},{8,0},{16,24},{24,16},{1,9},{9,1},{17,25},{25,17},{2,10},{10... | collective-permute-start | bytes 442376 | tf_op jit(solution)/shard_map/ppermute | solution.py:640
  123.7 6.8 %collective-permute-start.41 = (bf16[576,128]{1,0:T(8,128)(2,1)S(1)}, bf16[576,128]{1,0:T(8,128)(2,1)S(1)}, u32[]{:S(2)}, u32[]{:S(2)}) collective-permute-start(bf16[576,128]{1,0:T(8,128)(2,1)S(1)} %get-tuple-element.273), channel_id=1, source_target_pairs={{0,16},{8,24},{16,0},{24,8},{1,17},{9,25},{17,1},{25,9},{2,18},{10... | collective-permute-start | bytes 442376 | tf_op jit(solution)/shard_map/ppermute | solution.py:640
  124.5 8.0 %collective-permute-start.42 = (bf16[576,128]{1,0:T(8,128)(2,1)S(1)}, bf16[576,128]{1,0:T(8,128)(2,1)S(1)}, u32[]{:S(2)}, u32[]{:S(2)}) collective-permute-start(bf16[576,128]{1,0:T(8,128)(2,1)S(1)} %get-tuple-element.274), channel_id=1, source_target_pairs={{0,24},{8,16},{16,8},{24,0},{1,25},{9,17},{17,9},{25,1},{2,26},{10... | collective-permute-start | bytes 442376 | tf_op jit(solution)/shard_map/ppermute | solution.py:640
  127.1 7.2 %collective-permute-start.45 = (bf16[576,128]{1,0:T(8,128)(2,1)S(1)}, bf16[576,128]{1,0:T(8,128)(2,1)S(1)}, u32[]{:S(2)}, u32[]{:S(2)}) collective-permute-start(bf16[576,128]{1,0:T(8,128)(2,1)S(1)} %get-tuple-element.278), channel_id=1, source_target_pairs={{0,3},{1,2},{2,1},{3,0},{4,7},{5,6},{6,5},{7,4},{8,11},{9,10},{10,... | collective-permute-start | bytes 442376 | tf_op jit(solution)/shard_map/ppermute | solution.py:631
  135.0 11.9 %collective-permute-start.46 = (bf16[576,128]{1,0:T(8,128)(2,1)S(1)}, bf16[576,128]{1,0:T(8,128)(2,1)S(1)}, u32[]{:S(2)}, u32[]{:S(2)}) collective-permute-start(bf16[576,128]{1,0:T(8,128)(2,1)S(1)} %get-tuple-element.292), channel_id=1, source_target_pairs={{0,1},{1,0},{2,3},{3,2},{4,5},{5,4},{6,7},{7,6},{8,9},{9,8},{10,11... | collective-permute-start | bytes 442376 | tf_op jit(solution)/shard_map/ppermute | solution.py:631
  137.1 12.2 %collective-permute-start.47 = (bf16[576,128]{1,0:T(8,128)(2,1)S(1)}, bf16[576,128]{1,0:T(8,128)(2,1)S(1)}, u32[]{:S(2)}, u32[]{:S(2)}) collective-permute-start(bf16[576,128]{1,0:T(8,128)(2,1)S(1)} %get-tuple-element.293), channel_id=1, source_target_pairs={{0,2},{1,3},{2,0},{3,1},{4,6},{5,7},{6,4},{7,5},{8,10},{9,11},{10,... | collective-permute-start | bytes 442376 | tf_op jit(solution)/shard_map/ppermute | solution.py:631
  137.6 11.6 %collective-permute-start.48 = (bf16[576,128]{1,0:T(8,128)(2,1)S(1)}, bf16[576,128]{1,0:T(8,128)(2,1)S(1)}, u32[]{:S(2)}, u32[]{:S(2)}) collective-permute-start(bf16[576,128]{1,0:T(8,128)(2,1)S(1)} %get-tuple-element.294), channel_id=1, source_target_pairs={{0,3},{1,2},{2,1},{3,0},{4,7},{5,6},{6,5},{7,4},{8,11},{9,10},{10,... | collective-permute-start | bytes 442376 | tf_op jit(solution)/shard_map/ppermute | solution.py:631
  139.5 5.7 %copy-start = (f32[2,9,64,128]{3,2,1,0:T(8,128)S(1)}, f32[2,9,64,128]{3,2,1,0:T(8,128)}, u32[]{:S(2)}) copy-start(f32[2,9,64,128]{3,2,1,0:T(8,128)} %refs_1_.3) | copy-start | bytes 1769476
  139.5 5.7 %copy-start.3 = (f32[2,9,64,128]{3,2,1,0:T(8,128)S(1)}, f32[2,9,64,128]{3,2,1,0:T(8,128)}, u32[]{:S(2)}) copy-start(f32[2,9,64,128]{3,2,1,0:T(8,128)} %refs_5_.6) | copy-start | bytes 1769476
  139.5 5.7 %copy-start.4 = (f32[2,9,64,128]{3,2,1,0:T(8,128)S(1)}, f32[2,9,64,128]{3,2,1,0:T(8,128)}, u32[]{:S(2)}) copy-start(f32[2,9,64,128]{3,2,1,0:T(8,128)} %refs_6_.4) | copy-start | bytes 1769476
  143.3 12.0 %collective-permute-start.49 = (bf16[256,512]{1,0:T(8,128)(2,1)}, bf16[256,512]{1,0:T(8,128)(2,1)S(1)}, u32[]{:S(2)}, u32[]{:S(2)}) collective-permute-start(bf16[256,512]{1,0:T(8,128)(2,1)} %get-tuple-element.307), channel_id=1, source_target_pairs={{0,8},{8,0},{16,24},{24,16},{1,9},{9,1},{17,25},{25,17},{2,10},{10... | collective-permute-start | bytes 786440 | tf_op jit(solution)/shard_map/ppermute | solution.py:640
  144.5 10.8 %collective-permute-start.50 = (bf16[256,512]{1,0:T(8,128)(2,1)S(1)}, bf16[256,512]{1,0:T(8,128)(2,1)S(1)}, u32[]{:S(2)}, u32[]{:S(2)}) collective-permute-start(bf16[256,512]{1,0:T(8,128)(2,1)S(1)} %get-tuple-element.308), channel_id=1, source_target_pairs={{0,16},{8,24},{16,0},{24,8},{1,17},{9,25},{17,1},{25,9},{2,18},{10... | collective-permute-start | bytes 786440 | tf_op jit(solution)/shard_map/ppermute | solution.py:640
  146.9 9.9 %collective-permute-start.51 = (bf16[256,512]{1,0:T(8,128)(2,1)S(1)}, bf16[256,512]{1,0:T(8,128)(2,1)S(1)}, u32[]{:S(2)}, u32[]{:S(2)}) collective-permute-start(bf16[256,512]{1,0:T(8,128)(2,1)S(1)} %get-tuple-element.309), channel_id=1, source_target_pairs={{0,24},{8,16},{16,8},{24,0},{1,25},{9,17},{17,9},{25,1},{2,26},{10... | collective-permute-start | bytes 786440 | tf_op jit(solution)/shard_map/ppermute | solution.py:640
  150.4 11.4 %copy-start.8 = (f32[4,512]{1,0:T(4,128)S(1)}, f32[4,512]{1,0:T(4,128)}, u32[]{:S(2)}) copy-start(f32[4,512]{1,0:T(4,128)} %refs_5_.7) | copy-start | bytes 24580
  150.4 11.4 %copy-start.9 = (f32[4,512]{1,0:T(4,128)S(1)}, f32[4,512]{1,0:T(4,128)}, u32[]{:S(2)}) copy-start(f32[4,512]{1,0:T(4,128)} %refs_6_.5) | copy-start | bytes 24580
  150.4 11.4 %all-to-all-start.4 = ((f32[32,2,128]{2,1,0:T(2,128)}), f32[32,2,128]{2,1,0:T(2,128)S(1)}, u32[]{:S(2)}, u32[]{:S(2)}) async-start(f32[32,2,128]{2,1,0:T(2,128)} %get-tuple-element.304), calls=%async_computation.4 | async-start | bytes 65536 | tf_op jit(solution)/shard_map/all_to_all | solution.py:827
